TPU v7x, 32 devices: a whole 2x2x4 slice. The times are simulated.
32 devices in a mesh: space: 8 (over y, x, core), band: 4 (over z).
Axes of the slice: x: 2, y: 2, z: 4, core: 2. Of those that a mesh axis runs over, the one named last changes fastest.
Arguments:
- orbitals: float32 [32, 48, 32, 128], P('band', 'space'), may hold values from -18 to 18
- previous: float32 [32, 48, 32, 128], P('band', 'space'), may hold values from -18 to 18
- potential: float32 [48, 32, 128], P('space'), may hold values from -4 to 4
- projectors: bfloat16 [32, 9, 6, 32, 128], P('space'), may hold values from -0.1875 to 0.1875
- strengths: float32 [32, 9], replicated, may hold values from -3 to 3
- atom_planes: int32 [32], replicated, may hold values from 0 to 47, as said below
Outputs:
- filtered: bfloat16 [32, 48, 32, 128], P('band', 'space')
- margin: float32 [32, 32], P('space', 'band')
- projection: float32 [32, 32], P('space', 'band')
Inputs may be any that keep to these rules, and one draw needn't show every extreme that they name: `atom_planes`: entry a is the first plane of atom a's box of 6 planes. In each aligned block of 4 entries (block s) every box starts at one of the planes s * 6 to s * 6 + 5, and in every block one atom starts at the first of these planes and another at the last.
All inputs are finite; a program needn't handle non-finite values.
Results may differ from a plain program's by a relative error of at most 0.0065.
Values may be sent and summed in bfloat16 or wider, within the bound.
No kernel may reach another device: no remote copies, remote signals or barrier semaphores. Data moves between devices by JAX's collectives and lax.ppermute only.
A program may use at most 192 MiB of HBM per device.

v0:
```python
import jax
import jax.numpy as jnp
from jax import lax
from jax.sharding import PartitionSpec as P

HALO = 6
BOX = 6
NPJ = 9


stencil_weights = (
    -5369.0 / 1800.0,
    12.0 / 7.0,
    -15.0 / 56.0,
    10.0 / 189.0,
    -1.0 / 112.0,
    2.0 / 1925.0,
    -1.0 / 16632.0,
)
center = 5.5
halfwidth = 5.5


def with_halo(block, sides, width):
    for axis, dim in sides:
        count = lax.axis_size(axis)
        forward = [(i, i + 1) for i in range(count - 1)]
        forward.append((count - 1, 0))
        backward = [(target, source) for source, target in forward]
        low = lax.ppermute(
            lax.slice_in_dim(block, block.shape[dim] - width, None, axis=dim), axis, forward
        )
        high = lax.ppermute(lax.slice_in_dim(block, 0, width, axis=dim), axis, backward)
        block = jnp.concatenate([low, block, high], axis=dim)
    return block


def shifted(value, axis, steps):
    count = lax.axis_size(axis)
    pairs = [(source, (source + steps) % count) for source in range(count)]
    return lax.ppermute(value, axis, pairs)


def laplace_axis(field, axis):
    total = stencil_weights[0] * field
    for offset in range(1, HALO + 1):
        total = total + stencil_weights[offset] * (
            jnp.roll(field, offset, axis) + jnp.roll(field, -offset, axis)
        )
    return total


def place_table(first_planes, projector_block, base, window, total_planes):
    box_rows = jnp.arange(BOX, dtype=jnp.int32)
    planes_out = jnp.arange(window, dtype=jnp.int32)
    relative = (first_planes[:, None] + box_rows[None, :] - base) % total_planes
    placer = (planes_out[None, None, :] == relative[:, :, None]).astype(jnp.float32)
    return jnp.einsum(
        "apq,ajpyz->ajqyz",
        placer,
        projector_block.astype(jnp.float32),
        precision=lax.Precision.HIGHEST,
    )


def shards(orbitals, previous, potential, projectors, strengths, atom_planes):
    band_dev, slab_planes, cells_y, cells_z = orbitals.shape
    space_count = lax.axis_size("space")
    total_planes = slab_planes * space_count
    extended = with_halo(orbitals, (("space", 1),), HALO)
    along_x = stencil_weights[0] * orbitals
    for offset in range(1, HALO + 1):
        ahead = extended[:, HALO + offset : HALO + offset + slab_planes]
        behind = extended[:, HALO - offset : HALO - offset + slab_planes]
        along_x = along_x + stencil_weights[offset] * (ahead + behind)
    kinetic = -0.5 * (along_x + laplace_axis(orbitals, 2) + laplace_axis(orbitals, 3))
    device_index = lax.axis_index("space")
    atom_count = projectors.shape[0]
    own_start = device_index * atom_count
    own_planes = lax.dynamic_slice_in_dim(atom_planes, own_start, atom_count, 0)
    own_strengths = lax.dynamic_slice_in_dim(strengths, own_start, atom_count, 0)
    table = place_table(
        own_planes, projectors, device_index * slab_planes, slab_planes + HALO, total_planes
    )
    table_flat = table.reshape(atom_count * NPJ, -1)
    upper = extended[:, HALO:].reshape(band_dev, -1)
    coefficients = lax.dot_general(
        table_flat,
        upper,
        (((1,), (1,)), ((), ())),
        precision=lax.Precision.HIGHEST,
        preferred_element_type=jnp.float32,
    )
    weighted = coefficients * own_strengths.reshape(-1)[:, None]
    added = lax.dot_general(
        weighted,
        table_flat,
        (((0,), (0,)), ((), ())),
        precision=lax.Precision.HIGHEST,
        preferred_element_type=jnp.float32,
    )
    added = added.reshape(band_dev, slab_planes + HALO, cells_y, cells_z)
    arrived = shifted(added[:, slab_planes:].astype(jnp.bfloat16), "space", 1).astype(jnp.float32)
    padding = jnp.zeros((band_dev, slab_planes - HALO, cells_y, cells_z), jnp.float32)
    projected_term = added[:, :slab_planes] + jnp.concatenate([arrived, padding], 1)
    hamil = kinetic + potential[None] * orbitals + projected_term
    filtered = (2.0 / halfwidth * (hamil - center * orbitals) - previous).astype(jnp.bfloat16)
    scale = 1.0 / (slab_planes * space_count * cells_y * cells_z)
    filtered_flat = filtered.reshape(band_dev, -1)
    panel_flat = orbitals.astype(jnp.bfloat16).reshape(band_dev, -1)
    columns_right = jnp.concatenate([filtered_flat, panel_flat], 0)
    piece = lax.all_gather(filtered, "band", axis=0, tiled=True)
    rows = piece.reshape(piece.shape[0], -1)
    products = lax.dot_general(
        rows, columns_right, (((1,), (1,)), ((), ())), preferred_element_type=jnp.float32
    )
    partial_sums = products * scale
    shares = lax.psum_scatter(partial_sums, "space", scatter_dimension=0, tiled=True)
    margin = shares[:, :band_dev]
    projection = shares[:, band_dev:]
    return (filtered, margin, projection)


def solution(mesh):
    in_specs = (
        P("band", "space", None, None),
        P("band", "space", None, None),
        P("space", None, None),
        P("space", None, None, None, None),
        P(),
        P(),
    )
    out_specs = (P("band", "space", None, None), P("space", "band"), P("space", "band"))
    return jax.shard_map(shards, mesh=mesh, in_specs=in_specs, out_specs=out_specs, check_vma=False)
```

profile of v0, /device:TPU:0, one launch (start us, length us, event | category | flops | bytes accessed | tf_op | source)
XLA Modules:
  0.0 171.8 jit_solution(11825079170893317238)
XLA Ops:
  7.2 1.7 copy.130
  8.9 0.5 collective-permute-start.1
  9.4 2.9 %collective-permute-start = (f32[8,6,32,128]{3,0,2,1:T(8,128)S(1)}, f32[8,6,32,128]{3,0,2,1:T(8,128)}, u32[]{:S(2)}, u32[]{:S(2)}) collective-permute-start(f32[8,6,32,128]{3,0,2,1:T(8,128)S(1)} %copy.130), channel_id=1, source_target_pairs={{4,0},{8,4},{12,8},{16,12},{20,16},{24,20},{28,24},{0,28},{5,1},{9... | collective-permute-start | bytes 2359304 | tf_op jit(solution)/shard_map/ppermute | solution.py:33
  12.4 1.2 fusion.86
  13.6 1.2 fusion.84
  14.8 1.2 fusion.82
  16.0 0.7 fusion.83
  16.7 1.2 fusion.80
  17.9 0.7 fusion.81
  18.6 1.2 fusion.78
  19.8 0.7 fusion.79
  20.5 1.1 fusion.76
  21.7 0.7 fusion.77
  22.3 1.4 fusion.74
  23.7 1.4 fusion.75
  25.2 1.4 fusion.72
  26.6 1.4 fusion.73
  28.1 1.4 fusion.70
  29.5 1.4 fusion.71
  30.9 1.4 fusion.68
  32.3 1.4 fusion.69
  33.7 1.5 fusion.66
  35.3 1.7 %convolution_bitcast_fusion = f32[4,9,12,32,128]{4,2,3,1,0:T(8,128)S(1)} fusion(bf16[4,9,6,32,128]{4,3,2,1,0:T(8,128)(2,1)S(1)} %copy-done, s32[4,6]{1,0:T(4,128)S(1)} %add_select_fusion), kind=kOutput, calls=%fused_computation.2 | convolution fusion | flops 21233952 | bytes 8847456 | tf_op jit(solution)/shard_map/apq,ajpyz->ajqyz/dot_general | solution.py:58
  37.1 5.9 %copy.185 = f32[4,9,12,32,128]{4,3,2,1,0:T(8,128)} copy(f32[4,9,12,32,128]{4,2,3,1,0:T(8,128)S(1)} %convolution_bitcast_fusion) | data formatting | bytes 14155776 | tf_op jit(solution)/shard_map/apq,ajpyz->ajqyz/transpose | solution.py:58
  43.0 7.8 %reshape.53 = f32[36,49152]{1,0:T(8,128)} reshape(f32[4,9,12,32,128]{4,3,2,1,0:T(8,128)} %copy.185) | data formatting | bytes 14155776 | tf_op jit(solution)/shard_map/reshape | solution.py:85
  50.8 1.4 fusion.67
  52.3 0.1 copy.186
  52.5 4.7 %copy.194 = f32[5,8,384,128]{3,2,1,0:T(8,128)S(1)} copy(f32[5,8,384,128]{3,1,2,0:T(8,128)} %bitcast.38) | data formatting | bytes 15728640
  57.2 0.7 slice.369
  58.0 1.4 fusion.64
  59.4 1.9 %constant_dynamic-update-slice_fusion.3 = f32[8,12,32,128]{3,0,2,1:T(8,128)S(1)} fusion(f32[8,6,32,128]{3,0,2,1:T(8,128)} %collective-permute-done.1), kind=kLoop, calls=%fused_computation.82 | loop fusion | bytes 1572864
  61.3 0.2 copy-done.2
  61.4 0.5 constant_dynamic-update-slice_fusion.2
  61.9 1.2 constant_dynamic-update-slice_fusion
  63.1 6.2 %fusion.9 = f32[36,8,1,1]{0,1,3,2:T(8,128)S(1)} fusion(f32[36,49152]{1,0:T(8,128)S(1)} %bitcast.40, f32[8,49152]{1,0:T(8,128)S(1)} %bitcast.43, f32[36]{0:T(128)S(1)} %mul.132), kind=kOutput, calls=%fused_computation.9 | convolution fusion | flops 169869600 | bytes 8652048 | tf_op jit(solution)/shard_map/dot_general | solution.py:87
  69.3 8.1 %fusion = f32[8,12,32,128]{3,0,2,1:T(8,128)S(1)} fusion(f32[36,8,1,1]{0,1,3,2:T(8,128)S(1)} %fusion.9, f32[12,32,128,36]{2,1,0,3:T(8,128)S(1)} %bitcast.41), kind=kOutput, calls=%fused_computation | convolution fusion | flops 169869312 | bytes 8651904 | tf_op jit(solution)/shard_map/dot_general | solution.py:95
  77.6 1.5 fusion.65
  79.1 6.7 %collective-permute-done.2 = bf16[8,6,32,128]{3,0,2,1:T(8,128)(2,1)} collective-permute-done((bf16[8,6,32,128]{3,0,2,1:T(8,128)(2,1)S(1)}, bf16[8,6,32,128]{3,0,2,1:T(8,128)(2,1)}, u32[]{:S(2)}, u32[]{:S(2)}) %collective-permute-start.2) | collective-permute-done | bytes 393248 | tf_op jit(solution)/shard_map/ppermute | solution.py:41
  85.8 12.3 %fusion.14 = bf16[8,6,32,128]{3,0,2,1:T(8,128)(2,1)} fusion(f32[8,12,32,128]{3,0,2,1:T(8,128)S(1)} %fusion, f32[8,12,32,128]{3,0,2,1:T(8,128)S(1)} %get-tuple-element.60, f32[8,12,32,128]{3,0,2,1:T(8,128)S(1)} %constant_dynamic-update-slice_fusion, f32[8,6,31,128]{3,0,2,1:T(8,128)} %get-tuple-element.57, f32[8,6,1,128]{3,0,2,1:T(8,128)S(1)} %get-tuple-element.59, ...), kind=kLoop, calls=%fused_computation.16 | loop fusion | flops 18087936 | bytes 31555584 | tf_op jit(solution)/shard_map/convert_element_type | solution.py:107
  98.2 0.3 copy.212
  98.4 0.3 copy-done.13
  98.7 0.6 dynamic-slice
  99.9 0.8 copy.191
  100.8 36.2 %all-gather.2.cloned.1.call-done = bf16[32,6,32,128]{3,0,2,1:T(8,128)(2,1)} async-done(((bf16[8,6,32,128]{3,0,2,1:T(8,128)(2,1)}), bf16[32,6,32,128]{3,0,2,1:T(8,128)(2,1)}) %all-gather.2.cloned.1.call-update) | async-done | bytes 1572880 | tf_op jit(solution)/shard_map/all_gather | solution.py:112
  137.0 2.0 %copy.190 = bf16[32,6,32,128]{3,2,1,0:T(8,128)(2,1)S(1)} copy(bf16[32,6,32,128]{3,0,2,1:T(8,128)(2,1)} %all-gather.2.cloned.1.call-done) | data formatting | bytes 3145728 | tf_op jit(solution)/shard_map/all_gather | solution.py:112
  139.0 1.0 fusion.6
  140.1 24.3 %all-reduce = f32[32,16]{1,0:T(8,128)S(1)} all-reduce(f32[32,16]{1,0:T(8,128)S(1)} %fusion.6), channel_id=2, replica_groups=mesh['space'=8,'band'=4] {'space'}, use_global_device_ids=true, to_apply=%region_0.1.clone | all-reduce | flops 512 | bytes 4096
  164.3 0.7 fusion.88
  (45 shorter events, 0.7 us)
Async XLA Ops:
  7.2 28.2 %copy-start = (bf16[4,9,6,32,128]{4,3,2,1,0:T(8,128)(2,1)S(1)}, bf16[4,9,6,32,128]{4,3,2,1,0:T(8,128)(2,1)}, u32[]{:S(2)}) copy-start(bf16[4,9,6,32,128]{4,3,2,1,0:T(8,128)(2,1)} %param.9) | copy-start | bytes 5308420
  7.2 129.8 %all-gather.2.cloned.1.call-start = ((), (), s32[]{:S(2)}) async-start(), calls=%async_computation | async-start | bytes 1966080 | tf_op jit(solution)/shard_map/all_gather | solution.py:112
  8.9 50.4 %collective-permute-start.1 = (f32[8,6,32,128]{3,0,2,1:T(8,128)S(1)}, f32[8,6,32,128]{3,0,2,1:T(8,128)}, u32[]{:S(2)}, u32[]{:S(2)}) collective-permute-start(f32[8,6,32,128]{3,0,2,1:T(8,128)S(1)} %copy.130), channel_id=1, source_target_pairs={{0,4},{4,8},{8,12},{12,16},{16,20},{20,24},{24,28},{28,0},{1,5},{5... | collective-permute-start | bytes 2359304 | tf_op jit(solution)/shard_map/ppermute | solution.py:30
  9.4 52.5 %collective-permute-start = (f32[8,6,32,128]{3,0,2,1:T(8,128)S(1)}, f32[8,6,32,128]{3,0,2,1:T(8,128)}, u32[]{:S(2)}, u32[]{:S(2)}) collective-permute-start(f32[8,6,32,128]{3,0,2,1:T(8,128)S(1)} %copy.130), channel_id=1, source_target_pairs={{4,0},{8,4},{12,8},{16,12},{20,16},{24,20},{28,24},{0,28},{5,1},{9... | collective-permute-start | bytes 2359304 | tf_op jit(solution)/shard_map/ppermute | solution.py:33
  33.7 1.5 copy-start.12
  50.8 1.5 copy-start.11
  57.2 5.9 %slice-start = ((s8[7864320]{0:T(1024)(128)(4,1)}), s8[4194304]{0:T(1024)(128)(4,1)S(1)}, s32[]{:S(2)}) async-start(s8[7864320]{0:T(1024)(128)(4,1)} %bitcast.39), calls=%async_computation.1 | async-start | bytes 8388608
  57.2 5.9 %slice-start.1 = ((s8[7864320]{0:T(1024)(128)(4,1)}), s8[3670016]{0:T(1024)(128)(4,1)S(1)}, s32[]{:S(2)}) async-start(s8[7864320]{0:T(1024)(128)(4,1)} %bitcast.39), calls=%async_computation.2 | async-start | bytes 7340032
  59.4 2.1 %copy-start.2 = (f32[8,6,32,128]{3,2,1,0:T(8,128)S(1)}, f32[8,6,32,128]{3,2,1,0:T(8,128)}, u32[]{:S(2)}) copy-start(f32[8,6,32,128]{3,2,1,0:T(8,128)} %param.6) | copy-start | bytes 2359300
  69.3 16.4 %copy-start.8 = (f32[8,6,32,126]{3,0,2,1:T(8,128)S(1)}, f32[8,6,32,126]{3,0,2,1:T(8,128)}, u32[]{:S(2)}) copy-start(f32[8,6,32,126]{3,0,2,1:T(8,128)} %get-tuple-element.28) | copy-start | bytes 2322436
  69.3 16.4 %copy-start.9 = (f32[8,6,32,126]{3,0,2,1:T(8,128)S(1)}, f32[8,6,32,126]{3,0,2,1:T(8,128)}, u32[]{:S(2)}) copy-start(f32[8,6,32,126]{3,0,2,1:T(8,128)} %get-tuple-element.29) | copy-start | bytes 2322436
  69.3 16.4 %copy-start.10 = (f32[8,6,6,128]{3,0,2,1:T(8,128)S(1)}, f32[8,6,6,128]{3,0,2,1:T(8,128)}, u32[]{:S(2)}) copy-start(f32[8,6,6,128]{3,0,2,1:T(8,128)} %get-tuple-element.39) | copy-start | bytes 442372
  77.5 8.3 %collective-permute-start.2 = (bf16[8,6,32,128]{3,0,2,1:T(8,128)(2,1)S(1)}, bf16[8,6,32,128]{3,0,2,1:T(8,128)(2,1)}, u32[]{:S(2)}, u32[]{:S(2)}) collective-permute-start(bf16[8,6,32,128]{3,0,2,1:T(8,128)(2,1)S(1)} %slice.432), channel_id=1, source_target_pairs={{0,4},{4,8},{8,12},{12,16},{16,20},{20,24},{24,28},{28,0},{1,5},{5... | collective-permute-start | bytes 1179656 | tf_op jit(solution)/shard_map/ppermute | solution.py:41
  77.6 8.2 %copy-start.4 = (f32[8,6,32,127]{3,0,2,1:T(8,128)S(1)}, f32[8,6,32,127]{3,0,2,1:T(8,128)}, u32[]{:S(2)}) copy-start(f32[8,6,32,127]{3,0,2,1:T(8,128)} %get-tuple-element.32) | copy-start | bytes 2340868
  77.6 8.2 %copy-start.5 = (f32[8,6,32,127]{3,0,2,1:T(8,128)S(1)}, f32[8,6,32,127]{3,0,2,1:T(8,128)}, u32[]{:S(2)}) copy-start(f32[8,6,32,127]{3,0,2,1:T(8,128)} %get-tuple-element.33) | copy-start | bytes 2340868
  77.6 8.2 %copy-start.6 = (f32[8,6,32,1]{3,0,2,1:T(8,128)S(1)}, f32[8,6,32,1]{3,0,2,1:T(8,128)}, u32[]{:S(2)}) copy-start(f32[8,6,32,1]{3,0,2,1:T(8,128)} %get-tuple-element.34) | copy-start | bytes 18436
  77.6 8.2 %copy-start.7 = (f32[8,6,32,1]{3,0,2,1:T(8,128)S(1)}, f32[8,6,32,1]{3,0,2,1:T(8,128)}, u32[]{:S(2)}) copy-start(f32[8,6,32,1]{3,0,2,1:T(8,128)} %get-tuple-element.35) | copy-start | bytes 18436
  98.0 0.7 copy-start.13
  98.1 1.9 %copy-start.3 = (bf16[8,6,32,128]{3,0,2,1:T(8,128)(2,1)S(1)}, bf16[8,6,32,128]{3,0,2,1:T(8,128)(2,1)}, u32[]{:S(2)}) copy-start(bf16[8,6,32,128]{3,0,2,1:T(8,128)(2,1)} %fusion.14) | copy-start | bytes 1179652
  139.0 26.0 %copy-start.1 = (bf16[4,9,6,32,128]{4,3,2,1,0:T(8,128)(2,1)S(1)}, bf16[4,9,6,32,128]{4,3,2,1,0:T(8,128)(2,1)}, u32[]{:S(2)}) copy-start(bf16[4,9,6,32,128]{4,3,2,1,0:T(8,128)(2,1)} %param.9) | copy-start | bytes 5308420
Sparse Core Ops, SparseCore 0:
  98.2 38.7 all-gather.1
where the time goes:
time: 172 us
  local copies, waits for them, and re-layouts  56.7 us (33%)
  waiting for transfers between devices  42.9 us (25%)
  blocking collectives  24.3 us (14%)
  matrix products  17.1 us (10%)
  between operations  15 us (9%)
  other arithmetic  12.4 us (7%)
  starting transfers between devices  3.55 us (2%)
    all_gather x1, waiting for transfers between devices, shards(): piece = lax.all_gather(filtered, 'band', axis=0, tiled=True)  36.2 us
    slice x24, local copies, waits for them, and re-layouts, laplace_axis(): jnp.roll(field, -offset, axis)  27.1 us
    unnamed x1, blocking collectives  24.3 us
    convert_element_type x1, other arithmetic, shards(): (2.0 / halfwidth * (hamil - center * orbitals) - previous).astype(jnp.bfl...  12.3 us
    unnamed x40, local copies, waits for them, and re-layouts  11.2 us
    dot_general x1, matrix products, shards(): lax.dot_general(weighted, table_flat, (((0,), (0,)), ((), ())), precision...  8.06 us
    reshape x1, local copies, waits for them, and re-layouts, shards(): table_flat = table.reshape(atom_count * NPJ, -1)  7.78 us
    ppermute x1, waiting for transfers between devices, shifted(): return lax.ppermute(value, axis, pairs)  6.66 us
  transfers between devices with their start and end apart: 4, of which 2 were waited for; matrix products, arithmetic and copies ran while one was open for 31% of the time, Pallas kernels for 0%

commit v1 on v0

v1 whole, which is shorter than its diff:
```python
import jax
import jax.numpy as jnp
import numpy as np
from jax import lax
from jax.experimental import pallas as pl
from jax.experimental.pallas import tpu as pltpu
from jax.sharding import PartitionSpec as P

HALO = 6
BOX = 6
NPJ = 9
HALF = 16

stencil_weights = (
    -5369.0 / 1800.0,
    12.0 / 7.0,
    -15.0 / 56.0,
    10.0 / 189.0,
    -1.0 / 112.0,
    2.0 / 1925.0,
    -1.0 / 16632.0,
)
center = 5.5
halfwidth = 5.5
outer = 2.0 / halfwidth
kinetic_weights = [-0.5 * outer * w for w in stencil_weights]

F32 = jnp.float32
BF16 = jnp.bfloat16


def params(vmem=48 * 2**20):
    return pltpu.CompilerParams(vmem_limit_bytes=vmem)


def circulant(n):
    c = np.zeros((n, n), np.float64)
    for i in range(n):
        c[i, i] += kinetic_weights[0]
        for m in range(1, HALO + 1):
            c[i, (i + m) % n] += kinetic_weights[m]
            c[i, (i - m) % n] += kinetic_weights[m]
    return c


def split_hi_lo(m):
    hi = np.asarray(m, np.float32).astype(jnp.bfloat16)
    lo = (m - hi.astype(np.float64)).astype(np.float32).astype(jnp.bfloat16)
    return hi, lo


def dot(a, b, dims=((1,), (0,))):
    return lax.dot_general(a, b, (dims, ((), ())), preferred_element_type=F32)


def local_kernel(psi_ref, prev_ref, pot_ref, cz_ref, cy_ref, g_ref):
    bands, planes, ny, nz = psi_ref.shape
    rows = bands * ny
    for x in range(planes):
        psi3 = psi_ref[:, x]
        psi = psi3.reshape(rows, nz)
        hi = psi.astype(BF16)
        lo = (psi - hi.astype(F32)).astype(BF16)
        both = jnp.concatenate([hi, lo], axis=1)
        along_z = dot(both, cz_ref[0 : 2 * nz]) + dot(hi, cz_ref[2 * nz : 3 * nz])
        pair = dot(cy_ref[0], both)
        along_y = pair[:, :nz] + pair[:, nz:] + dot(cy_ref[1], hi)
        total = (along_z + along_y).reshape(bands, ny, nz)
        total = total + (outer * pot_ref[x] + (kinetic_weights[0] - outer * center))[None] * psi3
        for m in range(1, HALO + 1):
            if x + m < planes:
                total = total + kinetic_weights[m] * psi_ref[:, x + m]
            if x - m >= 0:
                total = total + kinetic_weights[m] * psi_ref[:, x - m]
        g_ref[x] = total - prev_ref[:, x]


def projector_kernel(offs_ref, own_ref, upper_ref, proj_ref, s_ref, near_ref, next_ref, ext, acc):
    planes, bands, ny, nz = own_ref.shape
    atoms, npj = proj_ref.shape[:2]
    ext[0:planes] = own_ref[...]
    ext[planes : 2 * planes] = upper_ref[...]
    acc[...] = jnp.zeros_like(acc)
    rows, cols = bands * HALF, npj * HALF
    row_y = lax.broadcasted_iota(jnp.int32, (rows, cols), 0) % HALF
    col_y = lax.broadcasted_iota(jnp.int32, (rows, cols), 1) % HALF
    mask = jnp.where(row_y == col_y, 1.0, 0.0).astype(F32)
    gi = lax.broadcasted_iota(jnp.int32, (cols, cols), 0) // HALF
    gj = lax.broadcasted_iota(jnp.int32, (cols, cols), 1) // HALF
    group = jnp.where(gi == gj, 1.0, 0.0).astype(BF16)
    halves = [slice(h * HALF, (h + 1) * HALF) for h in range(ny // HALF)]

    def table(a, sl):
        return jnp.concatenate(
            [proj_ref[a, :, p, sl, :].reshape(cols, nz) for p in range(BOX)], axis=1
        )

    parts = []
    for a in range(atoms):
        start = offs_ref[a]
        total = None
        for sl in halves:
            left = jnp.concatenate(
                [ext[start + p, :, sl, :].reshape(rows, nz) for p in range(BOX)], axis=1
            )
            d = dot(left, table(a, sl), ((1,), (1,)))
            total = d if total is None else total + d
        parts.append((total * mask).reshape(bands, HALF, cols).sum(axis=1))
    e = jnp.concatenate(parts, axis=0)
    e_hi = e.astype(BF16)
    e_lo = (e - e_hi.astype(F32)).astype(BF16)
    coef = dot(e_hi, group) + dot(e_lo, group)
    for a in range(atoms):
        start = offs_ref[a]
        w = coef[a * bands : (a + 1) * bands] * s_ref[a : a + 1, :]
        full = jnp.broadcast_to(w[:, None, :], (bands, HALF, cols)).reshape(rows, cols) * mask
        full = full.astype(BF16)
        for sl in halves:
            out = dot(full, table(a, sl))
            for p in range(BOX):
                acc[start + p, :, sl, :] += out[:, p * nz : (p + 1) * nz].reshape(bands, HALF, nz)
    near_ref[...] = acc[0:planes]
    next_ref[...] = acc[planes : planes + BOX - 1].astype(BF16)


def halo_kernel(g_ref, near_ref, upper_ref, lower_ref, out_ref):
    planes = g_ref.shape[0]
    for x in range(planes):
        total = g_ref[x] + near_ref[x]
        for m in range(1, HALO + 1):
            if x + m >= planes:
                total = total + kinetic_weights[m] * upper_ref[x + m - planes].astype(F32)
            if x - m < 0:
                total = total + kinetic_weights[m] * lower_ref[x - m + planes].astype(F32)
        out_ref[x] = total


def finish_kernel(g_ref, arrived_ref, out_ref):
    planes = g_ref.shape[0]
    reach = arrived_ref.shape[0]
    for x in range(planes):
        total = g_ref[x]
        if x < reach:
            total = total + arrived_ref[x].astype(F32)
        out_ref[:, x] = total.astype(BF16)


def shards(orbitals, previous, potential, projectors, strengths, atom_planes):
    bands, planes, ny, nz = orbitals.shape
    n_space = lax.axis_size("space")
    n_band = lax.axis_size("band")
    atoms = projectors.shape[0]
    me = lax.axis_index("space")
    forward = [(i, (i + 1) % n_space) for i in range(n_space)]
    backward = [(target, source) for source, target in forward]

    psi16 = orbitals.astype(BF16)
    own = jnp.transpose(psi16, (1, 0, 2, 3))
    upper = lax.ppermute(own, "space", backward)
    lower = lax.ppermute(own, "space", forward)

    def to_quarters(block):
        cut = block.reshape(bands, n_band, planes * ny // n_band, nz)
        return lax.all_to_all(jnp.transpose(cut, (1, 0, 2, 3)), "band", 0, 0)

    panel = to_quarters(psi16)

    cz = circulant(nz)
    cz_hi, cz_lo = split_hi_lo(cz)
    cz_const = jnp.asarray(np.concatenate([cz_hi, cz_hi, cz_lo], axis=0))
    cy = np.kron(np.eye(bands), circulant(ny))
    cy_const = jnp.asarray(np.stack(split_hi_lo(cy)))
    shape = (planes, bands, ny, nz)
    g = pl.pallas_call(
        local_kernel,
        out_shape=jax.ShapeDtypeStruct(shape, F32),
        compiler_params=params(),
        name="local_part",
    )(orbitals, previous, potential, cz_const, cy_const)

    own_start = me * atoms
    offs = lax.dynamic_slice_in_dim(atom_planes, own_start, atoms, 0) - me * planes
    s = lax.dynamic_slice_in_dim(strengths, own_start, atoms, 0) * outer
    s_wide = jnp.repeat(s, HALF, axis=1)
    vm = pl.BlockSpec(memory_space=pltpu.VMEM)
    near, beyond = pl.pallas_call(
        projector_kernel,
        out_shape=(
            jax.ShapeDtypeStruct(shape, F32),
            jax.ShapeDtypeStruct((BOX - 1, bands, ny, nz), BF16),
        ),
        in_specs=[pl.BlockSpec(memory_space=pltpu.SMEM), vm, vm, vm, vm],
        out_specs=(vm, vm),
        scratch_shapes=[
            pltpu.VMEM((2 * planes, bands, ny, nz), BF16),
            pltpu.VMEM((2 * planes, bands, ny, nz), F32),
        ],
        compiler_params=params(),
        name="projector_part",
    )(offs, own, upper, projectors, s_wide)
    arrived = lax.ppermute(beyond, "space", forward)
    g = pl.pallas_call(
        halo_kernel,
        out_shape=jax.ShapeDtypeStruct(shape, F32),
        compiler_params=params(),
        name="halo_part",
    )(g, near, upper, lower)
    filtered = pl.pallas_call(
        finish_kernel,
        out_shape=jax.ShapeDtypeStruct((bands, planes, ny, nz), BF16),
        compiler_params=params(),
        name="finish",
    )(g, arrived)
    mine = to_quarters(filtered)
    total_bands = n_band * bands
    left = mine.reshape(total_bands, -1)
    right = jnp.concatenate([left, panel.reshape(total_bands, -1)], axis=0)
    scale = 1.0 / (planes * n_space * ny * nz)
    products = dot(left, right, ((1,), (1,))) * scale
    out_rows = total_bands // n_space
    pieces = products.reshape(n_space, out_rows, 2, n_band, bands)
    pieces = jnp.transpose(pieces, (0, 3, 1, 2, 4)).reshape(n_space * n_band, out_rows, 2 * bands)
    got = lax.all_to_all(pieces, ("space", "band"), 0, 0)
    share = got.sum(axis=0)
    return filtered, share[:, :bands], share[:, bands:]


def solution(mesh):
    in_specs = (
        P("band", "space", None, None),
        P("band", "space", None, None),
        P("space", None, None),
        P("space", None, None, None, None),
        P(),
        P(),
    )
    out_specs = (P("band", "space", None, None), P("space", "band"), P("space", "band"))
    return jax.shard_map(shards, mesh=mesh, in_specs=in_specs, out_specs=out_specs, check_vma=False)
```

time: 172 us -> 54.4 us (0.32)
  local copies, waits for them, and re-layouts: 56.7 us -> 8.46 us
  waiting for transfers between devices: 42.9 us -> 12.3 us
  matrix products: 17.1 us -> 0.33 us
  between operations: 15 us -> 0.77 us
  blocking collectives: 24.3 us -> 11.2 us
  other arithmetic: 12.4 us -> 1.55 us
  starting transfers between devices: 3.55 us -> 13.5 us
  Pallas kernels: 0 us -> 5.75 us
    all_gather x1 -> x0, waiting for transfers between devices: 36.2 us -> none  [shards(): piece = lax.all_gather(filtered, 'band', axis=0, tiled=True)]
    slice x26 -> x1, local copies, waits for them, and re-layouts: 27.8 us -> 0.65 us  [shards(): return (filtered, share[:, :bands], share[:, bands:])]
    unnamed x1 -> x0, blocking collectives: 24.3 us -> none
    dot_general x4 -> x1, matrix products: 17.1 us -> 0.33 us  [dot(): return lax.dot_general(a, b, (dims, ((), ())), preferred_element_type=F32)]
    convert_element_type x2 -> x0, other arithmetic: 12.3 us -> none  [the longest x1 12.3 us: shards(): (2.0 / halfwidth * (hamil - center * orbitals) - previous).astype(jnp.bfl...]
    all_to_all x0 -> x1, blocking collectives: none -> 11.2 us  [shards(): got = lax.all_to_all(pieces, ('space', 'band'), 0, 0)]
    all_to_all x0 -> x2, starting transfers between devices: none -> 10.1 us  [to_quarters(): return lax.all_to_all(jnp.transpose(cut, (1, 0, 2, 3)), 'band', 0, 0)]
    unnamed x40 -> x19, local copies, waits for them, and re-layouts: 11.2 us -> 3.23 us
  transfers between devices with their start and end apart: 4 -> 5, of which waited for: 2 -> 2; matrix products, arithmetic and copies ran while one was open for 31% -> 14% of each run, Pallas kernels for 0% -> 11%
where the time goes in v1:
time: 54.4 us; the launch traced here: 53.9 us
  starting transfers between devices  13.5 us (25%)
  waiting for transfers between devices  12.3 us (23%)
  blocking collectives  11.2 us (21%)
  local copies, waits for them, and re-layouts  8.46 us (16%)
  Pallas kernels  5.75 us (11%)
  other arithmetic  1.55 us (3%)
  between operations  0.77 us (1%)
    all_to_all x1, blocking collectives, shards(): got = lax.all_to_all(pieces, ('space', 'band'), 0, 0)  11.2 us
    all_to_all x2, starting transfers between devices, to_quarters(): return lax.all_to_all(jnp.transpose(cut, (1, 0, 2, 3)), 'band', 0, 0)  10.1 us
    all_to_all x2, waiting for transfers between devices, to_quarters(): return lax.all_to_all(jnp.transpose(cut, (1, 0, 2, 3)), 'band', 0, 0)  7.79 us
    ppermute x1, waiting for transfers between devices, shards(): arrived = lax.ppermute(beyond, 'space', forward)  4.46 us
    ppermute x1, starting transfers between devices, shards(): upper = lax.ppermute(own, 'space', backward)  3.39 us
    unnamed x19, local copies, waits for them, and re-layouts  3.23 us
    pallas_call x1, Pallas kernels, shards(): pl.pallas_call(projector_kernel, out_shape=(jax.ShapeDtypeStruct(shape, F...  2.09 us
    reshape x1, local copies, waits for them, and re-layouts, to_quarters(): cut = block.reshape(bands, n_band, planes * ny // n_band, nz)  1.77 us
  transfers between devices with their start and end apart: 5, of which 2 were waited for; matrix products, arithmetic and copies ran while one was open for 14% of the time, Pallas kernels for 11%

profile of v1, /device:TPU:0, one launch (start us, length us, event | category | flops | bytes accessed | tf_op | source)
XLA Modules:
  0.0 53.9 jit_solution(3440463689763208102)
XLA Ops:
  0.6 0.0 copy-start
  0.6 0.0 copy-start.1
  0.7 1.3 %copy.47 = bf16[8,6,32,128]{3,2,0,1:T(8,128)(2,1)S(1)} copy(f32[8,6,32,128]{3,2,1,0:T(8,128)} %psi_ref.1) | data formatting | bytes 1179648 | tf_op args[0]
  1.9 0.0 copy-start.2
  1.9 3.4 %collective-permute-start = (bf16[6,8,32,128]{3,2,1,0:T(8,128)(2,1)S(1)}, bf16[6,8,32,128]{3,2,1,0:T(8,128)(2,1)S(1)}, u32[]{:S(2)}, u32[]{:S(2)}) collective-permute-start(bf16[6,8,32,128]{3,2,1,0:T(8,128)(2,1)S(1)} %bitcast.26), channel_id=1, source_target_pairs={{4,0},{8,4},{12,8},{16,12},{20,16},{24,20},{28,24},{0,28},{5,1},{9... | collective-permute-start | bytes 1179656 | tf_op jit(solution)/shard_map/ppermute | solution.py:159
  5.3 0.0 collective-permute-start.1
  5.3 0.0 copy-done.1
  5.3 0.1 copy.41
  5.4 0.8 %copy.30 = bf16[4,8,48,128]{3,2,1,0:T(8,128)(2,1)} copy(bf16[4,8,48,128]{3,2,0,1:T(8,128)(2,1)S(1)} %bitcast.29) | data formatting | bytes 786432 | tf_op jit(solution)/shard_map/transpose | solution.py:164
  6.2 0.0 copy-start.5
  6.2 0.0 copy-start.6
  6.2 5.0 %all-to-all-start.1 = ((bf16[4,8,48,128]{3,2,1,0:T(8,128)(2,1)}), bf16[4,8,48,128]{3,2,1,0:T(8,128)(2,1)}, u32[]{:S(2)}, u32[]{:S(2)}) async-start(bf16[4,8,48,128]{3,2,1,0:T(8,128)(2,1)} %copy.30), calls=%async_computation.1 | async-start | bytes 786432 | tf_op jit(solution)/shard_map/all_to_all | solution.py:164
  11.2 0.0 copy-done
  11.2 0.1 constant_dynamic-slice_fusion
  11.3 0.7 %copy.33 = f32[4,9]{1,0:T(4,128)} copy(f32[4,9]{0,1:T(8,128)S(1)} %constant_dynamic-slice_fusion) | data formatting | bytes 288
  12.0 0.7 %broadcast_multiply_fusion = f32[4,9]{1,0:T(4,128)S(1)} fusion(f32[4,9]{1,0:T(4,128)} %copy.33), kind=kLoop, calls=%fused_computation.9 | loop fusion | flops 36 | bytes 288 | tf_op jit(solution)/shard_map/mul | solution.py:183
  12.6 0.7 %broadcast_in_dim.3 = f32[4,9,16]{2,1,0:T(8,128)} broadcast(f32[4,9]{1,0:T(4,128)S(1)} %broadcast_multiply_fusion), dimensions={0,1} | broadcast | bytes 2448 | tf_op jit(solution)/shard_map/broadcast_in_dim | solution.py:184
  13.3 0.8 %reshape.27.s_ref = f32[4,144]{1,0:T(4,128)S(1)} reshape(f32[4,9,16]{2,1,0:T(8,128)} %broadcast_in_dim.3) | data formatting | bytes 4608 | tf_op jit(solution)/shard_map/reshape | solution.py:184
  14.2 0.0 copy-start.3
  14.2 0.0 copy-start.4
  14.2 0.8 %dynamic-slice_subtract_fusion.offs_ref = s32[4]{0:T(128)S(1)} fusion(s32[32]{0:T(128)} %param.13, s32[]{:T(128)S(6)} %select_n.4, s32[]{:T(128)S(6)} %mul.19), kind=kLoop, calls=%fused_computation.10 | loop fusion | flops 4 | bytes 40 | tf_op jit(solution)/shard_map/sub | solution.py:182
  15.0 0.0 collective-permute-done.upper_ref
  15.0 0.0 copy-done.2
  15.0 2.1 %projector_part.1 = (f32[6,8,32,128]{3,2,1,0:T(8,128)S(1)}, bf16[5,8,32,128]{3,2,1,0:T(8,128)(2,1)S(1)}) custom-call(s32[4]{0:T(128)S(1)} %dynamic-slice_subtract_fusion.offs_ref, bf16[6,8,32,128]{3,2,1,0:T(8,128)(2,1)S(1)} %bitcast.28, bf16[6,8,32,128]{3,2,1,0:T(8,128)(2,1)S(1)} %collective-permute-done.upper_ref, ...), custom_call_target="tpu_custom_call" | custom-call | tf_op jit(solution)/shard_map/projector_part/pallas_call | solution.py:186
  17.1 0.1 collective-permute-start.2
  17.2 0.0 copy-done.5
  17.2 0.0 copy-done.6
  17.2 0.0 copy-done.3
  17.2 0.0 copy-done.4
  17.2 1.2 %local_part.1.g_ref = f32[6,8,32,128]{3,2,1,0:T(8,128)S(1)} custom-call(f32[8,6,32,128]{3,2,1,0:T(8,128)S(1)} %copy-done.1, f32[8,6,32,128]{3,2,1,0:T(8,128)S(1)} %copy-done.3, f32[6,32,128]{2,1,0:T(8,128)S(1)} %copy-done.5, bf16[384,128]{1,0:T(8,128)(2,1)S(1)} %copy-done.6, bf16[2,256,256]{2,1,0:T(8,128)(2,1)S(1)} %copy-done.4), custom_call_target="tpu_custom_call" | custom-call | tf_op jit(solution)/shard_map/local_part/pallas_call | solution.py:174
  18.4 0.0 collective-permute-done.1.lower_ref
  18.5 1.6 %halo_part.1.g_ref = f32[6,8,32,128]{3,2,1,0:T(8,128)S(1)} custom-call(f32[6,8,32,128]{3,2,1,0:T(8,128)S(1)} %local_part.1.g_ref, f32[6,8,32,128]{3,2,1,0:T(8,128)S(1)} %get-tuple-element.5.near_ref, bf16[6,8,32,128]{3,2,1,0:T(8,128)(2,1)S(1)} %collective-permute-done.upper_ref, bf16[6,8,32,128]{3,2,1,0:T(8,128)(2,1)} %collective-permute-done.1.lower_ref), custom_call_target="tpu_custom_call" | custom-call | tf_op jit(solution)/shard_map/halo_part/pallas_call | solution.py:202
  20.1 4.5 %collective-permute-done.2.arrived_ref = bf16[5,8,32,128]{3,2,1,0:T(8,128)(2,1)S(1)} collective-permute-done((bf16[5,8,32,128]{3,2,1,0:T(8,128)(2,1)S(1)}, bf16[5,8,32,128]{3,2,1,0:T(8,128)(2,1)S(1)}, u32[]{:S(2)}, u32[]{:S(2)}) %collective-permute-start.2) | collective-permute-done | bytes 327712 | tf_op jit(solution)/shard_map/ppermute | solution.py:201
  24.6 0.8 %finish.1 = bf16[8,6,32,128]{3,2,1,0:T(8,128)(2,1)} custom-call(f32[6,8,32,128]{3,2,1,0:T(8,128)S(1)} %halo_part.1.g_ref, bf16[5,8,32,128]{3,2,1,0:T(8,128)(2,1)S(1)} %collective-permute-done.2.arrived_ref), custom_call_target="tpu_custom_call" | custom-call | tf_op jit(solution)/shard_map/finish/pallas_call | solution.py:208
  25.4 1.8 %copy.45 = bf16[8,4,48,128]{3,2,0,1:T(8,128)(2,1)} copy(bf16[8,4,48,128]{3,2,1,0:T(8,128)(2,1)} %bitcast.30) | data formatting | bytes 786432 | tf_op jit(solution)/shard_map/reshape | solution.py:163
  27.1 0.0 all-to-all-done.1
  27.1 5.1 %all-to-all-start = ((bf16[4,8,48,128]{3,2,1,0:T(8,128)(2,1)}), bf16[4,8,48,128]{3,2,1,0:T(8,128)(2,1)S(1)}, u32[]{:S(2)}, u32[]{:S(2)}) async-start(bf16[4,8,48,128]{3,2,1,0:T(8,128)(2,1)} %bitcast.23), calls=%async_computation | async-start | bytes 786432 | tf_op jit(solution)/shard_map/all_to_all | solution.py:164
  32.2 1.1 %copy.43 = bf16[4,8,48,128]{3,1,2,0:T(8,128)(2,1)S(1)} copy(bf16[4,8,48,128]{3,2,1,0:T(8,128)(2,1)} %all-to-all-done.1) | data formatting | bytes 786432
  33.3 7.8 %all-to-all-done = bf16[4,8,48,128]{3,2,1,0:T(8,128)(2,1)S(1)} async-done(((bf16[4,8,48,128]{3,2,1,0:T(8,128)(2,1)}), bf16[4,8,48,128]{3,2,1,0:T(8,128)(2,1)S(1)}, u32[]{:S(2)}, u32[]{:S(2)}) %all-to-all-start) | async-done | bytes 393248 | tf_op jit(solution)/shard_map/all_to_all | solution.py:164
  41.1 0.1 copy.44
  41.2 0.3 convolution_multiply_fusion
  41.5 0.2 reshape.32
  41.7 0.1 copy.46
  41.8 0.1 reshape.33
  42.0 11.2 %all_to_all.15 = f32[32,4,16]{2,1,0:T(4,128)S(1)} all-to-all(f32[32,4,16]{2,1,0:T(4,128)S(1)} %copy.32), channel_id=1, replica_groups=mesh['space'=8,'band'=4] {'space','band'}, dimensions={0} | all-to-all | bytes 16384 | tf_op jit(solution)/shard_map/all_to_all | solution.py:223
  53.2 0.7 %fusion.4 = (f32[4,8]{1,0:T(4,128)}, f32[4,8]{1,0:T(4,128)}) fusion(f32[4,16]{1,0:T(4,128)S(1)} %reduce_sum.9), kind=kLoop, calls=%fused_computation.13 | loop fusion | bytes 512 | tf_op jit(solution)/shard_map/slice | solution.py:225
  (3 shorter events, 0.1 us)
Async XLA Ops:
  0.6 10.6 %copy-start = (f32[32,9]{0,1:T(8,128)S(1)}, f32[32,9]{0,1:T(8,128)}, u32[]{:S(2)}) copy-start(f32[32,9]{0,1:T(8,128)} %param.12) | copy-start | bytes 3460
  0.6 4.7 %copy-start.1 = (f32[8,6,32,128]{3,2,1,0:T(8,128)S(1)}, f32[8,6,32,128]{3,2,1,0:T(8,128)}, u32[]{:S(2)}) copy-start(f32[8,6,32,128]{3,2,1,0:T(8,128)} %psi_ref.1) | copy-start | bytes 2359300
  1.9 13.1 %copy-start.2 = (bf16[4,9,6,32,128]{4,3,2,1,0:T(8,128)(2,1)S(1)}, bf16[4,9,6,32,128]{4,3,2,1,0:T(8,128)(2,1)}, u32[]{:S(2)}) copy-start(bf16[4,9,6,32,128]{4,3,2,1,0:T(8,128)(2,1)} %proj_ref.1) | copy-start | bytes 5308420
  1.9 13.1 %collective-permute-start = (bf16[6,8,32,128]{3,2,1,0:T(8,128)(2,1)S(1)}, bf16[6,8,32,128]{3,2,1,0:T(8,128)(2,1)S(1)}, u32[]{:S(2)}, u32[]{:S(2)}) collective-permute-start(bf16[6,8,32,128]{3,2,1,0:T(8,128)(2,1)S(1)} %bitcast.26), channel_id=1, source_target_pairs={{4,0},{8,4},{12,8},{16,12},{20,16},{24,20},{28,24},{0,28},{5,1},{9... | collective-permute-start | bytes 1179656 | tf_op jit(solution)/shard_map/ppermute | solution.py:159
  5.3 13.1 %collective-permute-start.1 = (bf16[6,8,32,128]{3,2,1,0:T(8,128)(2,1)S(1)}, bf16[6,8,32,128]{3,2,1,0:T(8,128)(2,1)}, u32[]{:S(2)}, u32[]{:S(2)}) collective-permute-start(bf16[6,8,32,128]{3,2,1,0:T(8,128)(2,1)S(1)} %bitcast.27), channel_id=1, source_target_pairs={{0,4},{4,8},{8,12},{12,16},{16,20},{20,24},{24,28},{28,0},{1,5},{5... | collective-permute-start | bytes 1179656 | tf_op jit(solution)/shard_map/ppermute | solution.py:160
  6.2 11.0 %copy-start.5 = (f32[6,32,128]{2,1,0:T(8,128)S(1)}, f32[6,32,128]{2,1,0:T(8,128)}, u32[]{:S(2)}) copy-start(f32[6,32,128]{2,1,0:T(8,128)} %pot_ref.1) | copy-start | bytes 294916
  6.2 11.0 %copy-start.6 = (bf16[384,128]{1,0:T(8,128)(2,1)S(1)}, bf16[384,128]{1,0:T(8,128)(2,1)}, u32[]{:S(2)}) copy-start(bf16[384,128]{1,0:T(8,128)(2,1)} %constant.24.clone.cz_ref) | copy-start | bytes 294916
  6.2 20.9 %all-to-all-start.1 = ((bf16[4,8,48,128]{3,2,1,0:T(8,128)(2,1)}), bf16[4,8,48,128]{3,2,1,0:T(8,128)(2,1)}, u32[]{:S(2)}, u32[]{:S(2)}) async-start(bf16[4,8,48,128]{3,2,1,0:T(8,128)(2,1)} %copy.30), calls=%async_computation.1 | async-start | bytes 786432 | tf_op jit(solution)/shard_map/all_to_all | solution.py:164
  14.2 3.0 %copy-start.3 = (f32[8,6,32,128]{3,2,1,0:T(8,128)S(1)}, f32[8,6,32,128]{3,2,1,0:T(8,128)}, u32[]{:S(2)}) copy-start(f32[8,6,32,128]{3,2,1,0:T(8,128)} %prev_ref.1) | copy-start | bytes 2359300
  14.2 3.0 %copy-start.4 = (bf16[2,256,256]{2,1,0:T(8,128)(2,1)S(1)}, bf16[2,256,256]{2,1,0:T(8,128)(2,1)}, u32[]{:S(2)}) copy-start(bf16[2,256,256]{2,1,0:T(8,128)(2,1)} %constant.25.clone.cy_ref) | copy-start | bytes 786436
  17.1 7.5 %collective-permute-start.2 = (bf16[5,8,32,128]{3,2,1,0:T(8,128)(2,1)S(1)}, bf16[5,8,32,128]{3,2,1,0:T(8,128)(2,1)S(1)}, u32[]{:S(2)}, u32[]{:S(2)}) collective-permute-start(bf16[5,8,32,128]{3,2,1,0:T(8,128)(2,1)S(1)} %get-tuple-element.6), channel_id=1, source_target_pairs={{0,4},{4,8},{8,12},{12,16},{16,20},{20,24},{24,28},{28,0},{1,5},{5... | collective-permute-start | bytes 983048 | tf_op jit(solution)/shard_map/ppermute | solution.py:201
  27.1 14.0 %all-to-all-start = ((bf16[4,8,48,128]{3,2,1,0:T(8,128)(2,1)}), bf16[4,8,48,128]{3,2,1,0:T(8,128)(2,1)S(1)}, u32[]{:S(2)}, u32[]{:S(2)}) async-start(bf16[4,8,48,128]{3,2,1,0:T(8,128)(2,1)} %bitcast.23), calls=%async_computation | async-start | bytes 786432 | tf_op jit(solution)/shard_map/all_to_all | solution.py:164

commit v2 on v1

v2 whole, which is shorter than its diff:
```python
from functools import partial

import jax
import jax.numpy as jnp
import numpy as np
from jax import lax
from jax.experimental import pallas as pl
from jax.experimental.pallas import tpu as pltpu
from jax.sharding import PartitionSpec as P

HALO = 6
BOX = 6
NPJ = 9
HALF = 16

stencil_weights = (
    -5369.0 / 1800.0,
    12.0 / 7.0,
    -15.0 / 56.0,
    10.0 / 189.0,
    -1.0 / 112.0,
    2.0 / 1925.0,
    -1.0 / 16632.0,
)
center = 5.5
halfwidth = 5.5
outer = 2.0 / halfwidth
kinetic_weights = [-0.5 * outer * w for w in stencil_weights]

F32 = jnp.float32
BF16 = jnp.bfloat16


def params(vmem=48 * 2**20):
    return pltpu.CompilerParams(vmem_limit_bytes=vmem)


def circulant(n):
    c = np.zeros((n, n), np.float64)
    for i in range(n):
        c[i, i] += kinetic_weights[0]
        for m in range(1, HALO + 1):
            c[i, (i + m) % n] += kinetic_weights[m]
            c[i, (i - m) % n] += kinetic_weights[m]
    return c


def split_hi_lo(m):
    hi = np.asarray(m, np.float32).astype(jnp.bfloat16)
    lo = (m - hi.astype(np.float64)).astype(np.float32).astype(jnp.bfloat16)
    return hi, lo


def dot(a, b, dims=((1,), (0,))):
    return lax.dot_general(a, b, (dims, ((), ())), preferred_element_type=F32)


def plane_rows(x, ny):
    return slice(x * ny, (x + 1) * ny)


def pieces_of(ref, index, count, rows, outs):
    for shift, out in enumerate(outs):
        quarter = lax.rem(index + shift, count)
        begin = pl.multiple_of(quarter * rows, 8)
        out[...] = ref[:, pl.ds(begin, rows), :].astype(out.dtype)


def cast_kernel(count, psi_ref, half_ref, *outs):
    half_ref[...] = psi_ref[...].astype(BF16)
    rows = psi_ref.shape[1] // count
    pieces_of(psi_ref, lax.axis_index("band"), count, rows, outs)


def local_kernel(planes, psi_ref, prev_ref, pot_ref, cz_ref, cy_ref, g_ref):
    bands, cells, nz = psi_ref.shape
    ny = cells // planes
    rows = bands * ny
    for x in range(planes):
        here = plane_rows(x, ny)
        psi3 = psi_ref[:, here]
        psi = psi3.reshape(rows, nz)
        hi = psi.astype(BF16)
        lo = (psi - hi.astype(F32)).astype(BF16)
        both = jnp.concatenate([hi, lo], axis=1)
        along_z = dot(both, cz_ref[0 : 2 * nz]) + dot(hi, cz_ref[2 * nz : 3 * nz])
        pair = dot(cy_ref[0], both)
        along_y = pair[:, :nz] + pair[:, nz:] + dot(cy_ref[1], hi)
        total = (along_z + along_y).reshape(bands, ny, nz)
        site = outer * pot_ref[here] + (kinetic_weights[0] - outer * center)
        total = total + site[None] * psi3
        for m in range(1, HALO + 1):
            if x + m < planes:
                total = total + kinetic_weights[m] * psi_ref[:, plane_rows(x + m, ny)]
            if x - m >= 0:
                total = total + kinetic_weights[m] * psi_ref[:, plane_rows(x - m, ny)]
        g_ref[:, here] = total - prev_ref[:, here]


def projector_kernel(
    planes, first_ref, strength_ref, own_ref, upper_ref, proj_ref, near_ref, next_ref, ext, acc
):
    bands, cells, nz = own_ref.shape
    ny = cells // planes
    atoms, npj = proj_ref.shape[:2]
    me = lax.axis_index("space")
    for x in range(planes):
        ext[x] = own_ref[:, plane_rows(x, ny)]
        ext[planes + x] = upper_ref[:, plane_rows(x, ny)]
    acc[...] = jnp.zeros_like(acc)
    rows, cols = bands * HALF, npj * HALF
    row_y = lax.broadcasted_iota(jnp.int32, (rows, cols), 0) % HALF
    col_y = lax.broadcasted_iota(jnp.int32, (rows, cols), 1) % HALF
    mask = jnp.where(row_y == col_y, 1.0, 0.0).astype(F32)
    gi = lax.broadcasted_iota(jnp.int32, (cols, cols), 0) // HALF
    gj = lax.broadcasted_iota(jnp.int32, (cols, cols), 1) // HALF
    group = jnp.where(gi == gj, 1.0, 0.0).astype(BF16)
    owner = lax.broadcasted_iota(jnp.int32, (1, cols), 1) // HALF
    halves = [slice(h * HALF, (h + 1) * HALF) for h in range(ny // HALF)]
    starts = [first_ref[me * atoms + a] - me * planes for a in range(atoms)]

    def table(a, sl):
        return jnp.concatenate(
            [proj_ref[a, :, p, sl, :].reshape(cols, nz) for p in range(BOX)], axis=1
        )

    parts = []
    for a in range(atoms):
        total = None
        for sl in halves:
            left = jnp.concatenate(
                [ext[starts[a] + p, :, sl, :].reshape(rows, nz) for p in range(BOX)], axis=1
            )
            d = dot(left, table(a, sl), ((1,), (1,)))
            total = d if total is None else total + d
        parts.append((total * mask).reshape(bands, HALF, cols).sum(axis=1))
    e = jnp.concatenate(parts, axis=0)
    e_hi = e.astype(BF16)
    e_lo = (e - e_hi.astype(F32)).astype(BF16)
    coef = dot(e_hi, group) + dot(e_lo, group)
    for a in range(atoms):
        scale = jnp.zeros((1, cols), F32)
        for j in range(npj):
            scale = jnp.where(owner == j, outer * strength_ref[me * atoms + a, j], scale)
        w = coef[a * bands : (a + 1) * bands] * scale
        full = jnp.broadcast_to(w[:, None, :], (bands, HALF, cols)).reshape(rows, cols) * mask
        full = full.astype(BF16)
        for sl in halves:
            out = dot(full, table(a, sl))
            for p in range(BOX):
                acc[starts[a] + p, :, sl, :] += out[:, p * nz : (p + 1) * nz].reshape(
                    bands, HALF, nz
                )
    for x in range(planes):
        near_ref[:, plane_rows(x, ny)] = acc[x]
    for x in range(BOX - 1):
        next_ref[:, plane_rows(x, ny)] = acc[planes + x].astype(BF16)


def halo_kernel(planes, g_ref, near_ref, upper_ref, lower_ref, out_ref):
    ny = g_ref.shape[1] // planes
    for x in range(planes):
        here = plane_rows(x, ny)
        total = g_ref[:, here] + near_ref[:, here]
        for m in range(1, HALO + 1):
            if x + m >= planes:
                there = plane_rows(x + m - planes, ny)
                total = total + kinetic_weights[m] * upper_ref[:, there].astype(F32)
            if x - m < 0:
                there = plane_rows(x - m + planes, ny)
                total = total + kinetic_weights[m] * lower_ref[:, there].astype(F32)
        out_ref[:, here] = total


def finish_kernel(count, g_ref, arrived_ref, out_ref, *rest):
    outs, total = rest[:-1], rest[-1]
    reach = arrived_ref.shape[1]
    total[:, :reach] = g_ref[:, :reach] + arrived_ref[...].astype(F32)
    total[:, reach:] = g_ref[:, reach:]
    out_ref[...] = total[...].astype(BF16)
    rows = g_ref.shape[1] // count
    pieces_of(total, lax.axis_index("band"), count, rows, outs)


def split_kernel(count, prod_ref, *outs):
    bands = prod_ref.shape[0] // count
    me = lax.axis_index("band")
    for back, out in enumerate(outs):
        for j in range(count):
            shift = lax.rem(me - j + count, count)
            rows = pl.ds(pl.multiple_of(shift * bands, 8), bands)
            block = prod_ref[rows, :]
            cols = [block[:, (h * count + back) * bands : (h * count + back + 1) * bands] for h in (0, 1)]
            out[j * bands : (j + 1) * bands, :] = jnp.concatenate(cols, axis=1)


def sum_kernel(count, *refs):
    parts, outs, held = refs[:-count - 1], refs[-count - 1 : -1], refs[-1]
    total = parts[0][...]
    for part in parts[1:]:
        total = total + part[...]
    rows = total.shape[0] // count
    for i in range(count):
        held[i] = total[i * rows : (i + 1) * rows]
    me = lax.axis_index("space")
    for shift, out in enumerate(outs):
        out[...] = held[lax.rem(me + shift, count)]


def last_kernel(*refs):
    parts, outs = refs[:-2], refs[-2:]
    total = parts[0][...]
    for part in parts[1:]:
        total = total + part[...]
    bands = outs[0].shape[1]
    outs[0][...] = total[:, :bands]
    outs[1][...] = total[:, bands:]


def cyclic(value, axis, steps):
    count = lax.axis_size(axis)
    return lax.ppermute(value, axis, [(i, (i + steps) % count) for i in range(count)])


def struct(shape, kind=F32):
    return jax.ShapeDtypeStruct(shape, kind)


def call(kernel, name, out_shape, args, **extra):
    return pl.pallas_call(
        kernel, out_shape=out_shape, compiler_params=params(), name=name, **extra
    )(*args)


def shards(orbitals, previous, potential, projectors, strengths, atom_planes):
    bands, planes, ny, nz = orbitals.shape
    n_space = lax.axis_size("space")
    n_band = lax.axis_size("band")
    cells = planes * ny
    whole = (bands, cells, nz)
    quarter = (bands, cells // n_band, nz)
    psi = orbitals.reshape(whole)
    prev = previous.reshape(whole)
    pot = potential.reshape(cells, nz)

    half, *panel = call(
        partial(cast_kernel, n_band),
        "cast",
        (struct(whole, BF16),) + (struct(quarter, BF16),) * n_band,
        (psi,),
    )
    upper = cyclic(half, "space", -1)
    lower = cyclic(half, "space", 1)
    panel = [cyclic(piece, "band", shift) if shift else piece for shift, piece in enumerate(panel)]

    cz_hi, cz_lo = split_hi_lo(circulant(nz))
    cz = jnp.asarray(np.concatenate([cz_hi, cz_hi, cz_lo], axis=0))
    cy = jnp.asarray(np.stack(split_hi_lo(np.kron(np.eye(bands), circulant(ny)))))
    g = call(partial(local_kernel, planes), "local_part", struct(whole), (psi, prev, pot, cz, cy))
    upper, g = lax.optimization_barrier((upper, g))

    vm = pl.BlockSpec(memory_space=pltpu.VMEM)
    sm = pl.BlockSpec(memory_space=pltpu.SMEM)
    near, beyond = call(
        partial(projector_kernel, planes),
        "projector_part",
        (struct(whole), struct((bands, (BOX - 1) * ny, nz), BF16)),
        (atom_planes, strengths, half, upper, projectors),
        in_specs=[sm, sm, vm, vm, vm],
        out_specs=(vm, vm),
        scratch_shapes=[
            pltpu.VMEM((2 * planes, bands, ny, nz), BF16),
            pltpu.VMEM((2 * planes, bands, ny, nz), F32),
        ],
    )
    arrived = cyclic(beyond, "space", 1)
    g = call(partial(halo_kernel, planes), "halo_part", struct(whole), (g, near, upper, lower))
    filtered, *mine = call(
        partial(finish_kernel, n_band),
        "finish",
        (struct(whole, BF16),) + (struct(quarter, BF16),) * n_band,
        (g, arrived),
        scratch_shapes=[pltpu.VMEM(whole, F32)],
    )
    mine = [cyclic(piece, "band", shift) if shift else piece for shift, piece in enumerate(mine)]
    total_bands = n_band * bands
    left = jnp.concatenate(mine, axis=0).reshape(total_bands, -1)
    right = jnp.concatenate([left, jnp.concatenate(panel, axis=0).reshape(total_bands, -1)], axis=0)
    products = dot(left, right, ((1,), (1,))) * (1.0 / (cells * n_space * nz))
    blocks = call(
        partial(split_kernel, n_band),
        "split",
        (struct((total_bands, 2 * bands)),) * n_band,
        (products,),
    )
    blocks = [cyclic(b, "band", -shift) if shift else b for shift, b in enumerate(blocks)]
    out_rows = total_bands // n_space
    shares = call(
        partial(sum_kernel, n_space),
        "band_sum",
        (struct((out_rows, 2 * bands)),) * n_space,
        blocks,
        scratch_shapes=[pltpu.VMEM((n_space, out_rows, 2 * bands), F32)],
    )
    shares = [cyclic(b, "space", shift) if shift else b for shift, b in enumerate(shares)]
    margin, projection = call(
        last_kernel, "space_sum", (struct((out_rows, bands)), struct((out_rows, bands))), shares
    )
    return filtered.reshape(orbitals.shape), margin, projection


def solution(mesh):
    in_specs = (
        P("band", "space", None, None),
        P("band", "space", None, None),
        P("space", None, None),
        P("space", None, None, None, None),
        P(),
        P(),
    )
    out_specs = (P("band", "space", None, None), P("space", "band"), P("space", "band"))
    return jax.shard_map(shards, mesh=mesh, in_specs=in_specs, out_specs=out_specs, check_vma=False)
```

time: 54.4 us -> 57.7 us (1.061)
  starting transfers between devices: 13.5 us -> 27.9 us
  blocking collectives: 11.2 us -> 0 us
  waiting for transfers between devices: 12.3 us -> 14.8 us
  other arithmetic: 1.55 us -> 0.1 us
  local copies, waits for them, and re-layouts: 8.46 us -> 7.07 us
    ppermute x3 -> x19, starting transfers between devices: 3.45 us -> 27.9 us  [cyclic(): lax.ppermute(value, axis, [(i, (i + steps) % count) for i in range(count)])]
    all_to_all x1 -> x0, blocking collectives: 11.2 us -> none  [shards(): got = lax.all_to_all(pieces, ('space', 'band'), 0, 0)]
    ppermute x3 -> x19, waiting for transfers between devices: 4.47 us -> 14.8 us  [cyclic(): lax.ppermute(value, axis, [(i, (i + steps) % count) for i in range(count)])]
    all_to_all x2 -> x0, starting transfers between devices: 10.1 us -> none  [to_quarters(): return lax.all_to_all(jnp.transpose(cut, (1, 0, 2, 3)), 'band', 0, 0)]
    all_to_all x2 -> x0, waiting for transfers between devices: 7.79 us -> none  [to_quarters(): return lax.all_to_all(jnp.transpose(cut, (1, 0, 2, 3)), 'band', 0, 0)]
    unnamed x19 -> x17, local copies, waits for them, and re-layouts: 3.23 us -> 6.91 us
    reshape x6 -> x1, local copies, waits for them, and re-layouts: 3.01 us -> 0.16 us  [shards(): jnp.concatenate(panel, axis=0).reshape(total_bands, -1)]
    sub x1 -> x0, other arithmetic: 0.82 us -> none  [shards(): lax.dynamic_slice_in_dim(atom_planes, own_start, atoms, 0) - me * planes]
  transfers between devices with their start and end apart: 5 -> 19, of which waited for: 2 -> 11; matrix products, arithmetic and copies ran while one was open for 14% -> 1% of each run, Pallas kernels for 11% -> 9%
where the time goes in v2:
time: 57.7 us; the launch traced here: 56.7 us
  starting transfers between devices  27.9 us (48%)
  waiting for transfers between devices  14.8 us (26%)
  local copies, waits for them, and re-layouts  7.07 us (12%)
  Pallas kernels  5.78 us (10%)
  between operations  0.74 us (1%)
    ppermute x19, starting transfers between devices, cyclic(): lax.ppermute(value, axis, [(i, (i + steps) % count) for i in range(count)])  27.9 us
    ppermute x19, waiting for transfers between devices, cyclic(): lax.ppermute(value, axis, [(i, (i + steps) % count) for i in range(count)])  14.8 us
    unnamed x17, local copies, waits for them, and re-layouts  6.91 us
    pallas_call x8, Pallas kernels, call(): pl.pallas_call(kernel, out_shape=out_shape, compiler_params=params(), nam...  5.78 us
  transfers between devices with their start and end apart: 19, of which 11 were waited for; matrix products, arithmetic and copies ran while one was open for 1% of the time, Pallas kernels for 9%

profile of v2, /device:TPU:0, one launch (start us, length us, event | category | flops | bytes accessed | tf_op | source)
XLA Modules:
  0.0 56.7 jit_solution(10418145971633834378)
XLA Ops:
  0.6 0.0 copy-start
  0.6 1.1 %copy-done = f32[8,6,32,128]{3,2,1,0:T(8,128)S(1)} copy-done((f32[8,6,32,128]{3,2,1,0:T(8,128)S(1)}, f32[8,6,32,128]{3,2,1,0:T(8,128)}, u32[]{:S(2)}) %copy-start) | copy-done | bytes 786456
  1.8 0.1 cast.1
  1.8 0.0 copy-start.7
  1.9 3.4 %collective-permute-start = (bf16[8,192,128]{2,1,0:T(8,128)(2,1)S(1)}, bf16[8,192,128]{2,1,0:T(8,128)(2,1)S(1)}, u32[]{:S(2)}, u32[]{:S(2)}) collective-permute-start(bf16[8,192,128]{2,1,0:T(8,128)(2,1)S(1)} %get-tuple-element.31.own_ref), channel_id=1, source_target_pairs={{0,28},{4,0},{8,4},{12,8},{16,12},{20,16},{24,20},{28,24},{1,29},{... | collective-permute-start | bytes 1179656 | tf_op jit(solution)/shard_map/ppermute | solution.py:222
  5.2 0.8 %copy.11.strength_ref = f32[32,9]{1,0:T(8,128)S(1)} copy(f32[32,9]{0,1:T(8,128)} %param.12) | data formatting | bytes 2304 | tf_op args[4]
  6.0 1.1 %copy-done.1 = f32[8,6,32,128]{3,2,1,0:T(8,128)S(1)} copy-done((f32[8,6,32,128]{3,2,1,0:T(8,128)S(1)}, f32[8,6,32,128]{3,2,1,0:T(8,128)}, u32[]{:S(2)}) %copy-start.1) | copy-done | bytes 786456
  7.2 1.1 %copy-done.3 = f32[8,6,32,128]{3,2,1,0:T(8,128)S(1)} copy-done((f32[8,6,32,128]{3,2,1,0:T(8,128)S(1)}, f32[8,6,32,128]{3,2,1,0:T(8,128)}, u32[]{:S(2)}) %copy-start.3) | copy-done | bytes 786456
  8.3 0.9 %copy-done.4 = bf16[2,256,256]{2,1,0:T(8,128)(2,1)S(1)} copy-done((bf16[2,256,256]{2,1,0:T(8,128)(2,1)S(1)}, bf16[2,256,256]{2,1,0:T(8,128)(2,1)}, u32[]{:S(2)}) %copy-start.4) | copy-done | bytes 262168
  9.2 0.9 %copy-done.5 = f32[6,32,128]{2,1,0:T(8,128)S(1)} copy-done((f32[6,32,128]{2,1,0:T(8,128)S(1)}, f32[6,32,128]{2,1,0:T(8,128)}, u32[]{:S(2)}) %copy-start.5) | copy-done | bytes 98328
  10.1 0.9 %copy-done.6 = bf16[384,128]{1,0:T(8,128)(2,1)S(1)} copy-done((bf16[384,128]{1,0:T(8,128)(2,1)S(1)}, bf16[384,128]{1,0:T(8,128)(2,1)}, u32[]{:S(2)}) %copy-start.6) | copy-done | bytes 98328
  11.0 1.1 %local_part.1.g_ref = f32[8,192,128]{2,1,0:T(8,128)S(1)} custom-call(f32[8,192,128]{2,1,0:T(8,128)S(1)} %bitcast.12, f32[8,192,128]{2,1,0:T(8,128)S(1)} %bitcast.13, f32[192,128]{1,0:T(8,128)S(1)} %bitcast.14, bf16[384,128]{1,0:T(8,128)(2,1)S(1)} %copy-done.6, bf16[2,256,256]{2,1,0:T(8,128)(2,1)S(1)} %copy-done.4), custom_call_target="tpu_custom_call" | custom-call | tf_op jit(solution)/shard_map/local_part/pallas_call | solution.py:230
  12.1 1.7 %collective-permute-done.upper_ref = bf16[8,192,128]{2,1,0:T(8,128)(2,1)S(1)} collective-permute-done((bf16[8,192,128]{2,1,0:T(8,128)(2,1)S(1)}, bf16[8,192,128]{2,1,0:T(8,128)(2,1)S(1)}, u32[]{:S(2)}, u32[]{:S(2)}) %collective-permute-start) | collective-permute-done | bytes 393248 | tf_op jit(solution)/shard_map/ppermute | solution.py:222
  13.9 2.4 %projector_part.1 = (f32[8,192,128]{2,1,0:T(8,128)S(1)}, bf16[8,160,128]{2,1,0:T(8,128)(2,1)S(1)}) custom-call(s32[32]{0:T(128)S(1)} %copy-done.7, f32[32,9]{1,0:T(8,128)S(1)} %copy.11.strength_ref, bf16[8,192,128]{2,1,0:T(8,128)(2,1)S(1)} %get-tuple-element.31.own_ref, bf16[8,192,128]{2,1,0:T(8,128)(2,1)S(1)} %collective-permute-done.upper_ref, ...), custom_call_target="tpu_custom_call" | custom-call | tf_op jit(solution)/shard_map/projector_part/pallas_call | solution.py:230
  16.2 0.1 collective-permute-start.2
  16.3 1.6 %collective-permute-start.6 = (bf16[8,48,128]{2,1,0:T(8,128)(2,1)S(1)}, bf16[8,48,128]{2,1,0:T(8,128)(2,1)S(1)}, u32[]{:S(2)}, u32[]{:S(2)}) collective-permute-start(bf16[8,48,128]{2,1,0:T(8,128)(2,1)S(1)} %get-tuple-element.42), channel_id=1, source_target_pairs={{0,1},{1,2},{2,3},{3,0},{4,5},{5,6},{6,7},{7,4},{8,9},{9,10},{10,1... | collective-permute-start | bytes 294920 | tf_op jit(solution)/shard_map/ppermute | solution.py:222
  17.9 2.6 %collective-permute-start.7 = (bf16[8,48,128]{2,1,0:T(8,128)(2,1)S(1)}, bf16[8,48,128]{2,1,0:T(8,128)(2,1)S(1)}, u32[]{:S(2)}, u32[]{:S(2)}) collective-permute-start(bf16[8,48,128]{2,1,0:T(8,128)(2,1)S(1)} %get-tuple-element.43), channel_id=1, source_target_pairs={{0,2},{1,3},{2,0},{3,1},{4,6},{5,7},{6,4},{7,5},{8,10},{9,11},{10,... | collective-permute-start | bytes 294920 | tf_op jit(solution)/shard_map/ppermute | solution.py:222
  20.5 1.3 %collective-permute-start.8 = (bf16[8,48,128]{2,1,0:T(8,128)(2,1)S(1)}, bf16[8,48,128]{2,1,0:T(8,128)(2,1)S(1)}, u32[]{:S(2)}, u32[]{:S(2)}) collective-permute-start(bf16[8,48,128]{2,1,0:T(8,128)(2,1)S(1)} %get-tuple-element.44), channel_id=1, source_target_pairs={{0,3},{1,0},{2,1},{3,2},{4,7},{5,4},{6,5},{7,6},{8,11},{9,8},{10,9... | collective-permute-start | bytes 294920 | tf_op jit(solution)/shard_map/ppermute | solution.py:222
  21.9 0.6 %halo_part.1.g_ref = f32[8,192,128]{2,1,0:T(8,128)S(1)} custom-call(f32[8,192,128]{2,1,0:T(8,128)S(1)} %local_part.1.g_ref, f32[8,192,128]{2,1,0:T(8,128)S(1)} %get-tuple-element.34.near_ref, bf16[8,192,128]{2,1,0:T(8,128)(2,1)S(1)} %collective-permute-done.upper_ref, bf16[8,192,128]{2,1,0:T(8,128)(2,1)S(1)} %collective-permute-done.1.lower_ref), custom_call_target="tpu_custom_call" | custom-call | tf_op jit(solution)/shard_map/halo_part/pallas_call | solution.py:230
  22.4 1.4 %collective-permute-done.2.arrived_ref = bf16[8,160,128]{2,1,0:T(8,128)(2,1)S(1)} collective-permute-done((bf16[8,160,128]{2,1,0:T(8,128)(2,1)S(1)}, bf16[8,160,128]{2,1,0:T(8,128)(2,1)S(1)}, u32[]{:S(2)}, u32[]{:S(2)}) %collective-permute-start.2) | collective-permute-done | bytes 327712 | tf_op jit(solution)/shard_map/ppermute | solution.py:222
  23.8 0.9 %finish.1 = (bf16[8,192,128]{2,1,0:T(8,128)(2,1)}, bf16[8,48,128]{2,1,0:T(8,128)(2,1)S(1)}, bf16[8,48,128]{2,1,0:T(8,128)(2,1)S(1)}, bf16[8,48,128]{2,1,0:T(8,128)(2,1)S(1)}, bf16[8,48,128]{2,1,0:T(8,128)(2,1)S(1)}) custom-call(f32[8,192,128]{2,1,0:T(8,128)S(1)} %halo_part.1.g_ref, bf16[8,160,128]{2,1,0:T(8,128)(2,1)S(1)} %collective-permute-done.2.arrived_ref), custom_call_target="tpu_custom_call" | custom-call | tf_op jit(solution)/shard_map/finish/pallas_call | solution.py:230
  24.7 1.6 %collective-permute-start.3 = (bf16[8,48,128]{2,1,0:T(8,128)(2,1)S(1)}, bf16[8,48,128]{2,1,0:T(8,128)(2,1)S(1)}, u32[]{:S(2)}, u32[]{:S(2)}) collective-permute-start(bf16[8,48,128]{2,1,0:T(8,128)(2,1)S(1)} %get-tuple-element.38), channel_id=1, source_target_pairs={{0,1},{1,2},{2,3},{3,0},{4,5},{5,6},{6,7},{7,4},{8,9},{9,10},{10,1... | collective-permute-start | bytes 294920 | tf_op jit(solution)/shard_map/ppermute | solution.py:222
  26.3 2.6 %collective-permute-start.4 = (bf16[8,48,128]{2,1,0:T(8,128)(2,1)S(1)}, bf16[8,48,128]{2,1,0:T(8,128)(2,1)S(1)}, u32[]{:S(2)}, u32[]{:S(2)}) collective-permute-start(bf16[8,48,128]{2,1,0:T(8,128)(2,1)S(1)} %get-tuple-element.39), channel_id=1, source_target_pairs={{0,2},{1,3},{2,0},{3,1},{4,6},{5,7},{6,4},{7,5},{8,10},{9,11},{10,... | collective-permute-start | bytes 294920 | tf_op jit(solution)/shard_map/ppermute | solution.py:222
  28.9 1.3 %collective-permute-start.5 = (bf16[8,48,128]{2,1,0:T(8,128)(2,1)S(1)}, bf16[8,48,128]{2,1,0:T(8,128)(2,1)S(1)}, u32[]{:S(2)}, u32[]{:S(2)}) collective-permute-start(bf16[8,48,128]{2,1,0:T(8,128)(2,1)S(1)} %get-tuple-element.40), channel_id=1, source_target_pairs={{0,3},{1,0},{2,1},{3,2},{4,7},{5,4},{6,5},{7,6},{8,11},{9,8},{10,9... | collective-permute-start | bytes 294920 | tf_op jit(solution)/shard_map/ppermute | solution.py:222
  30.3 0.1 pad_maximum_fusion.1
  30.3 0.9 %collective-permute-done.3 = bf16[8,48,128]{2,1,0:T(8,128)(2,1)S(1)} collective-permute-done((bf16[8,48,128]{2,1,0:T(8,128)(2,1)S(1)}, bf16[8,48,128]{2,1,0:T(8,128)(2,1)S(1)}, u32[]{:S(2)}, u32[]{:S(2)}) %collective-permute-start.3) | collective-permute-done | bytes 98336 | tf_op jit(solution)/shard_map/ppermute | solution.py:222
  31.3 3.8 %collective-permute-done.4 = bf16[8,48,128]{2,1,0:T(8,128)(2,1)S(1)} collective-permute-done((bf16[8,48,128]{2,1,0:T(8,128)(2,1)S(1)}, bf16[8,48,128]{2,1,0:T(8,128)(2,1)S(1)}, u32[]{:S(2)}, u32[]{:S(2)}) %collective-permute-start.4) | collective-permute-done | bytes 98336 | tf_op jit(solution)/shard_map/ppermute | solution.py:222
  35.1 0.3 collective-permute-done.5
  35.4 0.1 pad_maximum_fusion
  35.4 0.2 copy_bitcast_fusion
  35.6 0.3 convolution_multiply_fusion.prod_ref
  35.9 0.1 split.1
  36.0 3.2 %collective-permute-start.9 = (f32[32,16]{1,0:T(8,128)S(1)}, f32[32,16]{1,0:T(8,128)S(1)}, u32[]{:S(2)}, u32[]{:S(2)}) collective-permute-start(f32[32,16]{1,0:T(8,128)S(1)} %get-tuple-element.46), channel_id=1, source_target_pairs={{0,3},{1,0},{2,1},{3,2},{4,7},{5,4},{6,5},{7,6},{8,11},{9,8},{10,9... | collective-permute-start | bytes 6152 | tf_op jit(solution)/shard_map/ppermute | solution.py:222
  39.3 0.4 collective-permute-start.10
  39.7 0.2 collective-permute-start.11
  39.9 0.8 %collective-permute-done.9.refs_1_ = f32[32,16]{1,0:T(8,128)S(1)} collective-permute-done((f32[32,16]{1,0:T(8,128)S(1)}, f32[32,16]{1,0:T(8,128)S(1)}, u32[]{:S(2)}, u32[]{:S(2)}) %collective-permute-start.9) | collective-permute-done | bytes 2080 | tf_op jit(solution)/shard_map/ppermute | solution.py:222
  40.7 3.2 %collective-permute-done.10.refs_2_ = f32[32,16]{1,0:T(8,128)S(1)} collective-permute-done((f32[32,16]{1,0:T(8,128)S(1)}, f32[32,16]{1,0:T(8,128)S(1)}, u32[]{:S(2)}, u32[]{:S(2)}) %collective-permute-start.10) | collective-permute-done | bytes 2080 | tf_op jit(solution)/shard_map/ppermute | solution.py:222
  43.9 1.3 %collective-permute-done.11.refs_3_ = f32[32,16]{1,0:T(8,128)S(1)} collective-permute-done((f32[32,16]{1,0:T(8,128)S(1)}, f32[32,16]{1,0:T(8,128)S(1)}, u32[]{:S(2)}, u32[]{:S(2)}) %collective-permute-start.11) | collective-permute-done | bytes 2080 | tf_op jit(solution)/shard_map/ppermute | solution.py:222
  45.2 0.1 collective-permute-start.12
  45.3 3.9 %collective-permute-start.13 = (f32[4,16]{1,0:T(4,128)S(1)}, f32[4,16]{1,0:T(4,128)S(1)}, u32[]{:S(2)}, u32[]{:S(2)}) collective-permute-start(f32[4,16]{1,0:T(4,128)S(1)} %get-tuple-element.51), channel_id=1, source_target_pairs={{0,8},{4,12},{8,16},{12,20},{16,24},{20,28},{24,0},{28,4},{1,9},{5... | collective-permute-start | bytes 776 | tf_op jit(solution)/shard_map/ppermute | solution.py:222
  49.2 1.6 %collective-permute-start.14 = (f32[4,16]{1,0:T(4,128)S(1)}, f32[4,16]{1,0:T(4,128)S(1)}, u32[]{:S(2)}, u32[]{:S(2)}) collective-permute-start(f32[4,16]{1,0:T(4,128)S(1)} %get-tuple-element.52), channel_id=1, source_target_pairs={{0,12},{4,16},{8,20},{12,24},{16,28},{20,0},{24,4},{28,8},{1,13},{... | collective-permute-start | bytes 776 | tf_op jit(solution)/shard_map/ppermute | solution.py:222
  50.7 1.3 %collective-permute-start.15 = (f32[4,16]{1,0:T(4,128)S(1)}, f32[4,16]{1,0:T(4,128)S(1)}, u32[]{:S(2)}, u32[]{:S(2)}) collective-permute-start(f32[4,16]{1,0:T(4,128)S(1)} %get-tuple-element.53), channel_id=1, source_target_pairs={{0,16},{4,20},{8,24},{12,28},{16,0},{20,4},{24,8},{28,12},{1,17},{... | collective-permute-start | bytes 776 | tf_op jit(solution)/shard_map/ppermute | solution.py:222
  52.0 1.2 %collective-permute-start.17 = (f32[4,16]{1,0:T(4,128)S(1)}, f32[4,16]{1,0:T(4,128)S(1)}, u32[]{:S(2)}, u32[]{:S(2)}) collective-permute-start(f32[4,16]{1,0:T(4,128)S(1)} %get-tuple-element.55), channel_id=1, source_target_pairs={{0,24},{4,28},{8,0},{12,4},{16,8},{20,12},{24,16},{28,20},{1,25},{... | collective-permute-start | bytes 776 | tf_op jit(solution)/shard_map/ppermute | solution.py:222
  53.2 1.5 %collective-permute-start.18 = (f32[4,16]{1,0:T(4,128)S(1)}, f32[4,16]{1,0:T(4,128)S(1)}, u32[]{:S(2)}, u32[]{:S(2)}) collective-permute-start(f32[4,16]{1,0:T(4,128)S(1)} %get-tuple-element.56), channel_id=1, source_target_pairs={{0,28},{4,0},{8,4},{12,8},{16,12},{20,16},{24,20},{28,24},{1,29},{... | collective-permute-start | bytes 776 | tf_op jit(solution)/shard_map/ppermute | solution.py:222
  54.7 0.3 collective-permute-done.16.refs_5_
  55.0 0.6 %collective-permute-done.17.refs_6_ = f32[4,16]{1,0:T(4,128)S(1)} collective-permute-done((f32[4,16]{1,0:T(4,128)S(1)}, f32[4,16]{1,0:T(4,128)S(1)}, u32[]{:S(2)}, u32[]{:S(2)}) %collective-permute-start.17) | collective-permute-done | bytes 288 | tf_op jit(solution)/shard_map/ppermute | solution.py:222
  55.6 0.4 collective-permute-done.18.refs_7_
  56.0 0.7 %space_sum.1 = (f32[4,8]{1,0:T(4,128)}, f32[4,8]{1,0:T(4,128)}) custom-call(f32[4,16]{1,0:T(4,128)S(1)} %get-tuple-element.49.refs_0_, f32[4,16]{1,0:T(4,128)S(1)} %collective-permute-done.12.refs_1_, f32[4,16]{1,0:T(4,128)S(1)} %collective-permute-done.13.refs_2_, f32[4,16]{1,0:T(4,128)S(1)} %collective-permute-done.14.refs_3_, ...), custom_call_target="tpu_custom_call" | custom-call | tf_op jit(solution)/shard_map/space_sum/pallas_call | solution.py:230
  (19 shorter events, 0.1 us)
Async XLA Ops:
  0.6 1.1 %copy-start = (f32[8,6,32,128]{3,2,1,0:T(8,128)S(1)}, f32[8,6,32,128]{3,2,1,0:T(8,128)}, u32[]{:S(2)}) copy-start(f32[8,6,32,128]{3,2,1,0:T(8,128)} %param.8) | copy-start | bytes 2359300
  1.8 12.0 %copy-start.7 = (s32[32]{0:T(128)S(1)}, s32[32]{0:T(128)}, u32[]{:S(2)}) copy-start(s32[32]{0:T(128)} %first_ref.1) | copy-start | bytes 388
  1.9 12.0 %collective-permute-start = (bf16[8,192,128]{2,1,0:T(8,128)(2,1)S(1)}, bf16[8,192,128]{2,1,0:T(8,128)(2,1)S(1)}, u32[]{:S(2)}, u32[]{:S(2)}) collective-permute-start(bf16[8,192,128]{2,1,0:T(8,128)(2,1)S(1)} %get-tuple-element.31.own_ref), channel_id=1, source_target_pairs={{0,28},{4,0},{8,4},{12,8},{16,12},{20,16},{24,20},{28,24},{1,29},{... | collective-permute-start | bytes 1179656 | tf_op jit(solution)/shard_map/ppermute | solution.py:222
  5.2 16.6 %collective-permute-start.1 = (bf16[8,192,128]{2,1,0:T(8,128)(2,1)S(1)}, bf16[8,192,128]{2,1,0:T(8,128)(2,1)S(1)}, u32[]{:S(2)}, u32[]{:S(2)}) collective-permute-start(bf16[8,192,128]{2,1,0:T(8,128)(2,1)S(1)} %get-tuple-element.31.own_ref), channel_id=1, source_target_pairs={{0,4},{4,8},{8,12},{12,16},{16,20},{20,24},{24,28},{28,0},{1,5},{5... | collective-permute-start | bytes 1179656 | tf_op jit(solution)/shard_map/ppermute | solution.py:222
  6.0 1.1 %copy-start.1 = (f32[8,6,32,128]{3,2,1,0:T(8,128)S(1)}, f32[8,6,32,128]{3,2,1,0:T(8,128)}, u32[]{:S(2)}) copy-start(f32[8,6,32,128]{3,2,1,0:T(8,128)} %param.8) | copy-start | bytes 2359300
  7.2 1.1 %copy-start.3 = (f32[8,6,32,128]{3,2,1,0:T(8,128)S(1)}, f32[8,6,32,128]{3,2,1,0:T(8,128)}, u32[]{:S(2)}) copy-start(f32[8,6,32,128]{3,2,1,0:T(8,128)} %param.9) | copy-start | bytes 2359300
  8.3 0.9 %copy-start.4 = (bf16[2,256,256]{2,1,0:T(8,128)(2,1)S(1)}, bf16[2,256,256]{2,1,0:T(8,128)(2,1)}, u32[]{:S(2)}) copy-start(bf16[2,256,256]{2,1,0:T(8,128)(2,1)} %constant.7.clone.cy_ref) | copy-start | bytes 786436
  9.2 0.9 %copy-start.5 = (f32[6,32,128]{2,1,0:T(8,128)S(1)}, f32[6,32,128]{2,1,0:T(8,128)}, u32[]{:S(2)}) copy-start(f32[6,32,128]{2,1,0:T(8,128)} %param.10) | copy-start | bytes 294916
  10.1 0.9 %copy-start.6 = (bf16[384,128]{1,0:T(8,128)(2,1)S(1)}, bf16[384,128]{1,0:T(8,128)(2,1)}, u32[]{:S(2)}) copy-start(bf16[384,128]{1,0:T(8,128)(2,1)} %constant.6.clone.cz_ref) | copy-start | bytes 294916
  11.0 2.8 %copy-start.2 = (bf16[4,9,6,32,128]{4,3,2,1,0:T(8,128)(2,1)S(1)}, bf16[4,9,6,32,128]{4,3,2,1,0:T(8,128)(2,1)}, u32[]{:S(2)}) copy-start(bf16[4,9,6,32,128]{4,3,2,1,0:T(8,128)(2,1)} %proj_ref.1) | copy-start | bytes 5308420
  16.2 7.6 %collective-permute-start.2 = (bf16[8,160,128]{2,1,0:T(8,128)(2,1)S(1)}, bf16[8,160,128]{2,1,0:T(8,128)(2,1)S(1)}, u32[]{:S(2)}, u32[]{:S(2)}) collective-permute-start(bf16[8,160,128]{2,1,0:T(8,128)(2,1)S(1)} %get-tuple-element.35), channel_id=1, source_target_pairs={{0,4},{4,8},{8,12},{12,16},{16,20},{20,24},{24,28},{28,0},{1,5},{5... | collective-permute-start | bytes 983048 | tf_op jit(solution)/shard_map/ppermute | solution.py:222
  16.3 12.6 %collective-permute-start.6 = (bf16[8,48,128]{2,1,0:T(8,128)(2,1)S(1)}, bf16[8,48,128]{2,1,0:T(8,128)(2,1)S(1)}, u32[]{:S(2)}, u32[]{:S(2)}) collective-permute-start(bf16[8,48,128]{2,1,0:T(8,128)(2,1)S(1)} %get-tuple-element.42), channel_id=1, source_target_pairs={{0,1},{1,2},{2,3},{3,0},{4,5},{5,6},{6,7},{7,4},{8,9},{9,10},{10,1... | collective-permute-start | bytes 294920 | tf_op jit(solution)/shard_map/ppermute | solution.py:222
  17.9 12.4 %collective-permute-start.7 = (bf16[8,48,128]{2,1,0:T(8,128)(2,1)S(1)}, bf16[8,48,128]{2,1,0:T(8,128)(2,1)S(1)}, u32[]{:S(2)}, u32[]{:S(2)}) collective-permute-start(bf16[8,48,128]{2,1,0:T(8,128)(2,1)S(1)} %get-tuple-element.43), channel_id=1, source_target_pairs={{0,2},{1,3},{2,0},{3,1},{4,6},{5,7},{6,4},{7,5},{8,10},{9,11},{10,... | collective-permute-start | bytes 294920 | tf_op jit(solution)/shard_map/ppermute | solution.py:222
  20.5 9.8 %collective-permute-start.8 = (bf16[8,48,128]{2,1,0:T(8,128)(2,1)S(1)}, bf16[8,48,128]{2,1,0:T(8,128)(2,1)S(1)}, u32[]{:S(2)}, u32[]{:S(2)}) collective-permute-start(bf16[8,48,128]{2,1,0:T(8,128)(2,1)S(1)} %get-tuple-element.44), channel_id=1, source_target_pairs={{0,3},{1,0},{2,1},{3,2},{4,7},{5,4},{6,5},{7,6},{8,11},{9,8},{10,9... | collective-permute-start | bytes 294920 | tf_op jit(solution)/shard_map/ppermute | solution.py:222
  24.7 6.5 %collective-permute-start.3 = (bf16[8,48,128]{2,1,0:T(8,128)(2,1)S(1)}, bf16[8,48,128]{2,1,0:T(8,128)(2,1)S(1)}, u32[]{:S(2)}, u32[]{:S(2)}) collective-permute-start(bf16[8,48,128]{2,1,0:T(8,128)(2,1)S(1)} %get-tuple-element.38), channel_id=1, source_target_pairs={{0,1},{1,2},{2,3},{3,0},{4,5},{5,6},{6,7},{7,4},{8,9},{9,10},{10,1... | collective-permute-start | bytes 294920 | tf_op jit(solution)/shard_map/ppermute | solution.py:222
  26.3 8.8 %collective-permute-start.4 = (bf16[8,48,128]{2,1,0:T(8,128)(2,1)S(1)}, bf16[8,48,128]{2,1,0:T(8,128)(2,1)S(1)}, u32[]{:S(2)}, u32[]{:S(2)}) collective-permute-start(bf16[8,48,128]{2,1,0:T(8,128)(2,1)S(1)} %get-tuple-element.39), channel_id=1, source_target_pairs={{0,2},{1,3},{2,0},{3,1},{4,6},{5,7},{6,4},{7,5},{8,10},{9,11},{10,... | collective-permute-start | bytes 294920 | tf_op jit(solution)/shard_map/ppermute | solution.py:222
  28.9 6.4 %collective-permute-start.5 = (bf16[8,48,128]{2,1,0:T(8,128)(2,1)S(1)}, bf16[8,48,128]{2,1,0:T(8,128)(2,1)S(1)}, u32[]{:S(2)}, u32[]{:S(2)}) collective-permute-start(bf16[8,48,128]{2,1,0:T(8,128)(2,1)S(1)} %get-tuple-element.40), channel_id=1, source_target_pairs={{0,3},{1,0},{2,1},{3,2},{4,7},{5,4},{6,5},{7,6},{8,11},{9,8},{10,9... | collective-permute-start | bytes 294920 | tf_op jit(solution)/shard_map/ppermute | solution.py:222
  36.0 4.7 %collective-permute-start.9 = (f32[32,16]{1,0:T(8,128)S(1)}, f32[32,16]{1,0:T(8,128)S(1)}, u32[]{:S(2)}, u32[]{:S(2)}) collective-permute-start(f32[32,16]{1,0:T(8,128)S(1)} %get-tuple-element.46), channel_id=1, source_target_pairs={{0,3},{1,0},{2,1},{3,2},{4,7},{5,4},{6,5},{7,6},{8,11},{9,8},{10,9... | collective-permute-start | bytes 6152 | tf_op jit(solution)/shard_map/ppermute | solution.py:222
  39.3 4.6 %collective-permute-start.10 = (f32[32,16]{1,0:T(8,128)S(1)}, f32[32,16]{1,0:T(8,128)S(1)}, u32[]{:S(2)}, u32[]{:S(2)}) collective-permute-start(f32[32,16]{1,0:T(8,128)S(1)} %get-tuple-element.47), channel_id=1, source_target_pairs={{0,2},{1,3},{2,0},{3,1},{4,6},{5,7},{6,4},{7,5},{8,10},{9,11},{10,... | collective-permute-start | bytes 6152 | tf_op jit(solution)/shard_map/ppermute | solution.py:222
  39.7 5.5 %collective-permute-start.11 = (f32[32,16]{1,0:T(8,128)S(1)}, f32[32,16]{1,0:T(8,128)S(1)}, u32[]{:S(2)}, u32[]{:S(2)}) collective-permute-start(f32[32,16]{1,0:T(8,128)S(1)} %get-tuple-element.48), channel_id=1, source_target_pairs={{0,1},{1,2},{2,3},{3,0},{4,5},{5,6},{6,7},{7,4},{8,9},{9,10},{10,1... | collective-permute-start | bytes 6152 | tf_op jit(solution)/shard_map/ppermute | solution.py:222
  45.2 6.8 %collective-permute-start.12 = (f32[4,16]{1,0:T(4,128)S(1)}, f32[4,16]{1,0:T(4,128)S(1)}, u32[]{:S(2)}, u32[]{:S(2)}) collective-permute-start(f32[4,16]{1,0:T(4,128)S(1)} %get-tuple-element.50), channel_id=1, source_target_pairs={{0,4},{4,8},{8,12},{12,16},{16,20},{20,24},{24,28},{28,0},{1,5},{5... | collective-permute-start | bytes 776 | tf_op jit(solution)/shard_map/ppermute | solution.py:222
  45.3 7.9 %collective-permute-start.13 = (f32[4,16]{1,0:T(4,128)S(1)}, f32[4,16]{1,0:T(4,128)S(1)}, u32[]{:S(2)}, u32[]{:S(2)}) collective-permute-start(f32[4,16]{1,0:T(4,128)S(1)} %get-tuple-element.51), channel_id=1, source_target_pairs={{0,8},{4,12},{8,16},{12,20},{16,24},{20,28},{24,0},{28,4},{1,9},{5... | collective-permute-start | bytes 776 | tf_op jit(solution)/shard_map/ppermute | solution.py:222
  49.2 5.6 %collective-permute-start.14 = (f32[4,16]{1,0:T(4,128)S(1)}, f32[4,16]{1,0:T(4,128)S(1)}, u32[]{:S(2)}, u32[]{:S(2)}) collective-permute-start(f32[4,16]{1,0:T(4,128)S(1)} %get-tuple-element.52), channel_id=1, source_target_pairs={{0,12},{4,16},{8,20},{12,24},{16,28},{20,0},{24,4},{28,8},{1,13},{... | collective-permute-start | bytes 776 | tf_op jit(solution)/shard_map/ppermute | solution.py:222
  50.7 4.0 %collective-permute-start.15 = (f32[4,16]{1,0:T(4,128)S(1)}, f32[4,16]{1,0:T(4,128)S(1)}, u32[]{:S(2)}, u32[]{:S(2)}) collective-permute-start(f32[4,16]{1,0:T(4,128)S(1)} %get-tuple-element.53), channel_id=1, source_target_pairs={{0,16},{4,20},{8,24},{12,28},{16,0},{20,4},{24,8},{28,12},{1,17},{... | collective-permute-start | bytes 776 | tf_op jit(solution)/shard_map/ppermute | solution.py:222
  52.0 3.0 %collective-permute-start.16 = (f32[4,16]{1,0:T(4,128)S(1)}, f32[4,16]{1,0:T(4,128)S(1)}, u32[]{:S(2)}, u32[]{:S(2)}) collective-permute-start(f32[4,16]{1,0:T(4,128)S(1)} %get-tuple-element.54), channel_id=1, source_target_pairs={{0,20},{4,24},{8,28},{12,0},{16,4},{20,8},{24,12},{28,16},{1,21},{... | collective-permute-start | bytes 776 | tf_op jit(solution)/shard_map/ppermute | solution.py:222
  52.0 3.6 %collective-permute-start.17 = (f32[4,16]{1,0:T(4,128)S(1)}, f32[4,16]{1,0:T(4,128)S(1)}, u32[]{:S(2)}, u32[]{:S(2)}) collective-permute-start(f32[4,16]{1,0:T(4,128)S(1)} %get-tuple-element.55), channel_id=1, source_target_pairs={{0,24},{4,28},{8,0},{12,4},{16,8},{20,12},{24,16},{28,20},{1,25},{... | collective-permute-start | bytes 776 | tf_op jit(solution)/shard_map/ppermute | solution.py:222
  53.2 2.8 %collective-permute-start.18 = (f32[4,16]{1,0:T(4,128)S(1)}, f32[4,16]{1,0:T(4,128)S(1)}, u32[]{:S(2)}, u32[]{:S(2)}) collective-permute-start(f32[4,16]{1,0:T(4,128)S(1)} %get-tuple-element.56), channel_id=1, source_target_pairs={{0,28},{4,0},{8,4},{12,8},{16,12},{20,16},{24,20},{28,24},{1,29},{... | collective-permute-start | bytes 776 | tf_op jit(solution)/shard_map/ppermute | solution.py:222

commit v3 on v2

--- a/solution.py
+++ b/solution.py
@@ -2,7 +2,6 @@
 
 import jax
 import jax.numpy as jnp
-import numpy as np
 from jax import lax
 from jax.experimental import pallas as pl
 from jax.experimental.pallas import tpu as pltpu
@@ -31,24 +30,22 @@
 BF16 = jnp.bfloat16
 
 
-def params(vmem=48 * 2**20):
+def params(vmem):
     return pltpu.CompilerParams(vmem_limit_bytes=vmem)
 
 
-def circulant(n):
-    c = np.zeros((n, n), np.float64)
-    for i in range(n):
-        c[i, i] += kinetic_weights[0]
-        for m in range(1, HALO + 1):
-            c[i, (i + m) % n] += kinetic_weights[m]
-            c[i, (i - m) % n] += kinetic_weights[m]
-    return c
-
-
-def split_hi_lo(m):
-    hi = np.asarray(m, np.float32).astype(jnp.bfloat16)
-    lo = (m - hi.astype(np.float64)).astype(np.float32).astype(jnp.bfloat16)
-    return hi, lo
+def circulant(n, blocks):
+    size = n * blocks
+    row = lax.broadcasted_iota(jnp.int32, (size, size), 0)
+    col = lax.broadcasted_iota(jnp.int32, (size, size), 1)
+    ahead = jnp.bitwise_and(col - row, n - 1)
+    reach = jnp.minimum(ahead, n - ahead)
+    value = jnp.zeros((size, size), F32)
+    for m, weight in enumerate(kinetic_weights):
+        value = jnp.where(reach == m, weight, value)
+    value = jnp.where(row // n == col // n, value, 0.0)
+    hi = value.astype(BF16)
+    return hi, (value - hi.astype(F32)).astype(BF16)
 
 
 def dot(a, b, dims=((1,), (0,))):
@@ -59,9 +56,13 @@
     return slice(x * ny, (x + 1) * ny)
 
 
+def partners(count):
+    return [0, *range(count // 2, count), *range(1, count // 2)]
+
+
 def pieces_of(ref, index, count, rows, outs):
-    for shift, out in enumerate(outs):
-        quarter = lax.rem(index + shift, count)
+    for bits, out in zip(partners(count), outs):
+        quarter = jnp.bitwise_xor(index, bits)
         begin = pl.multiple_of(quarter * rows, 8)
         out[...] = ref[:, pl.ds(begin, rows), :].astype(out.dtype)
 
@@ -72,10 +73,22 @@
     pieces_of(psi_ref, lax.axis_index("band"), count, rows, outs)
 
 
-def local_kernel(planes, psi_ref, prev_ref, pot_ref, cz_ref, cy_ref, g_ref):
+def local_kernel(planes, psi_ref, prev_hbm, pot_hbm, g_ref, half_ref, prev_ref, pot_ref, sems):
+    copies = [
+        pltpu.make_async_copy(prev_hbm, prev_ref, sems.at[0]),
+        pltpu.make_async_copy(pot_hbm, pot_ref, sems.at[1]),
+    ]
+    for copy in copies:
+        copy.start()
+    half_ref[...] = psi_ref[...].astype(BF16)
     bands, cells, nz = psi_ref.shape
     ny = cells // planes
     rows = bands * ny
+    cz_hi, cz_lo = circulant(nz, 1)
+    cz_twice = jnp.concatenate([cz_hi, cz_hi], axis=0)
+    cy_hi, cy_lo = circulant(ny, bands)
+    for copy in copies:
+        copy.wait()
     for x in range(planes):
         here = plane_rows(x, ny)
         psi3 = psi_ref[:, here]
@@ -83,9 +96,9 @@
         hi = psi.astype(BF16)
         lo = (psi - hi.astype(F32)).astype(BF16)
         both = jnp.concatenate([hi, lo], axis=1)
-        along_z = dot(both, cz_ref[0 : 2 * nz]) + dot(hi, cz_ref[2 * nz : 3 * nz])
-        pair = dot(cy_ref[0], both)
-        along_y = pair[:, :nz] + pair[:, nz:] + dot(cy_ref[1], hi)
+        along_z = dot(both, cz_twice) + dot(hi, cz_lo)
+        pair = dot(cy_hi, both)
+        along_y = pair[:, :nz] + pair[:, nz:] + dot(cy_lo, hi)
         total = (along_z + along_y).reshape(bands, ny, nz)
         site = outer * pot_ref[here] + (kinetic_weights[0] - outer * center)
         total = total + site[None] * psi3
@@ -141,7 +154,7 @@
     for a in range(atoms):
         scale = jnp.zeros((1, cols), F32)
         for j in range(npj):
-            scale = jnp.where(owner == j, outer * strength_ref[me * atoms + a, j], scale)
+            scale = jnp.where(owner == j, outer * strength_ref[j, me * atoms + a], scale)
         w = coef[a * bands : (a + 1) * bands] * scale
         full = jnp.broadcast_to(w[:, None, :], (bands, HALF, cols)).reshape(rows, cols) * mask
         full = full.astype(BF16)
@@ -182,39 +195,26 @@
     pieces_of(total, lax.axis_index("band"), count, rows, outs)
 
 
-def split_kernel(count, prod_ref, *outs):
-    bands = prod_ref.shape[0] // count
+def split_kernel(n_space, n_band, prod_ref, out_ref, held):
+    bands = prod_ref.shape[0] // n_band
     me = lax.axis_index("band")
-    for back, out in enumerate(outs):
-        for j in range(count):
-            shift = lax.rem(me - j + count, count)
-            rows = pl.ds(pl.multiple_of(shift * bands, 8), bands)
-            block = prod_ref[rows, :]
-            cols = [block[:, (h * count + back) * bands : (h * count + back + 1) * bands] for h in (0, 1)]
-            out[j * bands : (j + 1) * bands, :] = jnp.concatenate(cols, axis=1)
-
-
-def sum_kernel(count, *refs):
-    parts, outs, held = refs[:-count - 1], refs[-count - 1 : -1], refs[-1]
-    total = parts[0][...]
-    for part in parts[1:]:
-        total = total + part[...]
-    rows = total.shape[0] // count
-    for i in range(count):
-        held[i] = total[i * rows : (i + 1) * rows]
-    me = lax.axis_index("space")
-    for shift, out in enumerate(outs):
-        out[...] = held[lax.rem(me + shift, count)]
-
-
-def last_kernel(*refs):
-    parts, outs = refs[:-2], refs[-2:]
-    total = parts[0][...]
-    for part in parts[1:]:
-        total = total + part[...]
-    bands = outs[0].shape[1]
-    outs[0][...] = total[:, :bands]
-    outs[1][...] = total[:, bands:]
+    for p, bits in enumerate(partners(n_band)):
+        begin = pl.multiple_of(jnp.bitwise_xor(me, bits) * bands, 8)
+        held[pl.ds(begin, bands), :] = prod_ref[p * bands : (p + 1) * bands]
+    rows = held.shape[0] // n_space
+    for p, bits in enumerate(partners(n_band)):
+        cols = [slice((h * n_band + p) * bands, (h * n_band + p + 1) * bands) for h in (0, 1)]
+        pair = jnp.concatenate([held[:, c] for c in cols], axis=1)
+        owner = jnp.bitwise_xor(me, bits)
+        for i in range(n_space):
+            out_ref[i * n_band + owner] = pair[i * rows : (i + 1) * rows]
+
+
+def last_kernel(got_ref, margin_ref, projection_ref):
+    total = got_ref[...].sum(axis=0)
+    bands = margin_ref.shape[1]
+    margin_ref[...] = total[:, :bands]
+    projection_ref[...] = total[:, bands:]
 
 
 def cyclic(value, axis, steps):
@@ -222,13 +222,23 @@
     return lax.ppermute(value, axis, [(i, (i + steps) % count) for i in range(count)])
 
 
+def mirrored(value, axis, bits):
+    count = lax.axis_size(axis)
+    return lax.ppermute(value, axis, [(i, i ^ bits) for i in range(count)])
+
+
+def exchanged(pieces):
+    offsets = partners(len(pieces))
+    return [mirrored(p, "band", bits) if bits else p for bits, p in zip(offsets, pieces)]
+
+
 def struct(shape, kind=F32):
     return jax.ShapeDtypeStruct(shape, kind)
 
 
-def call(kernel, name, out_shape, args, **extra):
+def call(kernel, name, out_shape, args, vmem=48, **extra):
     return pl.pallas_call(
-        kernel, out_shape=out_shape, compiler_params=params(), name=name, **extra
+        kernel, out_shape=out_shape, compiler_params=params(vmem * 2**20), name=name, **extra
     )(*args)
 
 
@@ -243,6 +253,10 @@
     prev = previous.reshape(whole)
     pot = potential.reshape(cells, nz)
 
+    vm = pl.BlockSpec(memory_space=pltpu.VMEM)
+    sm = pl.BlockSpec(memory_space=pltpu.SMEM)
+    anywhere = pl.BlockSpec(memory_space=pl.ANY)
+
     half, *panel = call(
         partial(cast_kernel, n_band),
         "cast",
@@ -250,22 +264,30 @@
         (psi,),
     )
     upper = cyclic(half, "space", -1)
-    lower = cyclic(half, "space", 1)
-    panel = [cyclic(piece, "band", shift) if shift else piece for shift, piece in enumerate(panel)]
-
-    cz_hi, cz_lo = split_hi_lo(circulant(nz))
-    cz = jnp.asarray(np.concatenate([cz_hi, cz_hi, cz_lo], axis=0))
-    cy = jnp.asarray(np.stack(split_hi_lo(np.kron(np.eye(bands), circulant(ny)))))
-    g = call(partial(local_kernel, planes), "local_part", struct(whole), (psi, prev, pot, cz, cy))
+    panel = exchanged(panel)
+
+    g, again = call(
+        partial(local_kernel, planes),
+        "local_part",
+        (struct(whole), struct(whole, BF16)),
+        (psi, prev, pot),
+        vmem=58,
+        in_specs=[vm, anywhere, anywhere],
+        out_specs=(vm, vm),
+        scratch_shapes=[
+            pltpu.VMEM(whole, F32),
+            pltpu.VMEM(pot.shape, F32),
+            pltpu.SemaphoreType.DMA((2,)),
+        ],
+    )
+    lower = cyclic(again, "space", 1)
     upper, g = lax.optimization_barrier((upper, g))
 
-    vm = pl.BlockSpec(memory_space=pltpu.VMEM)
-    sm = pl.BlockSpec(memory_space=pltpu.SMEM)
     near, beyond = call(
         partial(projector_kernel, planes),
         "projector_part",
         (struct(whole), struct((bands, (BOX - 1) * ny, nz), BF16)),
-        (atom_planes, strengths, half, upper, projectors),
+        (atom_planes, strengths.T, half, upper, projectors),
         in_specs=[sm, sm, vm, vm, vm],
         out_specs=(vm, vm),
         scratch_shapes=[
@@ -282,29 +304,22 @@
         (g, arrived),
         scratch_shapes=[pltpu.VMEM(whole, F32)],
     )
-    mine = [cyclic(piece, "band", shift) if shift else piece for shift, piece in enumerate(mine)]
+    mine = exchanged(mine)
     total_bands = n_band * bands
     left = jnp.concatenate(mine, axis=0).reshape(total_bands, -1)
     right = jnp.concatenate([left, jnp.concatenate(panel, axis=0).reshape(total_bands, -1)], axis=0)
     products = dot(left, right, ((1,), (1,))) * (1.0 / (cells * n_space * nz))
-    blocks = call(
-        partial(split_kernel, n_band),
+    out_rows = total_bands // n_space
+    pieces = call(
+        partial(split_kernel, n_space, n_band),
         "split",
-        (struct((total_bands, 2 * bands)),) * n_band,
+        struct((n_space * n_band, out_rows, 2 * bands)),
         (products,),
-    )
-    blocks = [cyclic(b, "band", -shift) if shift else b for shift, b in enumerate(blocks)]
-    out_rows = total_bands // n_space
-    shares = call(
-        partial(sum_kernel, n_space),
-        "band_sum",
-        (struct((out_rows, 2 * bands)),) * n_space,
-        blocks,
-        scratch_shapes=[pltpu.VMEM((n_space, out_rows, 2 * bands), F32)],
-    )
-    shares = [cyclic(b, "space", shift) if shift else b for shift, b in enumerate(shares)]
+        scratch_shapes=[pltpu.VMEM(products.shape, F32)],
+    )
+    got = lax.all_to_all(pieces, ("space", "band"), 0, 0)
     margin, projection = call(
-        last_kernel, "space_sum", (struct((out_rows, bands)), struct((out_rows, bands))), shares
+        last_kernel, "last_sum", (struct((out_rows, bands)), struct((out_rows, bands))), (got,)
     )
     return filtered.reshape(orbitals.shape), margin, projection
 

time: 57.7 us -> 48.2 us (0.84); the launches traced: 56.7 us -> 48 us
  starting transfers between devices: 27.9 us -> 11.9 us
  blocking collectives: 0 us -> 14.3 us
  local copies, waits for them, and re-layouts: 7.07 us -> 1.3 us
  waiting for transfers between devices: 14.8 us -> 10.5 us
  Pallas kernels: 5.78 us -> 8.81 us
    ppermute x19 -> x3, starting transfers between devices: 27.9 us -> 3.5 us  [cyclic(): lax.ppermute(value, axis, [(i, (i + steps) % count) for i in range(count)])]
    all_to_all x0 -> x1, blocking collectives: none -> 14.3 us  [shards(): got = lax.all_to_all(pieces, ('space', 'band'), 0, 0)]
    ppermute x19 -> x3, waiting for transfers between devices: 14.8 us -> 4.7 us  [cyclic(): lax.ppermute(value, axis, [(i, (i + steps) % count) for i in range(count)])]
    ppermute x0 -> x6, starting transfers between devices: none -> 8.41 us  [mirrored(): return lax.ppermute(value, axis, [(i, i ^ bits) for i in range(count)])]
    ppermute x0 -> x6, waiting for transfers between devices: none -> 5.83 us  [mirrored(): return lax.ppermute(value, axis, [(i, i ^ bits) for i in range(count)])]
    unnamed x17 -> x10, local copies, waits for them, and re-layouts: 6.91 us -> 1.15 us
    pallas_call x8 -> x7, Pallas kernels: 5.78 us -> 8.81 us  [call(): pl.pallas_call(kernel, out_shape=out_shape, compiler_params=params(vmem *...]
  transfers between devices with their start and end apart: 19 -> 9, of which waited for: 11 -> 5; matrix products, arithmetic and copies ran while one was open for 1% -> 0% of each run, Pallas kernels for 9% -> 17%
where the time goes in v3:
time: 48.2 us; the launch traced here: 48 us
  blocking collectives  14.3 us (30%)
  starting transfers between devices  11.9 us (25%)
  waiting for transfers between devices  10.5 us (22%)
  Pallas kernels  8.81 us (18%)
  local copies, waits for them, and re-layouts  1.3 us (3%)
  between operations  0.73 us (2%)
    all_to_all x1, blocking collectives, shards(): got = lax.all_to_all(pieces, ('space', 'band'), 0, 0)  14.3 us
    pallas_call x7, Pallas kernels, call(): pl.pallas_call(kernel, out_shape=out_shape, compiler_params=params(vmem *...  8.81 us
    ppermute x6, starting transfers between devices, mirrored(): return lax.ppermute(value, axis, [(i, i ^ bits) for i in range(count)])  8.41 us
    ppermute x6, waiting for transfers between devices, mirrored(): return lax.ppermute(value, axis, [(i, i ^ bits) for i in range(count)])  5.83 us
    ppermute x3, waiting for transfers between devices, cyclic(): lax.ppermute(value, axis, [(i, (i + steps) % count) for i in range(count)])  4.7 us
    ppermute x3, starting transfers between devices, cyclic(): lax.ppermute(value, axis, [(i, (i + steps) % count) for i in range(count)])  3.5 us
    unnamed x10, local copies, waits for them, and re-layouts  1.15 us
  transfers between devices with their start and end apart: 9, of which 5 were waited for; matrix products, arithmetic and copies ran while one was open for 0% of the time, Pallas kernels for 17%

profile of v3, /device:TPU:0, one launch (start us, length us, event | category | flops | bytes accessed | tf_op | source)
XLA Modules:
  0.0 48.0 jit_solution(2644740395133826314)
XLA Ops:
  0.6 0.0 copy-start.4
  0.6 0.0 copy-start
  0.7 1.1 %copy-done = f32[8,6,32,128]{3,2,1,0:T(8,128)S(1)} copy-done((f32[8,6,32,128]{3,2,1,0:T(8,128)S(1)}, f32[8,6,32,128]{3,2,1,0:T(8,128)}, u32[]{:S(2)}) %copy-start) | copy-done | bytes 786456
  1.8 0.0 copy-start.1
  1.8 0.0 copy-start.3
  1.8 0.1 cast.1
  1.9 3.4 %collective-permute-start = (bf16[8,192,128]{2,1,0:T(8,128)(2,1)S(1)}, bf16[8,192,128]{2,1,0:T(8,128)(2,1)S(1)}, u32[]{:S(2)}, u32[]{:S(2)}) collective-permute-start(bf16[8,192,128]{2,1,0:T(8,128)(2,1)S(1)} %get-tuple-element.21.own_ref), channel_id=1, source_target_pairs={{0,28},{4,0},{8,4},{12,8},{16,12},{20,16},{24,20},{28,24},{1,29},{... | collective-permute-start | bytes 1179656 | tf_op jit(solution)/shard_map/ppermute | solution.py:222
  5.3 4.2 %local_part.1 = (f32[8,192,128]{2,1,0:T(8,128)}, bf16[8,192,128]{2,1,0:T(8,128)(2,1)}) custom-call(f32[8,192,128]{2,1,0:T(8,128)} %bitcast.12, f32[8,192,128]{2,1,0:T(8,128)} %bitcast.17, f32[192,128]{1,0:T(8,128)} %bitcast.18), custom_call_target="tpu_custom_call" | custom-call | tf_op jit(solution)/shard_map/local_part/pallas_call | solution.py:240
  9.5 0.0 copy-start.2
  9.5 0.1 collective-permute-start.1
  9.6 1.4 %collective-permute-done.upper_ref = bf16[8,192,128]{2,1,0:T(8,128)(2,1)S(1)} collective-permute-done((bf16[8,192,128]{2,1,0:T(8,128)(2,1)S(1)}, bf16[8,192,128]{2,1,0:T(8,128)(2,1)S(1)}, u32[]{:S(2)}, u32[]{:S(2)}) %collective-permute-start) | collective-permute-done | bytes 393248 | tf_op jit(solution)/shard_map/ppermute | solution.py:222
  11.0 0.0 copy-done.4
  11.0 0.0 copy-done.1
  11.0 0.0 copy-done.3
  11.0 2.2 %projector_part.1 = (f32[8,192,128]{2,1,0:T(8,128)S(1)}, bf16[8,160,128]{2,1,0:T(8,128)(2,1)S(1)}) custom-call(s32[32]{0:T(128)S(1)} %copy-done.4, f32[9,32]{1,0:T(8,128)S(1)} %bitcast.14, bf16[8,192,128]{2,1,0:T(8,128)(2,1)S(1)} %get-tuple-element.21.own_ref, bf16[8,192,128]{2,1,0:T(8,128)(2,1)S(1)} %collective-permute-done.upper_ref, ...), custom_call_target="tpu_custom_call" | custom-call | tf_op jit(solution)/shard_map/projector_part/pallas_call | solution.py:240
  13.2 0.1 collective-permute-start.2
  13.3 2.7 %collective-permute-start.6 = (bf16[8,48,128]{2,1,0:T(8,128)(2,1)S(1)}, bf16[8,48,128]{2,1,0:T(8,128)(2,1)S(1)}, u32[]{:S(2)}, u32[]{:S(2)}) collective-permute-start(bf16[8,48,128]{2,1,0:T(8,128)(2,1)S(1)} %get-tuple-element.34), channel_id=1, source_target_pairs={{0,2},{1,3},{2,0},{3,1},{4,6},{5,7},{6,4},{7,5},{8,10},{9,11},{10,... | collective-permute-start | bytes 294920 | tf_op jit(solution)/shard_map/ppermute | solution.py:227
  16.0 1.3 %collective-permute-start.7 = (bf16[8,48,128]{2,1,0:T(8,128)(2,1)S(1)}, bf16[8,48,128]{2,1,0:T(8,128)(2,1)S(1)}, u32[]{:S(2)}, u32[]{:S(2)}) collective-permute-start(bf16[8,48,128]{2,1,0:T(8,128)(2,1)S(1)} %get-tuple-element.35), channel_id=1, source_target_pairs={{0,3},{1,2},{2,1},{3,0},{4,7},{5,6},{6,5},{7,4},{8,11},{9,10},{10,... | collective-permute-start | bytes 294920 | tf_op jit(solution)/shard_map/ppermute | solution.py:227
  17.3 0.2 collective-permute-start.8
  17.5 0.3 collective-permute-done.1.lower_ref
  17.9 0.0 copy-done.2
  17.9 0.6 %halo_part.1.g_ref = f32[8,192,128]{2,1,0:T(8,128)S(1)} custom-call(f32[8,192,128]{2,1,0:T(8,128)S(1)} %copy-done.2, f32[8,192,128]{2,1,0:T(8,128)S(1)} %get-tuple-element.25.near_ref, bf16[8,192,128]{2,1,0:T(8,128)(2,1)S(1)} %collective-permute-done.upper_ref, bf16[8,192,128]{2,1,0:T(8,128)(2,1)S(1)} %collective-permute-done.1.lower_ref), custom_call_target="tpu_custom_call" | custom-call | tf_op jit(solution)/shard_map/halo_part/pallas_call | solution.py:240
  18.5 2.9 %collective-permute-done.2.arrived_ref = bf16[8,160,128]{2,1,0:T(8,128)(2,1)S(1)} collective-permute-done((bf16[8,160,128]{2,1,0:T(8,128)(2,1)S(1)}, bf16[8,160,128]{2,1,0:T(8,128)(2,1)S(1)}, u32[]{:S(2)}, u32[]{:S(2)}) %collective-permute-start.2) | collective-permute-done | bytes 327712 | tf_op jit(solution)/shard_map/ppermute | solution.py:222
  21.4 0.9 %finish.1 = (bf16[8,192,128]{2,1,0:T(8,128)(2,1)}, bf16[8,48,128]{2,1,0:T(8,128)(2,1)S(1)}, bf16[8,48,128]{2,1,0:T(8,128)(2,1)S(1)}, bf16[8,48,128]{2,1,0:T(8,128)(2,1)S(1)}, bf16[8,48,128]{2,1,0:T(8,128)(2,1)S(1)}) custom-call(f32[8,192,128]{2,1,0:T(8,128)S(1)} %halo_part.1.g_ref, bf16[8,160,128]{2,1,0:T(8,128)(2,1)S(1)} %collective-permute-done.2.arrived_ref), custom_call_target="tpu_custom_call" | custom-call | tf_op jit(solution)/shard_map/finish/pallas_call | solution.py:240
  22.3 2.6 %collective-permute-start.3 = (bf16[8,48,128]{2,1,0:T(8,128)(2,1)S(1)}, bf16[8,48,128]{2,1,0:T(8,128)(2,1)S(1)}, u32[]{:S(2)}, u32[]{:S(2)}) collective-permute-start(bf16[8,48,128]{2,1,0:T(8,128)(2,1)S(1)} %get-tuple-element.30), channel_id=1, source_target_pairs={{0,2},{1,3},{2,0},{3,1},{4,6},{5,7},{6,4},{7,5},{8,10},{9,11},{10,... | collective-permute-start | bytes 294920 | tf_op jit(solution)/shard_map/ppermute | solution.py:227
  24.9 1.4 %collective-permute-start.4 = (bf16[8,48,128]{2,1,0:T(8,128)(2,1)S(1)}, bf16[8,48,128]{2,1,0:T(8,128)(2,1)S(1)}, u32[]{:S(2)}, u32[]{:S(2)}) collective-permute-start(bf16[8,48,128]{2,1,0:T(8,128)(2,1)S(1)} %get-tuple-element.31), channel_id=1, source_target_pairs={{0,3},{1,2},{2,1},{3,0},{4,7},{5,6},{6,5},{7,4},{8,11},{9,10},{10,... | collective-permute-start | bytes 294920 | tf_op jit(solution)/shard_map/ppermute | solution.py:227
  26.2 0.0 collective-permute-done.6
  26.2 0.2 collective-permute-start.5
  26.5 0.0 collective-permute-done.7
  26.5 0.0 collective-permute-done.8
  26.5 0.1 pad_maximum_fusion.1
  26.5 5.2 %collective-permute-done.3 = bf16[8,48,128]{2,1,0:T(8,128)(2,1)S(1)} collective-permute-done((bf16[8,48,128]{2,1,0:T(8,128)(2,1)S(1)}, bf16[8,48,128]{2,1,0:T(8,128)(2,1)S(1)}, u32[]{:S(2)}, u32[]{:S(2)}) %collective-permute-start.3) | collective-permute-done | bytes 98336 | tf_op jit(solution)/shard_map/ppermute | solution.py:227
  31.8 0.0 collective-permute-done.4
  31.8 0.6 %collective-permute-done.5 = bf16[8,48,128]{2,1,0:T(8,128)(2,1)S(1)} collective-permute-done((bf16[8,48,128]{2,1,0:T(8,128)(2,1)S(1)}, bf16[8,48,128]{2,1,0:T(8,128)(2,1)S(1)}, u32[]{:S(2)}, u32[]{:S(2)}) %collective-permute-start.5) | collective-permute-done | bytes 98336 | tf_op jit(solution)/shard_map/ppermute | solution.py:227
  32.4 0.1 pad_maximum_fusion
  32.4 0.2 copy_bitcast_fusion
  32.6 0.3 convolution_multiply_fusion.prod_ref
  32.9 0.1 split.1
  33.0 14.3 %all_to_all.5.got_ref = f32[32,4,16]{2,1,0:T(4,128)S(1)} all-to-all(f32[32,4,16]{2,1,0:T(4,128)S(1)} %split.1), channel_id=1, replica_groups=mesh['space'=8,'band'=4] {'space','band'}, dimensions={0} | all-to-all | bytes 16384 | tf_op jit(solution)/shard_map/all_to_all | solution.py:320
  47.3 0.7 %last_sum.1 = (f32[4,8]{1,0:T(4,128)}, f32[4,8]{1,0:T(4,128)}) custom-call(f32[32,4,16]{2,1,0:T(4,128)S(1)} %all_to_all.5.got_ref), custom_call_target="tpu_custom_call" | custom-call | tf_op jit(solution)/shard_map/last_sum/pallas_call | solution.py:240
Async XLA Ops:
  0.6 10.4 %copy-start.4 = (s32[32]{0:T(128)S(1)}, s32[32]{0:T(128)}, u32[]{:S(2)}) copy-start(s32[32]{0:T(128)} %first_ref.1) | copy-start | bytes 388
  0.6 1.1 %copy-start = (f32[8,6,32,128]{3,2,1,0:T(8,128)S(1)}, f32[8,6,32,128]{3,2,1,0:T(8,128)}, u32[]{:S(2)}) copy-start(f32[8,6,32,128]{3,2,1,0:T(8,128)} %param.6) | copy-start | bytes 2359300
  1.8 9.2 %copy-start.1 = (bf16[4,9,6,32,128]{4,3,2,1,0:T(8,128)(2,1)S(1)}, bf16[4,9,6,32,128]{4,3,2,1,0:T(8,128)(2,1)}, u32[]{:S(2)}) copy-start(bf16[4,9,6,32,128]{4,3,2,1,0:T(8,128)(2,1)} %proj_ref.1) | copy-start | bytes 5308420
  1.8 9.2 %copy-start.3 = (f32[32,9]{0,1:T(8,128)S(1)}, f32[32,9]{0,1:T(8,128)}, u32[]{:S(2)}) copy-start(f32[32,9]{0,1:T(8,128)} %param.10) | copy-start | bytes 3460
  1.9 9.2 %collective-permute-start = (bf16[8,192,128]{2,1,0:T(8,128)(2,1)S(1)}, bf16[8,192,128]{2,1,0:T(8,128)(2,1)S(1)}, u32[]{:S(2)}, u32[]{:S(2)}) collective-permute-start(bf16[8,192,128]{2,1,0:T(8,128)(2,1)S(1)} %get-tuple-element.21.own_ref), channel_id=1, source_target_pairs={{0,28},{4,0},{8,4},{12,8},{16,12},{20,16},{24,20},{28,24},{1,29},{... | collective-permute-start | bytes 1179656 | tf_op jit(solution)/shard_map/ppermute | solution.py:222
  9.5 8.4 %copy-start.2 = (f32[8,192,128]{2,1,0:T(8,128)S(1)}, f32[8,192,128]{2,1,0:T(8,128)}, u32[]{:S(2)}) copy-start(f32[8,192,128]{2,1,0:T(8,128)} %get-tuple-element.23.g_ref) | copy-start | bytes 2359300
  9.5 8.4 %collective-permute-start.1 = (bf16[8,192,128]{2,1,0:T(8,128)(2,1)}, bf16[8,192,128]{2,1,0:T(8,128)(2,1)S(1)}, u32[]{:S(2)}, u32[]{:S(2)}) collective-permute-start(bf16[8,192,128]{2,1,0:T(8,128)(2,1)} %get-tuple-element.26), channel_id=1, source_target_pairs={{0,4},{4,8},{8,12},{12,16},{16,20},{20,24},{24,28},{28,0},{1,5},{5... | collective-permute-start | bytes 1179656 | tf_op jit(solution)/shard_map/ppermute | solution.py:222
  13.2 8.2 %collective-permute-start.2 = (bf16[8,160,128]{2,1,0:T(8,128)(2,1)S(1)}, bf16[8,160,128]{2,1,0:T(8,128)(2,1)S(1)}, u32[]{:S(2)}, u32[]{:S(2)}) collective-permute-start(bf16[8,160,128]{2,1,0:T(8,128)(2,1)S(1)} %get-tuple-element.27), channel_id=1, source_target_pairs={{0,4},{4,8},{8,12},{12,16},{16,20},{20,24},{24,28},{28,0},{1,5},{5... | collective-permute-start | bytes 983048 | tf_op jit(solution)/shard_map/ppermute | solution.py:222
  13.3 12.9 %collective-permute-start.6 = (bf16[8,48,128]{2,1,0:T(8,128)(2,1)S(1)}, bf16[8,48,128]{2,1,0:T(8,128)(2,1)S(1)}, u32[]{:S(2)}, u32[]{:S(2)}) collective-permute-start(bf16[8,48,128]{2,1,0:T(8,128)(2,1)S(1)} %get-tuple-element.34), channel_id=1, source_target_pairs={{0,2},{1,3},{2,0},{3,1},{4,6},{5,7},{6,4},{7,5},{8,10},{9,11},{10,... | collective-permute-start | bytes 294920 | tf_op jit(solution)/shard_map/ppermute | solution.py:227
  16.0 10.5 %collective-permute-start.7 = (bf16[8,48,128]{2,1,0:T(8,128)(2,1)S(1)}, bf16[8,48,128]{2,1,0:T(8,128)(2,1)S(1)}, u32[]{:S(2)}, u32[]{:S(2)}) collective-permute-start(bf16[8,48,128]{2,1,0:T(8,128)(2,1)S(1)} %get-tuple-element.35), channel_id=1, source_target_pairs={{0,3},{1,2},{2,1},{3,0},{4,7},{5,6},{6,5},{7,4},{8,11},{9,10},{10,... | collective-permute-start | bytes 294920 | tf_op jit(solution)/shard_map/ppermute | solution.py:227
  17.3 9.2 %collective-permute-start.8 = (bf16[8,48,128]{2,1,0:T(8,128)(2,1)S(1)}, bf16[8,48,128]{2,1,0:T(8,128)(2,1)S(1)}, u32[]{:S(2)}, u32[]{:S(2)}) collective-permute-start(bf16[8,48,128]{2,1,0:T(8,128)(2,1)S(1)} %get-tuple-element.36), channel_id=1, source_target_pairs={{0,1},{1,0},{2,3},{3,2},{4,5},{5,4},{6,7},{7,6},{8,9},{9,8},{10,11... | collective-permute-start | bytes 294920 | tf_op jit(solution)/shard_map/ppermute | solution.py:227
  22.3 9.5 %collective-permute-start.3 = (bf16[8,48,128]{2,1,0:T(8,128)(2,1)S(1)}, bf16[8,48,128]{2,1,0:T(8,128)(2,1)S(1)}, u32[]{:S(2)}, u32[]{:S(2)}) collective-permute-start(bf16[8,48,128]{2,1,0:T(8,128)(2,1)S(1)} %get-tuple-element.30), channel_id=1, source_target_pairs={{0,2},{1,3},{2,0},{3,1},{4,6},{5,7},{6,4},{7,5},{8,10},{9,11},{10,... | collective-permute-start | bytes 294920 | tf_op jit(solution)/shard_map/ppermute | solution.py:227
  24.9 6.9 %collective-permute-start.4 = (bf16[8,48,128]{2,1,0:T(8,128)(2,1)S(1)}, bf16[8,48,128]{2,1,0:T(8,128)(2,1)S(1)}, u32[]{:S(2)}, u32[]{:S(2)}) collective-permute-start(bf16[8,48,128]{2,1,0:T(8,128)(2,1)S(1)} %get-tuple-element.31), channel_id=1, source_target_pairs={{0,3},{1,2},{2,1},{3,0},{4,7},{5,6},{6,5},{7,4},{8,11},{9,10},{10,... | collective-permute-start | bytes 294920 | tf_op jit(solution)/shard_map/ppermute | solution.py:227
  26.2 6.1 %collective-permute-start.5 = (bf16[8,48,128]{2,1,0:T(8,128)(2,1)S(1)}, bf16[8,48,128]{2,1,0:T(8,128)(2,1)S(1)}, u32[]{:S(2)}, u32[]{:S(2)}) collective-permute-start(bf16[8,48,128]{2,1,0:T(8,128)(2,1)S(1)} %get-tuple-element.32), channel_id=1, source_target_pairs={{0,1},{1,0},{2,3},{3,2},{4,5},{5,4},{6,7},{7,6},{8,9},{9,8},{10,11... | collective-permute-start | bytes 294920 | tf_op jit(solution)/shard_map/ppermute | solution.py:227

commit v4 on v3

--- a/solution.py
+++ b/solution.py
@@ -43,7 +43,7 @@
     value = jnp.zeros((size, size), F32)
     for m, weight in enumerate(kinetic_weights):
         value = jnp.where(reach == m, weight, value)
-    value = jnp.where(row // n == col // n, value, 0.0)
+    value = jnp.where(jnp.bitwise_xor(row, col) < n, value, 0.0)
     hi = value.astype(BF16)
     return hi, (value - hi.astype(F32)).astype(BF16)
 
@@ -110,8 +110,47 @@
         g_ref[:, here] = total - prev_ref[:, here]
 
 
-def projector_kernel(
-    planes, first_ref, strength_ref, own_ref, upper_ref, proj_ref, near_ref, next_ref, ext, acc
+def same_cell(rows, cols):
+    row = lax.broadcasted_iota(jnp.int32, (rows, cols), 0)
+    col = lax.broadcasted_iota(jnp.int32, (rows, cols), 1)
+    return jnp.where(jnp.bitwise_and(row - col, HALF - 1) == 0, 1.0, 0.0).astype(F32)
+
+
+def table(proj_ref, a, p):
+    npj, ny, nz = proj_ref.shape[1], proj_ref.shape[3], proj_ref.shape[4]
+    halves = [
+        proj_ref[a, :, p, h * HALF : (h + 1) * HALF, :].reshape(npj * HALF, nz)
+        for h in range(ny // HALF)
+    ]
+    return jnp.concatenate(halves, axis=1)
+
+
+def spread_weights(w_ref, bands, atoms, mask):
+    cols = mask.shape[1]
+    out = []
+    for a in range(atoms):
+        w = w_ref[a * bands : (a + 1) * bands]
+        full = jnp.broadcast_to(w[:, None, :], (bands, HALF, cols)).reshape(bands * HALF, cols)
+        out.append((full * mask).astype(BF16))
+    return out
+
+
+def spread_plane(weights, proj_ref, plane_of, valid):
+    total = None
+    for a, w in enumerate(weights):
+        p = jnp.clip(plane_of[a], 0, BOX - 1)
+        term = dot(w, table(proj_ref, a, p)) * jnp.where(valid[a], 1.0, 0.0)
+        total = term if total is None else total + term
+    nz = proj_ref.shape[4]
+    rows = total.shape[0]
+    return [
+        total[:, h * nz : (h + 1) * nz].reshape(rows // HALF, HALF, nz)
+        for h in range(total.shape[1] // nz)
+    ]
+
+
+def coefficient_kernel(
+    planes, first_ref, strength_ref, own_ref, upper_ref, proj_ref, w_ref, next_ref, ext
 ):
     bands, cells, nz = own_ref.shape
     ny = cells // planes
@@ -119,34 +158,27 @@
     me = lax.axis_index("space")
     for x in range(planes):
         ext[x] = own_ref[:, plane_rows(x, ny)]
-        ext[planes + x] = upper_ref[:, plane_rows(x, ny)]
-    acc[...] = jnp.zeros_like(acc)
+        if x < BOX - 1:
+            ext[planes + x] = upper_ref[:, plane_rows(x, ny)]
     rows, cols = bands * HALF, npj * HALF
-    row_y = lax.broadcasted_iota(jnp.int32, (rows, cols), 0) % HALF
-    col_y = lax.broadcasted_iota(jnp.int32, (rows, cols), 1) % HALF
-    mask = jnp.where(row_y == col_y, 1.0, 0.0).astype(F32)
-    gi = lax.broadcasted_iota(jnp.int32, (cols, cols), 0) // HALF
-    gj = lax.broadcasted_iota(jnp.int32, (cols, cols), 1) // HALF
-    group = jnp.where(gi == gj, 1.0, 0.0).astype(BF16)
-    owner = lax.broadcasted_iota(jnp.int32, (1, cols), 1) // HALF
-    halves = [slice(h * HALF, (h + 1) * HALF) for h in range(ny // HALF)]
+    mask = same_cell(rows, cols)
+    gi = lax.broadcasted_iota(jnp.int32, (cols, cols), 0)
+    gj = lax.broadcasted_iota(jnp.int32, (cols, cols), 1)
+    group = jnp.where(jnp.bitwise_xor(gi, gj) < HALF, 1.0, 0.0).astype(BF16)
+    owner = lax.broadcasted_iota(jnp.int32, (1, cols), 1)
     starts = [first_ref[me * atoms + a] - me * planes for a in range(atoms)]
-
-    def table(a, sl):
-        return jnp.concatenate(
-            [proj_ref[a, :, p, sl, :].reshape(cols, nz) for p in range(BOX)], axis=1
-        )
+    halves = range(ny // HALF)
 
     parts = []
     for a in range(atoms):
-        total = None
-        for sl in halves:
-            left = jnp.concatenate(
-                [ext[starts[a] + p, :, sl, :].reshape(rows, nz) for p in range(BOX)], axis=1
-            )
-            d = dot(left, table(a, sl), ((1,), (1,)))
-            total = d if total is None else total + d
-        parts.append((total * mask).reshape(bands, HALF, cols).sum(axis=1))
+        left = [
+            ext[starts[a] + p, :, h * HALF : (h + 1) * HALF, :].reshape(rows, nz)
+            for p in range(BOX)
+            for h in halves
+        ]
+        right = [table(proj_ref, a, p) for p in range(BOX)]
+        d = dot(jnp.concatenate(left, axis=1), jnp.concatenate(right, axis=1), ((1,), (1,)))
+        parts.append((d * mask).reshape(bands, HALF, cols).sum(axis=1))
     e = jnp.concatenate(parts, axis=0)
     e_hi = e.astype(BF16)
     e_lo = (e - e_hi.astype(F32)).astype(BF16)
@@ -154,45 +186,61 @@
     for a in range(atoms):
         scale = jnp.zeros((1, cols), F32)
         for j in range(npj):
-            scale = jnp.where(owner == j, outer * strength_ref[j, me * atoms + a], scale)
-        w = coef[a * bands : (a + 1) * bands] * scale
-        full = jnp.broadcast_to(w[:, None, :], (bands, HALF, cols)).reshape(rows, cols) * mask
-        full = full.astype(BF16)
-        for sl in halves:
-            out = dot(full, table(a, sl))
-            for p in range(BOX):
-                acc[starts[a] + p, :, sl, :] += out[:, p * nz : (p + 1) * nz].reshape(
-                    bands, HALF, nz
-                )
+            scale = jnp.where(owner >= j * HALF, outer * strength_ref[j, me * atoms + a], scale)
+        w_ref[a * bands : (a + 1) * bands] = coef[a * bands : (a + 1) * bands] * scale
+    weights = spread_weights(w_ref, bands, atoms, mask)
+    for q in range(BOX - 1):
+        blocks = spread_plane(
+            weights, proj_ref, [planes + q - s for s in starts], [planes + q - s < BOX for s in starts]
+        )
+        for h in halves:
+            begin = q * ny + h * HALF
+            next_ref[:, begin : begin + HALF] = blocks[h].astype(BF16)
+
+
+def near_kernel(planes, first_ref, w_ref, g_ref, upper_ref, lower_ref, proj_ref, out_ref):
+    bands, cells, nz = g_ref.shape
+    ny = cells // planes
+    atoms, npj = proj_ref.shape[:2]
+    me = lax.axis_index("space")
+    starts = [first_ref[me * atoms + a] - me * planes for a in range(atoms)]
+    weights = spread_weights(w_ref, bands, atoms, same_cell(bands * HALF, npj * HALF))
     for x in range(planes):
-        near_ref[:, plane_rows(x, ny)] = acc[x]
-    for x in range(BOX - 1):
-        next_ref[:, plane_rows(x, ny)] = acc[planes + x].astype(BF16)
-
-
-def halo_kernel(planes, g_ref, near_ref, upper_ref, lower_ref, out_ref):
-    ny = g_ref.shape[1] // planes
-    for x in range(planes):
-        here = plane_rows(x, ny)
-        total = g_ref[:, here] + near_ref[:, here]
-        for m in range(1, HALO + 1):
-            if x + m >= planes:
-                there = plane_rows(x + m - planes, ny)
-                total = total + kinetic_weights[m] * upper_ref[:, there].astype(F32)
-            if x - m < 0:
-                there = plane_rows(x - m + planes, ny)
-                total = total + kinetic_weights[m] * lower_ref[:, there].astype(F32)
-        out_ref[:, here] = total
-
-
-def finish_kernel(count, g_ref, arrived_ref, out_ref, *rest):
-    outs, total = rest[:-1], rest[-1]
+        blocks = spread_plane(
+            weights, proj_ref, [x - s for s in starts], [jnp.logical_and(x >= s, x - s < BOX) for s in starts]
+        )
+        for h, block in enumerate(blocks):
+            def here(plane):
+                return slice(plane * ny + h * HALF, plane * ny + (h + 1) * HALF)
+
+            total = g_ref[:, here(x)] + block
+            for m in range(1, HALO + 1):
+                if x + m >= planes:
+                    there = here(x + m - planes)
+                    total = total + kinetic_weights[m] * upper_ref[:, there].astype(F32)
+                if x - m < 0:
+                    there = here(x - m + planes)
+                    total = total + kinetic_weights[m] * lower_ref[:, there].astype(F32)
+            out_ref[:, here(x)] = total
+
+
+def with_arrived(g_ref, arrived_ref, total):
     reach = arrived_ref.shape[1]
     total[:, :reach] = g_ref[:, :reach] + arrived_ref[...].astype(F32)
     total[:, reach:] = g_ref[:, reach:]
-    out_ref[...] = total[...].astype(BF16)
+
+
+def finish_kernel(count, g_ref, arrived_ref, *rest):
+    outs, total = rest[:-1], rest[-1]
+    with_arrived(g_ref, arrived_ref, total)
     rows = g_ref.shape[1] // count
     pieces_of(total, lax.axis_index("band"), count, rows, outs)
+
+
+def output_kernel(g_ref, arrived_ref, out_ref):
+    reach = arrived_ref.shape[1]
+    out_ref[:, :reach] = (g_ref[:, :reach] + arrived_ref[...].astype(F32)).astype(BF16)
+    out_ref[:, reach:] = g_ref[:, reach:].astype(BF16)
 
 
 def split_kernel(n_space, n_band, prod_ref, out_ref, held):
@@ -283,27 +331,36 @@
     lower = cyclic(again, "space", 1)
     upper, g = lax.optimization_barrier((upper, g))
 
-    near, beyond = call(
-        partial(projector_kernel, planes),
-        "projector_part",
-        (struct(whole), struct((bands, (BOX - 1) * ny, nz), BF16)),
+    w, beyond = call(
+        partial(coefficient_kernel, planes),
+        "coefficients",
+        (
+            struct((projectors.shape[0] * bands, projectors.shape[1] * HALF)),
+            struct((bands, (BOX - 1) * ny, nz), BF16),
+        ),
         (atom_planes, strengths.T, half, upper, projectors),
         in_specs=[sm, sm, vm, vm, vm],
         out_specs=(vm, vm),
-        scratch_shapes=[
-            pltpu.VMEM((2 * planes, bands, ny, nz), BF16),
-            pltpu.VMEM((2 * planes, bands, ny, nz), F32),
-        ],
+        scratch_shapes=[pltpu.VMEM((planes + BOX - 1, bands, ny, nz), BF16)],
     )
     arrived = cyclic(beyond, "space", 1)
-    g = call(partial(halo_kernel, planes), "halo_part", struct(whole), (g, near, upper, lower))
-    filtered, *mine = call(
+    g = call(
+        partial(near_kernel, planes),
+        "near_part",
+        struct(whole),
+        (atom_planes, w, g, upper, lower, projectors),
+        in_specs=[sm, vm, vm, vm, vm, vm],
+        out_specs=vm,
+        cost_estimate=pl.CostEstimate(flops=2 * 10**10, bytes_accessed=4 * 2**20, transcendentals=0),
+    )
+    mine = call(
         partial(finish_kernel, n_band),
         "finish",
-        (struct(whole, BF16),) + (struct(quarter, BF16),) * n_band,
+        (struct(quarter, BF16),) * n_band,
         (g, arrived),
         scratch_shapes=[pltpu.VMEM(whole, F32)],
     )
+    filtered = call(output_kernel, "output", struct(whole, BF16), (g, arrived))
     mine = exchanged(mine)
     total_bands = n_band * bands
     left = jnp.concatenate(mine, axis=0).reshape(total_bands, -1)

time: 48.2 us -> 46.6 us (0.967)
  blocking collectives: 14.3 us -> 0 us
  waiting for transfers between devices: 10.5 us -> 18.1 us
  starting transfers between devices: 11.9 us -> 15.5 us
  Pallas kernels: 8.81 us -> 10.2 us
    all_to_all x1 -> x0, blocking collectives: 14.3 us -> none  [shards(): got = lax.all_to_all(pieces, ('space', 'band'), 0, 0)]
    all_to_all x0 -> x1, waiting for transfers between devices: none -> 6.69 us  [shards(): got = lax.all_to_all(pieces, ('space', 'band'), 0, 0)]
    all_to_all x0 -> x1, starting transfers between devices: none -> 3.58 us  [shards(): got = lax.all_to_all(pieces, ('space', 'band'), 0, 0)]
    pallas_call x7 -> x8, Pallas kernels: 8.81 us -> 10.2 us  [call(): pl.pallas_call(kernel, out_shape=out_shape, compiler_params=params(vmem *...]
    ppermute x3, waiting for transfers between devices: 4.7 us -> 5.82 us  [cyclic(): lax.ppermute(value, axis, [(i, (i + steps) % count) for i in range(count)])]
  transfers between devices with their start and end apart: 9 -> 10, of which waited for: 5 -> 6; matrix products, arithmetic and copies ran while one was open for 0% -> 0% of each run, Pallas kernels for 17% -> 19%
where the time goes in v4:
time: 46.6 us; the launch traced here: 46.3 us
  waiting for transfers between devices  18.1 us (39%)
  starting transfers between devices  15.5 us (33%)
  Pallas kernels  10.2 us (22%)
  local copies, waits for them, and re-layouts  1.3 us (3%)
  between operations  0.76 us (2%)
    pallas_call x8, Pallas kernels, call(): pl.pallas_call(kernel, out_shape=out_shape, compiler_params=params(vmem *...  10.2 us
    ppermute x6, starting transfers between devices, mirrored(): return lax.ppermute(value, axis, [(i, i ^ bits) for i in range(count)])  8.46 us
    all_to_all x1, waiting for transfers between devices, shards(): got = lax.all_to_all(pieces, ('space', 'band'), 0, 0)  6.69 us
    ppermute x3, waiting for transfers between devices, cyclic(): lax.ppermute(value, axis, [(i, (i + steps) % count) for i in range(count)])  5.82 us
    ppermute x6, waiting for transfers between devices, mirrored(): return lax.ppermute(value, axis, [(i, i ^ bits) for i in range(count)])  5.6 us
    all_to_all x1, starting transfers between devices, shards(): got = lax.all_to_all(pieces, ('space', 'band'), 0, 0)  3.58 us
    ppermute x3, starting transfers between devices, cyclic(): lax.ppermute(value, axis, [(i, (i + steps) % count) for i in range(count)])  3.5 us
    unnamed x10, local copies, waits for them, and re-layouts  1.15 us
  transfers between devices with their start and end apart: 10, of which 6 were waited for; matrix products, arithmetic and copies ran while one was open for 0% of the time, Pallas kernels for 19%

profile of v4, /device:TPU:0, one launch (start us, length us, event | category | flops | bytes accessed | tf_op | source)
XLA Modules:
  0.0 46.3 jit_solution(1772878027459434004)
XLA Ops:
  0.6 0.0 copy-start.3
  0.6 0.0 copy-start
  0.7 1.1 %copy-done = f32[8,6,32,128]{3,2,1,0:T(8,128)S(1)} copy-done((f32[8,6,32,128]{3,2,1,0:T(8,128)S(1)}, f32[8,6,32,128]{3,2,1,0:T(8,128)}, u32[]{:S(2)}) %copy-start) | copy-done | bytes 786456
  1.8 0.0 copy-start.1
  1.8 0.0 copy-start.2
  1.8 0.1 cast.1
  1.9 3.4 %collective-permute-start = (bf16[8,192,128]{2,1,0:T(8,128)(2,1)S(1)}, bf16[8,192,128]{2,1,0:T(8,128)(2,1)S(1)}, u32[]{:S(2)}, u32[]{:S(2)}) collective-permute-start(bf16[8,192,128]{2,1,0:T(8,128)(2,1)S(1)} %get-tuple-element.20.own_ref), channel_id=1, source_target_pairs={{0,28},{4,0},{8,4},{12,8},{16,12},{20,16},{24,20},{28,24},{1,29},{... | collective-permute-start | bytes 1179656 | tf_op jit(solution)/shard_map/ppermute | solution.py:270
  5.3 4.2 %local_part.1 = (f32[8,192,128]{2,1,0:T(8,128)}, bf16[8,192,128]{2,1,0:T(8,128)(2,1)}) custom-call(f32[8,192,128]{2,1,0:T(8,128)} %bitcast.12, f32[8,192,128]{2,1,0:T(8,128)} %bitcast.17, f32[192,128]{1,0:T(8,128)} %bitcast.19), custom_call_target="tpu_custom_call" | custom-call | tf_op jit(solution)/shard_map/local_part/pallas_call | solution.py:288
  9.5 0.0 copy-start.4
  9.5 0.1 collective-permute-start.1
  9.6 2.7 %collective-permute-start.6 = (bf16[8,48,128]{2,1,0:T(8,128)(2,1)S(1)}, bf16[8,48,128]{2,1,0:T(8,128)(2,1)S(1)}, u32[]{:S(2)}, u32[]{:S(2)}) collective-permute-start(bf16[8,48,128]{2,1,0:T(8,128)(2,1)S(1)} %get-tuple-element.32), channel_id=1, source_target_pairs={{0,2},{1,3},{2,0},{3,1},{4,6},{5,7},{6,4},{7,5},{8,10},{9,11},{10,... | collective-permute-start | bytes 294920 | tf_op jit(solution)/shard_map/ppermute | solution.py:275
  12.2 1.3 %collective-permute-start.7 = (bf16[8,48,128]{2,1,0:T(8,128)(2,1)S(1)}, bf16[8,48,128]{2,1,0:T(8,128)(2,1)S(1)}, u32[]{:S(2)}, u32[]{:S(2)}) collective-permute-start(bf16[8,48,128]{2,1,0:T(8,128)(2,1)S(1)} %get-tuple-element.33), channel_id=1, source_target_pairs={{0,3},{1,2},{2,1},{3,0},{4,7},{5,6},{6,5},{7,4},{8,11},{9,10},{10,... | collective-permute-start | bytes 294920 | tf_op jit(solution)/shard_map/ppermute | solution.py:275
  13.6 0.2 collective-permute-start.8
  13.8 0.0 collective-permute-done.upper_ref
  13.8 0.0 copy-done.3
  13.8 0.0 copy-done.1
  13.8 0.0 copy-done.2
  13.8 2.0 %coefficients.1 = (f32[32,144]{1,0:T(8,128)S(1)}, bf16[8,160,128]{2,1,0:T(8,128)(2,1)S(1)}) custom-call(s32[32]{0:T(128)S(1)} %copy-done.3, f32[9,32]{1,0:T(8,128)S(1)} %bitcast.14, bf16[8,192,128]{2,1,0:T(8,128)(2,1)S(1)} %get-tuple-element.20.own_ref, bf16[8,192,128]{2,1,0:T(8,128)(2,1)S(1)} %collective-permute-done.upper_ref, ...), custom_call_target="tpu_custom_call" | custom-call | tf_op jit(solution)/shard_map/coefficients/pallas_call | solution.py:288
  15.8 0.1 collective-permute-start.2
  15.9 2.0 %collective-permute-done.1.lower_ref = bf16[8,192,128]{2,1,0:T(8,128)(2,1)S(1)} collective-permute-done((bf16[8,192,128]{2,1,0:T(8,128)(2,1)}, bf16[8,192,128]{2,1,0:T(8,128)(2,1)S(1)}, u32[]{:S(2)}, u32[]{:S(2)}) %collective-permute-start.1) | collective-permute-done | bytes 393248 | tf_op jit(solution)/shard_map/ppermute | solution.py:270
  17.8 0.0 copy-done.4
  17.9 1.6 %near_part.1.g_ref = f32[8,192,128]{2,1,0:T(8,128)S(1)} custom-call(s32[32]{0:T(128)S(1)} %copy-done.3, f32[32,144]{1,0:T(8,128)S(1)} %get-tuple-element.23.w_ref, f32[8,192,128]{2,1,0:T(8,128)S(1)} %copy-done.4, bf16[8,192,128]{2,1,0:T(8,128)(2,1)S(1)} %collective-permute-done.upper_ref, bf16[8,192,128]{2,1,0:T(8,128)(2,1)S(1)} %collective-permute-done.1.lower_ref, ...), custom_call_target="tpu_custom_call" | custom-call | flops 20000000000 | bytes 4194304 | tf_op jit(solution)/shard_map/near_part/pallas_call | solution.py:288
  19.4 3.8 %collective-permute-done.2.arrived_ref = bf16[8,160,128]{2,1,0:T(8,128)(2,1)S(1)} collective-permute-done((bf16[8,160,128]{2,1,0:T(8,128)(2,1)S(1)}, bf16[8,160,128]{2,1,0:T(8,128)(2,1)S(1)}, u32[]{:S(2)}, u32[]{:S(2)}) %collective-permute-start.2) | collective-permute-done | bytes 327712 | tf_op jit(solution)/shard_map/ppermute | solution.py:270
  23.2 0.1 finish.1
  23.4 2.9 %collective-permute-start.3 = (bf16[8,48,128]{2,1,0:T(8,128)(2,1)S(1)}, bf16[8,48,128]{2,1,0:T(8,128)(2,1)S(1)}, u32[]{:S(2)}, u32[]{:S(2)}) collective-permute-start(bf16[8,48,128]{2,1,0:T(8,128)(2,1)S(1)} %get-tuple-element.28), channel_id=1, source_target_pairs={{0,2},{1,3},{2,0},{3,1},{4,6},{5,7},{6,4},{7,5},{8,10},{9,11},{10,... | collective-permute-start | bytes 294920 | tf_op jit(solution)/shard_map/ppermute | solution.py:275
  26.3 1.3 %collective-permute-start.4 = (bf16[8,48,128]{2,1,0:T(8,128)(2,1)S(1)}, bf16[8,48,128]{2,1,0:T(8,128)(2,1)S(1)}, u32[]{:S(2)}, u32[]{:S(2)}) collective-permute-start(bf16[8,48,128]{2,1,0:T(8,128)(2,1)S(1)} %get-tuple-element.29), channel_id=1, source_target_pairs={{0,3},{1,2},{2,1},{3,0},{4,7},{5,6},{6,5},{7,4},{8,11},{9,10},{10,... | collective-permute-start | bytes 294920 | tf_op jit(solution)/shard_map/ppermute | solution.py:275
  27.6 0.0 collective-permute-done.6
  27.6 0.0 collective-permute-start.5
  27.6 0.0 collective-permute-done.7
  27.6 0.0 collective-permute-done.8
  27.6 0.1 pad_maximum_fusion.1
  27.7 1.7 %collective-permute-done.3 = bf16[8,48,128]{2,1,0:T(8,128)(2,1)S(1)} collective-permute-done((bf16[8,48,128]{2,1,0:T(8,128)(2,1)S(1)}, bf16[8,48,128]{2,1,0:T(8,128)(2,1)S(1)}, u32[]{:S(2)}, u32[]{:S(2)}) %collective-permute-start.3) | collective-permute-done | bytes 98336 | tf_op jit(solution)/shard_map/ppermute | solution.py:275
  29.4 3.4 %collective-permute-done.4 = bf16[8,48,128]{2,1,0:T(8,128)(2,1)S(1)} collective-permute-done((bf16[8,48,128]{2,1,0:T(8,128)(2,1)S(1)}, bf16[8,48,128]{2,1,0:T(8,128)(2,1)S(1)}, u32[]{:S(2)}, u32[]{:S(2)}) %collective-permute-start.4) | collective-permute-done | bytes 98336 | tf_op jit(solution)/shard_map/ppermute | solution.py:275
  32.8 0.5 %collective-permute-done.5 = bf16[8,48,128]{2,1,0:T(8,128)(2,1)S(1)} collective-permute-done((bf16[8,48,128]{2,1,0:T(8,128)(2,1)S(1)}, bf16[8,48,128]{2,1,0:T(8,128)(2,1)S(1)}, u32[]{:S(2)}, u32[]{:S(2)}) %collective-permute-start.5) | collective-permute-done | bytes 98336 | tf_op jit(solution)/shard_map/ppermute | solution.py:275
  33.3 0.1 pad_maximum_fusion
  33.3 0.2 copy_bitcast_fusion
  33.5 0.3 convolution_multiply_fusion.prod_ref
  33.8 0.7 %split.1 = f32[32,4,16]{2,1,0:T(4,128)} custom-call(f32[32,64]{1,0:T(8,128)S(1)} %convolution_multiply_fusion.prod_ref), custom_call_target="tpu_custom_call" | custom-call | tf_op jit(solution)/shard_map/split/pallas_call | solution.py:288
  34.6 3.6 %all-to-all-start = ((f32[32,4,16]{2,1,0:T(4,128)}), f32[32,4,16]{2,1,0:T(4,128)S(1)}, u32[]{:S(2)}, u32[]{:S(2)}) async-start(f32[32,4,16]{2,1,0:T(4,128)} %split.1), calls=%async_computation | async-start | bytes 131072 | tf_op jit(solution)/shard_map/all_to_all | solution.py:377
  38.2 0.8 %output.1 = bf16[8,192,128]{2,1,0:T(8,128)(2,1)} custom-call(f32[8,192,128]{2,1,0:T(8,128)S(1)} %near_part.1.g_ref, bf16[8,160,128]{2,1,0:T(8,128)(2,1)S(1)} %collective-permute-done.2.arrived_ref), custom_call_target="tpu_custom_call" | custom-call | tf_op jit(solution)/shard_map/output/pallas_call | solution.py:288
  39.0 6.7 %all-to-all-done.got_ref = f32[32,4,16]{2,1,0:T(4,128)S(1)} async-done(((f32[32,4,16]{2,1,0:T(4,128)}), f32[32,4,16]{2,1,0:T(4,128)S(1)}, u32[]{:S(2)}, u32[]{:S(2)}) %all-to-all-start) | async-done | bytes 8224 | tf_op jit(solution)/shard_map/all_to_all | solution.py:377
  45.7 0.7 %last_sum.1 = (f32[4,8]{1,0:T(4,128)}, f32[4,8]{1,0:T(4,128)}) custom-call(f32[32,4,16]{2,1,0:T(4,128)S(1)} %all-to-all-done.got_ref), custom_call_target="tpu_custom_call" | custom-call | tf_op jit(solution)/shard_map/last_sum/pallas_call | solution.py:288
Async XLA Ops:
  0.6 13.2 %copy-start.3 = (s32[32]{0:T(128)S(1)}, s32[32]{0:T(128)}, u32[]{:S(2)}) copy-start(s32[32]{0:T(128)} %first_ref.3) | copy-start | bytes 388
  0.6 1.1 %copy-start = (f32[8,6,32,128]{3,2,1,0:T(8,128)S(1)}, f32[8,6,32,128]{3,2,1,0:T(8,128)}, u32[]{:S(2)}) copy-start(f32[8,6,32,128]{3,2,1,0:T(8,128)} %param.6) | copy-start | bytes 2359300
  1.8 12.0 %copy-start.1 = (bf16[4,9,6,32,128]{4,3,2,1,0:T(8,128)(2,1)S(1)}, bf16[4,9,6,32,128]{4,3,2,1,0:T(8,128)(2,1)}, u32[]{:S(2)}) copy-start(bf16[4,9,6,32,128]{4,3,2,1,0:T(8,128)(2,1)} %proj_ref.3) | copy-start | bytes 5308420
  1.8 12.0 %copy-start.2 = (f32[32,9]{0,1:T(8,128)S(1)}, f32[32,9]{0,1:T(8,128)}, u32[]{:S(2)}) copy-start(f32[32,9]{0,1:T(8,128)} %param.10) | copy-start | bytes 3460
  1.9 11.9 %collective-permute-start = (bf16[8,192,128]{2,1,0:T(8,128)(2,1)S(1)}, bf16[8,192,128]{2,1,0:T(8,128)(2,1)S(1)}, u32[]{:S(2)}, u32[]{:S(2)}) collective-permute-start(bf16[8,192,128]{2,1,0:T(8,128)(2,1)S(1)} %get-tuple-element.20.own_ref), channel_id=1, source_target_pairs={{0,28},{4,0},{8,4},{12,8},{16,12},{20,16},{24,20},{28,24},{1,29},{... | collective-permute-start | bytes 1179656 | tf_op jit(solution)/shard_map/ppermute | solution.py:270
  9.5 8.4 %copy-start.4 = (f32[8,192,128]{2,1,0:T(8,128)S(1)}, f32[8,192,128]{2,1,0:T(8,128)}, u32[]{:S(2)}) copy-start(f32[8,192,128]{2,1,0:T(8,128)} %get-tuple-element.24.g_ref) | copy-start | bytes 2359300
  9.5 8.4 %collective-permute-start.1 = (bf16[8,192,128]{2,1,0:T(8,128)(2,1)}, bf16[8,192,128]{2,1,0:T(8,128)(2,1)S(1)}, u32[]{:S(2)}, u32[]{:S(2)}) collective-permute-start(bf16[8,192,128]{2,1,0:T(8,128)(2,1)} %get-tuple-element.25), channel_id=1, source_target_pairs={{0,4},{4,8},{8,12},{12,16},{16,20},{20,24},{24,28},{28,0},{1,5},{5... | collective-permute-start | bytes 1179656 | tf_op jit(solution)/shard_map/ppermute | solution.py:270
  9.6 18.1 %collective-permute-start.6 = (bf16[8,48,128]{2,1,0:T(8,128)(2,1)S(1)}, bf16[8,48,128]{2,1,0:T(8,128)(2,1)S(1)}, u32[]{:S(2)}, u32[]{:S(2)}) collective-permute-start(bf16[8,48,128]{2,1,0:T(8,128)(2,1)S(1)} %get-tuple-element.32), channel_id=1, source_target_pairs={{0,2},{1,3},{2,0},{3,1},{4,6},{5,7},{6,4},{7,5},{8,10},{9,11},{10,... | collective-permute-start | bytes 294920 | tf_op jit(solution)/shard_map/ppermute | solution.py:275
  12.2 15.4 %collective-permute-start.7 = (bf16[8,48,128]{2,1,0:T(8,128)(2,1)S(1)}, bf16[8,48,128]{2,1,0:T(8,128)(2,1)S(1)}, u32[]{:S(2)}, u32[]{:S(2)}) collective-permute-start(bf16[8,48,128]{2,1,0:T(8,128)(2,1)S(1)} %get-tuple-element.33), channel_id=1, source_target_pairs={{0,3},{1,2},{2,1},{3,0},{4,7},{5,6},{6,5},{7,4},{8,11},{9,10},{10,... | collective-permute-start | bytes 294920 | tf_op jit(solution)/shard_map/ppermute | solution.py:275
  13.6 14.1 %collective-permute-start.8 = (bf16[8,48,128]{2,1,0:T(8,128)(2,1)S(1)}, bf16[8,48,128]{2,1,0:T(8,128)(2,1)S(1)}, u32[]{:S(2)}, u32[]{:S(2)}) collective-permute-start(bf16[8,48,128]{2,1,0:T(8,128)(2,1)S(1)} %get-tuple-element.34), channel_id=1, source_target_pairs={{0,1},{1,0},{2,3},{3,2},{4,5},{5,4},{6,7},{7,6},{8,9},{9,8},{10,11... | collective-permute-start | bytes 294920 | tf_op jit(solution)/shard_map/ppermute | solution.py:275
  15.8 7.5 %collective-permute-start.2 = (bf16[8,160,128]{2,1,0:T(8,128)(2,1)S(1)}, bf16[8,160,128]{2,1,0:T(8,128)(2,1)S(1)}, u32[]{:S(2)}, u32[]{:S(2)}) collective-permute-start(bf16[8,160,128]{2,1,0:T(8,128)(2,1)S(1)} %get-tuple-element.26), channel_id=1, source_target_pairs={{0,4},{4,8},{8,12},{12,16},{16,20},{20,24},{24,28},{28,0},{1,5},{5... | collective-permute-start | bytes 983048 | tf_op jit(solution)/shard_map/ppermute | solution.py:270
  23.4 6.0 %collective-permute-start.3 = (bf16[8,48,128]{2,1,0:T(8,128)(2,1)S(1)}, bf16[8,48,128]{2,1,0:T(8,128)(2,1)S(1)}, u32[]{:S(2)}, u32[]{:S(2)}) collective-permute-start(bf16[8,48,128]{2,1,0:T(8,128)(2,1)S(1)} %get-tuple-element.28), channel_id=1, source_target_pairs={{0,2},{1,3},{2,0},{3,1},{4,6},{5,7},{6,4},{7,5},{8,10},{9,11},{10,... | collective-permute-start | bytes 294920 | tf_op jit(solution)/shard_map/ppermute | solution.py:275
  26.3 6.5 %collective-permute-start.4 = (bf16[8,48,128]{2,1,0:T(8,128)(2,1)S(1)}, bf16[8,48,128]{2,1,0:T(8,128)(2,1)S(1)}, u32[]{:S(2)}, u32[]{:S(2)}) collective-permute-start(bf16[8,48,128]{2,1,0:T(8,128)(2,1)S(1)} %get-tuple-element.29), channel_id=1, source_target_pairs={{0,3},{1,2},{2,1},{3,0},{4,7},{5,6},{6,5},{7,4},{8,11},{9,10},{10,... | collective-permute-start | bytes 294920 | tf_op jit(solution)/shard_map/ppermute | solution.py:275
  27.6 5.7 %collective-permute-start.5 = (bf16[8,48,128]{2,1,0:T(8,128)(2,1)S(1)}, bf16[8,48,128]{2,1,0:T(8,128)(2,1)S(1)}, u32[]{:S(2)}, u32[]{:S(2)}) collective-permute-start(bf16[8,48,128]{2,1,0:T(8,128)(2,1)S(1)} %get-tuple-element.30), channel_id=1, source_target_pairs={{0,1},{1,0},{2,3},{3,2},{4,5},{5,4},{6,7},{7,6},{8,9},{9,8},{10,11... | collective-permute-start | bytes 294920 | tf_op jit(solution)/shard_map/ppermute | solution.py:275
  34.6 11.1 %all-to-all-start = ((f32[32,4,16]{2,1,0:T(4,128)}), f32[32,4,16]{2,1,0:T(4,128)S(1)}, u32[]{:S(2)}, u32[]{:S(2)}) async-start(f32[32,4,16]{2,1,0:T(4,128)} %split.1), calls=%async_computation | async-start | bytes 131072 | tf_op jit(solution)/shard_map/all_to_all | solution.py:377

commit v5 on v4

--- a/solution.py
+++ b/solution.py
@@ -73,41 +73,19 @@
     pieces_of(psi_ref, lax.axis_index("band"), count, rows, outs)
 
 
-def local_kernel(planes, psi_ref, prev_hbm, pot_hbm, g_ref, half_ref, prev_ref, pot_ref, sems):
-    copies = [
-        pltpu.make_async_copy(prev_hbm, prev_ref, sems.at[0]),
-        pltpu.make_async_copy(pot_hbm, pot_ref, sems.at[1]),
-    ]
-    for copy in copies:
-        copy.start()
-    half_ref[...] = psi_ref[...].astype(BF16)
-    bands, cells, nz = psi_ref.shape
-    ny = cells // planes
-    rows = bands * ny
-    cz_hi, cz_lo = circulant(nz, 1)
-    cz_twice = jnp.concatenate([cz_hi, cz_hi], axis=0)
-    cy_hi, cy_lo = circulant(ny, bands)
-    for copy in copies:
-        copy.wait()
-    for x in range(planes):
-        here = plane_rows(x, ny)
-        psi3 = psi_ref[:, here]
-        psi = psi3.reshape(rows, nz)
-        hi = psi.astype(BF16)
-        lo = (psi - hi.astype(F32)).astype(BF16)
-        both = jnp.concatenate([hi, lo], axis=1)
-        along_z = dot(both, cz_twice) + dot(hi, cz_lo)
-        pair = dot(cy_hi, both)
-        along_y = pair[:, :nz] + pair[:, nz:] + dot(cy_lo, hi)
-        total = (along_z + along_y).reshape(bands, ny, nz)
-        site = outer * pot_ref[here] + (kinetic_weights[0] - outer * center)
-        total = total + site[None] * psi3
-        for m in range(1, HALO + 1):
-            if x + m < planes:
-                total = total + kinetic_weights[m] * psi_ref[:, plane_rows(x + m, ny)]
-            if x - m >= 0:
-                total = total + kinetic_weights[m] * psi_ref[:, plane_rows(x - m, ny)]
-        g_ref[:, here] = total - prev_ref[:, here]
+def yz_part(psi, cz, cy):
+    bands, ny, nz = psi.shape
+    flat = psi.reshape(bands * ny, nz)
+    hi = flat.astype(BF16)
+    lo = (flat - hi.astype(F32)).astype(BF16)
+    both = jnp.concatenate([hi, lo], axis=1)
+    along_z = dot(both, cz[0]) + dot(hi, cz[1])
+    size = cy[0].shape[0]
+    along_y = []
+    for begin in range(0, bands * ny, size):
+        pair = dot(cy[0], both[begin : begin + size])
+        along_y.append(pair[:, :nz] + pair[:, nz:] + dot(cy[1], hi[begin : begin + size]))
+    return (along_z + jnp.concatenate(along_y, axis=0)).reshape(bands, ny, nz)
 
 
 def same_cell(rows, cols):
@@ -198,8 +176,28 @@
             next_ref[:, begin : begin + HALF] = blocks[h].astype(BF16)
 
 
-def near_kernel(planes, first_ref, w_ref, g_ref, upper_ref, lower_ref, proj_ref, out_ref):
-    bands, cells, nz = g_ref.shape
+def local_kernel(planes, psi_ref, g_ref, half_ref):
+    half_ref[...] = psi_ref[...].astype(BF16)
+    bands, cells, nz = psi_ref.shape
+    ny = cells // planes
+    cz_hi, cz_lo = circulant(nz, 1)
+    cz = (jnp.concatenate([cz_hi, cz_hi], axis=0), cz_lo)
+    cy = circulant(ny, bands // 2)
+    for x in range(planes):
+        here = plane_rows(x, ny)
+        psi = psi_ref[:, here]
+        total = yz_part(psi, cz, cy) + (kinetic_weights[0] - outer * center) * psi
+        for m in range(1, HALO + 1):
+            for target in (x + m, x - m):
+                if 0 <= target < planes:
+                    total = total + kinetic_weights[m] * psi_ref[:, plane_rows(target, ny)]
+        g_ref[:, here] = total
+
+
+def near_kernel(
+    planes, first_ref, g_ref, psi_ref, prev_ref, pot_ref, w_ref, upper_ref, lower_ref, proj_ref, out_ref
+):
+    bands, cells, nz = psi_ref.shape
     ny = cells // planes
     atoms, npj = proj_ref.shape[:2]
     me = lax.axis_index("space")
@@ -209,19 +207,17 @@
         blocks = spread_plane(
             weights, proj_ref, [x - s for s in starts], [jnp.logical_and(x >= s, x - s < BOX) for s in starts]
         )
-        for h, block in enumerate(blocks):
-            def here(plane):
-                return slice(plane * ny + h * HALF, plane * ny + (h + 1) * HALF)
-
-            total = g_ref[:, here(x)] + block
-            for m in range(1, HALO + 1):
-                if x + m >= planes:
-                    there = here(x + m - planes)
-                    total = total + kinetic_weights[m] * upper_ref[:, there].astype(F32)
-                if x - m < 0:
-                    there = here(x - m + planes)
-                    total = total + kinetic_weights[m] * lower_ref[:, there].astype(F32)
-            out_ref[:, here(x)] = total
+        here = plane_rows(x, ny)
+        total = g_ref[:, here] + jnp.concatenate(blocks, axis=1)
+        total = total + (outer * pot_ref[here])[None] * psi_ref[:, here] - prev_ref[:, here]
+        for m in range(1, HALO + 1):
+            if x + m >= planes:
+                there = plane_rows(x + m - planes, ny)
+                total = total + kinetic_weights[m] * upper_ref[:, there].astype(F32)
+            if x - m < 0:
+                there = plane_rows(x - m + planes, ny)
+                total = total + kinetic_weights[m] * lower_ref[:, there].astype(F32)
+        out_ref[:, here] = total
 
 
 def with_arrived(g_ref, arrived_ref, total):
@@ -237,10 +233,14 @@
     pieces_of(total, lax.axis_index("band"), count, rows, outs)
 
 
-def output_kernel(g_ref, arrived_ref, out_ref):
+def output_kernel(g_ref, arrived_ref, *rest):
+    pieces, (out_ref, panel_ref) = rest[:-2], rest[-2:]
     reach = arrived_ref.shape[1]
     out_ref[:, :reach] = (g_ref[:, :reach] + arrived_ref[...].astype(F32)).astype(BF16)
     out_ref[:, reach:] = g_ref[:, reach:].astype(BF16)
+    bands = g_ref.shape[0]
+    for p, piece in enumerate(pieces):
+        panel_ref[p * bands : (p + 1) * bands] = piece[...]
 
 
 def split_kernel(n_space, n_band, prod_ref, out_ref, held):
@@ -318,19 +318,11 @@
         partial(local_kernel, planes),
         "local_part",
         (struct(whole), struct(whole, BF16)),
-        (psi, prev, pot),
-        vmem=58,
-        in_specs=[vm, anywhere, anywhere],
-        out_specs=(vm, vm),
-        scratch_shapes=[
-            pltpu.VMEM(whole, F32),
-            pltpu.VMEM(pot.shape, F32),
-            pltpu.SemaphoreType.DMA((2,)),
-        ],
+        (psi,),
+        cost_estimate=pl.CostEstimate(flops=10**9, bytes_accessed=2**20, transcendentals=0),
     )
     lower = cyclic(again, "space", 1)
     upper, g = lax.optimization_barrier((upper, g))
-
     w, beyond = call(
         partial(coefficient_kernel, planes),
         "coefficients",
@@ -348,8 +340,8 @@
         partial(near_kernel, planes),
         "near_part",
         struct(whole),
-        (atom_planes, w, g, upper, lower, projectors),
-        in_specs=[sm, vm, vm, vm, vm, vm],
+        (atom_planes, g, psi, prev, pot, w, upper, lower, projectors),
+        in_specs=[sm] + [vm] * 8,
         out_specs=vm,
         cost_estimate=pl.CostEstimate(flops=2 * 10**10, bytes_accessed=4 * 2**20, transcendentals=0),
     )
@@ -360,11 +352,16 @@
         (g, arrived),
         scratch_shapes=[pltpu.VMEM(whole, F32)],
     )
-    filtered = call(output_kernel, "output", struct(whole, BF16), (g, arrived))
     mine = exchanged(mine)
     total_bands = n_band * bands
+    filtered, panels = call(
+        output_kernel,
+        "output",
+        (struct(whole, BF16), struct((total_bands, *quarter[1:]), BF16)),
+        (g, arrived, *panel),
+    )
     left = jnp.concatenate(mine, axis=0).reshape(total_bands, -1)
-    right = jnp.concatenate([left, jnp.concatenate(panel, axis=0).reshape(total_bands, -1)], axis=0)
+    right = jnp.concatenate([left, panels.reshape(total_bands, -1)], axis=0)
     products = dot(left, right, ((1,), (1,))) * (1.0 / (cells * n_space * nz))
     out_rows = total_bands // n_space
     pieces = call(

time: 46.6 us -> 45.9 us (0.985)
  blocking collectives: 0 us -> 10.3 us
  waiting for transfers between devices: 18.1 us -> 14 us
  Pallas kernels: 10.2 us -> 6.66 us
  starting transfers between devices: 15.5 us -> 12.3 us
    all_to_all x0 -> x1, blocking collectives: none -> 10.3 us  [shards(): got = lax.all_to_all(pieces, ('space', 'band'), 0, 0)]
    all_to_all x1 -> x0, waiting for transfers between devices: 6.69 us -> none  [shards(): got = lax.all_to_all(pieces, ('space', 'band'), 0, 0)]
    ppermute x3, waiting for transfers between devices: 5.82 us -> 9.67 us  [cyclic(): lax.ppermute(value, axis, [(i, (i + steps) % count) for i in range(count)])]
    all_to_all x1 -> x0, starting transfers between devices: 3.58 us -> none  [shards(): got = lax.all_to_all(pieces, ('space', 'band'), 0, 0)]
    pallas_call x8, Pallas kernels: 10.2 us -> 6.66 us  [call(): pl.pallas_call(kernel, out_shape=out_shape, compiler_params=params(vmem *...]
    ppermute x6, waiting for transfers between devices: 5.6 us -> 4.35 us  [mirrored(): return lax.ppermute(value, axis, [(i, i ^ bits) for i in range(count)])]
    unnamed x10 -> x14, local copies, waits for them, and re-layouts: 1.15 us -> 1.17 us
  transfers between devices with their start and end apart: 10 -> 9, of which waited for: 6 -> 5; matrix products, arithmetic and copies ran while one was open for 0% -> 0% of each run, Pallas kernels for 19% -> 13%
where the time goes in v5:
time: 45.9 us; the launch traced here: 45.8 us
  waiting for transfers between devices  14 us (31%)
  starting transfers between devices  12.3 us (27%)
  blocking collectives  10.3 us (22%)
  Pallas kernels  6.66 us (15%)
  local copies, waits for them, and re-layouts  1.32 us (3%)
  between operations  0.79 us (2%)
    all_to_all x1, blocking collectives, shards(): got = lax.all_to_all(pieces, ('space', 'band'), 0, 0)  10.3 us
    ppermute x3, waiting for transfers between devices, cyclic(): lax.ppermute(value, axis, [(i, (i + steps) % count) for i in range(count)])  9.67 us
    ppermute x6, starting transfers between devices, mirrored(): return lax.ppermute(value, axis, [(i, i ^ bits) for i in range(count)])  8.76 us
    pallas_call x8, Pallas kernels, call(): pl.pallas_call(kernel, out_shape=out_shape, compiler_params=params(vmem *...  6.66 us
    ppermute x6, waiting for transfers between devices, mirrored(): return lax.ppermute(value, axis, [(i, i ^ bits) for i in range(count)])  4.35 us
    ppermute x3, starting transfers between devices, cyclic(): lax.ppermute(value, axis, [(i, (i + steps) % count) for i in range(count)])  3.5 us
    unnamed x14, local copies, waits for them, and re-layouts  1.17 us
  transfers between devices with their start and end apart: 9, of which 5 were waited for; matrix products, arithmetic and copies ran while one was open for 0% of the time, Pallas kernels for 13%

profile of v5, /device:TPU:0, one launch (start us, length us, event | category | flops | bytes accessed | tf_op | source)
XLA Modules:
  0.0 45.8 jit_solution(12661543092974378826)
XLA Ops:
  0.6 0.0 copy-start.1
  0.6 1.1 %copy-done.1 = f32[8,6,32,128]{3,2,1,0:T(8,128)S(1)} copy-done((f32[8,6,32,128]{3,2,1,0:T(8,128)S(1)}, f32[8,6,32,128]{3,2,1,0:T(8,128)}, u32[]{:S(2)}) %copy-start.1) | copy-done | bytes 786456
  1.8 0.1 cast.1
  1.8 0.0 copy-start
  1.9 0.0 copy-start.3
  1.9 0.0 copy-start.4
  1.9 3.4 %collective-permute-start = (bf16[8,192,128]{2,1,0:T(8,128)(2,1)S(1)}, bf16[8,192,128]{2,1,0:T(8,128)(2,1)S(1)}, u32[]{:S(2)}, u32[]{:S(2)}) collective-permute-start(bf16[8,192,128]{2,1,0:T(8,128)(2,1)S(1)} %get-tuple-element.22.own_ref), channel_id=1, source_target_pairs={{0,28},{4,0},{8,4},{12,8},{16,12},{20,16},{24,20},{28,24},{1,29},{... | collective-permute-start | bytes 1179656 | tf_op jit(solution)/shard_map/ppermute | solution.py:270
  5.3 1.1 %local_part.1 = (f32[8,192,128]{2,1,0:T(8,128)S(1)}, bf16[8,192,128]{2,1,0:T(8,128)(2,1)S(1)}) custom-call(f32[8,192,128]{2,1,0:T(8,128)S(1)} %bitcast.13), custom_call_target="tpu_custom_call" | custom-call | flops 1000000000 | bytes 1048576 | tf_op jit(solution)/shard_map/local_part/pallas_call | solution.py:288
  6.3 0.0 copy-start.2
  6.3 0.0 copy-start.5
  6.4 0.0 copy-start.6
  6.4 0.1 collective-permute-start.1
  6.4 2.7 %collective-permute-start.3 = (bf16[8,48,128]{2,1,0:T(8,128)(2,1)S(1)}, bf16[8,48,128]{2,1,0:T(8,128)(2,1)S(1)}, u32[]{:S(2)}, u32[]{:S(2)}) collective-permute-start(bf16[8,48,128]{2,1,0:T(8,128)(2,1)S(1)} %get-tuple-element.30), channel_id=1, source_target_pairs={{0,2},{1,3},{2,0},{3,1},{4,6},{5,7},{6,4},{7,5},{8,10},{9,11},{10,... | collective-permute-start | bytes 294920 | tf_op jit(solution)/shard_map/ppermute | solution.py:275
  9.1 1.3 %collective-permute-start.4 = (bf16[8,48,128]{2,1,0:T(8,128)(2,1)S(1)}, bf16[8,48,128]{2,1,0:T(8,128)(2,1)S(1)}, u32[]{:S(2)}, u32[]{:S(2)}) collective-permute-start(bf16[8,48,128]{2,1,0:T(8,128)(2,1)S(1)} %get-tuple-element.31), channel_id=1, source_target_pairs={{0,3},{1,2},{2,1},{3,0},{4,7},{5,6},{6,5},{7,4},{8,11},{9,10},{10,... | collective-permute-start | bytes 294920 | tf_op jit(solution)/shard_map/ppermute | solution.py:275
  10.4 0.2 collective-permute-start.5
  10.7 3.9 %collective-permute-done.upper_ref = bf16[8,192,128]{2,1,0:T(8,128)(2,1)S(1)} collective-permute-done((bf16[8,192,128]{2,1,0:T(8,128)(2,1)S(1)}, bf16[8,192,128]{2,1,0:T(8,128)(2,1)S(1)}, u32[]{:S(2)}, u32[]{:S(2)}) %collective-permute-start) | collective-permute-done | bytes 393248 | tf_op jit(solution)/shard_map/ppermute | solution.py:270
  14.6 0.0 copy-done
  14.6 0.0 copy-done.3
  14.6 0.0 copy-done.4
  14.6 2.0 %coefficients.1 = (f32[32,144]{1,0:T(8,128)S(1)}, bf16[8,160,128]{2,1,0:T(8,128)(2,1)S(1)}) custom-call(s32[32]{0:T(128)S(1)} %copy-done.4, f32[9,32]{1,0:T(8,128)S(1)} %bitcast.16, bf16[8,192,128]{2,1,0:T(8,128)(2,1)S(1)} %get-tuple-element.22.own_ref, bf16[8,192,128]{2,1,0:T(8,128)(2,1)S(1)} %collective-permute-done.upper_ref, ...), custom_call_target="tpu_custom_call" | custom-call | tf_op jit(solution)/shard_map/coefficients/pallas_call | solution.py:288
  16.6 0.1 collective-permute-start.2
  16.7 0.0 collective-permute-done.1.lower_ref
  16.7 0.0 copy-done.2
  16.7 0.0 copy-done.5
  16.7 0.0 copy-done.6
  16.7 1.8 %near_part.1.g_ref = f32[8,192,128]{2,1,0:T(8,128)S(1)} custom-call(s32[32]{0:T(128)S(1)} %copy-done.4, f32[8,192,128]{2,1,0:T(8,128)S(1)} %get-tuple-element.24.g_ref, f32[8,192,128]{2,1,0:T(8,128)S(1)} %bitcast.14, f32[8,192,128]{2,1,0:T(8,128)S(1)} %bitcast.17, f32[192,128]{1,0:T(8,128)S(1)} %bitcast.18, f32[32,144]{1,0:T(8,128)S(1)} %get-tuple-element.26.w_ref, ...), custom_call_target="tpu_custom_call" | custom-call | flops 20000000000 | bytes 4194304 | tf_op jit(solution)/shard_map/near_part/pallas_call | solution.py:288
  18.5 5.8 %collective-permute-done.2.arrived_ref = bf16[8,160,128]{2,1,0:T(8,128)(2,1)S(1)} collective-permute-done((bf16[8,160,128]{2,1,0:T(8,128)(2,1)S(1)}, bf16[8,160,128]{2,1,0:T(8,128)(2,1)S(1)}, u32[]{:S(2)}, u32[]{:S(2)}) %collective-permute-start.2) | collective-permute-done | bytes 327712 | tf_op jit(solution)/shard_map/ppermute | solution.py:270
  24.2 0.1 finish.1
  24.4 2.6 %collective-permute-start.6 = (bf16[8,48,128]{2,1,0:T(8,128)(2,1)S(1)}, bf16[8,48,128]{2,1,0:T(8,128)(2,1)S(1)}, u32[]{:S(2)}, u32[]{:S(2)}) collective-permute-start(bf16[8,48,128]{2,1,0:T(8,128)(2,1)S(1)} %get-tuple-element.35), channel_id=1, source_target_pairs={{0,2},{1,3},{2,0},{3,1},{4,6},{5,7},{6,4},{7,5},{8,10},{9,11},{10,... | collective-permute-start | bytes 294920 | tf_op jit(solution)/shard_map/ppermute | solution.py:275
  27.0 1.4 %collective-permute-start.7 = (bf16[8,48,128]{2,1,0:T(8,128)(2,1)S(1)}, bf16[8,48,128]{2,1,0:T(8,128)(2,1)S(1)}, u32[]{:S(2)}, u32[]{:S(2)}) collective-permute-start(bf16[8,48,128]{2,1,0:T(8,128)(2,1)S(1)} %get-tuple-element.36), channel_id=1, source_target_pairs={{0,3},{1,2},{2,1},{3,0},{4,7},{5,6},{6,5},{7,4},{8,11},{9,10},{10,... | collective-permute-start | bytes 294920 | tf_op jit(solution)/shard_map/ppermute | solution.py:275
  28.4 0.0 collective-permute-done.3.rest_1_
  28.4 0.5 %collective-permute-start.8 = (bf16[8,48,128]{2,1,0:T(8,128)(2,1)S(1)}, bf16[8,48,128]{2,1,0:T(8,128)(2,1)S(1)}, u32[]{:S(2)}, u32[]{:S(2)}) collective-permute-start(bf16[8,48,128]{2,1,0:T(8,128)(2,1)S(1)} %get-tuple-element.37), channel_id=1, source_target_pairs={{0,1},{1,0},{2,3},{3,2},{4,5},{5,4},{6,7},{7,6},{8,9},{9,8},{10,11... | collective-permute-start | bytes 294920 | tf_op jit(solution)/shard_map/ppermute | solution.py:275
  28.9 0.0 collective-permute-done.4.rest_2_
  28.9 0.0 collective-permute-done.5.rest_3_
  28.9 0.8 %output.1 = (bf16[8,192,128]{2,1,0:T(8,128)(2,1)}, bf16[32,48,128]{2,1,0:T(8,128)(2,1)S(1)}) custom-call(f32[8,192,128]{2,1,0:T(8,128)S(1)} %near_part.1.g_ref, bf16[8,160,128]{2,1,0:T(8,128)(2,1)S(1)} %collective-permute-done.2.arrived_ref, bf16[8,48,128]{2,1,0:T(8,128)(2,1)S(1)} %get-tuple-element.29.rest_0_, ...), custom_call_target="tpu_custom_call" | custom-call | tf_op jit(solution)/shard_map/output/pallas_call | solution.py:288
  29.7 0.2 collective-permute-done.6
  30.0 3.6 %collective-permute-done.7 = bf16[8,48,128]{2,1,0:T(8,128)(2,1)S(1)} collective-permute-done((bf16[8,48,128]{2,1,0:T(8,128)(2,1)S(1)}, bf16[8,48,128]{2,1,0:T(8,128)(2,1)S(1)}, u32[]{:S(2)}, u32[]{:S(2)}) %collective-permute-start.7) | collective-permute-done | bytes 98336 | tf_op jit(solution)/shard_map/ppermute | solution.py:275
  33.6 0.5 %collective-permute-done.8 = bf16[8,48,128]{2,1,0:T(8,128)(2,1)S(1)} collective-permute-done((bf16[8,48,128]{2,1,0:T(8,128)(2,1)S(1)}, bf16[8,48,128]{2,1,0:T(8,128)(2,1)S(1)}, u32[]{:S(2)}, u32[]{:S(2)}) %collective-permute-start.8) | collective-permute-done | bytes 98336 | tf_op jit(solution)/shard_map/ppermute | solution.py:275
  34.1 0.1 pad_maximum_fusion
  34.1 0.2 copy_bitcast_fusion
  34.3 0.3 convolution_multiply_fusion.prod_ref
  34.6 0.1 split.1
  34.8 10.3 %all_to_all.5.got_ref = f32[32,4,16]{2,1,0:T(4,128)S(1)} all-to-all(f32[32,4,16]{2,1,0:T(4,128)S(1)} %split.1), channel_id=1, replica_groups=mesh['space'=8,'band'=4] {'space','band'}, dimensions={0} | all-to-all | bytes 16384 | tf_op jit(solution)/shard_map/all_to_all | solution.py:374
  45.1 0.7 %last_sum.1 = (f32[4,8]{1,0:T(4,128)}, f32[4,8]{1,0:T(4,128)}) custom-call(f32[32,4,16]{2,1,0:T(4,128)S(1)} %all_to_all.5.got_ref), custom_call_target="tpu_custom_call" | custom-call | tf_op jit(solution)/shard_map/last_sum/pallas_call | solution.py:288
Async XLA Ops:
  0.6 1.1 %copy-start.1 = (f32[8,6,32,128]{3,2,1,0:T(8,128)S(1)}, f32[8,6,32,128]{3,2,1,0:T(8,128)}, u32[]{:S(2)}) copy-start(f32[8,6,32,128]{3,2,1,0:T(8,128)} %param.6) | copy-start | bytes 2359300
  1.8 12.7 %copy-start = (bf16[4,9,6,32,128]{4,3,2,1,0:T(8,128)(2,1)S(1)}, bf16[4,9,6,32,128]{4,3,2,1,0:T(8,128)(2,1)}, u32[]{:S(2)}) copy-start(bf16[4,9,6,32,128]{4,3,2,1,0:T(8,128)(2,1)} %proj_ref.3) | copy-start | bytes 5308420
  1.9 12.7 %copy-start.3 = (f32[32,9]{0,1:T(8,128)S(1)}, f32[32,9]{0,1:T(8,128)}, u32[]{:S(2)}) copy-start(f32[32,9]{0,1:T(8,128)} %param.10) | copy-start | bytes 3460
  1.9 12.7 %copy-start.4 = (s32[32]{0:T(128)S(1)}, s32[32]{0:T(128)}, u32[]{:S(2)}) copy-start(s32[32]{0:T(128)} %first_ref.3) | copy-start | bytes 388
  1.9 12.7 %collective-permute-start = (bf16[8,192,128]{2,1,0:T(8,128)(2,1)S(1)}, bf16[8,192,128]{2,1,0:T(8,128)(2,1)S(1)}, u32[]{:S(2)}, u32[]{:S(2)}) collective-permute-start(bf16[8,192,128]{2,1,0:T(8,128)(2,1)S(1)} %get-tuple-element.22.own_ref), channel_id=1, source_target_pairs={{0,28},{4,0},{8,4},{12,8},{16,12},{20,16},{24,20},{28,24},{1,29},{... | collective-permute-start | bytes 1179656 | tf_op jit(solution)/shard_map/ppermute | solution.py:270
  6.3 10.3 %copy-start.2 = (f32[8,6,32,128]{3,2,1,0:T(8,128)S(1)}, f32[8,6,32,128]{3,2,1,0:T(8,128)}, u32[]{:S(2)}) copy-start(f32[8,6,32,128]{3,2,1,0:T(8,128)} %param.6) | copy-start | bytes 2359300
  6.3 10.3 %copy-start.5 = (f32[8,6,32,128]{3,2,1,0:T(8,128)S(1)}, f32[8,6,32,128]{3,2,1,0:T(8,128)}, u32[]{:S(2)}) copy-start(f32[8,6,32,128]{3,2,1,0:T(8,128)} %param.7) | copy-start | bytes 2359300
  6.4 10.3 %copy-start.6 = (f32[6,32,128]{2,1,0:T(8,128)S(1)}, f32[6,32,128]{2,1,0:T(8,128)}, u32[]{:S(2)}) copy-start(f32[6,32,128]{2,1,0:T(8,128)} %param.8) | copy-start | bytes 294916
  6.4 10.3 %collective-permute-start.1 = (bf16[8,192,128]{2,1,0:T(8,128)(2,1)S(1)}, bf16[8,192,128]{2,1,0:T(8,128)(2,1)S(1)}, u32[]{:S(2)}, u32[]{:S(2)}) collective-permute-start(bf16[8,192,128]{2,1,0:T(8,128)(2,1)S(1)} %get-tuple-element.27), channel_id=1, source_target_pairs={{0,4},{4,8},{8,12},{12,16},{16,20},{20,24},{24,28},{28,0},{1,5},{5... | collective-permute-start | bytes 1179656 | tf_op jit(solution)/shard_map/ppermute | solution.py:270
  6.4 22.0 %collective-permute-start.3 = (bf16[8,48,128]{2,1,0:T(8,128)(2,1)S(1)}, bf16[8,48,128]{2,1,0:T(8,128)(2,1)S(1)}, u32[]{:S(2)}, u32[]{:S(2)}) collective-permute-start(bf16[8,48,128]{2,1,0:T(8,128)(2,1)S(1)} %get-tuple-element.30), channel_id=1, source_target_pairs={{0,2},{1,3},{2,0},{3,1},{4,6},{5,7},{6,4},{7,5},{8,10},{9,11},{10,... | collective-permute-start | bytes 294920 | tf_op jit(solution)/shard_map/ppermute | solution.py:275
  9.1 19.8 %collective-permute-start.4 = (bf16[8,48,128]{2,1,0:T(8,128)(2,1)S(1)}, bf16[8,48,128]{2,1,0:T(8,128)(2,1)S(1)}, u32[]{:S(2)}, u32[]{:S(2)}) collective-permute-start(bf16[8,48,128]{2,1,0:T(8,128)(2,1)S(1)} %get-tuple-element.31), channel_id=1, source_target_pairs={{0,3},{1,2},{2,1},{3,0},{4,7},{5,6},{6,5},{7,4},{8,11},{9,10},{10,... | collective-permute-start | bytes 294920 | tf_op jit(solution)/shard_map/ppermute | solution.py:275
  10.4 18.5 %collective-permute-start.5 = (bf16[8,48,128]{2,1,0:T(8,128)(2,1)S(1)}, bf16[8,48,128]{2,1,0:T(8,128)(2,1)S(1)}, u32[]{:S(2)}, u32[]{:S(2)}) collective-permute-start(bf16[8,48,128]{2,1,0:T(8,128)(2,1)S(1)} %get-tuple-element.32), channel_id=1, source_target_pairs={{0,1},{1,0},{2,3},{3,2},{4,5},{5,4},{6,7},{7,6},{8,9},{9,8},{10,11... | collective-permute-start | bytes 294920 | tf_op jit(solution)/shard_map/ppermute | solution.py:275
  16.6 7.6 %collective-permute-start.2 = (bf16[8,160,128]{2,1,0:T(8,128)(2,1)S(1)}, bf16[8,160,128]{2,1,0:T(8,128)(2,1)S(1)}, u32[]{:S(2)}, u32[]{:S(2)}) collective-permute-start(bf16[8,160,128]{2,1,0:T(8,128)(2,1)S(1)} %get-tuple-element.28), channel_id=1, source_target_pairs={{0,4},{4,8},{8,12},{12,16},{16,20},{20,24},{24,28},{28,0},{1,5},{5... | collective-permute-start | bytes 983048 | tf_op jit(solution)/shard_map/ppermute | solution.py:270
  24.4 5.6 %collective-permute-start.6 = (bf16[8,48,128]{2,1,0:T(8,128)(2,1)S(1)}, bf16[8,48,128]{2,1,0:T(8,128)(2,1)S(1)}, u32[]{:S(2)}, u32[]{:S(2)}) collective-permute-start(bf16[8,48,128]{2,1,0:T(8,128)(2,1)S(1)} %get-tuple-element.35), channel_id=1, source_target_pairs={{0,2},{1,3},{2,0},{3,1},{4,6},{5,7},{6,4},{7,5},{8,10},{9,11},{10,... | collective-permute-start | bytes 294920 | tf_op jit(solution)/shard_map/ppermute | solution.py:275
  27.0 6.6 %collective-permute-start.7 = (bf16[8,48,128]{2,1,0:T(8,128)(2,1)S(1)}, bf16[8,48,128]{2,1,0:T(8,128)(2,1)S(1)}, u32[]{:S(2)}, u32[]{:S(2)}) collective-permute-start(bf16[8,48,128]{2,1,0:T(8,128)(2,1)S(1)} %get-tuple-element.36), channel_id=1, source_target_pairs={{0,3},{1,2},{2,1},{3,0},{4,7},{5,6},{6,5},{7,4},{8,11},{9,10},{10,... | collective-permute-start | bytes 294920 | tf_op jit(solution)/shard_map/ppermute | solution.py:275
  28.4 5.7 %collective-permute-start.8 = (bf16[8,48,128]{2,1,0:T(8,128)(2,1)S(1)}, bf16[8,48,128]{2,1,0:T(8,128)(2,1)S(1)}, u32[]{:S(2)}, u32[]{:S(2)}) collective-permute-start(bf16[8,48,128]{2,1,0:T(8,128)(2,1)S(1)} %get-tuple-element.37), channel_id=1, source_target_pairs={{0,1},{1,0},{2,3},{3,2},{4,5},{5,4},{6,7},{7,6},{8,9},{9,8},{10,11... | collective-permute-start | bytes 294920 | tf_op jit(solution)/shard_map/ppermute | solution.py:275

commit v6 on v5

--- a/solution.py
+++ b/solution.py
@@ -57,7 +57,7 @@
 
 
 def partners(count):
-    return [0, *range(count // 2, count), *range(1, count // 2)]
+    return [0, *reversed(range(1, count))]
 
 
 def pieces_of(ref, index, count, rows, outs):
@@ -176,26 +176,16 @@
             next_ref[:, begin : begin + HALF] = blocks[h].astype(BF16)
 
 
-def local_kernel(planes, psi_ref, g_ref, half_ref):
-    half_ref[...] = psi_ref[...].astype(BF16)
-    bands, cells, nz = psi_ref.shape
-    ny = cells // planes
-    cz_hi, cz_lo = circulant(nz, 1)
-    cz = (jnp.concatenate([cz_hi, cz_hi], axis=0), cz_lo)
-    cy = circulant(ny, bands // 2)
-    for x in range(planes):
-        here = plane_rows(x, ny)
-        psi = psi_ref[:, here]
-        total = yz_part(psi, cz, cy) + (kinetic_weights[0] - outer * center) * psi
-        for m in range(1, HALO + 1):
-            for target in (x + m, x - m):
-                if 0 <= target < planes:
-                    total = total + kinetic_weights[m] * psi_ref[:, plane_rows(target, ny)]
-        g_ref[:, here] = total
-
-
-def near_kernel(
-    planes, first_ref, g_ref, psi_ref, prev_ref, pot_ref, w_ref, upper_ref, lower_ref, proj_ref, out_ref
+def again_kernel(half_ref, *refs):
+    refs[-1][...] = half_ref[...]
+
+
+def near_kernel(planes, unused, first_ref, *refs):
+    near_body(planes, first_ref, *refs[unused:])
+
+
+def near_body(
+    planes, first_ref, psi_ref, prev_ref, pot_ref, w_ref, upper_ref, lower_ref, proj_ref, out_ref
 ):
     bands, cells, nz = psi_ref.shape
     ny = cells // planes
@@ -203,20 +193,27 @@
     me = lax.axis_index("space")
     starts = [first_ref[me * atoms + a] - me * planes for a in range(atoms)]
     weights = spread_weights(w_ref, bands, atoms, same_cell(bands * HALF, npj * HALF))
+    cz_hi, cz_lo = circulant(nz, 1)
+    cz = (jnp.concatenate([cz_hi, cz_hi], axis=0), cz_lo)
+    cy = circulant(ny, bands // 2)
     for x in range(planes):
         blocks = spread_plane(
             weights, proj_ref, [x - s for s in starts], [jnp.logical_and(x >= s, x - s < BOX) for s in starts]
         )
         here = plane_rows(x, ny)
-        total = g_ref[:, here] + jnp.concatenate(blocks, axis=1)
-        total = total + (outer * pot_ref[here])[None] * psi_ref[:, here] - prev_ref[:, here]
+        psi = psi_ref[:, here]
+        total = yz_part(psi, cz, cy) + jnp.concatenate(blocks, axis=1)
+        site = outer * pot_ref[here] + (kinetic_weights[0] - outer * center)
+        total = total + site[None] * psi - prev_ref[:, here]
         for m in range(1, HALO + 1):
-            if x + m >= planes:
-                there = plane_rows(x + m - planes, ny)
-                total = total + kinetic_weights[m] * upper_ref[:, there].astype(F32)
-            if x - m < 0:
-                there = plane_rows(x - m + planes, ny)
-                total = total + kinetic_weights[m] * lower_ref[:, there].astype(F32)
+            for target in (x + m, x - m):
+                if target >= planes:
+                    value = upper_ref[:, plane_rows(target - planes, ny)].astype(F32)
+                elif target < 0:
+                    value = lower_ref[:, plane_rows(target + planes, ny)].astype(F32)
+                else:
+                    value = psi_ref[:, plane_rows(target, ny)]
+                total = total + kinetic_weights[m] * value
         out_ref[:, here] = total
 
 
@@ -314,15 +311,16 @@
     upper = cyclic(half, "space", -1)
     panel = exchanged(panel)
 
-    g, again = call(
-        partial(local_kernel, planes),
-        "local_part",
-        (struct(whole), struct(whole, BF16)),
-        (psi,),
+    again = call(
+        again_kernel,
+        "again",
+        struct(whole, BF16),
+        (half, panel[3]),
+        in_specs=[vm] + [anywhere] * 1,
+        out_specs=vm,
         cost_estimate=pl.CostEstimate(flops=10**9, bytes_accessed=2**20, transcendentals=0),
     )
     lower = cyclic(again, "space", 1)
-    upper, g = lax.optimization_barrier((upper, g))
     w, beyond = call(
         partial(coefficient_kernel, planes),
         "coefficients",
@@ -334,16 +332,17 @@
         in_specs=[sm, sm, vm, vm, vm],
         out_specs=(vm, vm),
         scratch_shapes=[pltpu.VMEM((planes + BOX - 1, bands, ny, nz), BF16)],
+        cost_estimate=pl.CostEstimate(flops=10**10, bytes_accessed=2**20, transcendentals=0),
     )
     arrived = cyclic(beyond, "space", 1)
     g = call(
-        partial(near_kernel, planes),
+        partial(near_kernel, planes, 1),
         "near_part",
         struct(whole),
-        (atom_planes, g, psi, prev, pot, w, upper, lower, projectors),
-        in_specs=[sm] + [vm] * 8,
+        (atom_planes, panel[2], psi, prev, pot, w, upper, lower, projectors),
+        in_specs=[sm] + [anywhere] * 1 + [vm] * 7,
         out_specs=vm,
-        cost_estimate=pl.CostEstimate(flops=2 * 10**10, bytes_accessed=4 * 2**20, transcendentals=0),
+        cost_estimate=pl.CostEstimate(flops=2*10**10, bytes_accessed=4 * 2**20, transcendentals=0),
     )
     mine = call(
         partial(finish_kernel, n_band),

time: 45.9 us -> 45 us (0.980)
  waiting for transfers between devices: 14 us -> 12.5 us
  blocking collectives: 10.3 us -> 11 us
    ppermute x3, waiting for transfers between devices: 9.67 us -> 3.71 us  [cyclic(): lax.ppermute(value, axis, [(i, (i + steps) % count) for i in range(count)])]
    ppermute x6, waiting for transfers between devices: 4.35 us -> 8.78 us  [mirrored(): return lax.ppermute(value, axis, [(i, i ^ bits) for i in range(count)])]
    all_to_all x1, blocking collectives: 10.3 us -> 11 us  [shards(): got = lax.all_to_all(pieces, ('space', 'band'), 0, 0)]
where the time goes in v6:
time: 45 us; the launch traced here: 44.8 us
  waiting for transfers between devices  12.5 us (28%)
  starting transfers between devices  12.3 us (27%)
  blocking collectives  11 us (24%)
  Pallas kernels  6.49 us (14%)
  local copies, waits for them, and re-layouts  1.39 us (3%)
  between operations  0.74 us (2%)
    all_to_all x1, blocking collectives, shards(): got = lax.all_to_all(pieces, ('space', 'band'), 0, 0)  11 us
    ppermute x6, starting transfers between devices, mirrored(): return lax.ppermute(value, axis, [(i, i ^ bits) for i in range(count)])  8.84 us
    ppermute x6, waiting for transfers between devices, mirrored(): return lax.ppermute(value, axis, [(i, i ^ bits) for i in range(count)])  8.78 us
    pallas_call x8, Pallas kernels, call(): pl.pallas_call(kernel, out_shape=out_shape, compiler_params=params(vmem *...  6.49 us
    ppermute x3, waiting for transfers between devices, cyclic(): lax.ppermute(value, axis, [(i, (i + steps) % count) for i in range(count)])  3.71 us
    ppermute x3, starting transfers between devices, cyclic(): lax.ppermute(value, axis, [(i, (i + steps) % count) for i in range(count)])  3.5 us
    unnamed x14, local copies, waits for them, and re-layouts  1.24 us
  transfers between devices with their start and end apart: 9, of which 5 were waited for; matrix products, arithmetic and copies ran while one was open for 0% of the time, Pallas kernels for 13%

profile of v6, /device:TPU:0, one launch (start us, length us, event | category | flops | bytes accessed | tf_op | source)
XLA Modules:
  0.0 44.8 jit_solution(1174744819220937264)
XLA Ops:
  0.6 0.0 copy-start
  0.6 1.1 %copy-done = f32[8,6,32,128]{3,2,1,0:T(8,128)S(1)} copy-done((f32[8,6,32,128]{3,2,1,0:T(8,128)S(1)}, f32[8,6,32,128]{3,2,1,0:T(8,128)}, u32[]{:S(2)}) %copy-start) | copy-done | bytes 786456
  1.8 0.1 cast.1
  1.8 3.4 %collective-permute-start.1 = (bf16[8,192,128]{2,1,0:T(8,128)(2,1)S(1)}, bf16[8,192,128]{2,1,0:T(8,128)(2,1)S(1)}, u32[]{:S(2)}, u32[]{:S(2)}) collective-permute-start(bf16[8,192,128]{2,1,0:T(8,128)(2,1)S(1)} %get-tuple-element.19.own_ref.half_ref), channel_id=1, source_target_pairs={{0,28},{4,0},{8,4},{12,8},{16,12},{20,16},{24,20},{28,24},{1,29},{... | collective-permute-start | bytes 1179656 | tf_op jit(solution)/shard_map/ppermute | solution.py:267
  5.2 1.6 %collective-permute-start.2 = (bf16[8,48,128]{2,1,0:T(8,128)(2,1)S(1)}, bf16[8,48,128]{2,1,0:T(8,128)(2,1)S(1)}, u32[]{:S(2)}, u32[]{:S(2)}) collective-permute-start(bf16[8,48,128]{2,1,0:T(8,128)(2,1)S(1)} %get-tuple-element.21), channel_id=1, source_target_pairs={{0,1},{1,0},{2,3},{3,2},{4,5},{5,4},{6,7},{7,6},{8,9},{9,8},{10,11... | collective-permute-start | bytes 294920 | tf_op jit(solution)/shard_map/ppermute | solution.py:272
  6.8 2.6 %collective-permute-start = (bf16[8,48,128]{2,1,0:T(8,128)(2,1)S(1)}, bf16[8,48,128]{2,1,0:T(8,128)(2,1)S(1)}, u32[]{:S(2)}, u32[]{:S(2)}) collective-permute-start(bf16[8,48,128]{2,1,0:T(8,128)(2,1)S(1)} %get-tuple-element.18), channel_id=1, source_target_pairs={{0,2},{1,3},{2,0},{3,1},{4,6},{5,7},{6,4},{7,5},{8,10},{9,11},{10,... | collective-permute-start | bytes 294920 | tf_op jit(solution)/shard_map/ppermute | solution.py:272
  9.4 0.0 copy-start.2
  9.4 0.0 copy-start.5
  9.4 0.0 copy-start.6
  9.4 0.2 collective-permute-start.5
  9.6 1.1 %collective-permute-done.2.refs_0_.rest_3_ = bf16[8,48,128]{2,1,0:T(8,128)(2,1)S(1)} collective-permute-done((bf16[8,48,128]{2,1,0:T(8,128)(2,1)S(1)}, bf16[8,48,128]{2,1,0:T(8,128)(2,1)S(1)}, u32[]{:S(2)}, u32[]{:S(2)}) %collective-permute-start.2) | collective-permute-done | bytes 98336 | tf_op jit(solution)/shard_map/ppermute | solution.py:272
  10.7 0.1 collective-permute-start.3
  10.8 0.0 collective-permute-done.1.upper_ref.refs_5_
  10.8 0.1 copy-done.2
  10.9 0.0 copy-done.5
  10.9 0.0 copy-done.6
  10.9 0.0 copy-start.1
  10.9 0.0 copy-start.3
  10.9 0.0 copy-start.4
  10.9 2.0 %coefficients.1 = (f32[32,144]{1,0:T(8,128)S(1)}, bf16[8,160,128]{2,1,0:T(8,128)(2,1)S(1)}) custom-call(s32[32]{0:T(128)S(1)} %copy-done.6, f32[9,32]{1,0:T(8,128)S(1)} %bitcast.17, bf16[8,192,128]{2,1,0:T(8,128)(2,1)S(1)} %get-tuple-element.19.own_ref.half_ref, bf16[8,192,128]{2,1,0:T(8,128)(2,1)S(1)} %collective-permute-done.1.upper_ref.refs_5_, ...), custom_call_target="tpu_custom_call" | custom-call | flops 10000000000 | bytes 1048576 | tf_op jit(solution)/shard_map/coefficients/pallas_call | solution.py:285
  12.9 0.1 collective-permute-start.4
  13.0 3.0 %collective-permute-done.refs_0_.rest_2_ = bf16[8,48,128]{2,1,0:T(8,128)(2,1)S(1)} collective-permute-done((bf16[8,48,128]{2,1,0:T(8,128)(2,1)S(1)}, bf16[8,48,128]{2,1,0:T(8,128)(2,1)S(1)}, u32[]{:S(2)}, u32[]{:S(2)}) %collective-permute-start) | collective-permute-done | bytes 98336 | tf_op jit(solution)/shard_map/ppermute | solution.py:272
  16.0 2.8 %collective-permute-done.3.refs_6_ = bf16[8,192,128]{2,1,0:T(8,128)(2,1)S(1)} collective-permute-done((bf16[8,192,128]{2,1,0:T(8,128)(2,1)S(1)}, bf16[8,192,128]{2,1,0:T(8,128)(2,1)S(1)}, u32[]{:S(2)}, u32[]{:S(2)}) %collective-permute-start.3) | collective-permute-done | bytes 393248 | tf_op jit(solution)/shard_map/ppermute | solution.py:267
  18.9 0.0 copy-done.1
  18.9 0.0 copy-done.3
  18.9 0.0 copy-done.4
  18.9 2.6 %near_part.1.g_ref = f32[8,192,128]{2,1,0:T(8,128)S(1)} custom-call(s32[32]{0:T(128)S(1)} %copy-done.6, bf16[8,48,128]{2,1,0:T(8,128)(2,1)S(1)} %collective-permute-done.refs_0_.rest_2_, f32[8,192,128]{2,1,0:T(8,128)S(1)} %bitcast.13, f32[8,192,128]{2,1,0:T(8,128)S(1)} %bitcast.15, f32[192,128]{1,0:T(8,128)S(1)} %bitcast.16, ...), custom_call_target="tpu_custom_call" | custom-call | flops 20000000000 | bytes 4194304 | tf_op jit(solution)/shard_map/near_part/pallas_call | solution.py:285
  21.5 0.9 %collective-permute-done.4.arrived_ref = bf16[8,160,128]{2,1,0:T(8,128)(2,1)S(1)} collective-permute-done((bf16[8,160,128]{2,1,0:T(8,128)(2,1)S(1)}, bf16[8,160,128]{2,1,0:T(8,128)(2,1)S(1)}, u32[]{:S(2)}, u32[]{:S(2)}) %collective-permute-start.4) | collective-permute-done | bytes 327712 | tf_op jit(solution)/shard_map/ppermute | solution.py:267
  22.4 0.1 finish.1
  22.5 1.9 %collective-permute-start.8 = (bf16[8,48,128]{2,1,0:T(8,128)(2,1)S(1)}, bf16[8,48,128]{2,1,0:T(8,128)(2,1)S(1)}, u32[]{:S(2)}, u32[]{:S(2)}) collective-permute-start(bf16[8,48,128]{2,1,0:T(8,128)(2,1)S(1)} %get-tuple-element.29), channel_id=1, source_target_pairs={{0,1},{1,0},{2,3},{3,2},{4,5},{5,4},{6,7},{7,6},{8,9},{9,8},{10,11... | collective-permute-start | bytes 294920 | tf_op jit(solution)/shard_map/ppermute | solution.py:272
  24.4 1.5 %collective-permute-start.7 = (bf16[8,48,128]{2,1,0:T(8,128)(2,1)S(1)}, bf16[8,48,128]{2,1,0:T(8,128)(2,1)S(1)}, u32[]{:S(2)}, u32[]{:S(2)}) collective-permute-start(bf16[8,48,128]{2,1,0:T(8,128)(2,1)S(1)} %get-tuple-element.28), channel_id=1, source_target_pairs={{0,2},{1,3},{2,0},{3,1},{4,6},{5,7},{6,4},{7,5},{8,10},{9,11},{10,... | collective-permute-start | bytes 294920 | tf_op jit(solution)/shard_map/ppermute | solution.py:272
  25.9 1.1 %collective-permute-start.6 = (bf16[8,48,128]{2,1,0:T(8,128)(2,1)S(1)}, bf16[8,48,128]{2,1,0:T(8,128)(2,1)S(1)}, u32[]{:S(2)}, u32[]{:S(2)}) collective-permute-start(bf16[8,48,128]{2,1,0:T(8,128)(2,1)S(1)} %get-tuple-element.27), channel_id=1, source_target_pairs={{0,3},{1,2},{2,1},{3,0},{4,7},{5,6},{6,5},{7,4},{8,11},{9,10},{10,... | collective-permute-start | bytes 294920 | tf_op jit(solution)/shard_map/ppermute | solution.py:272
  27.0 0.0 collective-permute-done.5.rest_1_
  27.0 0.8 %output.1 = (bf16[8,192,128]{2,1,0:T(8,128)(2,1)}, bf16[32,48,128]{2,1,0:T(8,128)(2,1)S(1)}) custom-call(f32[8,192,128]{2,1,0:T(8,128)S(1)} %near_part.1.g_ref, bf16[8,160,128]{2,1,0:T(8,128)(2,1)S(1)} %collective-permute-done.4.arrived_ref, bf16[8,48,128]{2,1,0:T(8,128)(2,1)S(1)} %get-tuple-element.23.rest_0_, ...), custom_call_target="tpu_custom_call" | custom-call | tf_op jit(solution)/shard_map/output/pallas_call | solution.py:285
  27.8 0.0 collective-permute-done.8
  27.8 4.7 %collective-permute-done.7 = bf16[8,48,128]{2,1,0:T(8,128)(2,1)S(1)} collective-permute-done((bf16[8,48,128]{2,1,0:T(8,128)(2,1)S(1)}, bf16[8,48,128]{2,1,0:T(8,128)(2,1)S(1)}, u32[]{:S(2)}, u32[]{:S(2)}) %collective-permute-start.7) | collective-permute-done | bytes 98336 | tf_op jit(solution)/shard_map/ppermute | solution.py:272
  32.5 0.0 collective-permute-done.6
  32.5 0.1 pad_maximum_fusion
  32.5 0.2 copy_bitcast_fusion
  32.7 0.3 convolution_multiply_fusion.prod_ref
  33.0 0.1 split.1
  33.2 11.0 %all_to_all.5.got_ref = f32[32,4,16]{2,1,0:T(4,128)S(1)} all-to-all(f32[32,4,16]{2,1,0:T(4,128)S(1)} %split.1), channel_id=1, replica_groups=mesh['space'=8,'band'=4] {'space','band'}, dimensions={0} | all-to-all | bytes 16384 | tf_op jit(solution)/shard_map/all_to_all | solution.py:373
  44.2 0.7 %last_sum.1 = (f32[4,8]{1,0:T(4,128)}, f32[4,8]{1,0:T(4,128)}) custom-call(f32[32,4,16]{2,1,0:T(4,128)S(1)} %all_to_all.5.got_ref), custom_call_target="tpu_custom_call" | custom-call | tf_op jit(solution)/shard_map/last_sum/pallas_call | solution.py:285
  (1 shorter events, 0.0 us)
Async XLA Ops:
  0.6 1.1 %copy-start = (f32[8,6,32,128]{3,2,1,0:T(8,128)S(1)}, f32[8,6,32,128]{3,2,1,0:T(8,128)}, u32[]{:S(2)}) copy-start(f32[8,6,32,128]{3,2,1,0:T(8,128)} %param.6) | copy-start | bytes 2359300
  1.8 8.9 %collective-permute-start.1 = (bf16[8,192,128]{2,1,0:T(8,128)(2,1)S(1)}, bf16[8,192,128]{2,1,0:T(8,128)(2,1)S(1)}, u32[]{:S(2)}, u32[]{:S(2)}) collective-permute-start(bf16[8,192,128]{2,1,0:T(8,128)(2,1)S(1)} %get-tuple-element.19.own_ref.half_ref), channel_id=1, source_target_pairs={{0,28},{4,0},{8,4},{12,8},{16,12},{20,16},{24,20},{28,24},{1,29},{... | collective-permute-start | bytes 1179656 | tf_op jit(solution)/shard_map/ppermute | solution.py:267
  5.2 5.4 %collective-permute-start.2 = (bf16[8,48,128]{2,1,0:T(8,128)(2,1)S(1)}, bf16[8,48,128]{2,1,0:T(8,128)(2,1)S(1)}, u32[]{:S(2)}, u32[]{:S(2)}) collective-permute-start(bf16[8,48,128]{2,1,0:T(8,128)(2,1)S(1)} %get-tuple-element.21), channel_id=1, source_target_pairs={{0,1},{1,0},{2,3},{3,2},{4,5},{5,4},{6,7},{7,6},{8,9},{9,8},{10,11... | collective-permute-start | bytes 294920 | tf_op jit(solution)/shard_map/ppermute | solution.py:272
  6.8 9.2 %collective-permute-start = (bf16[8,48,128]{2,1,0:T(8,128)(2,1)S(1)}, bf16[8,48,128]{2,1,0:T(8,128)(2,1)S(1)}, u32[]{:S(2)}, u32[]{:S(2)}) collective-permute-start(bf16[8,48,128]{2,1,0:T(8,128)(2,1)S(1)} %get-tuple-element.18), channel_id=1, source_target_pairs={{0,2},{1,3},{2,0},{3,1},{4,6},{5,7},{6,4},{7,5},{8,10},{9,11},{10,... | collective-permute-start | bytes 294920 | tf_op jit(solution)/shard_map/ppermute | solution.py:272
  9.4 1.5 %copy-start.2 = (bf16[4,9,6,32,128]{4,3,2,1,0:T(8,128)(2,1)S(1)}, bf16[4,9,6,32,128]{4,3,2,1,0:T(8,128)(2,1)}, u32[]{:S(2)}) copy-start(bf16[4,9,6,32,128]{4,3,2,1,0:T(8,128)(2,1)} %refs_7_.1) | copy-start | bytes 5308420
  9.4 1.5 %copy-start.5 = (f32[32,9]{0,1:T(8,128)S(1)}, f32[32,9]{0,1:T(8,128)}, u32[]{:S(2)}) copy-start(f32[32,9]{0,1:T(8,128)} %param.10) | copy-start | bytes 3460
  9.4 1.5 %copy-start.6 = (s32[32]{0:T(128)S(1)}, s32[32]{0:T(128)}, u32[]{:S(2)}) copy-start(s32[32]{0:T(128)} %first_ref.3) | copy-start | bytes 388
  9.4 17.6 %collective-permute-start.5 = (bf16[8,48,128]{2,1,0:T(8,128)(2,1)S(1)}, bf16[8,48,128]{2,1,0:T(8,128)(2,1)S(1)}, u32[]{:S(2)}, u32[]{:S(2)}) collective-permute-start(bf16[8,48,128]{2,1,0:T(8,128)(2,1)S(1)} %get-tuple-element.24), channel_id=1, source_target_pairs={{0,3},{1,2},{2,1},{3,0},{4,7},{5,6},{6,5},{7,4},{8,11},{9,10},{10,... | collective-permute-start | bytes 294920 | tf_op jit(solution)/shard_map/ppermute | solution.py:272
  10.7 8.2 %collective-permute-start.3 = (bf16[8,192,128]{2,1,0:T(8,128)(2,1)S(1)}, bf16[8,192,128]{2,1,0:T(8,128)(2,1)S(1)}, u32[]{:S(2)}, u32[]{:S(2)}) collective-permute-start(bf16[8,192,128]{2,1,0:T(8,128)(2,1)S(1)} %again.1), channel_id=1, source_target_pairs={{0,4},{4,8},{8,12},{12,16},{16,20},{20,24},{24,28},{28,0},{1,5},{5... | collective-permute-start | bytes 1179656 | tf_op jit(solution)/shard_map/ppermute | solution.py:267
  10.9 8.0 %copy-start.1 = (f32[8,6,32,128]{3,2,1,0:T(8,128)S(1)}, f32[8,6,32,128]{3,2,1,0:T(8,128)}, u32[]{:S(2)}) copy-start(f32[8,6,32,128]{3,2,1,0:T(8,128)} %param.6) | copy-start | bytes 2359300
  10.9 8.0 %copy-start.3 = (f32[8,6,32,128]{3,2,1,0:T(8,128)S(1)}, f32[8,6,32,128]{3,2,1,0:T(8,128)}, u32[]{:S(2)}) copy-start(f32[8,6,32,128]{3,2,1,0:T(8,128)} %param.7) | copy-start | bytes 2359300
  10.9 8.0 %copy-start.4 = (f32[6,32,128]{2,1,0:T(8,128)S(1)}, f32[6,32,128]{2,1,0:T(8,128)}, u32[]{:S(2)}) copy-start(f32[6,32,128]{2,1,0:T(8,128)} %param.8) | copy-start | bytes 294916
  12.9 9.5 %collective-permute-start.4 = (bf16[8,160,128]{2,1,0:T(8,128)(2,1)S(1)}, bf16[8,160,128]{2,1,0:T(8,128)(2,1)S(1)}, u32[]{:S(2)}, u32[]{:S(2)}) collective-permute-start(bf16[8,160,128]{2,1,0:T(8,128)(2,1)S(1)} %get-tuple-element.22), channel_id=1, source_target_pairs={{0,4},{4,8},{8,12},{12,16},{16,20},{20,24},{24,28},{28,0},{1,5},{5... | collective-permute-start | bytes 983048 | tf_op jit(solution)/shard_map/ppermute | solution.py:267
  22.5 5.3 %collective-permute-start.8 = (bf16[8,48,128]{2,1,0:T(8,128)(2,1)S(1)}, bf16[8,48,128]{2,1,0:T(8,128)(2,1)S(1)}, u32[]{:S(2)}, u32[]{:S(2)}) collective-permute-start(bf16[8,48,128]{2,1,0:T(8,128)(2,1)S(1)} %get-tuple-element.29), channel_id=1, source_target_pairs={{0,1},{1,0},{2,3},{3,2},{4,5},{5,4},{6,7},{7,6},{8,9},{9,8},{10,11... | collective-permute-start | bytes 294920 | tf_op jit(solution)/shard_map/ppermute | solution.py:272
  24.4 8.1 %collective-permute-start.7 = (bf16[8,48,128]{2,1,0:T(8,128)(2,1)S(1)}, bf16[8,48,128]{2,1,0:T(8,128)(2,1)S(1)}, u32[]{:S(2)}, u32[]{:S(2)}) collective-permute-start(bf16[8,48,128]{2,1,0:T(8,128)(2,1)S(1)} %get-tuple-element.28), channel_id=1, source_target_pairs={{0,2},{1,3},{2,0},{3,1},{4,6},{5,7},{6,4},{7,5},{8,10},{9,11},{10,... | collective-permute-start | bytes 294920 | tf_op jit(solution)/shard_map/ppermute | solution.py:272
  25.9 6.6 %collective-permute-start.6 = (bf16[8,48,128]{2,1,0:T(8,128)(2,1)S(1)}, bf16[8,48,128]{2,1,0:T(8,128)(2,1)S(1)}, u32[]{:S(2)}, u32[]{:S(2)}) collective-permute-start(bf16[8,48,128]{2,1,0:T(8,128)(2,1)S(1)} %get-tuple-element.27), channel_id=1, source_target_pairs={{0,3},{1,2},{2,1},{3,0},{4,7},{5,6},{6,5},{7,4},{8,11},{9,10},{10,... | collective-permute-start | bytes 294920 | tf_op jit(solution)/shard_map/ppermute | solution.py:272

commit v7 on v6

--- a/solution.py
+++ b/solution.py
@@ -57,7 +57,7 @@
 
 
 def partners(count):
-    return [0, *reversed(range(1, count))]
+    return range(count)
 
 
 def pieces_of(ref, index, count, rows, outs):
@@ -128,7 +128,7 @@
 
 
 def coefficient_kernel(
-    planes, first_ref, strength_ref, own_ref, upper_ref, proj_ref, w_ref, next_ref, ext
+    planes, first_ref, strength_ref, own_ref, upper_ref, proj_ref, ahead_ref, w_ref, next_ref, ext
 ):
     bands, cells, nz = own_ref.shape
     ny = cells // planes
@@ -173,19 +173,24 @@
         )
         for h in halves:
             begin = q * ny + h * HALF
-            next_ref[:, begin : begin + HALF] = blocks[h].astype(BF16)
-
-
-def again_kernel(half_ref, *refs):
-    refs[-1][...] = half_ref[...]
-
-
-def near_kernel(planes, unused, first_ref, *refs):
-    near_body(planes, first_ref, *refs[unused:])
-
-
-def near_body(
-    planes, first_ref, psi_ref, prev_ref, pot_ref, w_ref, upper_ref, lower_ref, proj_ref, out_ref
+            block = blocks[h] + ahead_ref[:, begin : begin + HALF]
+            next_ref[:, begin : begin + HALF] = block.astype(BF16)
+    rest = slice((BOX - 1) * ny, planes * ny)
+    next_ref[:, rest] = ahead_ref[:, rest].astype(BF16)
+
+
+def ahead_kernel(planes, psi_ref, out_ref):
+    ny = psi_ref.shape[1] // planes
+    for x in range(planes):
+        total = None
+        for m in range(x + 1, HALO + 1):
+            term = kinetic_weights[m] * psi_ref[:, plane_rows(planes + x - m, ny)]
+            total = term if total is None else total + term
+        out_ref[:, plane_rows(x, ny)] = total
+
+
+def near_kernel(
+    planes, first_ref, psi_ref, prev_ref, pot_ref, w_ref, upper_ref, proj_ref, out_ref
 ):
     bands, cells, nz = psi_ref.shape
     ny = cells // planes
@@ -209,32 +214,24 @@
             for target in (x + m, x - m):
                 if target >= planes:
                     value = upper_ref[:, plane_rows(target - planes, ny)].astype(F32)
-                elif target < 0:
-                    value = lower_ref[:, plane_rows(target + planes, ny)].astype(F32)
+                elif target >= 0:
+                    value = psi_ref[:, plane_rows(target, ny)]
                 else:
-                    value = psi_ref[:, plane_rows(target, ny)]
+                    continue
                 total = total + kinetic_weights[m] * value
         out_ref[:, here] = total
 
 
-def with_arrived(g_ref, arrived_ref, total):
-    reach = arrived_ref.shape[1]
-    total[:, :reach] = g_ref[:, :reach] + arrived_ref[...].astype(F32)
-    total[:, reach:] = g_ref[:, reach:]
-
-
 def finish_kernel(count, g_ref, arrived_ref, *rest):
     outs, total = rest[:-1], rest[-1]
-    with_arrived(g_ref, arrived_ref, total)
+    total[...] = g_ref[...] + arrived_ref[...].astype(F32)
     rows = g_ref.shape[1] // count
     pieces_of(total, lax.axis_index("band"), count, rows, outs)
 
 
 def output_kernel(g_ref, arrived_ref, *rest):
     pieces, (out_ref, panel_ref) = rest[:-2], rest[-2:]
-    reach = arrived_ref.shape[1]
-    out_ref[:, :reach] = (g_ref[:, :reach] + arrived_ref[...].astype(F32)).astype(BF16)
-    out_ref[:, reach:] = g_ref[:, reach:].astype(BF16)
+    out_ref[...] = (g_ref[...] + arrived_ref[...].astype(F32)).astype(BF16)
     bands = g_ref.shape[0]
     for p, piece in enumerate(pieces):
         panel_ref[p * bands : (p + 1) * bands] = piece[...]
@@ -311,38 +308,34 @@
     upper = cyclic(half, "space", -1)
     panel = exchanged(panel)
 
-    again = call(
-        again_kernel,
-        "again",
-        struct(whole, BF16),
-        (half, panel[3]),
-        in_specs=[vm] + [anywhere] * 1,
-        out_specs=vm,
+    ahead = call(
+        partial(ahead_kernel, planes),
+        "ahead",
+        struct(whole),
+        (psi,),
         cost_estimate=pl.CostEstimate(flops=10**9, bytes_accessed=2**20, transcendentals=0),
     )
-    lower = cyclic(again, "space", 1)
     w, beyond = call(
         partial(coefficient_kernel, planes),
         "coefficients",
         (
             struct((projectors.shape[0] * bands, projectors.shape[1] * HALF)),
-            struct((bands, (BOX - 1) * ny, nz), BF16),
+            struct(whole, BF16),
         ),
-        (atom_planes, strengths.T, half, upper, projectors),
-        in_specs=[sm, sm, vm, vm, vm],
+        (atom_planes, strengths.T, half, upper, projectors, ahead),
+        in_specs=[sm, sm, vm, vm, vm, vm],
         out_specs=(vm, vm),
         scratch_shapes=[pltpu.VMEM((planes + BOX - 1, bands, ny, nz), BF16)],
-        cost_estimate=pl.CostEstimate(flops=10**10, bytes_accessed=2**20, transcendentals=0),
     )
     arrived = cyclic(beyond, "space", 1)
     g = call(
-        partial(near_kernel, planes, 1),
+        partial(near_kernel, planes),
         "near_part",
         struct(whole),
-        (atom_planes, panel[2], psi, prev, pot, w, upper, lower, projectors),
-        in_specs=[sm] + [anywhere] * 1 + [vm] * 7,
+        (atom_planes, psi, prev, pot, w, upper, projectors),
+        in_specs=[sm] + [vm] * 6,
         out_specs=vm,
-        cost_estimate=pl.CostEstimate(flops=2*10**10, bytes_accessed=4 * 2**20, transcendentals=0),
+        cost_estimate=pl.CostEstimate(flops=2 * 10**10, bytes_accessed=4 * 2**20, transcendentals=0),
     )
     mine = call(
         partial(finish_kernel, n_band),

time: 45 us -> 44.3 us (0.984)
  waiting for transfers between devices: 12.5 us -> 10.6 us
  blocking collectives: 11 us -> 12 us
    ppermute x6, waiting for transfers between devices: 8.78 us -> 4.04 us  [mirrored(): return lax.ppermute(value, axis, [(i, i ^ bits) for i in range(count)])]
    ppermute x3 -> x2, waiting for transfers between devices: 3.71 us -> 6.58 us  [cyclic(): lax.ppermute(value, axis, [(i, (i + steps) % count) for i in range(count)])]
    all_to_all x1, blocking collectives: 11 us -> 12 us  [shards(): got = lax.all_to_all(pieces, ('space', 'band'), 0, 0)]
    ppermute x3 -> x2, starting transfers between devices: 3.5 us -> 3.44 us  [cyclic(): lax.ppermute(value, axis, [(i, (i + steps) % count) for i in range(count)])]
  transfers between devices with their start and end apart: 9 -> 8, of which waited for: 5 -> 4; matrix products, arithmetic and copies ran while one was open for 0% -> 0% of each run, Pallas kernels for 13% -> 13%
where the time goes in v7:
time: 44.3 us; the launch traced here: 44.1 us
  starting transfers between devices  12.3 us (28%)
  blocking collectives  12 us (27%)
  waiting for transfers between devices  10.6 us (24%)
  Pallas kernels  6.4 us (14%)
  local copies, waits for them, and re-layouts  1.65 us (4%)
  between operations  0.74 us (2%)
    all_to_all x1, blocking collectives, shards(): got = lax.all_to_all(pieces, ('space', 'band'), 0, 0)  12 us
    ppermute x6, starting transfers between devices, mirrored(): return lax.ppermute(value, axis, [(i, i ^ bits) for i in range(count)])  8.84 us
    ppermute x2, waiting for transfers between devices, cyclic(): lax.ppermute(value, axis, [(i, (i + steps) % count) for i in range(count)])  6.58 us
    pallas_call x8, Pallas kernels, call(): pl.pallas_call(kernel, out_shape=out_shape, compiler_params=params(vmem *...  6.4 us
    ppermute x6, waiting for transfers between devices, mirrored(): return lax.ppermute(value, axis, [(i, i ^ bits) for i in range(count)])  4.04 us
    ppermute x2, starting transfers between devices, cyclic(): lax.ppermute(value, axis, [(i, (i + steps) % count) for i in range(count)])  3.44 us
    unnamed x14, local copies, waits for them, and re-layouts  1.5 us
  transfers between devices with their start and end apart: 8, of which 4 were waited for; matrix products, arithmetic and copies ran while one was open for 0% of the time, Pallas kernels for 13%

profile of v7, /device:TPU:0, one launch (start us, length us, event | category | flops | bytes accessed | tf_op | source)
XLA Modules:
  0.0 44.1 jit_solution(6673702247963553405)
XLA Ops:
  0.6 0.0 copy-start.1
  0.6 1.1 %copy-done.1 = f32[8,6,32,128]{3,2,1,0:T(8,128)S(1)} copy-done((f32[8,6,32,128]{3,2,1,0:T(8,128)S(1)}, f32[8,6,32,128]{3,2,1,0:T(8,128)}, u32[]{:S(2)}) %copy-start.1) | copy-done | bytes 786456
  1.8 0.1 cast.1
  1.8 3.4 %collective-permute-start = (bf16[8,192,128]{2,1,0:T(8,128)(2,1)S(1)}, bf16[8,192,128]{2,1,0:T(8,128)(2,1)S(1)}, u32[]{:S(2)}, u32[]{:S(2)}) collective-permute-start(bf16[8,192,128]{2,1,0:T(8,128)(2,1)S(1)} %get-tuple-element.18.own_ref), channel_id=1, source_target_pairs={{0,28},{4,0},{8,4},{12,8},{16,12},{20,16},{24,20},{28,24},{1,29},{... | collective-permute-start | bytes 1179656 | tf_op jit(solution)/shard_map/ppermute | solution.py:264
  5.2 1.6 %collective-permute-start.2 = (bf16[8,48,128]{2,1,0:T(8,128)(2,1)S(1)}, bf16[8,48,128]{2,1,0:T(8,128)(2,1)S(1)}, u32[]{:S(2)}, u32[]{:S(2)}) collective-permute-start(bf16[8,48,128]{2,1,0:T(8,128)(2,1)S(1)} %get-tuple-element.22), channel_id=1, source_target_pairs={{0,1},{1,0},{2,3},{3,2},{4,5},{5,4},{6,7},{7,6},{8,9},{9,8},{10,11... | collective-permute-start | bytes 294920 | tf_op jit(solution)/shard_map/ppermute | solution.py:269
  6.8 2.6 %collective-permute-start.3 = (bf16[8,48,128]{2,1,0:T(8,128)(2,1)S(1)}, bf16[8,48,128]{2,1,0:T(8,128)(2,1)S(1)}, u32[]{:S(2)}, u32[]{:S(2)}) collective-permute-start(bf16[8,48,128]{2,1,0:T(8,128)(2,1)S(1)} %get-tuple-element.23), channel_id=1, source_target_pairs={{0,2},{1,3},{2,0},{3,1},{4,6},{5,7},{6,4},{7,5},{8,10},{9,11},{10,... | collective-permute-start | bytes 294920 | tf_op jit(solution)/shard_map/ppermute | solution.py:269
  9.4 0.0 copy-start
  9.4 0.0 copy-start.3
  9.4 0.0 copy-start.4
  9.4 0.2 collective-permute-start.4
  9.6 0.2 ahead.1.ahead_ref
  9.8 0.7 %collective-permute-done.upper_ref = bf16[8,192,128]{2,1,0:T(8,128)(2,1)S(1)} collective-permute-done((bf16[8,192,128]{2,1,0:T(8,128)(2,1)S(1)}, bf16[8,192,128]{2,1,0:T(8,128)(2,1)S(1)}, u32[]{:S(2)}, u32[]{:S(2)}) %collective-permute-start) | collective-permute-done | bytes 393248 | tf_op jit(solution)/shard_map/ppermute | solution.py:264
  10.5 0.3 copy-done
  10.9 0.0 copy-done.3
  10.9 0.0 copy-done.4
  10.9 0.0 copy-start.2
  10.9 0.0 copy-start.5
  10.9 0.0 copy-start.6
  10.9 2.0 %coefficients.1 = (f32[32,144]{1,0:T(8,128)S(1)}, bf16[8,192,128]{2,1,0:T(8,128)(2,1)S(1)}) custom-call(s32[32]{0:T(128)S(1)} %copy-done.4, f32[9,32]{1,0:T(8,128)S(1)} %bitcast.16, bf16[8,192,128]{2,1,0:T(8,128)(2,1)S(1)} %get-tuple-element.18.own_ref, bf16[8,192,128]{2,1,0:T(8,128)(2,1)S(1)} %collective-permute-done.upper_ref, ...), custom_call_target="tpu_custom_call" | custom-call | tf_op jit(solution)/shard_map/coefficients/pallas_call | solution.py:282
  12.9 0.1 collective-permute-start.1
  13.0 0.0 copy-done.2
  13.0 0.0 copy-done.5
  13.0 0.0 copy-done.6
  13.0 2.3 %near_part.1.g_ref = f32[8,192,128]{2,1,0:T(8,128)S(1)} custom-call(s32[32]{0:T(128)S(1)} %copy-done.4, f32[8,192,128]{2,1,0:T(8,128)S(1)} %bitcast.14, f32[8,192,128]{2,1,0:T(8,128)S(1)} %bitcast.17, f32[192,128]{1,0:T(8,128)S(1)} %bitcast.18, f32[32,144]{1,0:T(8,128)S(1)} %get-tuple-element.19.w_ref, ...), custom_call_target="tpu_custom_call" | custom-call | flops 20000000000 | bytes 4194304 | tf_op jit(solution)/shard_map/near_part/pallas_call | solution.py:282
  15.3 5.9 %collective-permute-done.1.arrived_ref = bf16[8,192,128]{2,1,0:T(8,128)(2,1)S(1)} collective-permute-done((bf16[8,192,128]{2,1,0:T(8,128)(2,1)S(1)}, bf16[8,192,128]{2,1,0:T(8,128)(2,1)S(1)}, u32[]{:S(2)}, u32[]{:S(2)}) %collective-permute-start.1) | collective-permute-done | bytes 393248 | tf_op jit(solution)/shard_map/ppermute | solution.py:264
  21.2 0.1 finish.1
  21.4 3.7 %collective-permute-start.7 = (bf16[8,48,128]{2,1,0:T(8,128)(2,1)S(1)}, bf16[8,48,128]{2,1,0:T(8,128)(2,1)S(1)}, u32[]{:S(2)}, u32[]{:S(2)}) collective-permute-start(bf16[8,48,128]{2,1,0:T(8,128)(2,1)S(1)} %get-tuple-element.29), channel_id=1, source_target_pairs={{0,3},{1,2},{2,1},{3,0},{4,7},{5,6},{6,5},{7,4},{8,11},{9,10},{10,... | collective-permute-start | bytes 294920 | tf_op jit(solution)/shard_map/ppermute | solution.py:269
  25.0 0.0 collective-permute-start.6
  25.0 0.0 collective-permute-done.2.rest_1_
  25.1 0.8 %collective-permute-start.5 = (bf16[8,48,128]{2,1,0:T(8,128)(2,1)S(1)}, bf16[8,48,128]{2,1,0:T(8,128)(2,1)S(1)}, u32[]{:S(2)}, u32[]{:S(2)}) collective-permute-start(bf16[8,48,128]{2,1,0:T(8,128)(2,1)S(1)} %get-tuple-element.27), channel_id=1, source_target_pairs={{0,1},{1,0},{2,3},{3,2},{4,5},{5,4},{6,7},{7,6},{8,9},{9,8},{10,11... | collective-permute-start | bytes 294920 | tf_op jit(solution)/shard_map/ppermute | solution.py:269
  25.8 0.0 collective-permute-done.3.rest_2_
  25.8 0.0 collective-permute-done.4.rest_3_
  25.8 0.9 %output.1 = (bf16[8,192,128]{2,1,0:T(8,128)(2,1)}, bf16[32,48,128]{2,1,0:T(8,128)(2,1)S(1)}) custom-call(f32[8,192,128]{2,1,0:T(8,128)S(1)} %near_part.1.g_ref, bf16[8,192,128]{2,1,0:T(8,128)(2,1)S(1)} %collective-permute-done.1.arrived_ref, bf16[8,48,128]{2,1,0:T(8,128)(2,1)S(1)} %get-tuple-element.21.rest_0_, ...), custom_call_target="tpu_custom_call" | custom-call | tf_op jit(solution)/shard_map/output/pallas_call | solution.py:282
  26.7 1.3 %collective-permute-done.7 = bf16[8,48,128]{2,1,0:T(8,128)(2,1)S(1)} collective-permute-done((bf16[8,48,128]{2,1,0:T(8,128)(2,1)S(1)}, bf16[8,48,128]{2,1,0:T(8,128)(2,1)S(1)}, u32[]{:S(2)}, u32[]{:S(2)}) %collective-permute-start.7) | collective-permute-done | bytes 98336 | tf_op jit(solution)/shard_map/ppermute | solution.py:269
  28.0 2.7 %collective-permute-done.6 = bf16[8,48,128]{2,1,0:T(8,128)(2,1)S(1)} collective-permute-done((bf16[8,48,128]{2,1,0:T(8,128)(2,1)S(1)}, bf16[8,48,128]{2,1,0:T(8,128)(2,1)S(1)}, u32[]{:S(2)}, u32[]{:S(2)}) %collective-permute-start.6) | collective-permute-done | bytes 98336 | tf_op jit(solution)/shard_map/ppermute | solution.py:269
  30.7 0.0 collective-permute-done.5
  30.7 0.1 pad_maximum_fusion
  30.8 0.2 copy_bitcast_fusion
  30.9 0.3 convolution_multiply_fusion.prod_ref
  31.3 0.1 split.1
  31.4 12.0 %all_to_all.5.got_ref = f32[32,4,16]{2,1,0:T(4,128)S(1)} all-to-all(f32[32,4,16]{2,1,0:T(4,128)S(1)} %split.1), channel_id=1, replica_groups=mesh['space'=8,'band'=4] {'space','band'}, dimensions={0} | all-to-all | bytes 16384 | tf_op jit(solution)/shard_map/all_to_all | solution.py:366
  43.4 0.7 %last_sum.1 = (f32[4,8]{1,0:T(4,128)}, f32[4,8]{1,0:T(4,128)}) custom-call(f32[32,4,16]{2,1,0:T(4,128)S(1)} %all_to_all.5.got_ref), custom_call_target="tpu_custom_call" | custom-call | tf_op jit(solution)/shard_map/last_sum/pallas_call | solution.py:282
Async XLA Ops:
  0.6 1.1 %copy-start.1 = (f32[8,6,32,128]{3,2,1,0:T(8,128)S(1)}, f32[8,6,32,128]{3,2,1,0:T(8,128)}, u32[]{:S(2)}) copy-start(f32[8,6,32,128]{3,2,1,0:T(8,128)} %param.6) | copy-start | bytes 2359300
  1.8 8.7 %collective-permute-start = (bf16[8,192,128]{2,1,0:T(8,128)(2,1)S(1)}, bf16[8,192,128]{2,1,0:T(8,128)(2,1)S(1)}, u32[]{:S(2)}, u32[]{:S(2)}) collective-permute-start(bf16[8,192,128]{2,1,0:T(8,128)(2,1)S(1)} %get-tuple-element.18.own_ref), channel_id=1, source_target_pairs={{0,28},{4,0},{8,4},{12,8},{16,12},{20,16},{24,20},{28,24},{1,29},{... | collective-permute-start | bytes 1179656 | tf_op jit(solution)/shard_map/ppermute | solution.py:264
  5.2 19.8 %collective-permute-start.2 = (bf16[8,48,128]{2,1,0:T(8,128)(2,1)S(1)}, bf16[8,48,128]{2,1,0:T(8,128)(2,1)S(1)}, u32[]{:S(2)}, u32[]{:S(2)}) collective-permute-start(bf16[8,48,128]{2,1,0:T(8,128)(2,1)S(1)} %get-tuple-element.22), channel_id=1, source_target_pairs={{0,1},{1,0},{2,3},{3,2},{4,5},{5,4},{6,7},{7,6},{8,9},{9,8},{10,11... | collective-permute-start | bytes 294920 | tf_op jit(solution)/shard_map/ppermute | solution.py:269
  6.8 19.0 %collective-permute-start.3 = (bf16[8,48,128]{2,1,0:T(8,128)(2,1)S(1)}, bf16[8,48,128]{2,1,0:T(8,128)(2,1)S(1)}, u32[]{:S(2)}, u32[]{:S(2)}) collective-permute-start(bf16[8,48,128]{2,1,0:T(8,128)(2,1)S(1)} %get-tuple-element.23), channel_id=1, source_target_pairs={{0,2},{1,3},{2,0},{3,1},{4,6},{5,7},{6,4},{7,5},{8,10},{9,11},{10,... | collective-permute-start | bytes 294920 | tf_op jit(solution)/shard_map/ppermute | solution.py:269
  9.4 1.5 %copy-start = (bf16[4,9,6,32,128]{4,3,2,1,0:T(8,128)(2,1)S(1)}, bf16[4,9,6,32,128]{4,3,2,1,0:T(8,128)(2,1)}, u32[]{:S(2)}) copy-start(bf16[4,9,6,32,128]{4,3,2,1,0:T(8,128)(2,1)} %proj_ref.3) | copy-start | bytes 5308420
  9.4 1.5 %copy-start.3 = (f32[32,9]{0,1:T(8,128)S(1)}, f32[32,9]{0,1:T(8,128)}, u32[]{:S(2)}) copy-start(f32[32,9]{0,1:T(8,128)} %param.10) | copy-start | bytes 3460
  9.4 1.5 %copy-start.4 = (s32[32]{0:T(128)S(1)}, s32[32]{0:T(128)}, u32[]{:S(2)}) copy-start(s32[32]{0:T(128)} %first_ref.3) | copy-start | bytes 388
  9.4 16.4 %collective-permute-start.4 = (bf16[8,48,128]{2,1,0:T(8,128)(2,1)S(1)}, bf16[8,48,128]{2,1,0:T(8,128)(2,1)S(1)}, u32[]{:S(2)}, u32[]{:S(2)}) collective-permute-start(bf16[8,48,128]{2,1,0:T(8,128)(2,1)S(1)} %get-tuple-element.24), channel_id=1, source_target_pairs={{0,3},{1,2},{2,1},{3,0},{4,7},{5,6},{6,5},{7,4},{8,11},{9,10},{10,... | collective-permute-start | bytes 294920 | tf_op jit(solution)/shard_map/ppermute | solution.py:269
  10.9 2.1 %copy-start.2 = (f32[8,6,32,128]{3,2,1,0:T(8,128)S(1)}, f32[8,6,32,128]{3,2,1,0:T(8,128)}, u32[]{:S(2)}) copy-start(f32[8,6,32,128]{3,2,1,0:T(8,128)} %param.6) | copy-start | bytes 2359300
  10.9 2.1 %copy-start.5 = (f32[8,6,32,128]{3,2,1,0:T(8,128)S(1)}, f32[8,6,32,128]{3,2,1,0:T(8,128)}, u32[]{:S(2)}) copy-start(f32[8,6,32,128]{3,2,1,0:T(8,128)} %param.7) | copy-start | bytes 2359300
  10.9 2.1 %copy-start.6 = (f32[6,32,128]{2,1,0:T(8,128)S(1)}, f32[6,32,128]{2,1,0:T(8,128)}, u32[]{:S(2)}) copy-start(f32[6,32,128]{2,1,0:T(8,128)} %param.8) | copy-start | bytes 294916
  12.9 8.3 %collective-permute-start.1 = (bf16[8,192,128]{2,1,0:T(8,128)(2,1)S(1)}, bf16[8,192,128]{2,1,0:T(8,128)(2,1)S(1)}, u32[]{:S(2)}, u32[]{:S(2)}) collective-permute-start(bf16[8,192,128]{2,1,0:T(8,128)(2,1)S(1)} %get-tuple-element.20), channel_id=1, source_target_pairs={{0,4},{4,8},{8,12},{12,16},{16,20},{20,24},{24,28},{28,0},{1,5},{5... | collective-permute-start | bytes 1179656 | tf_op jit(solution)/shard_map/ppermute | solution.py:264
  21.4 6.6 %collective-permute-start.7 = (bf16[8,48,128]{2,1,0:T(8,128)(2,1)S(1)}, bf16[8,48,128]{2,1,0:T(8,128)(2,1)S(1)}, u32[]{:S(2)}, u32[]{:S(2)}) collective-permute-start(bf16[8,48,128]{2,1,0:T(8,128)(2,1)S(1)} %get-tuple-element.29), channel_id=1, source_target_pairs={{0,3},{1,2},{2,1},{3,0},{4,7},{5,6},{6,5},{7,4},{8,11},{9,10},{10,... | collective-permute-start | bytes 294920 | tf_op jit(solution)/shard_map/ppermute | solution.py:269
  25.0 5.7 %collective-permute-start.6 = (bf16[8,48,128]{2,1,0:T(8,128)(2,1)S(1)}, bf16[8,48,128]{2,1,0:T(8,128)(2,1)S(1)}, u32[]{:S(2)}, u32[]{:S(2)}) collective-permute-start(bf16[8,48,128]{2,1,0:T(8,128)(2,1)S(1)} %get-tuple-element.28), channel_id=1, source_target_pairs={{0,2},{1,3},{2,0},{3,1},{4,6},{5,7},{6,4},{7,5},{8,10},{9,11},{10,... | collective-permute-start | bytes 294920 | tf_op jit(solution)/shard_map/ppermute | solution.py:269
  25.1 5.7 %collective-permute-start.5 = (bf16[8,48,128]{2,1,0:T(8,128)(2,1)S(1)}, bf16[8,48,128]{2,1,0:T(8,128)(2,1)S(1)}, u32[]{:S(2)}, u32[]{:S(2)}) collective-permute-start(bf16[8,48,128]{2,1,0:T(8,128)(2,1)S(1)} %get-tuple-element.27), channel_id=1, source_target_pairs={{0,1},{1,0},{2,3},{3,2},{4,5},{5,4},{6,7},{7,6},{8,9},{9,8},{10,11... | collective-permute-start | bytes 294920 | tf_op jit(solution)/shard_map/ppermute | solution.py:269

commit v8 on v7

--- a/solution.py
+++ b/solution.py
@@ -67,8 +67,8 @@
         out[...] = ref[:, pl.ds(begin, rows), :].astype(out.dtype)
 
 
-def cast_kernel(count, psi_ref, half_ref, *outs):
-    half_ref[...] = psi_ref[...].astype(BF16)
+def cast_kernel(count, psi_ref, up_ref, *outs):
+    up_ref[...] = psi_ref[:, : up_ref.shape[1]].astype(BF16)
     rows = psi_ref.shape[1] // count
     pieces_of(psi_ref, lax.axis_index("band"), count, rows, outs)
 
@@ -103,16 +103,6 @@
     return jnp.concatenate(halves, axis=1)
 
 
-def spread_weights(w_ref, bands, atoms, mask):
-    cols = mask.shape[1]
-    out = []
-    for a in range(atoms):
-        w = w_ref[a * bands : (a + 1) * bands]
-        full = jnp.broadcast_to(w[:, None, :], (bands, HALF, cols)).reshape(bands * HALF, cols)
-        out.append((full * mask).astype(BF16))
-    return out
-
-
 def spread_plane(weights, proj_ref, plane_of, valid):
     total = None
     for a, w in enumerate(weights):
@@ -121,72 +111,91 @@
         total = term if total is None else total + term
     nz = proj_ref.shape[4]
     rows = total.shape[0]
-    return [
+    halves = [
         total[:, h * nz : (h + 1) * nz].reshape(rows // HALF, HALF, nz)
         for h in range(total.shape[1] // nz)
     ]
+    return jnp.concatenate(halves, axis=1)
+
+
+def turned(plane):
+    bands, ny, nz = plane.shape
+    plane = plane.astype(BF16)
+    parts = [
+        jnp.transpose(plane[:, h * HALF : (h + 1) * HALF].reshape(bands * HALF, nz))
+        for h in range(ny // HALF)
+    ]
+    return jnp.concatenate(parts, axis=0)
+
+
+def ahead_kernel(planes, psi_ref, ahead_ref, edge_ref, turned_ref):
+    ny = psi_ref.shape[1] // planes
+    for x in range(planes - 1):
+        total = None
+        for m in range(x + 1, HALO + 1):
+            term = kinetic_weights[m] * psi_ref[:, plane_rows(planes + x - m, ny)]
+            total = term if total is None else total + term
+        ahead_ref[:, plane_rows(x, ny)] = total
+    edge_ref[...] = psi_ref[:, plane_rows(planes - 1, ny)].astype(BF16)
+    for x in range(planes):
+        turned_ref[x] = turned(psi_ref[:, plane_rows(x, ny)])
 
 
 def coefficient_kernel(
-    planes, first_ref, strength_ref, own_ref, upper_ref, proj_ref, ahead_ref, w_ref, next_ref, ext
+    planes,
+    first_ref,
+    strength_ref,
+    turned_ref,
+    upper_ref,
+    proj_ref,
+    ahead_ref,
+    edge_ref,
+    w_ref,
+    next_ref,
+    edge_again_ref,
+    ext,
 ):
-    bands, cells, nz = own_ref.shape
-    ny = cells // planes
+    bands, cells, nz = upper_ref.shape
+    reach = BOX - 1
+    ny = cells // reach
     atoms, npj = proj_ref.shape[:2]
     me = lax.axis_index("space")
-    for x in range(planes):
-        ext[x] = own_ref[:, plane_rows(x, ny)]
-        if x < BOX - 1:
-            ext[planes + x] = upper_ref[:, plane_rows(x, ny)]
-    rows, cols = bands * HALF, npj * HALF
+    edge_again_ref[...] = edge_ref[...]
+    ext[0:planes] = turned_ref[...]
+    for x in range(reach):
+        ext[planes + x] = turned(upper_ref[:, plane_rows(x, ny)])
+    rows, cols = npj * HALF, bands * HALF
     mask = same_cell(rows, cols)
     gi = lax.broadcasted_iota(jnp.int32, (cols, cols), 0)
     gj = lax.broadcasted_iota(jnp.int32, (cols, cols), 1)
     group = jnp.where(jnp.bitwise_xor(gi, gj) < HALF, 1.0, 0.0).astype(BF16)
-    owner = lax.broadcasted_iota(jnp.int32, (1, cols), 1)
     starts = [first_ref[me * atoms + a] - me * planes for a in range(atoms)]
-    halves = range(ny // HALF)
 
     parts = []
     for a in range(atoms):
-        left = [
-            ext[starts[a] + p, :, h * HALF : (h + 1) * HALF, :].reshape(rows, nz)
-            for p in range(BOX)
-            for h in halves
-        ]
-        right = [table(proj_ref, a, p) for p in range(BOX)]
-        d = dot(jnp.concatenate(left, axis=1), jnp.concatenate(right, axis=1), ((1,), (1,)))
-        parts.append((d * mask).reshape(bands, HALF, cols).sum(axis=1))
+        left = jnp.concatenate([table(proj_ref, a, p) for p in range(BOX)], axis=1)
+        right = jnp.concatenate([ext[starts[a] + p] for p in range(BOX)], axis=0)
+        d = dot(left, right) * mask
+        parts.append(d.reshape(npj, HALF, cols).sum(axis=1))
     e = jnp.concatenate(parts, axis=0)
     e_hi = e.astype(BF16)
     e_lo = (e - e_hi.astype(F32)).astype(BF16)
     coef = dot(e_hi, group) + dot(e_lo, group)
+    weights = []
     for a in range(atoms):
-        scale = jnp.zeros((1, cols), F32)
-        for j in range(npj):
-            scale = jnp.where(owner >= j * HALF, outer * strength_ref[j, me * atoms + a], scale)
-        w_ref[a * bands : (a + 1) * bands] = coef[a * bands : (a + 1) * bands] * scale
-    weights = spread_weights(w_ref, bands, atoms, mask)
-    for q in range(BOX - 1):
-        blocks = spread_plane(
+        scaled = [
+            coef[a * npj + j : a * npj + j + 1] * (outer * strength_ref[j, me * atoms + a])
+            for j in range(npj)
+        ]
+        full = jnp.concatenate([jnp.broadcast_to(s, (HALF, cols)) for s in scaled], axis=0)
+        weights.append(jnp.transpose((full * mask)).astype(BF16))
+        w_ref[a] = weights[a]
+    for q in range(reach):
+        block = spread_plane(
             weights, proj_ref, [planes + q - s for s in starts], [planes + q - s < BOX for s in starts]
         )
-        for h in halves:
-            begin = q * ny + h * HALF
-            block = blocks[h] + ahead_ref[:, begin : begin + HALF]
-            next_ref[:, begin : begin + HALF] = block.astype(BF16)
-    rest = slice((BOX - 1) * ny, planes * ny)
-    next_ref[:, rest] = ahead_ref[:, rest].astype(BF16)
-
-
-def ahead_kernel(planes, psi_ref, out_ref):
-    ny = psi_ref.shape[1] // planes
-    for x in range(planes):
-        total = None
-        for m in range(x + 1, HALO + 1):
-            term = kinetic_weights[m] * psi_ref[:, plane_rows(planes + x - m, ny)]
-            total = term if total is None else total + term
-        out_ref[:, plane_rows(x, ny)] = total
+        here = plane_rows(q, ny)
+        next_ref[:, here] = (block + ahead_ref[:, here]).astype(BF16)
 
 
 def near_kernel(
@@ -197,43 +206,48 @@
     atoms, npj = proj_ref.shape[:2]
     me = lax.axis_index("space")
     starts = [first_ref[me * atoms + a] - me * planes for a in range(atoms)]
-    weights = spread_weights(w_ref, bands, atoms, same_cell(bands * HALF, npj * HALF))
+    weights = [w_ref[a] for a in range(atoms)]
     cz_hi, cz_lo = circulant(nz, 1)
     cz = (jnp.concatenate([cz_hi, cz_hi], axis=0), cz_lo)
     cy = circulant(ny, bands // 2)
     for x in range(planes):
-        blocks = spread_plane(
+        block = spread_plane(
             weights, proj_ref, [x - s for s in starts], [jnp.logical_and(x >= s, x - s < BOX) for s in starts]
         )
         here = plane_rows(x, ny)
         psi = psi_ref[:, here]
-        total = yz_part(psi, cz, cy) + jnp.concatenate(blocks, axis=1)
+        total = yz_part(psi, cz, cy) + block
         site = outer * pot_ref[here] + (kinetic_weights[0] - outer * center)
         total = total + site[None] * psi - prev_ref[:, here]
         for m in range(1, HALO + 1):
             for target in (x + m, x - m):
-                if target >= planes:
+                if 0 <= target < planes:
+                    total = total + kinetic_weights[m] * psi_ref[:, plane_rows(target, ny)]
+                elif planes <= target < planes + BOX - 1:
                     value = upper_ref[:, plane_rows(target - planes, ny)].astype(F32)
-                elif target >= 0:
-                    value = psi_ref[:, plane_rows(target, ny)]
-                else:
-                    continue
-                total = total + kinetic_weights[m] * value
+                    total = total + kinetic_weights[m] * value
         out_ref[:, here] = total
 
 
-def finish_kernel(count, g_ref, arrived_ref, *rest):
+def complete(g_ref, arrived_ref, below_ref, above_ref, out_ref):
+    cut = arrived_ref.shape[1]
+    out_ref[:, :cut] = (g_ref[:, :cut] + arrived_ref[...].astype(F32)).astype(out_ref.dtype)
+    edges = below_ref[...].astype(F32) + above_ref[...].astype(F32)
+    out_ref[:, cut:] = (g_ref[:, cut:] + kinetic_weights[HALO] * edges).astype(out_ref.dtype)
+
+
+def finish_kernel(count, g_ref, arrived_ref, below_ref, above_ref, *rest):
     outs, total = rest[:-1], rest[-1]
-    total[...] = g_ref[...] + arrived_ref[...].astype(F32)
+    complete(g_ref, arrived_ref, below_ref, above_ref, total)
     rows = g_ref.shape[1] // count
     pieces_of(total, lax.axis_index("band"), count, rows, outs)
 
 
-def output_kernel(g_ref, arrived_ref, *rest):
+def output_kernel(g_ref, arrived_ref, below_ref, above_ref, *rest):
     pieces, (out_ref, panel_ref) = rest[:-2], rest[-2:]
-    out_ref[...] = (g_ref[...] + arrived_ref[...].astype(F32)).astype(BF16)
+    complete(g_ref, arrived_ref, below_ref, above_ref, out_ref)
     bands = g_ref.shape[0]
-    for p, piece in enumerate(pieces):
+    for p, piece in enumerate(reversed(pieces)):
         panel_ref[p * bands : (p + 1) * bands] = piece[...]
 
 
@@ -299,35 +313,36 @@
     sm = pl.BlockSpec(memory_space=pltpu.SMEM)
     anywhere = pl.BlockSpec(memory_space=pl.ANY)
 
-    half, *panel = call(
+    most = (bands, (planes - 1) * ny, nz)
+    plane = (bands, ny, nz)
+    up, *panel = call(
         partial(cast_kernel, n_band),
         "cast",
-        (struct(whole, BF16),) + (struct(quarter, BF16),) * n_band,
+        (struct(most, BF16),) + (struct(quarter, BF16),) * n_band,
         (psi,),
     )
-    upper = cyclic(half, "space", -1)
+    upper = cyclic(up, "space", -1)
     panel = exchanged(panel)
-
-    ahead = call(
+    ahead, edge, own = call(
         partial(ahead_kernel, planes),
         "ahead",
-        struct(whole),
+        (struct(most), struct(plane, BF16), struct((planes, ny // HALF * nz, bands * HALF), BF16)),
         (psi,),
         cost_estimate=pl.CostEstimate(flops=10**9, bytes_accessed=2**20, transcendentals=0),
     )
-    w, beyond = call(
+    below = cyclic(edge, "space", 1)
+    atoms, npj = projectors.shape[:2]
+    w, beyond, edge = call(
         partial(coefficient_kernel, planes),
         "coefficients",
-        (
-            struct((projectors.shape[0] * bands, projectors.shape[1] * HALF)),
-            struct(whole, BF16),
-        ),
-        (atom_planes, strengths.T, half, upper, projectors, ahead),
-        in_specs=[sm, sm, vm, vm, vm, vm],
-        out_specs=(vm, vm),
-        scratch_shapes=[pltpu.VMEM((planes + BOX - 1, bands, ny, nz), BF16)],
+        (struct((atoms, bands * HALF, npj * HALF), BF16), struct(most, BF16), struct(plane, BF16)),
+        (atom_planes, strengths.T, own, upper, projectors, ahead, edge),
+        in_specs=[sm, sm] + [vm] * 5,
+        out_specs=(vm, vm, vm),
+        scratch_shapes=[pltpu.VMEM((planes + BOX - 1, *own.shape[1:]), BF16)],
     )
     arrived = cyclic(beyond, "space", 1)
+    above = cyclic(edge, "space", -1)
     g = call(
         partial(near_kernel, planes),
         "near_part",
@@ -341,7 +356,7 @@
         partial(finish_kernel, n_band),
         "finish",
         (struct(quarter, BF16),) * n_band,
-        (g, arrived),
+        (g, arrived, below, above),
         scratch_shapes=[pltpu.VMEM(whole, F32)],
     )
     mine = exchanged(mine)
@@ -350,7 +365,7 @@
         output_kernel,
         "output",
         (struct(whole, BF16), struct((total_bands, *quarter[1:]), BF16)),
-        (g, arrived, *panel),
+        (g, arrived, below, above, *reversed(panel)),
     )
     left = jnp.concatenate(mine, axis=0).reshape(total_bands, -1)
     right = jnp.concatenate([left, panels.reshape(total_bands, -1)], axis=0)

time: 44.3 us -> 44.3 us (level)
  starting transfers between devices: 12.3 us -> 16.4 us
  waiting for transfers between devices: 10.6 us -> 7.22 us
  blocking collectives: 12 us -> 11.2 us
    ppermute x2 -> x4, waiting for transfers between devices: 6.58 us -> 1.9 us  [cyclic(): lax.ppermute(value, axis, [(i, (i + steps) % count) for i in range(count)])]
    ppermute x2 -> x4, starting transfers between devices: 3.44 us -> 6.51 us  [cyclic(): lax.ppermute(value, axis, [(i, (i + steps) % count) for i in range(count)])]
    ppermute x6, waiting for transfers between devices: 4.04 us -> 5.33 us  [mirrored(): return lax.ppermute(value, axis, [(i, i ^ bits) for i in range(count)])]
    ppermute x6, starting transfers between devices: 8.84 us -> 9.93 us  [mirrored(): return lax.ppermute(value, axis, [(i, i ^ bits) for i in range(count)])]
    all_to_all x1, blocking collectives: 12 us -> 11.2 us  [shards(): got = lax.all_to_all(pieces, ('space', 'band'), 0, 0)]
  transfers between devices with their start and end apart: 8 -> 10, of which waited for: 4 -> 4; matrix products, arithmetic and copies ran while one was open for 0% -> 0% of each run, Pallas kernels for 13% -> 13%
where the time goes in v8:
time: 44.3 us; the launch traced here: 44.1 us
  starting transfers between devices  16.4 us (37%)
  blocking collectives  11.2 us (25%)
  waiting for transfers between devices  7.22 us (16%)
  Pallas kernels  6.75 us (15%)
  local copies, waits for them, and re-layouts  1.32 us (3%)
  between operations  0.76 us (2%)
    all_to_all x1, blocking collectives, shards(): got = lax.all_to_all(pieces, ('space', 'band'), 0, 0)  11.2 us
    ppermute x6, starting transfers between devices, mirrored(): return lax.ppermute(value, axis, [(i, i ^ bits) for i in range(count)])  9.93 us
    pallas_call x8, Pallas kernels, call(): pl.pallas_call(kernel, out_shape=out_shape, compiler_params=params(vmem *...  6.75 us
    ppermute x4, starting transfers between devices, cyclic(): lax.ppermute(value, axis, [(i, (i + steps) % count) for i in range(count)])  6.51 us
    ppermute x6, waiting for transfers between devices, mirrored(): return lax.ppermute(value, axis, [(i, i ^ bits) for i in range(count)])  5.33 us
    ppermute x4, waiting for transfers between devices, cyclic(): lax.ppermute(value, axis, [(i, (i + steps) % count) for i in range(count)])  1.9 us
    unnamed x14, local copies, waits for them, and re-layouts  1.16 us
  transfers between devices with their start and end apart: 10, of which 4 were waited for; matrix products, arithmetic and copies ran while one was open for 0% of the time, Pallas kernels for 13%

profile of v8, /device:TPU:0, one launch (start us, length us, event | category | flops | bytes accessed | tf_op | source)
XLA Modules:
  0.0 44.1 jit_solution(1909562878250184363)
XLA Ops:
  0.6 0.0 copy-start.1
  0.6 1.1 %copy-done.1 = f32[8,6,32,128]{3,2,1,0:T(8,128)S(1)} copy-done((f32[8,6,32,128]{3,2,1,0:T(8,128)S(1)}, f32[8,6,32,128]{3,2,1,0:T(8,128)}, u32[]{:S(2)}) %copy-start.1) | copy-done | bytes 786456
  1.8 0.1 cast.1
  1.8 0.0 copy-start
  1.9 0.0 copy-start.3
  1.9 0.0 copy-start.4
  1.9 3.4 %collective-permute-start = (bf16[8,160,128]{2,1,0:T(8,128)(2,1)S(1)}, bf16[8,160,128]{2,1,0:T(8,128)(2,1)S(1)}, u32[]{:S(2)}, u32[]{:S(2)}) collective-permute-start(bf16[8,160,128]{2,1,0:T(8,128)(2,1)S(1)} %get-tuple-element.23), channel_id=1, source_target_pairs={{0,28},{4,0},{8,4},{12,8},{16,12},{20,16},{24,20},{28,24},{1,29},{... | collective-permute-start | bytes 983048 | tf_op jit(solution)/shard_map/ppermute | solution.py:278
  5.3 0.3 ahead.1
  5.6 0.1 collective-permute-start.2
  5.7 3.7 %collective-permute-start.4 = (bf16[8,48,128]{2,1,0:T(8,128)(2,1)S(1)}, bf16[8,48,128]{2,1,0:T(8,128)(2,1)S(1)}, u32[]{:S(2)}, u32[]{:S(2)}) collective-permute-start(bf16[8,48,128]{2,1,0:T(8,128)(2,1)S(1)} %get-tuple-element.29), channel_id=1, source_target_pairs={{0,3},{1,2},{2,1},{3,0},{4,7},{5,6},{6,5},{7,4},{8,11},{9,10},{10,... | collective-permute-start | bytes 294920 | tf_op jit(solution)/shard_map/ppermute | solution.py:283
  9.3 0.0 collective-permute-start.5
  9.3 0.7 %collective-permute-done.upper_ref = bf16[8,160,128]{2,1,0:T(8,128)(2,1)S(1)} collective-permute-done((bf16[8,160,128]{2,1,0:T(8,128)(2,1)S(1)}, bf16[8,160,128]{2,1,0:T(8,128)(2,1)S(1)}, u32[]{:S(2)}, u32[]{:S(2)}) %collective-permute-start) | collective-permute-done | bytes 327712 | tf_op jit(solution)/shard_map/ppermute | solution.py:278
  10.0 0.0 copy-done
  10.0 0.0 copy-done.3
  10.0 0.0 copy-done.4
  10.0 0.0 copy-start.2
  10.0 0.0 copy-start.5
  10.0 0.0 copy-start.6
  10.0 2.2 %coefficients.1 = (bf16[4,128,144]{2,1,0:T(8,128)(2,1)S(1)}, bf16[8,160,128]{2,1,0:T(8,128)(2,1)S(1)}, bf16[8,32,128]{2,1,0:T(8,128)(2,1)S(1)}) custom-call(s32[32]{0:T(128)S(1)} %copy-done.4, f32[9,32]{1,0:T(8,128)S(1)} %bitcast.16, bf16[6,256,128]{2,1,0:T(8,128)(2,1)S(1)} %get-tuple-element.22.turned_ref, ...), custom_call_target="tpu_custom_call" | custom-call | tf_op jit(solution)/shard_map/coefficients/pallas_call | solution.py:296
  12.2 0.8 %collective-permute-start.1 = (bf16[8,160,128]{2,1,0:T(8,128)(2,1)S(1)}, bf16[8,160,128]{2,1,0:T(8,128)(2,1)S(1)}, u32[]{:S(2)}, u32[]{:S(2)}) collective-permute-start(bf16[8,160,128]{2,1,0:T(8,128)(2,1)S(1)} %get-tuple-element.27), channel_id=1, source_target_pairs={{0,4},{4,8},{8,12},{12,16},{16,20},{20,24},{24,28},{28,0},{1,5},{5... | collective-permute-start | bytes 983048 | tf_op jit(solution)/shard_map/ppermute | solution.py:278
  13.0 2.3 %collective-permute-start.3 = (bf16[8,32,128]{2,1,0:T(8,128)(2,1)S(1)}, bf16[8,32,128]{2,1,0:T(8,128)(2,1)S(1)}, u32[]{:S(2)}, u32[]{:S(2)}) collective-permute-start(bf16[8,32,128]{2,1,0:T(8,128)(2,1)S(1)} %get-tuple-element.28), channel_id=1, source_target_pairs={{0,28},{4,0},{8,4},{12,8},{16,12},{20,16},{24,20},{28,24},{1,29},{... | collective-permute-start | bytes 196616 | tf_op jit(solution)/shard_map/ppermute | solution.py:278
  15.3 0.0 copy-done.2
  15.3 0.0 copy-done.5
  15.3 0.0 copy-done.6
  15.3 2.3 %near_part.1.g_ref = f32[8,192,128]{2,1,0:T(8,128)S(1)} custom-call(s32[32]{0:T(128)S(1)} %copy-done.4, f32[8,192,128]{2,1,0:T(8,128)S(1)} %bitcast.14, f32[8,192,128]{2,1,0:T(8,128)S(1)} %bitcast.17, f32[192,128]{1,0:T(8,128)S(1)} %bitcast.18, bf16[4,128,144]{2,1,0:T(8,128)(2,1)S(1)} %get-tuple-element.26.w_ref, ...), custom_call_target="tpu_custom_call" | custom-call | flops 20000000000 | bytes 4194304 | tf_op jit(solution)/shard_map/near_part/pallas_call | solution.py:296
  17.7 0.0 collective-permute-done.2.below_ref
  17.7 1.8 %collective-permute-start.6 = (bf16[8,48,128]{2,1,0:T(8,128)(2,1)S(1)}, bf16[8,48,128]{2,1,0:T(8,128)(2,1)S(1)}, u32[]{:S(2)}, u32[]{:S(2)}) collective-permute-start(bf16[8,48,128]{2,1,0:T(8,128)(2,1)S(1)} %get-tuple-element.31), channel_id=1, source_target_pairs={{0,1},{1,0},{2,3},{3,2},{4,5},{5,4},{6,7},{7,6},{8,9},{9,8},{10,11... | collective-permute-start | bytes 294920 | tf_op jit(solution)/shard_map/ppermute | solution.py:283
  19.5 0.0 collective-permute-done.3.above_ref
  19.5 1.2 %collective-permute-done.1.arrived_ref = bf16[8,160,128]{2,1,0:T(8,128)(2,1)S(1)} collective-permute-done((bf16[8,160,128]{2,1,0:T(8,128)(2,1)S(1)}, bf16[8,160,128]{2,1,0:T(8,128)(2,1)S(1)}, u32[]{:S(2)}, u32[]{:S(2)}) %collective-permute-start.1) | collective-permute-done | bytes 327712 | tf_op jit(solution)/shard_map/ppermute | solution.py:278
  20.7 0.1 finish.1
  20.9 3.8 %collective-permute-start.9 = (bf16[8,48,128]{2,1,0:T(8,128)(2,1)S(1)}, bf16[8,48,128]{2,1,0:T(8,128)(2,1)S(1)}, u32[]{:S(2)}, u32[]{:S(2)}) collective-permute-start(bf16[8,48,128]{2,1,0:T(8,128)(2,1)S(1)} %get-tuple-element.37), channel_id=1, source_target_pairs={{0,3},{1,2},{2,1},{3,0},{4,7},{5,6},{6,5},{7,4},{8,11},{9,10},{10,... | collective-permute-start | bytes 294920 | tf_op jit(solution)/shard_map/ppermute | solution.py:283
  24.7 0.0 collective-permute-start.8
  24.7 0.0 collective-permute-done.4.rest_0_
  24.7 0.6 %collective-permute-start.7 = (bf16[8,48,128]{2,1,0:T(8,128)(2,1)S(1)}, bf16[8,48,128]{2,1,0:T(8,128)(2,1)S(1)}, u32[]{:S(2)}, u32[]{:S(2)}) collective-permute-start(bf16[8,48,128]{2,1,0:T(8,128)(2,1)S(1)} %get-tuple-element.35), channel_id=1, source_target_pairs={{0,1},{1,0},{2,3},{3,2},{4,5},{5,4},{6,7},{7,6},{8,9},{9,8},{10,11... | collective-permute-start | bytes 294920 | tf_op jit(solution)/shard_map/ppermute | solution.py:283
  25.3 0.0 collective-permute-done.5.rest_1_
  25.3 0.0 collective-permute-done.6.rest_2_
  25.3 0.9 %output.1 = (bf16[8,192,128]{2,1,0:T(8,128)(2,1)}, bf16[32,48,128]{2,1,0:T(8,128)(2,1)S(1)}) custom-call(f32[8,192,128]{2,1,0:T(8,128)S(1)} %near_part.1.g_ref, bf16[8,160,128]{2,1,0:T(8,128)(2,1)S(1)} %collective-permute-done.1.arrived_ref, bf16[8,32,128]{2,1,0:T(8,128)(2,1)S(1)} %collective-permute-done.2.below_ref, ...), custom_call_target="tpu_custom_call" | custom-call | tf_op jit(solution)/shard_map/output/pallas_call | solution.py:296
  26.2 1.9 %collective-permute-done.9 = bf16[8,48,128]{2,1,0:T(8,128)(2,1)S(1)} collective-permute-done((bf16[8,48,128]{2,1,0:T(8,128)(2,1)S(1)}, bf16[8,48,128]{2,1,0:T(8,128)(2,1)S(1)}, u32[]{:S(2)}, u32[]{:S(2)}) %collective-permute-start.9) | collective-permute-done | bytes 98336 | tf_op jit(solution)/shard_map/ppermute | solution.py:283
  28.1 3.4 %collective-permute-done.8 = bf16[8,48,128]{2,1,0:T(8,128)(2,1)S(1)} collective-permute-done((bf16[8,48,128]{2,1,0:T(8,128)(2,1)S(1)}, bf16[8,48,128]{2,1,0:T(8,128)(2,1)S(1)}, u32[]{:S(2)}, u32[]{:S(2)}) %collective-permute-start.8) | collective-permute-done | bytes 98336 | tf_op jit(solution)/shard_map/ppermute | solution.py:283
  31.5 0.0 collective-permute-done.7
  31.5 0.1 pad_maximum_fusion
  31.6 0.2 copy_bitcast_fusion
  31.7 0.3 convolution_multiply_fusion.prod_ref
  32.1 0.1 split.1
  32.2 11.2 %all_to_all.5.got_ref = f32[32,4,16]{2,1,0:T(4,128)S(1)} all-to-all(f32[32,4,16]{2,1,0:T(4,128)S(1)} %split.1), channel_id=1, replica_groups=mesh['space'=8,'band'=4] {'space','band'}, dimensions={0} | all-to-all | bytes 16384 | tf_op jit(solution)/shard_map/all_to_all | solution.py:381
  43.4 0.7 %last_sum.1 = (f32[4,8]{1,0:T(4,128)}, f32[4,8]{1,0:T(4,128)}) custom-call(f32[32,4,16]{2,1,0:T(4,128)S(1)} %all_to_all.5.got_ref), custom_call_target="tpu_custom_call" | custom-call | tf_op jit(solution)/shard_map/last_sum/pallas_call | solution.py:296
Async XLA Ops:
  0.6 1.1 %copy-start.1 = (f32[8,6,32,128]{3,2,1,0:T(8,128)S(1)}, f32[8,6,32,128]{3,2,1,0:T(8,128)}, u32[]{:S(2)}) copy-start(f32[8,6,32,128]{3,2,1,0:T(8,128)} %param.6) | copy-start | bytes 2359300
  1.8 8.2 %copy-start = (bf16[4,9,6,32,128]{4,3,2,1,0:T(8,128)(2,1)S(1)}, bf16[4,9,6,32,128]{4,3,2,1,0:T(8,128)(2,1)}, u32[]{:S(2)}) copy-start(bf16[4,9,6,32,128]{4,3,2,1,0:T(8,128)(2,1)} %proj_ref.3) | copy-start | bytes 5308420
  1.9 8.2 %copy-start.3 = (f32[32,9]{0,1:T(8,128)S(1)}, f32[32,9]{0,1:T(8,128)}, u32[]{:S(2)}) copy-start(f32[32,9]{0,1:T(8,128)} %param.10) | copy-start | bytes 3460
  1.9 8.1 %copy-start.4 = (s32[32]{0:T(128)S(1)}, s32[32]{0:T(128)}, u32[]{:S(2)}) copy-start(s32[32]{0:T(128)} %first_ref.3) | copy-start | bytes 388
  1.9 8.1 %collective-permute-start = (bf16[8,160,128]{2,1,0:T(8,128)(2,1)S(1)}, bf16[8,160,128]{2,1,0:T(8,128)(2,1)S(1)}, u32[]{:S(2)}, u32[]{:S(2)}) collective-permute-start(bf16[8,160,128]{2,1,0:T(8,128)(2,1)S(1)} %get-tuple-element.23), channel_id=1, source_target_pairs={{0,28},{4,0},{8,4},{12,8},{16,12},{20,16},{24,20},{28,24},{1,29},{... | collective-permute-start | bytes 983048 | tf_op jit(solution)/shard_map/ppermute | solution.py:278
  5.6 12.1 %collective-permute-start.2 = (bf16[8,32,128]{2,1,0:T(8,128)(2,1)S(1)}, bf16[8,32,128]{2,1,0:T(8,128)(2,1)S(1)}, u32[]{:S(2)}, u32[]{:S(2)}) collective-permute-start(bf16[8,32,128]{2,1,0:T(8,128)(2,1)S(1)} %get-tuple-element.25.edge_ref), channel_id=1, source_target_pairs={{0,4},{4,8},{8,12},{12,16},{16,20},{20,24},{24,28},{28,0},{1,5},{5... | collective-permute-start | bytes 196616 | tf_op jit(solution)/shard_map/ppermute | solution.py:278
  5.7 19.0 %collective-permute-start.4 = (bf16[8,48,128]{2,1,0:T(8,128)(2,1)S(1)}, bf16[8,48,128]{2,1,0:T(8,128)(2,1)S(1)}, u32[]{:S(2)}, u32[]{:S(2)}) collective-permute-start(bf16[8,48,128]{2,1,0:T(8,128)(2,1)S(1)} %get-tuple-element.29), channel_id=1, source_target_pairs={{0,3},{1,2},{2,1},{3,0},{4,7},{5,6},{6,5},{7,4},{8,11},{9,10},{10,... | collective-permute-start | bytes 294920 | tf_op jit(solution)/shard_map/ppermute | solution.py:283
  9.3 16.0 %collective-permute-start.5 = (bf16[8,48,128]{2,1,0:T(8,128)(2,1)S(1)}, bf16[8,48,128]{2,1,0:T(8,128)(2,1)S(1)}, u32[]{:S(2)}, u32[]{:S(2)}) collective-permute-start(bf16[8,48,128]{2,1,0:T(8,128)(2,1)S(1)} %get-tuple-element.30), channel_id=1, source_target_pairs={{0,2},{1,3},{2,0},{3,1},{4,6},{5,7},{6,4},{7,5},{8,10},{9,11},{10,... | collective-permute-start | bytes 294920 | tf_op jit(solution)/shard_map/ppermute | solution.py:283
  10.0 5.3 %copy-start.2 = (f32[8,6,32,128]{3,2,1,0:T(8,128)S(1)}, f32[8,6,32,128]{3,2,1,0:T(8,128)}, u32[]{:S(2)}) copy-start(f32[8,6,32,128]{3,2,1,0:T(8,128)} %param.6) | copy-start | bytes 2359300
  10.0 5.3 %copy-start.5 = (f32[8,6,32,128]{3,2,1,0:T(8,128)S(1)}, f32[8,6,32,128]{3,2,1,0:T(8,128)}, u32[]{:S(2)}) copy-start(f32[8,6,32,128]{3,2,1,0:T(8,128)} %param.7) | copy-start | bytes 2359300
  10.0 5.3 %copy-start.6 = (f32[6,32,128]{2,1,0:T(8,128)S(1)}, f32[6,32,128]{2,1,0:T(8,128)}, u32[]{:S(2)}) copy-start(f32[6,32,128]{2,1,0:T(8,128)} %param.8) | copy-start | bytes 294916
  12.2 8.5 %collective-permute-start.1 = (bf16[8,160,128]{2,1,0:T(8,128)(2,1)S(1)}, bf16[8,160,128]{2,1,0:T(8,128)(2,1)S(1)}, u32[]{:S(2)}, u32[]{:S(2)}) collective-permute-start(bf16[8,160,128]{2,1,0:T(8,128)(2,1)S(1)} %get-tuple-element.27), channel_id=1, source_target_pairs={{0,4},{4,8},{8,12},{12,16},{16,20},{20,24},{24,28},{28,0},{1,5},{5... | collective-permute-start | bytes 983048 | tf_op jit(solution)/shard_map/ppermute | solution.py:278
  13.0 6.4 %collective-permute-start.3 = (bf16[8,32,128]{2,1,0:T(8,128)(2,1)S(1)}, bf16[8,32,128]{2,1,0:T(8,128)(2,1)S(1)}, u32[]{:S(2)}, u32[]{:S(2)}) collective-permute-start(bf16[8,32,128]{2,1,0:T(8,128)(2,1)S(1)} %get-tuple-element.28), channel_id=1, source_target_pairs={{0,28},{4,0},{8,4},{12,8},{16,12},{20,16},{24,20},{28,24},{1,29},{... | collective-permute-start | bytes 196616 | tf_op jit(solution)/shard_map/ppermute | solution.py:278
  17.7 7.7 %collective-permute-start.6 = (bf16[8,48,128]{2,1,0:T(8,128)(2,1)S(1)}, bf16[8,48,128]{2,1,0:T(8,128)(2,1)S(1)}, u32[]{:S(2)}, u32[]{:S(2)}) collective-permute-start(bf16[8,48,128]{2,1,0:T(8,128)(2,1)S(1)} %get-tuple-element.31), channel_id=1, source_target_pairs={{0,1},{1,0},{2,3},{3,2},{4,5},{5,4},{6,7},{7,6},{8,9},{9,8},{10,11... | collective-permute-start | bytes 294920 | tf_op jit(solution)/shard_map/ppermute | solution.py:283
  20.9 7.3 %collective-permute-start.9 = (bf16[8,48,128]{2,1,0:T(8,128)(2,1)S(1)}, bf16[8,48,128]{2,1,0:T(8,128)(2,1)S(1)}, u32[]{:S(2)}, u32[]{:S(2)}) collective-permute-start(bf16[8,48,128]{2,1,0:T(8,128)(2,1)S(1)} %get-tuple-element.37), channel_id=1, source_target_pairs={{0,3},{1,2},{2,1},{3,0},{4,7},{5,6},{6,5},{7,4},{8,11},{9,10},{10,... | collective-permute-start | bytes 294920 | tf_op jit(solution)/shard_map/ppermute | solution.py:283
  24.7 6.8 %collective-permute-start.8 = (bf16[8,48,128]{2,1,0:T(8,128)(2,1)S(1)}, bf16[8,48,128]{2,1,0:T(8,128)(2,1)S(1)}, u32[]{:S(2)}, u32[]{:S(2)}) collective-permute-start(bf16[8,48,128]{2,1,0:T(8,128)(2,1)S(1)} %get-tuple-element.36), channel_id=1, source_target_pairs={{0,2},{1,3},{2,0},{3,1},{4,6},{5,7},{6,4},{7,5},{8,10},{9,11},{10,... | collective-permute-start | bytes 294920 | tf_op jit(solution)/shard_map/ppermute | solution.py:283
  24.7 6.8 %collective-permute-start.7 = (bf16[8,48,128]{2,1,0:T(8,128)(2,1)S(1)}, bf16[8,48,128]{2,1,0:T(8,128)(2,1)S(1)}, u32[]{:S(2)}, u32[]{:S(2)}) collective-permute-start(bf16[8,48,128]{2,1,0:T(8,128)(2,1)S(1)} %get-tuple-element.35), channel_id=1, source_target_pairs={{0,1},{1,0},{2,3},{3,2},{4,5},{5,4},{6,7},{7,6},{8,9},{9,8},{10,11... | collective-permute-start | bytes 294920 | tf_op jit(solution)/shard_map/ppermute | solution.py:283

commit v9 on v6

--- a/solution.py
+++ b/solution.py
@@ -103,16 +103,6 @@
     return jnp.concatenate(halves, axis=1)
 
 
-def spread_weights(w_ref, bands, atoms, mask):
-    cols = mask.shape[1]
-    out = []
-    for a in range(atoms):
-        w = w_ref[a * bands : (a + 1) * bands]
-        full = jnp.broadcast_to(w[:, None, :], (bands, HALF, cols)).reshape(bands * HALF, cols)
-        out.append((full * mask).astype(BF16))
-    return out
-
-
 def spread_plane(weights, proj_ref, plane_of, valid):
     total = None
     for a, w in enumerate(weights):
@@ -121,22 +111,48 @@
         total = term if total is None else total + term
     nz = proj_ref.shape[4]
     rows = total.shape[0]
-    return [
+    halves = [
         total[:, h * nz : (h + 1) * nz].reshape(rows // HALF, HALF, nz)
         for h in range(total.shape[1] // nz)
     ]
+    return jnp.concatenate(halves, axis=1)
+
+
+def local_kernel(planes, psi_ref, g_ref, ahead_ref, edge_ref):
+    bands, cells, nz = psi_ref.shape
+    ny = cells // planes
+    edge_ref[...] = psi_ref[:, plane_rows(planes - 1, ny)].astype(BF16)
+    for x in range(planes - 1):
+        total = None
+        for m in range(x + 1, HALO + 1):
+            term = kinetic_weights[m] * psi_ref[:, plane_rows(planes + x - m, ny)]
+            total = term if total is None else total + term
+        ahead_ref[:, plane_rows(x, ny)] = total
+    cz_hi, cz_lo = circulant(nz, 1)
+    cz = (jnp.concatenate([cz_hi, cz_hi], axis=0), cz_lo)
+    cy = circulant(ny, bands // 2)
+    for x in range(planes):
+        here = plane_rows(x, ny)
+        psi = psi_ref[:, here]
+        total = yz_part(psi, cz, cy) + (kinetic_weights[0] - outer * center) * psi
+        for m in range(1, HALO + 1):
+            for target in (x + m, x - m):
+                if 0 <= target < planes:
+                    total = total + kinetic_weights[m] * psi_ref[:, plane_rows(target, ny)]
+        g_ref[:, here] = total
 
 
 def coefficient_kernel(
-    planes, first_ref, strength_ref, own_ref, upper_ref, proj_ref, w_ref, next_ref, ext
+    planes, first_ref, strength_ref, own_ref, upper_ref, proj_ref, ahead_ref, w_ref, next_ref, ext
 ):
     bands, cells, nz = own_ref.shape
+    reach = BOX - 1
     ny = cells // planes
     atoms, npj = proj_ref.shape[:2]
     me = lax.axis_index("space")
     for x in range(planes):
         ext[x] = own_ref[:, plane_rows(x, ny)]
-        if x < BOX - 1:
+        if x < reach:
             ext[planes + x] = upper_ref[:, plane_rows(x, ny)]
     rows, cols = bands * HALF, npj * HALF
     mask = same_cell(rows, cols)
@@ -146,7 +162,6 @@
     owner = lax.broadcasted_iota(jnp.int32, (1, cols), 1)
     starts = [first_ref[me * atoms + a] - me * planes for a in range(atoms)]
     halves = range(ny // HALF)
-
     parts = []
     for a in range(atoms):
         left = [
@@ -161,82 +176,63 @@
     e_hi = e.astype(BF16)
     e_lo = (e - e_hi.astype(F32)).astype(BF16)
     coef = dot(e_hi, group) + dot(e_lo, group)
+    weights = []
     for a in range(atoms):
         scale = jnp.zeros((1, cols), F32)
         for j in range(npj):
             scale = jnp.where(owner >= j * HALF, outer * strength_ref[j, me * atoms + a], scale)
-        w_ref[a * bands : (a + 1) * bands] = coef[a * bands : (a + 1) * bands] * scale
-    weights = spread_weights(w_ref, bands, atoms, mask)
-    for q in range(BOX - 1):
-        blocks = spread_plane(
+        w = coef[a * bands : (a + 1) * bands] * scale
+        full = jnp.broadcast_to(w[:, None, :], (bands, HALF, cols)).reshape(rows, cols) * mask
+        weights.append(full.astype(BF16))
+        w_ref[a] = weights[a]
+    for q in range(reach):
+        block = spread_plane(
             weights, proj_ref, [planes + q - s for s in starts], [planes + q - s < BOX for s in starts]
         )
-        for h in halves:
-            begin = q * ny + h * HALF
-            next_ref[:, begin : begin + HALF] = blocks[h].astype(BF16)
-
-
-def again_kernel(half_ref, *refs):
-    refs[-1][...] = half_ref[...]
+        here = plane_rows(q, ny)
+        next_ref[:, here] = (block + ahead_ref[:, here]).astype(BF16)
 
 
 def near_kernel(planes, unused, first_ref, *refs):
-    near_body(planes, first_ref, *refs[unused:])
-
-
-def near_body(
-    planes, first_ref, psi_ref, prev_ref, pot_ref, w_ref, upper_ref, lower_ref, proj_ref, out_ref
-):
+    g_ref, psi_ref, prev_ref, pot_ref, w_ref, upper_ref, proj_ref, out_ref = refs[unused:]
     bands, cells, nz = psi_ref.shape
     ny = cells // planes
-    atoms, npj = proj_ref.shape[:2]
+    atoms = proj_ref.shape[0]
     me = lax.axis_index("space")
     starts = [first_ref[me * atoms + a] - me * planes for a in range(atoms)]
-    weights = spread_weights(w_ref, bands, atoms, same_cell(bands * HALF, npj * HALF))
-    cz_hi, cz_lo = circulant(nz, 1)
-    cz = (jnp.concatenate([cz_hi, cz_hi], axis=0), cz_lo)
-    cy = circulant(ny, bands // 2)
+    weights = [w_ref[a] for a in range(atoms)]
     for x in range(planes):
-        blocks = spread_plane(
+        block = spread_plane(
             weights, proj_ref, [x - s for s in starts], [jnp.logical_and(x >= s, x - s < BOX) for s in starts]
         )
         here = plane_rows(x, ny)
-        psi = psi_ref[:, here]
-        total = yz_part(psi, cz, cy) + jnp.concatenate(blocks, axis=1)
-        site = outer * pot_ref[here] + (kinetic_weights[0] - outer * center)
-        total = total + site[None] * psi - prev_ref[:, here]
-        for m in range(1, HALO + 1):
-            for target in (x + m, x - m):
-                if target >= planes:
-                    value = upper_ref[:, plane_rows(target - planes, ny)].astype(F32)
-                elif target < 0:
-                    value = lower_ref[:, plane_rows(target + planes, ny)].astype(F32)
-                else:
-                    value = psi_ref[:, plane_rows(target, ny)]
-                total = total + kinetic_weights[m] * value
+        total = g_ref[:, here] + block
+        total = total + (outer * pot_ref[here])[None] * psi_ref[:, here] - prev_ref[:, here]
+        for m in range(planes - x, HALO + 1):
+            value = upper_ref[:, plane_rows(x + m - planes, ny)].astype(F32)
+            total = total + kinetic_weights[m] * value
         out_ref[:, here] = total
 
 
-def with_arrived(g_ref, arrived_ref, total):
-    reach = arrived_ref.shape[1]
-    total[:, :reach] = g_ref[:, :reach] + arrived_ref[...].astype(F32)
-    total[:, reach:] = g_ref[:, reach:]
-
-
-def finish_kernel(count, g_ref, arrived_ref, *rest):
+def complete(g_ref, arrived_ref, below_ref, out_ref):
+    cut = arrived_ref.shape[1]
+    out_ref[:, :cut] = (g_ref[:, :cut] + arrived_ref[...].astype(F32)).astype(out_ref.dtype)
+    edge = kinetic_weights[HALO] * below_ref[...].astype(F32)
+    out_ref[:, cut:] = (g_ref[:, cut:] + edge).astype(out_ref.dtype)
+
+
+def finish_kernel(count, g_ref, arrived_ref, below_ref, *rest):
     outs, total = rest[:-1], rest[-1]
-    with_arrived(g_ref, arrived_ref, total)
+    complete(g_ref, arrived_ref, below_ref, total)
     rows = g_ref.shape[1] // count
     pieces_of(total, lax.axis_index("band"), count, rows, outs)
 
 
-def output_kernel(g_ref, arrived_ref, *rest):
+def output_kernel(g_ref, arrived_ref, below_ref, *rest):
     pieces, (out_ref, panel_ref) = rest[:-2], rest[-2:]
-    reach = arrived_ref.shape[1]
-    out_ref[:, :reach] = (g_ref[:, :reach] + arrived_ref[...].astype(F32)).astype(BF16)
-    out_ref[:, reach:] = g_ref[:, reach:].astype(BF16)
+    complete(g_ref, arrived_ref, below_ref, out_ref)
     bands = g_ref.shape[0]
-    for p, piece in enumerate(pieces):
+    for p, piece in enumerate(reversed(pieces)):
         panel_ref[p * bands : (p + 1) * bands] = piece[...]
 
 
@@ -302,6 +298,8 @@
     sm = pl.BlockSpec(memory_space=pltpu.SMEM)
     anywhere = pl.BlockSpec(memory_space=pl.ANY)
 
+    most = (bands, (planes - 1) * ny, nz)
+    plane = (bands, ny, nz)
     half, *panel = call(
         partial(cast_kernel, n_band),
         "cast",
@@ -310,36 +308,30 @@
     )
     upper = cyclic(half, "space", -1)
     panel = exchanged(panel)
-
-    again = call(
-        again_kernel,
-        "again",
-        struct(whole, BF16),
-        (half, panel[3]),
-        in_specs=[vm] + [anywhere] * 1,
-        out_specs=vm,
+    g, ahead, edge = call(
+        partial(local_kernel, planes),
+        "local_part",
+        (struct(whole), struct(most), struct(plane, BF16)),
+        (psi,),
         cost_estimate=pl.CostEstimate(flops=10**9, bytes_accessed=2**20, transcendentals=0),
     )
-    lower = cyclic(again, "space", 1)
+    below = cyclic(edge, "space", 1)
+    atoms, npj = projectors.shape[:2]
     w, beyond = call(
         partial(coefficient_kernel, planes),
         "coefficients",
-        (
-            struct((projectors.shape[0] * bands, projectors.shape[1] * HALF)),
-            struct((bands, (BOX - 1) * ny, nz), BF16),
-        ),
-        (atom_planes, strengths.T, half, upper, projectors),
-        in_specs=[sm, sm, vm, vm, vm],
+        (struct((atoms, bands * HALF, npj * HALF), BF16), struct(most, BF16)),
+        (atom_planes, strengths.T, half, upper, projectors, ahead),
+        in_specs=[sm, sm] + [vm] * 4,
         out_specs=(vm, vm),
         scratch_shapes=[pltpu.VMEM((planes + BOX - 1, bands, ny, nz), BF16)],
-        cost_estimate=pl.CostEstimate(flops=10**10, bytes_accessed=2**20, transcendentals=0),
     )
     arrived = cyclic(beyond, "space", 1)
     g = call(
         partial(near_kernel, planes, 1),
         "near_part",
         struct(whole),
-        (atom_planes, panel[2], psi, prev, pot, w, upper, lower, projectors),
+        (atom_planes, panel[1], g, psi, prev, pot, w, upper, projectors),
         in_specs=[sm] + [anywhere] * 1 + [vm] * 7,
         out_specs=vm,
         cost_estimate=pl.CostEstimate(flops=2*10**10, bytes_accessed=4 * 2**20, transcendentals=0),
@@ -348,7 +340,7 @@
         partial(finish_kernel, n_band),
         "finish",
         (struct(quarter, BF16),) * n_band,
-        (g, arrived),
+        (g, arrived, below),
         scratch_shapes=[pltpu.VMEM(whole, F32)],
     )
     mine = exchanged(mine)
@@ -357,7 +349,7 @@
         output_kernel,
         "output",
         (struct(whole, BF16), struct((total_bands, *quarter[1:]), BF16)),
-        (g, arrived, *panel),
+        (g, arrived, below, *reversed(panel)),
     )
     left = jnp.concatenate(mine, axis=0).reshape(total_bands, -1)
     right = jnp.concatenate([left, panels.reshape(total_bands, -1)], axis=0)

time: 45 us -> 43.4 us (0.964)
  waiting for transfers between devices: 12.5 us -> 9.93 us
  blocking collectives: 11 us -> 11.9 us
    ppermute x6, waiting for transfers between devices: 8.78 us -> 4.07 us  [mirrored(): return lax.ppermute(value, axis, [(i, i ^ bits) for i in range(count)])]
    ppermute x3, waiting for transfers between devices: 3.71 us -> 5.87 us  [cyclic(): lax.ppermute(value, axis, [(i, (i + steps) % count) for i in range(count)])]
    all_to_all x1, blocking collectives: 11 us -> 11.9 us  [shards(): got = lax.all_to_all(pieces, ('space', 'band'), 0, 0)]
  transfers between devices with their start and end apart: 9 -> 9, of which waited for: 5 -> 4; matrix products, arithmetic and copies ran while one was open for 0% -> 0% of each run, Pallas kernels for 13% -> 13%
where the time goes in v9:
time: 43.4 us; the launch traced here: 43.3 us
  starting transfers between devices  12.3 us (28%)
  blocking collectives  11.9 us (27%)
  waiting for transfers between devices  9.93 us (23%)
  Pallas kernels  6.57 us (15%)
  local copies, waits for them, and re-layouts  1.31 us (3%)
  between operations  0.8 us (2%)
    all_to_all x1, blocking collectives, shards(): got = lax.all_to_all(pieces, ('space', 'band'), 0, 0)  11.9 us
    ppermute x6, starting transfers between devices, mirrored(): return lax.ppermute(value, axis, [(i, i ^ bits) for i in range(count)])  8.83 us
    pallas_call x8, Pallas kernels, call(): pl.pallas_call(kernel, out_shape=out_shape, compiler_params=params(vmem *...  6.57 us
    ppermute x3, waiting for transfers between devices, cyclic(): lax.ppermute(value, axis, [(i, (i + steps) % count) for i in range(count)])  5.87 us
    ppermute x6, waiting for transfers between devices, mirrored(): return lax.ppermute(value, axis, [(i, i ^ bits) for i in range(count)])  4.07 us
    ppermute x3, starting transfers between devices, cyclic(): lax.ppermute(value, axis, [(i, (i + steps) % count) for i in range(count)])  3.5 us
    unnamed x14, local copies, waits for them, and re-layouts  1.16 us
  transfers between devices with their start and end apart: 9, of which 4 were waited for; matrix products, arithmetic and copies ran while one was open for 0% of the time, Pallas kernels for 13%

profile of v9, /device:TPU:0, one launch (start us, length us, event | category | flops | bytes accessed | tf_op | source)
XLA Modules:
  0.0 43.3 jit_solution(4602817999887117245)
XLA Ops:
  0.6 0.0 copy-start.1
  0.6 1.1 %copy-done.1 = f32[8,6,32,128]{3,2,1,0:T(8,128)S(1)} copy-done((f32[8,6,32,128]{3,2,1,0:T(8,128)S(1)}, f32[8,6,32,128]{3,2,1,0:T(8,128)}, u32[]{:S(2)}) %copy-start.1) | copy-done | bytes 786456
  1.8 0.1 cast.1
  1.8 3.4 %collective-permute-start.1 = (bf16[8,192,128]{2,1,0:T(8,128)(2,1)S(1)}, bf16[8,192,128]{2,1,0:T(8,128)(2,1)S(1)}, u32[]{:S(2)}, u32[]{:S(2)}) collective-permute-start(bf16[8,192,128]{2,1,0:T(8,128)(2,1)S(1)} %get-tuple-element.23.own_ref), channel_id=1, source_target_pairs={{0,28},{4,0},{8,4},{12,8},{16,12},{20,16},{24,20},{28,24},{1,29},{... | collective-permute-start | bytes 1179656 | tf_op jit(solution)/shard_map/ppermute | solution.py:263
  5.2 3.6 %collective-permute-start = (bf16[8,48,128]{2,1,0:T(8,128)(2,1)S(1)}, bf16[8,48,128]{2,1,0:T(8,128)(2,1)S(1)}, u32[]{:S(2)}, u32[]{:S(2)}) collective-permute-start(bf16[8,48,128]{2,1,0:T(8,128)(2,1)S(1)} %get-tuple-element.21), channel_id=1, source_target_pairs={{0,3},{1,2},{2,1},{3,0},{4,7},{5,6},{6,5},{7,4},{8,11},{9,10},{10,... | collective-permute-start | bytes 294920 | tf_op jit(solution)/shard_map/ppermute | solution.py:268
  8.8 0.0 collective-permute-start.4
  8.8 0.0 copy-start
  8.8 0.0 copy-start.3
  8.8 0.0 copy-start.4
  8.9 0.8 %collective-permute-start.5 = (bf16[8,48,128]{2,1,0:T(8,128)(2,1)S(1)}, bf16[8,48,128]{2,1,0:T(8,128)(2,1)S(1)}, u32[]{:S(2)}, u32[]{:S(2)}) collective-permute-start(bf16[8,48,128]{2,1,0:T(8,128)(2,1)S(1)} %get-tuple-element.29), channel_id=1, source_target_pairs={{0,2},{1,3},{2,0},{3,1},{4,6},{5,7},{6,4},{7,5},{8,10},{9,11},{10,... | collective-permute-start | bytes 294920 | tf_op jit(solution)/shard_map/ppermute | solution.py:268
  9.6 1.2 %local_part.1 = (f32[8,192,128]{2,1,0:T(8,128)S(1)}, f32[8,160,128]{2,1,0:T(8,128)S(1)}, bf16[8,32,128]{2,1,0:T(8,128)(2,1)S(1)}) custom-call(f32[8,192,128]{2,1,0:T(8,128)S(1)} %bitcast.13), custom_call_target="tpu_custom_call" | custom-call | flops 1000000000 | bytes 1048576 | tf_op jit(solution)/shard_map/local_part/pallas_call | solution.py:281
  10.9 0.1 collective-permute-start.3
  11.0 0.0 collective-permute-done.1.upper_ref.refs_6_
  11.0 0.0 copy-done
  11.0 0.0 copy-done.3
  11.0 0.0 copy-done.4
  11.0 0.0 copy-start.2
  11.0 0.0 copy-start.5
  11.0 0.0 copy-start.6
  11.0 2.0 %coefficients.1 = (bf16[4,128,144]{2,1,0:T(8,128)(2,1)S(1)}, bf16[8,160,128]{2,1,0:T(8,128)(2,1)S(1)}) custom-call(s32[32]{0:T(128)S(1)} %copy-done.4, f32[9,32]{1,0:T(8,128)S(1)} %bitcast.16, bf16[8,192,128]{2,1,0:T(8,128)(2,1)S(1)} %get-tuple-element.23.own_ref, bf16[8,192,128]{2,1,0:T(8,128)(2,1)S(1)} %collective-permute-done.1.upper_ref.refs_6_, ...), custom_call_target="tpu_custom_call" | custom-call | tf_op jit(solution)/shard_map/coefficients/pallas_call | solution.py:281
  13.0 0.1 collective-permute-start.2
  13.1 0.0 collective-permute-done.refs_0_.rest_2_
  13.1 0.0 copy-done.2
  13.1 0.0 copy-done.5
  13.1 0.0 copy-done.6
  13.1 1.5 %near_part.1.g_ref = f32[8,192,128]{2,1,0:T(8,128)S(1)} custom-call(s32[32]{0:T(128)S(1)} %copy-done.4, bf16[8,48,128]{2,1,0:T(8,128)(2,1)S(1)} %collective-permute-done.refs_0_.rest_2_, f32[8,192,128]{2,1,0:T(8,128)S(1)} %get-tuple-element.22.refs_1_, f32[8,192,128]{2,1,0:T(8,128)S(1)} %bitcast.14, f32[8,192,128]{2,1,0:T(8,128)S(1)} %bitcast.17, ...), custom_call_target="tpu_custom_call" | custom-call | flops 20000000000 | bytes 4194304 | tf_op jit(solution)/shard_map/near_part/pallas_call | solution.py:281
  14.6 0.9 %collective-permute-done.3.below_ref = bf16[8,32,128]{2,1,0:T(8,128)(2,1)S(1)} collective-permute-done((bf16[8,32,128]{2,1,0:T(8,128)(2,1)S(1)}, bf16[8,32,128]{2,1,0:T(8,128)(2,1)S(1)}, u32[]{:S(2)}, u32[]{:S(2)}) %collective-permute-start.3) | collective-permute-done | bytes 65568 | tf_op jit(solution)/shard_map/ppermute | solution.py:263
  15.5 5.0 %collective-permute-done.2.arrived_ref = bf16[8,160,128]{2,1,0:T(8,128)(2,1)S(1)} collective-permute-done((bf16[8,160,128]{2,1,0:T(8,128)(2,1)S(1)}, bf16[8,160,128]{2,1,0:T(8,128)(2,1)S(1)}, u32[]{:S(2)}, u32[]{:S(2)}) %collective-permute-start.2) | collective-permute-done | bytes 327712 | tf_op jit(solution)/shard_map/ppermute | solution.py:263
  20.5 0.1 finish.1
  20.6 3.7 %collective-permute-start.6 = (bf16[8,48,128]{2,1,0:T(8,128)(2,1)S(1)}, bf16[8,48,128]{2,1,0:T(8,128)(2,1)S(1)}, u32[]{:S(2)}, u32[]{:S(2)}) collective-permute-start(bf16[8,48,128]{2,1,0:T(8,128)(2,1)S(1)} %get-tuple-element.33), channel_id=1, source_target_pairs={{0,3},{1,2},{2,1},{3,0},{4,7},{5,6},{6,5},{7,4},{8,11},{9,10},{10,... | collective-permute-start | bytes 294920 | tf_op jit(solution)/shard_map/ppermute | solution.py:268
  24.3 0.0 collective-permute-start.7
  24.3 0.8 %collective-permute-start.8 = (bf16[8,48,128]{2,1,0:T(8,128)(2,1)S(1)}, bf16[8,48,128]{2,1,0:T(8,128)(2,1)S(1)}, u32[]{:S(2)}, u32[]{:S(2)}) collective-permute-start(bf16[8,48,128]{2,1,0:T(8,128)(2,1)S(1)} %get-tuple-element.35), channel_id=1, source_target_pairs={{0,1},{1,0},{2,3},{3,2},{4,5},{5,4},{6,7},{7,6},{8,9},{9,8},{10,11... | collective-permute-start | bytes 294920 | tf_op jit(solution)/shard_map/ppermute | solution.py:268
  25.1 0.0 collective-permute-done.4.rest_0_
  25.1 0.0 collective-permute-done.5.rest_1_
  25.1 0.8 %output.1 = (bf16[8,192,128]{2,1,0:T(8,128)(2,1)}, bf16[32,48,128]{2,1,0:T(8,128)(2,1)S(1)}) custom-call(f32[8,192,128]{2,1,0:T(8,128)S(1)} %near_part.1.g_ref, bf16[8,160,128]{2,1,0:T(8,128)(2,1)S(1)} %collective-permute-done.2.arrived_ref, bf16[8,32,128]{2,1,0:T(8,128)(2,1)S(1)} %collective-permute-done.3.below_ref, ...), custom_call_target="tpu_custom_call" | custom-call | tf_op jit(solution)/shard_map/output/pallas_call | solution.py:281
  25.9 1.3 %collective-permute-done.6 = bf16[8,48,128]{2,1,0:T(8,128)(2,1)S(1)} collective-permute-done((bf16[8,48,128]{2,1,0:T(8,128)(2,1)S(1)}, bf16[8,48,128]{2,1,0:T(8,128)(2,1)S(1)}, u32[]{:S(2)}, u32[]{:S(2)}) %collective-permute-start.6) | collective-permute-done | bytes 98336 | tf_op jit(solution)/shard_map/ppermute | solution.py:268
  27.2 2.7 %collective-permute-done.7 = bf16[8,48,128]{2,1,0:T(8,128)(2,1)S(1)} collective-permute-done((bf16[8,48,128]{2,1,0:T(8,128)(2,1)S(1)}, bf16[8,48,128]{2,1,0:T(8,128)(2,1)S(1)}, u32[]{:S(2)}, u32[]{:S(2)}) %collective-permute-start.7) | collective-permute-done | bytes 98336 | tf_op jit(solution)/shard_map/ppermute | solution.py:268
  29.9 0.0 collective-permute-done.8
  30.0 0.1 pad_maximum_fusion
  30.0 0.2 copy_bitcast_fusion
  30.2 0.3 convolution_multiply_fusion.prod_ref
  30.5 0.1 split.1
  30.7 11.9 %all_to_all.5.got_ref = f32[32,4,16]{2,1,0:T(4,128)S(1)} all-to-all(f32[32,4,16]{2,1,0:T(4,128)S(1)} %split.1), channel_id=1, replica_groups=mesh['space'=8,'band'=4] {'space','band'}, dimensions={0} | all-to-all | bytes 16384 | tf_op jit(solution)/shard_map/all_to_all | solution.py:365
  42.6 0.7 %last_sum.1 = (f32[4,8]{1,0:T(4,128)}, f32[4,8]{1,0:T(4,128)}) custom-call(f32[32,4,16]{2,1,0:T(4,128)S(1)} %all_to_all.5.got_ref), custom_call_target="tpu_custom_call" | custom-call | tf_op jit(solution)/shard_map/last_sum/pallas_call | solution.py:281
Async XLA Ops:
  0.6 1.1 %copy-start.1 = (f32[8,6,32,128]{3,2,1,0:T(8,128)S(1)}, f32[8,6,32,128]{3,2,1,0:T(8,128)}, u32[]{:S(2)}) copy-start(f32[8,6,32,128]{3,2,1,0:T(8,128)} %param.6) | copy-start | bytes 2359300
  1.8 9.1 %collective-permute-start.1 = (bf16[8,192,128]{2,1,0:T(8,128)(2,1)S(1)}, bf16[8,192,128]{2,1,0:T(8,128)(2,1)S(1)}, u32[]{:S(2)}, u32[]{:S(2)}) collective-permute-start(bf16[8,192,128]{2,1,0:T(8,128)(2,1)S(1)} %get-tuple-element.23.own_ref), channel_id=1, source_target_pairs={{0,28},{4,0},{8,4},{12,8},{16,12},{20,16},{24,20},{28,24},{1,29},{... | collective-permute-start | bytes 1179656 | tf_op jit(solution)/shard_map/ppermute | solution.py:263
  5.2 7.9 %collective-permute-start = (bf16[8,48,128]{2,1,0:T(8,128)(2,1)S(1)}, bf16[8,48,128]{2,1,0:T(8,128)(2,1)S(1)}, u32[]{:S(2)}, u32[]{:S(2)}) collective-permute-start(bf16[8,48,128]{2,1,0:T(8,128)(2,1)S(1)} %get-tuple-element.21), channel_id=1, source_target_pairs={{0,3},{1,2},{2,1},{3,0},{4,7},{5,6},{6,5},{7,4},{8,11},{9,10},{10,... | collective-permute-start | bytes 294920 | tf_op jit(solution)/shard_map/ppermute | solution.py:268
  8.8 16.3 %collective-permute-start.4 = (bf16[8,48,128]{2,1,0:T(8,128)(2,1)S(1)}, bf16[8,48,128]{2,1,0:T(8,128)(2,1)S(1)}, u32[]{:S(2)}, u32[]{:S(2)}) collective-permute-start(bf16[8,48,128]{2,1,0:T(8,128)(2,1)S(1)} %get-tuple-element.28), channel_id=1, source_target_pairs={{0,1},{1,0},{2,3},{3,2},{4,5},{5,4},{6,7},{7,6},{8,9},{9,8},{10,11... | collective-permute-start | bytes 294920 | tf_op jit(solution)/shard_map/ppermute | solution.py:268
  8.8 2.1 %copy-start = (bf16[4,9,6,32,128]{4,3,2,1,0:T(8,128)(2,1)S(1)}, bf16[4,9,6,32,128]{4,3,2,1,0:T(8,128)(2,1)}, u32[]{:S(2)}) copy-start(bf16[4,9,6,32,128]{4,3,2,1,0:T(8,128)(2,1)} %refs_7_.1) | copy-start | bytes 5308420
  8.8 2.1 %copy-start.3 = (f32[32,9]{0,1:T(8,128)S(1)}, f32[32,9]{0,1:T(8,128)}, u32[]{:S(2)}) copy-start(f32[32,9]{0,1:T(8,128)} %param.10) | copy-start | bytes 3460
  8.8 2.1 %copy-start.4 = (s32[32]{0:T(128)S(1)}, s32[32]{0:T(128)}, u32[]{:S(2)}) copy-start(s32[32]{0:T(128)} %first_ref.3) | copy-start | bytes 388
  8.9 16.2 %collective-permute-start.5 = (bf16[8,48,128]{2,1,0:T(8,128)(2,1)S(1)}, bf16[8,48,128]{2,1,0:T(8,128)(2,1)S(1)}, u32[]{:S(2)}, u32[]{:S(2)}) collective-permute-start(bf16[8,48,128]{2,1,0:T(8,128)(2,1)S(1)} %get-tuple-element.29), channel_id=1, source_target_pairs={{0,2},{1,3},{2,0},{3,1},{4,6},{5,7},{6,4},{7,5},{8,10},{9,11},{10,... | collective-permute-start | bytes 294920 | tf_op jit(solution)/shard_map/ppermute | solution.py:268
  10.9 4.6 %collective-permute-start.3 = (bf16[8,32,128]{2,1,0:T(8,128)(2,1)S(1)}, bf16[8,32,128]{2,1,0:T(8,128)(2,1)S(1)}, u32[]{:S(2)}, u32[]{:S(2)}) collective-permute-start(bf16[8,32,128]{2,1,0:T(8,128)(2,1)S(1)} %get-tuple-element.27), channel_id=1, source_target_pairs={{0,4},{4,8},{8,12},{12,16},{16,20},{20,24},{24,28},{28,0},{1,5},{5... | collective-permute-start | bytes 196616 | tf_op jit(solution)/shard_map/ppermute | solution.py:263
  11.0 2.1 %copy-start.2 = (f32[8,6,32,128]{3,2,1,0:T(8,128)S(1)}, f32[8,6,32,128]{3,2,1,0:T(8,128)}, u32[]{:S(2)}) copy-start(f32[8,6,32,128]{3,2,1,0:T(8,128)} %param.6) | copy-start | bytes 2359300
  11.0 2.1 %copy-start.5 = (f32[8,6,32,128]{3,2,1,0:T(8,128)S(1)}, f32[8,6,32,128]{3,2,1,0:T(8,128)}, u32[]{:S(2)}) copy-start(f32[8,6,32,128]{3,2,1,0:T(8,128)} %param.7) | copy-start | bytes 2359300
  11.0 2.1 %copy-start.6 = (f32[6,32,128]{2,1,0:T(8,128)S(1)}, f32[6,32,128]{2,1,0:T(8,128)}, u32[]{:S(2)}) copy-start(f32[6,32,128]{2,1,0:T(8,128)} %param.8) | copy-start | bytes 294916
  13.0 7.5 %collective-permute-start.2 = (bf16[8,160,128]{2,1,0:T(8,128)(2,1)S(1)}, bf16[8,160,128]{2,1,0:T(8,128)(2,1)S(1)}, u32[]{:S(2)}, u32[]{:S(2)}) collective-permute-start(bf16[8,160,128]{2,1,0:T(8,128)(2,1)S(1)} %get-tuple-element.26), channel_id=1, source_target_pairs={{0,4},{4,8},{8,12},{12,16},{16,20},{20,24},{24,28},{28,0},{1,5},{5... | collective-permute-start | bytes 983048 | tf_op jit(solution)/shard_map/ppermute | solution.py:263
  20.6 6.6 %collective-permute-start.6 = (bf16[8,48,128]{2,1,0:T(8,128)(2,1)S(1)}, bf16[8,48,128]{2,1,0:T(8,128)(2,1)S(1)}, u32[]{:S(2)}, u32[]{:S(2)}) collective-permute-start(bf16[8,48,128]{2,1,0:T(8,128)(2,1)S(1)} %get-tuple-element.33), channel_id=1, source_target_pairs={{0,3},{1,2},{2,1},{3,0},{4,7},{5,6},{6,5},{7,4},{8,11},{9,10},{10,... | collective-permute-start | bytes 294920 | tf_op jit(solution)/shard_map/ppermute | solution.py:268
  24.3 5.6 %collective-permute-start.7 = (bf16[8,48,128]{2,1,0:T(8,128)(2,1)S(1)}, bf16[8,48,128]{2,1,0:T(8,128)(2,1)S(1)}, u32[]{:S(2)}, u32[]{:S(2)}) collective-permute-start(bf16[8,48,128]{2,1,0:T(8,128)(2,1)S(1)} %get-tuple-element.34), channel_id=1, source_target_pairs={{0,2},{1,3},{2,0},{3,1},{4,6},{5,7},{6,4},{7,5},{8,10},{9,11},{10,... | collective-permute-start | bytes 294920 | tf_op jit(solution)/shard_map/ppermute | solution.py:268
  24.3 5.7 %collective-permute-start.8 = (bf16[8,48,128]{2,1,0:T(8,128)(2,1)S(1)}, bf16[8,48,128]{2,1,0:T(8,128)(2,1)S(1)}, u32[]{:S(2)}, u32[]{:S(2)}) collective-permute-start(bf16[8,48,128]{2,1,0:T(8,128)(2,1)S(1)} %get-tuple-element.35), channel_id=1, source_target_pairs={{0,1},{1,0},{2,3},{3,2},{4,5},{5,4},{6,7},{7,6},{8,9},{9,8},{10,11... | collective-permute-start | bytes 294920 | tf_op jit(solution)/shard_map/ppermute | solution.py:268

commit v10 on v9

--- a/solution.py
+++ b/solution.py
@@ -104,11 +104,11 @@
 
 
 def spread_plane(weights, proj_ref, plane_of, valid):
-    total = None
-    for a, w in enumerate(weights):
-        p = jnp.clip(plane_of[a], 0, BOX - 1)
-        term = dot(w, table(proj_ref, a, p)) * jnp.where(valid[a], 1.0, 0.0)
-        total = term if total is None else total + term
+    tables = []
+    for a in range(proj_ref.shape[0]):
+        part = table(proj_ref, a, jnp.clip(plane_of[a], 0, BOX - 1))
+        tables.append(part * jnp.where(valid[a], 1.0, 0.0).astype(BF16))
+    total = dot(weights, jnp.concatenate(tables, axis=0))
     nz = proj_ref.shape[4]
     rows = total.shape[0]
     halves = [
@@ -176,15 +176,16 @@
     e_hi = e.astype(BF16)
     e_lo = (e - e_hi.astype(F32)).astype(BF16)
     coef = dot(e_hi, group) + dot(e_lo, group)
-    weights = []
+    scaled = []
     for a in range(atoms):
         scale = jnp.zeros((1, cols), F32)
         for j in range(npj):
             scale = jnp.where(owner >= j * HALF, outer * strength_ref[j, me * atoms + a], scale)
-        w = coef[a * bands : (a + 1) * bands] * scale
-        full = jnp.broadcast_to(w[:, None, :], (bands, HALF, cols)).reshape(rows, cols) * mask
-        weights.append(full.astype(BF16))
-        w_ref[a] = weights[a]
+        scaled.append(coef[a * bands : (a + 1) * bands] * scale)
+    w = jnp.concatenate(scaled, axis=1)
+    full = jnp.broadcast_to(w[:, None, :], (bands, HALF, atoms * cols)).reshape(rows, atoms * cols)
+    weights = (full * same_cell(rows, atoms * cols)).astype(BF16)
+    w_ref[...] = weights
     for q in range(reach):
         block = spread_plane(
             weights, proj_ref, [planes + q - s for s in starts], [planes + q - s < BOX for s in starts]
@@ -200,7 +201,7 @@
     atoms = proj_ref.shape[0]
     me = lax.axis_index("space")
     starts = [first_ref[me * atoms + a] - me * planes for a in range(atoms)]
-    weights = [w_ref[a] for a in range(atoms)]
+    weights = w_ref[...]
     for x in range(planes):
         block = spread_plane(
             weights, proj_ref, [x - s for s in starts], [jnp.logical_and(x >= s, x - s < BOX) for s in starts]
@@ -236,7 +237,7 @@
         panel_ref[p * bands : (p + 1) * bands] = piece[...]
 
 
-def split_kernel(n_space, n_band, prod_ref, out_ref, held):
+def split_kernel(n_space, n_band, prod_ref, out_ref, held, pair):
     bands = prod_ref.shape[0] // n_band
     me = lax.axis_index("band")
     for p, bits in enumerate(partners(n_band)):
@@ -245,17 +246,21 @@
     rows = held.shape[0] // n_space
     for p, bits in enumerate(partners(n_band)):
         cols = [slice((h * n_band + p) * bands, (h * n_band + p + 1) * bands) for h in (0, 1)]
-        pair = jnp.concatenate([held[:, c] for c in cols], axis=1)
+        pair[p] = jnp.concatenate([held[:, c] for c in cols], axis=1)
         owner = jnp.bitwise_xor(me, bits)
+        lines = [pair[p, pl.ds(r, n_space, stride=rows), :] for r in range(rows)]
+        packed = jnp.concatenate(lines, axis=1)
         for i in range(n_space):
-            out_ref[i * n_band + owner] = pair[i * rows : (i + 1) * rows]
+            out_ref[i * n_band + owner] = packed[i : i + 1]
 
 
 def last_kernel(got_ref, margin_ref, projection_ref):
     total = got_ref[...].sum(axis=0)
-    bands = margin_ref.shape[1]
-    margin_ref[...] = total[:, :bands]
-    projection_ref[...] = total[:, bands:]
+    rows, bands = margin_ref.shape
+    for r in range(rows):
+        begin = 2 * r * bands
+        margin_ref[r : r + 1] = total[:, begin : begin + bands]
+        projection_ref[r : r + 1] = total[:, begin + bands : begin + 2 * bands]
 
 
 def cyclic(value, axis, steps):
@@ -320,7 +325,7 @@
     w, beyond = call(
         partial(coefficient_kernel, planes),
         "coefficients",
-        (struct((atoms, bands * HALF, npj * HALF), BF16), struct(most, BF16)),
+        (struct((bands * HALF, atoms * npj * HALF), BF16), struct(most, BF16)),
         (atom_planes, strengths.T, half, upper, projectors, ahead),
         in_specs=[sm, sm] + [vm] * 4,
         out_specs=(vm, vm),
@@ -358,9 +363,12 @@
     pieces = call(
         partial(split_kernel, n_space, n_band),
         "split",
-        struct((n_space * n_band, out_rows, 2 * bands)),
+        struct((n_space * n_band, 1, out_rows * 2 * bands)),
         (products,),
-        scratch_shapes=[pltpu.VMEM(products.shape, F32)],
+        scratch_shapes=[
+            pltpu.VMEM(products.shape, F32),
+            pltpu.VMEM((n_band, total_bands, 2 * bands), F32),
+        ],
     )
     got = lax.all_to_all(pieces, ("space", "band"), 0, 0)
     margin, projection = call(

time: 43.4 us -> 43.2 us (level)
  no operation moved by 1% of the time
where the time goes in v10:
time: 43.2 us; the launch traced here: 43 us
  starting transfers between devices  12.3 us (28%)
  blocking collectives  11.6 us (27%)
  waiting for transfers between devices  10.1 us (23%)
  Pallas kernels  6.48 us (15%)
  local copies, waits for them, and re-layouts  1.31 us (3%)
  between operations  0.8 us (2%)
    all_to_all x1, blocking collectives, shards(): got = lax.all_to_all(pieces, ('space', 'band'), 0, 0)  11.6 us
    ppermute x6, starting transfers between devices, mirrored(): return lax.ppermute(value, axis, [(i, i ^ bits) for i in range(count)])  8.83 us
    pallas_call x8, Pallas kernels, call(): pl.pallas_call(kernel, out_shape=out_shape, compiler_params=params(vmem *...  6.48 us
    ppermute x3, waiting for transfers between devices, cyclic(): lax.ppermute(value, axis, [(i, (i + steps) % count) for i in range(count)])  6.06 us
    ppermute x6, waiting for transfers between devices, mirrored(): return lax.ppermute(value, axis, [(i, i ^ bits) for i in range(count)])  4.07 us
    ppermute x3, starting transfers between devices, cyclic(): lax.ppermute(value, axis, [(i, (i + steps) % count) for i in range(count)])  3.5 us
    unnamed x14, local copies, waits for them, and re-layouts  1.16 us
  transfers between devices with their start and end apart: 9, of which 4 were waited for; matrix products, arithmetic and copies ran while one was open for 0% of the time, Pallas kernels for 13%

profile of v10, /device:TPU:0, one launch (start us, length us, event | category | flops | bytes accessed | tf_op | source)
XLA Modules:
  0.0 43.0 jit_solution(2626730781327824554)
XLA Ops:
  0.6 0.0 copy-start.1
  0.6 1.1 %copy-done.1 = f32[8,6,32,128]{3,2,1,0:T(8,128)S(1)} copy-done((f32[8,6,32,128]{3,2,1,0:T(8,128)S(1)}, f32[8,6,32,128]{3,2,1,0:T(8,128)}, u32[]{:S(2)}) %copy-start.1) | copy-done | bytes 786456
  1.8 0.1 cast.1
  1.8 3.4 %collective-permute-start.1 = (bf16[8,192,128]{2,1,0:T(8,128)(2,1)S(1)}, bf16[8,192,128]{2,1,0:T(8,128)(2,1)S(1)}, u32[]{:S(2)}, u32[]{:S(2)}) collective-permute-start(bf16[8,192,128]{2,1,0:T(8,128)(2,1)S(1)} %get-tuple-element.23.own_ref), channel_id=1, source_target_pairs={{0,28},{4,0},{8,4},{12,8},{16,12},{20,16},{24,20},{28,24},{1,29},{... | collective-permute-start | bytes 1179656 | tf_op jit(solution)/shard_map/ppermute | solution.py:268
  5.2 3.6 %collective-permute-start = (bf16[8,48,128]{2,1,0:T(8,128)(2,1)S(1)}, bf16[8,48,128]{2,1,0:T(8,128)(2,1)S(1)}, u32[]{:S(2)}, u32[]{:S(2)}) collective-permute-start(bf16[8,48,128]{2,1,0:T(8,128)(2,1)S(1)} %get-tuple-element.21), channel_id=1, source_target_pairs={{0,3},{1,2},{2,1},{3,0},{4,7},{5,6},{6,5},{7,4},{8,11},{9,10},{10,... | collective-permute-start | bytes 294920 | tf_op jit(solution)/shard_map/ppermute | solution.py:273
  8.8 0.0 collective-permute-start.4
  8.8 0.0 copy-start
  8.8 0.0 copy-start.3
  8.8 0.0 copy-start.4
  8.9 0.8 %collective-permute-start.5 = (bf16[8,48,128]{2,1,0:T(8,128)(2,1)S(1)}, bf16[8,48,128]{2,1,0:T(8,128)(2,1)S(1)}, u32[]{:S(2)}, u32[]{:S(2)}) collective-permute-start(bf16[8,48,128]{2,1,0:T(8,128)(2,1)S(1)} %get-tuple-element.29), channel_id=1, source_target_pairs={{0,2},{1,3},{2,0},{3,1},{4,6},{5,7},{6,4},{7,5},{8,10},{9,11},{10,... | collective-permute-start | bytes 294920 | tf_op jit(solution)/shard_map/ppermute | solution.py:273
  9.6 1.2 %local_part.1 = (f32[8,192,128]{2,1,0:T(8,128)S(1)}, f32[8,160,128]{2,1,0:T(8,128)S(1)}, bf16[8,32,128]{2,1,0:T(8,128)(2,1)S(1)}) custom-call(f32[8,192,128]{2,1,0:T(8,128)S(1)} %bitcast.13), custom_call_target="tpu_custom_call" | custom-call | flops 1000000000 | bytes 1048576 | tf_op jit(solution)/shard_map/local_part/pallas_call | solution.py:286
  10.9 0.1 collective-permute-start.3
  11.0 0.0 collective-permute-done.1.upper_ref.refs_6_
  11.0 0.0 copy-done
  11.0 0.0 copy-done.3
  11.0 0.0 copy-done.4
  11.0 0.0 copy-start.2
  11.0 0.0 copy-start.5
  11.0 0.0 copy-start.6
  11.0 2.0 %coefficients.1 = (bf16[128,576]{1,0:T(8,128)(2,1)S(1)}, bf16[8,160,128]{2,1,0:T(8,128)(2,1)S(1)}) custom-call(s32[32]{0:T(128)S(1)} %copy-done.4, f32[9,32]{1,0:T(8,128)S(1)} %bitcast.16, bf16[8,192,128]{2,1,0:T(8,128)(2,1)S(1)} %get-tuple-element.23.own_ref, bf16[8,192,128]{2,1,0:T(8,128)(2,1)S(1)} %collective-permute-done.1.upper_ref.refs_6_, ...), custom_call_target="tpu_custom_call" | custom-call | tf_op jit(solution)/shard_map/coefficients/pallas_call | solution.py:286
  13.0 0.1 collective-permute-start.2
  13.1 0.0 collective-permute-done.refs_0_.rest_2_
  13.1 0.0 copy-done.2
  13.1 0.0 copy-done.5
  13.1 0.0 copy-done.6
  13.2 1.3 %near_part.1.g_ref = f32[8,192,128]{2,1,0:T(8,128)S(1)} custom-call(s32[32]{0:T(128)S(1)} %copy-done.4, bf16[8,48,128]{2,1,0:T(8,128)(2,1)S(1)} %collective-permute-done.refs_0_.rest_2_, f32[8,192,128]{2,1,0:T(8,128)S(1)} %get-tuple-element.22.refs_1_, f32[8,192,128]{2,1,0:T(8,128)S(1)} %bitcast.14, f32[8,192,128]{2,1,0:T(8,128)S(1)} %bitcast.17, ...), custom_call_target="tpu_custom_call" | custom-call | flops 20000000000 | bytes 4194304 | tf_op jit(solution)/shard_map/near_part/pallas_call | solution.py:286
  14.4 1.1 %collective-permute-done.3.below_ref = bf16[8,32,128]{2,1,0:T(8,128)(2,1)S(1)} collective-permute-done((bf16[8,32,128]{2,1,0:T(8,128)(2,1)S(1)}, bf16[8,32,128]{2,1,0:T(8,128)(2,1)S(1)}, u32[]{:S(2)}, u32[]{:S(2)}) %collective-permute-start.3) | collective-permute-done | bytes 65568 | tf_op jit(solution)/shard_map/ppermute | solution.py:268
  15.5 5.0 %collective-permute-done.2.arrived_ref = bf16[8,160,128]{2,1,0:T(8,128)(2,1)S(1)} collective-permute-done((bf16[8,160,128]{2,1,0:T(8,128)(2,1)S(1)}, bf16[8,160,128]{2,1,0:T(8,128)(2,1)S(1)}, u32[]{:S(2)}, u32[]{:S(2)}) %collective-permute-start.2) | collective-permute-done | bytes 327712 | tf_op jit(solution)/shard_map/ppermute | solution.py:268
  20.5 0.1 finish.1
  20.6 3.7 %collective-permute-start.6 = (bf16[8,48,128]{2,1,0:T(8,128)(2,1)S(1)}, bf16[8,48,128]{2,1,0:T(8,128)(2,1)S(1)}, u32[]{:S(2)}, u32[]{:S(2)}) collective-permute-start(bf16[8,48,128]{2,1,0:T(8,128)(2,1)S(1)} %get-tuple-element.33), channel_id=1, source_target_pairs={{0,3},{1,2},{2,1},{3,0},{4,7},{5,6},{6,5},{7,4},{8,11},{9,10},{10,... | collective-permute-start | bytes 294920 | tf_op jit(solution)/shard_map/ppermute | solution.py:273
  24.3 0.0 collective-permute-start.7
  24.3 0.8 %collective-permute-start.8 = (bf16[8,48,128]{2,1,0:T(8,128)(2,1)S(1)}, bf16[8,48,128]{2,1,0:T(8,128)(2,1)S(1)}, u32[]{:S(2)}, u32[]{:S(2)}) collective-permute-start(bf16[8,48,128]{2,1,0:T(8,128)(2,1)S(1)} %get-tuple-element.35), channel_id=1, source_target_pairs={{0,1},{1,0},{2,3},{3,2},{4,5},{5,4},{6,7},{7,6},{8,9},{9,8},{10,11... | collective-permute-start | bytes 294920 | tf_op jit(solution)/shard_map/ppermute | solution.py:273
  25.1 0.0 collective-permute-done.4.rest_0_
  25.1 0.0 collective-permute-done.5.rest_1_
  25.1 0.8 %output.1 = (bf16[8,192,128]{2,1,0:T(8,128)(2,1)}, bf16[32,48,128]{2,1,0:T(8,128)(2,1)S(1)}) custom-call(f32[8,192,128]{2,1,0:T(8,128)S(1)} %near_part.1.g_ref, bf16[8,160,128]{2,1,0:T(8,128)(2,1)S(1)} %collective-permute-done.2.arrived_ref, bf16[8,32,128]{2,1,0:T(8,128)(2,1)S(1)} %collective-permute-done.3.below_ref, ...), custom_call_target="tpu_custom_call" | custom-call | tf_op jit(solution)/shard_map/output/pallas_call | solution.py:286
  25.9 1.3 %collective-permute-done.6 = bf16[8,48,128]{2,1,0:T(8,128)(2,1)S(1)} collective-permute-done((bf16[8,48,128]{2,1,0:T(8,128)(2,1)S(1)}, bf16[8,48,128]{2,1,0:T(8,128)(2,1)S(1)}, u32[]{:S(2)}, u32[]{:S(2)}) %collective-permute-start.6) | collective-permute-done | bytes 98336 | tf_op jit(solution)/shard_map/ppermute | solution.py:273
  27.2 2.7 %collective-permute-done.7 = bf16[8,48,128]{2,1,0:T(8,128)(2,1)S(1)} collective-permute-done((bf16[8,48,128]{2,1,0:T(8,128)(2,1)S(1)}, bf16[8,48,128]{2,1,0:T(8,128)(2,1)S(1)}, u32[]{:S(2)}, u32[]{:S(2)}) %collective-permute-start.7) | collective-permute-done | bytes 98336 | tf_op jit(solution)/shard_map/ppermute | solution.py:273
  29.9 0.0 collective-permute-done.8
  30.0 0.1 pad_maximum_fusion
  30.1 0.2 copy_bitcast_fusion
  30.2 0.3 convolution_multiply_fusion.prod_ref
  30.5 0.2 split.1
  30.8 11.6 %all_to_all.5.got_ref = f32[32,1,64]{2,1,0:T(1,128)S(1)} all-to-all(f32[32,1,64]{2,1,0:T(1,128)S(1)} %split.1), channel_id=1, replica_groups=mesh['space'=8,'band'=4] {'space','band'}, dimensions={0} | all-to-all | bytes 16384 | tf_op jit(solution)/shard_map/all_to_all | solution.py:373
  42.3 0.7 %last_sum.1 = (f32[4,8]{1,0:T(4,128)}, f32[4,8]{1,0:T(4,128)}) custom-call(f32[32,1,64]{2,1,0:T(1,128)S(1)} %all_to_all.5.got_ref), custom_call_target="tpu_custom_call" | custom-call | tf_op jit(solution)/shard_map/last_sum/pallas_call | solution.py:286
Async XLA Ops:
  0.6 1.1 %copy-start.1 = (f32[8,6,32,128]{3,2,1,0:T(8,128)S(1)}, f32[8,6,32,128]{3,2,1,0:T(8,128)}, u32[]{:S(2)}) copy-start(f32[8,6,32,128]{3,2,1,0:T(8,128)} %param.6) | copy-start | bytes 2359300
  1.8 9.1 %collective-permute-start.1 = (bf16[8,192,128]{2,1,0:T(8,128)(2,1)S(1)}, bf16[8,192,128]{2,1,0:T(8,128)(2,1)S(1)}, u32[]{:S(2)}, u32[]{:S(2)}) collective-permute-start(bf16[8,192,128]{2,1,0:T(8,128)(2,1)S(1)} %get-tuple-element.23.own_ref), channel_id=1, source_target_pairs={{0,28},{4,0},{8,4},{12,8},{16,12},{20,16},{24,20},{28,24},{1,29},{... | collective-permute-start | bytes 1179656 | tf_op jit(solution)/shard_map/ppermute | solution.py:268
  5.2 7.9 %collective-permute-start = (bf16[8,48,128]{2,1,0:T(8,128)(2,1)S(1)}, bf16[8,48,128]{2,1,0:T(8,128)(2,1)S(1)}, u32[]{:S(2)}, u32[]{:S(2)}) collective-permute-start(bf16[8,48,128]{2,1,0:T(8,128)(2,1)S(1)} %get-tuple-element.21), channel_id=1, source_target_pairs={{0,3},{1,2},{2,1},{3,0},{4,7},{5,6},{6,5},{7,4},{8,11},{9,10},{10,... | collective-permute-start | bytes 294920 | tf_op jit(solution)/shard_map/ppermute | solution.py:273
  8.8 16.3 %collective-permute-start.4 = (bf16[8,48,128]{2,1,0:T(8,128)(2,1)S(1)}, bf16[8,48,128]{2,1,0:T(8,128)(2,1)S(1)}, u32[]{:S(2)}, u32[]{:S(2)}) collective-permute-start(bf16[8,48,128]{2,1,0:T(8,128)(2,1)S(1)} %get-tuple-element.28), channel_id=1, source_target_pairs={{0,1},{1,0},{2,3},{3,2},{4,5},{5,4},{6,7},{7,6},{8,9},{9,8},{10,11... | collective-permute-start | bytes 294920 | tf_op jit(solution)/shard_map/ppermute | solution.py:273
  8.8 2.1 %copy-start = (bf16[4,9,6,32,128]{4,3,2,1,0:T(8,128)(2,1)S(1)}, bf16[4,9,6,32,128]{4,3,2,1,0:T(8,128)(2,1)}, u32[]{:S(2)}) copy-start(bf16[4,9,6,32,128]{4,3,2,1,0:T(8,128)(2,1)} %refs_7_.1) | copy-start | bytes 5308420
  8.8 2.1 %copy-start.3 = (f32[32,9]{0,1:T(8,128)S(1)}, f32[32,9]{0,1:T(8,128)}, u32[]{:S(2)}) copy-start(f32[32,9]{0,1:T(8,128)} %param.10) | copy-start | bytes 3460
  8.8 2.1 %copy-start.4 = (s32[32]{0:T(128)S(1)}, s32[32]{0:T(128)}, u32[]{:S(2)}) copy-start(s32[32]{0:T(128)} %first_ref.3) | copy-start | bytes 388
  8.9 16.2 %collective-permute-start.5 = (bf16[8,48,128]{2,1,0:T(8,128)(2,1)S(1)}, bf16[8,48,128]{2,1,0:T(8,128)(2,1)S(1)}, u32[]{:S(2)}, u32[]{:S(2)}) collective-permute-start(bf16[8,48,128]{2,1,0:T(8,128)(2,1)S(1)} %get-tuple-element.29), channel_id=1, source_target_pairs={{0,2},{1,3},{2,0},{3,1},{4,6},{5,7},{6,4},{7,5},{8,10},{9,11},{10,... | collective-permute-start | bytes 294920 | tf_op jit(solution)/shard_map/ppermute | solution.py:273
  10.9 4.6 %collective-permute-start.3 = (bf16[8,32,128]{2,1,0:T(8,128)(2,1)S(1)}, bf16[8,32,128]{2,1,0:T(8,128)(2,1)S(1)}, u32[]{:S(2)}, u32[]{:S(2)}) collective-permute-start(bf16[8,32,128]{2,1,0:T(8,128)(2,1)S(1)} %get-tuple-element.27), channel_id=1, source_target_pairs={{0,4},{4,8},{8,12},{12,16},{16,20},{20,24},{24,28},{28,0},{1,5},{5... | collective-permute-start | bytes 196616 | tf_op jit(solution)/shard_map/ppermute | solution.py:268
  11.0 2.1 %copy-start.2 = (f32[8,6,32,128]{3,2,1,0:T(8,128)S(1)}, f32[8,6,32,128]{3,2,1,0:T(8,128)}, u32[]{:S(2)}) copy-start(f32[8,6,32,128]{3,2,1,0:T(8,128)} %param.6) | copy-start | bytes 2359300
  11.0 2.1 %copy-start.5 = (f32[8,6,32,128]{3,2,1,0:T(8,128)S(1)}, f32[8,6,32,128]{3,2,1,0:T(8,128)}, u32[]{:S(2)}) copy-start(f32[8,6,32,128]{3,2,1,0:T(8,128)} %param.7) | copy-start | bytes 2359300
  11.0 2.1 %copy-start.6 = (f32[6,32,128]{2,1,0:T(8,128)S(1)}, f32[6,32,128]{2,1,0:T(8,128)}, u32[]{:S(2)}) copy-start(f32[6,32,128]{2,1,0:T(8,128)} %param.8) | copy-start | bytes 294916
  13.0 7.5 %collective-permute-start.2 = (bf16[8,160,128]{2,1,0:T(8,128)(2,1)S(1)}, bf16[8,160,128]{2,1,0:T(8,128)(2,1)S(1)}, u32[]{:S(2)}, u32[]{:S(2)}) collective-permute-start(bf16[8,160,128]{2,1,0:T(8,128)(2,1)S(1)} %get-tuple-element.26), channel_id=1, source_target_pairs={{0,4},{4,8},{8,12},{12,16},{16,20},{20,24},{24,28},{28,0},{1,5},{5... | collective-permute-start | bytes 983048 | tf_op jit(solution)/shard_map/ppermute | solution.py:268
  20.6 6.6 %collective-permute-start.6 = (bf16[8,48,128]{2,1,0:T(8,128)(2,1)S(1)}, bf16[8,48,128]{2,1,0:T(8,128)(2,1)S(1)}, u32[]{:S(2)}, u32[]{:S(2)}) collective-permute-start(bf16[8,48,128]{2,1,0:T(8,128)(2,1)S(1)} %get-tuple-element.33), channel_id=1, source_target_pairs={{0,3},{1,2},{2,1},{3,0},{4,7},{5,6},{6,5},{7,4},{8,11},{9,10},{10,... | collective-permute-start | bytes 294920 | tf_op jit(solution)/shard_map/ppermute | solution.py:273
  24.3 5.6 %collective-permute-start.7 = (bf16[8,48,128]{2,1,0:T(8,128)(2,1)S(1)}, bf16[8,48,128]{2,1,0:T(8,128)(2,1)S(1)}, u32[]{:S(2)}, u32[]{:S(2)}) collective-permute-start(bf16[8,48,128]{2,1,0:T(8,128)(2,1)S(1)} %get-tuple-element.34), channel_id=1, source_target_pairs={{0,2},{1,3},{2,0},{3,1},{4,6},{5,7},{6,4},{7,5},{8,10},{9,11},{10,... | collective-permute-start | bytes 294920 | tf_op jit(solution)/shard_map/ppermute | solution.py:273
  24.3 5.7 %collective-permute-start.8 = (bf16[8,48,128]{2,1,0:T(8,128)(2,1)S(1)}, bf16[8,48,128]{2,1,0:T(8,128)(2,1)S(1)}, u32[]{:S(2)}, u32[]{:S(2)}) collective-permute-start(bf16[8,48,128]{2,1,0:T(8,128)(2,1)S(1)} %get-tuple-element.35), channel_id=1, source_target_pairs={{0,1},{1,0},{2,3},{3,2},{4,5},{5,4},{6,7},{7,6},{8,9},{9,8},{10,11... | collective-permute-start | bytes 294920 | tf_op jit(solution)/shard_map/ppermute | solution.py:273

commit v11 on v10

--- a/solution.py
+++ b/solution.py
@@ -103,19 +103,57 @@
     return jnp.concatenate(halves, axis=1)
 
 
-def spread_plane(weights, proj_ref, plane_of, valid):
-    tables = []
-    for a in range(proj_ref.shape[0]):
-        part = table(proj_ref, a, jnp.clip(plane_of[a], 0, BOX - 1))
-        tables.append(part * jnp.where(valid[a], 1.0, 0.0).astype(BF16))
-    total = dot(weights, jnp.concatenate(tables, axis=0))
-    nz = proj_ref.shape[4]
+def halves_along(value, axis):
+    bands, ny, nz = value.shape
+    parts = [value[:, h * HALF : (h + 1) * HALF].reshape(bands * HALF, nz) for h in range(ny // HALF)]
+    return jnp.concatenate(parts, axis=axis)
+
+
+def spread(weights, tables, nz):
+    total = dot(weights, tables)
     rows = total.shape[0]
     halves = [
         total[:, h * nz : (h + 1) * nz].reshape(rows // HALF, HALF, nz)
         for h in range(total.shape[1] // nz)
     ]
     return jnp.concatenate(halves, axis=1)
+
+
+def overlap(field_ref, planes, ny, table_ref):
+    bands = field_ref.shape[0]
+    left = [halves_along(field_ref[:, plane_rows(x, ny)], 1) for x in range(planes)]
+    right = [table_ref[x] for x in range(planes)]
+    d = dot(jnp.concatenate(left, axis=1), jnp.concatenate(right, axis=1), ((1,), (1,)))
+    rows, cols = d.shape
+    return (d * same_cell(rows, cols)).reshape(bands, HALF, cols).sum(axis=1)
+
+
+def prepare_kernel(
+    planes, first_ref, strength_ref, own_ref, proj_ref, near_ref, far_ref, e_ref, s_ref
+):
+    ny = own_ref.shape[1] // planes
+    atoms, npj = proj_ref.shape[:2]
+    me = lax.axis_index("space")
+    for q in range(planes + BOX - 1):
+        parts = []
+        for a in range(atoms):
+            p = q - (first_ref[me * atoms + a] - me * planes)
+            inside = jnp.logical_and(p >= 0, p < BOX)
+            part = table(proj_ref, a, jnp.clip(p, 0, BOX - 1))
+            parts.append(part * jnp.where(inside, 1.0, 0.0).astype(BF16))
+        whole = jnp.concatenate(parts, axis=0)
+        if q < planes:
+            near_ref[q] = whole
+        else:
+            far_ref[q - planes] = whole
+    owner = lax.broadcasted_iota(jnp.int32, s_ref.shape, 1)
+    scale = jnp.zeros(s_ref.shape, F32)
+    for a in range(atoms):
+        for j in range(npj):
+            value = outer * strength_ref[j, me * atoms + a]
+            scale = jnp.where(owner >= (a * npj + j) * HALF, value, scale)
+    s_ref[...] = scale
+    e_ref[...] = overlap(own_ref, planes, ny, near_ref)
 
 
 def local_kernel(planes, psi_ref, g_ref, ahead_ref, edge_ref):
@@ -142,72 +180,41 @@
         g_ref[:, here] = total
 
 
-def coefficient_kernel(
-    planes, first_ref, strength_ref, own_ref, upper_ref, proj_ref, ahead_ref, w_ref, next_ref, ext
-):
-    bands, cells, nz = own_ref.shape
+def coefficient_kernel(planes, upper_ref, table_ref, e_ref, s_ref, ahead_ref, w_ref, next_ref):
+    bands, cells, nz = upper_ref.shape
+    ny = cells // planes
     reach = BOX - 1
-    ny = cells // planes
-    atoms, npj = proj_ref.shape[:2]
-    me = lax.axis_index("space")
-    for x in range(planes):
-        ext[x] = own_ref[:, plane_rows(x, ny)]
-        if x < reach:
-            ext[planes + x] = upper_ref[:, plane_rows(x, ny)]
-    rows, cols = bands * HALF, npj * HALF
-    mask = same_cell(rows, cols)
-    gi = lax.broadcasted_iota(jnp.int32, (cols, cols), 0)
-    gj = lax.broadcasted_iota(jnp.int32, (cols, cols), 1)
+    e = e_ref[...] + overlap(upper_ref, reach, ny, table_ref)
+    cols = e.shape[1]
+    tiles = -(-cols // nz)
+    e = jnp.concatenate([e, jnp.zeros((bands, tiles * nz - cols), F32)], axis=1)
+    e = jnp.concatenate([e[:, t * nz : (t + 1) * nz] for t in range(tiles)], axis=0)
+    gi = lax.broadcasted_iota(jnp.int32, (nz, nz), 0)
+    gj = lax.broadcasted_iota(jnp.int32, (nz, nz), 1)
     group = jnp.where(jnp.bitwise_xor(gi, gj) < HALF, 1.0, 0.0).astype(BF16)
-    owner = lax.broadcasted_iota(jnp.int32, (1, cols), 1)
-    starts = [first_ref[me * atoms + a] - me * planes for a in range(atoms)]
-    halves = range(ny // HALF)
-    parts = []
-    for a in range(atoms):
-        left = [
-            ext[starts[a] + p, :, h * HALF : (h + 1) * HALF, :].reshape(rows, nz)
-            for p in range(BOX)
-            for h in halves
-        ]
-        right = [table(proj_ref, a, p) for p in range(BOX)]
-        d = dot(jnp.concatenate(left, axis=1), jnp.concatenate(right, axis=1), ((1,), (1,)))
-        parts.append((d * mask).reshape(bands, HALF, cols).sum(axis=1))
-    e = jnp.concatenate(parts, axis=0)
     e_hi = e.astype(BF16)
     e_lo = (e - e_hi.astype(F32)).astype(BF16)
     coef = dot(e_hi, group) + dot(e_lo, group)
-    scaled = []
-    for a in range(atoms):
-        scale = jnp.zeros((1, cols), F32)
-        for j in range(npj):
-            scale = jnp.where(owner >= j * HALF, outer * strength_ref[j, me * atoms + a], scale)
-        scaled.append(coef[a * bands : (a + 1) * bands] * scale)
-    w = jnp.concatenate(scaled, axis=1)
-    full = jnp.broadcast_to(w[:, None, :], (bands, HALF, atoms * cols)).reshape(rows, atoms * cols)
-    weights = (full * same_cell(rows, atoms * cols)).astype(BF16)
+    coef = jnp.concatenate([coef[t * bands : (t + 1) * bands] for t in range(tiles)], axis=1)
+    w = coef[:, :cols] * s_ref[...]
+    rows = bands * HALF
+    full = jnp.broadcast_to(w[:, None, :], (bands, HALF, cols)).reshape(rows, cols)
+    weights = (full * same_cell(rows, cols)).astype(BF16)
     w_ref[...] = weights
     for q in range(reach):
-        block = spread_plane(
-            weights, proj_ref, [planes + q - s for s in starts], [planes + q - s < BOX for s in starts]
-        )
         here = plane_rows(q, ny)
-        next_ref[:, here] = (block + ahead_ref[:, here]).astype(BF16)
-
-
-def near_kernel(planes, unused, first_ref, *refs):
-    g_ref, psi_ref, prev_ref, pot_ref, w_ref, upper_ref, proj_ref, out_ref = refs[unused:]
+        block = spread(weights, table_ref[q], nz) + ahead_ref[:, here]
+        next_ref[:, here] = block.astype(BF16)
+
+
+def near_kernel(planes, unused, *refs):
+    g_ref, psi_ref, prev_ref, pot_ref, w_ref, upper_ref, table_ref, out_ref = refs[unused:]
     bands, cells, nz = psi_ref.shape
     ny = cells // planes
-    atoms = proj_ref.shape[0]
-    me = lax.axis_index("space")
-    starts = [first_ref[me * atoms + a] - me * planes for a in range(atoms)]
     weights = w_ref[...]
     for x in range(planes):
-        block = spread_plane(
-            weights, proj_ref, [x - s for s in starts], [jnp.logical_and(x >= s, x - s < BOX) for s in starts]
-        )
         here = plane_rows(x, ny)
-        total = g_ref[:, here] + block
+        total = g_ref[:, here] + spread(weights, table_ref[x], nz)
         total = total + (outer * pot_ref[here])[None] * psi_ref[:, here] - prev_ref[:, here]
         for m in range(planes - x, HALO + 1):
             value = upper_ref[:, plane_rows(x + m - planes, ny)].astype(F32)
@@ -322,22 +329,35 @@
     )
     below = cyclic(edge, "space", 1)
     atoms, npj = projectors.shape[:2]
+    cols = atoms * npj * HALF
+    tables, far_tables, e, s = call(
+        partial(prepare_kernel, planes),
+        "prepare",
+        (
+            struct((planes, cols, ny // HALF * nz), BF16),
+            struct((BOX - 1, cols, ny // HALF * nz), BF16),
+            struct((bands, cols)),
+            struct((1, cols)),
+        ),
+        (atom_planes, strengths.T, half, projectors),
+        in_specs=[sm, sm, vm, vm],
+        out_specs=(vm, vm, vm, vm),
+        cost_estimate=pl.CostEstimate(flops=10**9, bytes_accessed=2**20, transcendentals=0),
+    )
     w, beyond = call(
         partial(coefficient_kernel, planes),
         "coefficients",
-        (struct((bands * HALF, atoms * npj * HALF), BF16), struct(most, BF16)),
-        (atom_planes, strengths.T, half, upper, projectors, ahead),
-        in_specs=[sm, sm] + [vm] * 4,
-        out_specs=(vm, vm),
-        scratch_shapes=[pltpu.VMEM((planes + BOX - 1, bands, ny, nz), BF16)],
+        (struct((bands * HALF, cols), BF16), struct(most, BF16)),
+        (upper, far_tables, e, s, ahead),
+        cost_estimate=pl.CostEstimate(flops=10**9, bytes_accessed=2**20, transcendentals=0),
     )
     arrived = cyclic(beyond, "space", 1)
     g = call(
-        partial(near_kernel, planes, 1),
+        partial(near_kernel, planes, 2),
         "near_part",
         struct(whole),
-        (atom_planes, panel[1], g, psi, prev, pot, w, upper, projectors),
-        in_specs=[sm] + [anywhere] * 1 + [vm] * 7,
+        (panel[2], panel[1], g, psi, prev, pot, w, upper, tables),
+        in_specs=[anywhere] * 2 + [vm] * 7,
         out_specs=vm,
         cost_estimate=pl.CostEstimate(flops=2*10**10, bytes_accessed=4 * 2**20, transcendentals=0),
     )

time: 43.2 us -> 44.2 us (1.023)
  waiting for transfers between devices: 10.1 us -> 10.7 us
    ppermute x6, waiting for transfers between devices: 4.07 us -> 5.13 us  [mirrored(): return lax.ppermute(value, axis, [(i, i ^ bits) for i in range(count)])]
    ppermute x3, waiting for transfers between devices: 6.06 us -> 5.59 us  [cyclic(): lax.ppermute(value, axis, [(i, (i + steps) % count) for i in range(count)])]
    pallas_call x8 -> x9, Pallas kernels: 6.48 us -> 6.82 us  [call(): pl.pallas_call(kernel, out_shape=out_shape, compiler_params=params(vmem *...]
where the time goes in v11:
time: 44.2 us; the launch traced here: 44 us
  starting transfers between devices  12.2 us (28%)
  blocking collectives  11.8 us (27%)
  waiting for transfers between devices  10.7 us (24%)
  Pallas kernels  6.82 us (15%)
  local copies, waits for them, and re-layouts  1.31 us (3%)
  between operations  0.79 us (2%)
    all_to_all x1, blocking collectives, shards(): got = lax.all_to_all(pieces, ('space', 'band'), 0, 0)  11.8 us
    ppermute x6, starting transfers between devices, mirrored(): return lax.ppermute(value, axis, [(i, i ^ bits) for i in range(count)])  8.69 us
    pallas_call x9, Pallas kernels, call(): pl.pallas_call(kernel, out_shape=out_shape, compiler_params=params(vmem *...  6.82 us
    ppermute x3, waiting for transfers between devices, cyclic(): lax.ppermute(value, axis, [(i, (i + steps) % count) for i in range(count)])  5.59 us
    ppermute x6, waiting for transfers between devices, mirrored(): return lax.ppermute(value, axis, [(i, i ^ bits) for i in range(count)])  5.13 us
    ppermute x3, starting transfers between devices, cyclic(): lax.ppermute(value, axis, [(i, (i + steps) % count) for i in range(count)])  3.5 us
    unnamed x14, local copies, waits for them, and re-layouts  1.16 us
  transfers between devices with their start and end apart: 9, of which 4 were waited for; matrix products, arithmetic and copies ran while one was open for 0% of the time, Pallas kernels for 13%

profile of v11, /device:TPU:0, one launch (start us, length us, event | category | flops | bytes accessed | tf_op | source)
XLA Modules:
  0.0 44.0 jit_solution(3060478671071804799)
XLA Ops:
  0.6 0.0 copy-start
  0.6 1.1 %copy-done = f32[8,6,32,128]{3,2,1,0:T(8,128)S(1)} copy-done((f32[8,6,32,128]{3,2,1,0:T(8,128)S(1)}, f32[8,6,32,128]{3,2,1,0:T(8,128)}, u32[]{:S(2)}) %copy-start) | copy-done | bytes 786456
  1.8 0.1 cast.1
  1.8 3.4 %collective-permute-start.2 = (bf16[8,192,128]{2,1,0:T(8,128)(2,1)S(1)}, bf16[8,192,128]{2,1,0:T(8,128)(2,1)S(1)}, u32[]{:S(2)}, u32[]{:S(2)}) collective-permute-start(bf16[8,192,128]{2,1,0:T(8,128)(2,1)S(1)} %get-tuple-element.28.own_ref), channel_id=1, source_target_pairs={{0,28},{4,0},{8,4},{12,8},{16,12},{20,16},{24,20},{28,24},{1,29},{... | collective-permute-start | bytes 1179656 | tf_op jit(solution)/shard_map/ppermute | solution.py:275
  5.2 2.6 %collective-permute-start = (bf16[8,48,128]{2,1,0:T(8,128)(2,1)S(1)}, bf16[8,48,128]{2,1,0:T(8,128)(2,1)S(1)}, u32[]{:S(2)}, u32[]{:S(2)}) collective-permute-start(bf16[8,48,128]{2,1,0:T(8,128)(2,1)S(1)} %get-tuple-element.25), channel_id=1, source_target_pairs={{0,2},{1,3},{2,0},{3,1},{4,6},{5,7},{6,4},{7,5},{8,10},{9,11},{10,... | collective-permute-start | bytes 294920 | tf_op jit(solution)/shard_map/ppermute | solution.py:280
  7.8 1.3 %collective-permute-start.1 = (bf16[8,48,128]{2,1,0:T(8,128)(2,1)S(1)}, bf16[8,48,128]{2,1,0:T(8,128)(2,1)S(1)}, u32[]{:S(2)}, u32[]{:S(2)}) collective-permute-start(bf16[8,48,128]{2,1,0:T(8,128)(2,1)S(1)} %get-tuple-element.26), channel_id=1, source_target_pairs={{0,3},{1,2},{2,1},{3,0},{4,7},{5,6},{6,5},{7,4},{8,11},{9,10},{10,... | collective-permute-start | bytes 294920 | tf_op jit(solution)/shard_map/ppermute | solution.py:280
  9.2 0.0 copy-start.2
  9.2 0.0 copy-start.5
  9.2 0.0 copy-start.6
  9.2 0.3 collective-permute-start.5
  9.5 1.2 %local_part.1 = (f32[8,192,128]{2,1,0:T(8,128)S(1)}, f32[8,160,128]{2,1,0:T(8,128)S(1)}, bf16[8,32,128]{2,1,0:T(8,128)(2,1)S(1)}) custom-call(f32[8,192,128]{2,1,0:T(8,128)S(1)} %bitcast.13), custom_call_target="tpu_custom_call" | custom-call | flops 1000000000 | bytes 1048576 | tf_op jit(solution)/shard_map/local_part/pallas_call | solution.py:293
  10.7 0.1 collective-permute-start.4
  10.8 0.0 copy-done.2
  10.8 0.0 copy-done.5
  10.8 0.0 copy-done.6
  10.8 1.6 %prepare.1 = (bf16[6,576,256]{2,1,0:T(8,128)(2,1)S(1)}, bf16[5,576,256]{2,1,0:T(8,128)(2,1)S(1)}, f32[8,576]{1,0:T(8,128)S(1)}, f32[1,576]{1,0:T(1,128)S(1)}) custom-call(s32[32]{0:T(128)S(1)} %copy-done.6, f32[9,32]{1,0:T(8,128)S(1)} %bitcast.18, bf16[8,192,128]{2,1,0:T(8,128)(2,1)S(1)} %get-tuple-element.28.own_ref, bf16[4,9,6,32,128]{4,3,2,1,0:T(8,128)(2,1)S(1)} %copy-done.2), custom_call_target="tpu_custom_call" | custom-call | flops 1000000000 | bytes 1048576 | tf_op jit(solution)/shard_map/prepare/pallas_call | solution.py:293
  12.4 0.0 collective-permute-done.2.upper_ref.refs_7_
  12.4 0.0 copy-start.1
  12.4 0.0 copy-start.3
  12.4 0.0 copy-start.4
  12.5 1.3 %coefficients.1 = (bf16[128,576]{1,0:T(8,128)(2,1)S(1)}, bf16[8,160,128]{2,1,0:T(8,128)(2,1)S(1)}) custom-call(bf16[8,192,128]{2,1,0:T(8,128)(2,1)S(1)} %collective-permute-done.2.upper_ref.refs_7_, bf16[5,576,256]{2,1,0:T(8,128)(2,1)S(1)} %get-tuple-element.29.table_ref, f32[8,576]{1,0:T(8,128)S(1)} %get-tuple-element.30.e_ref, ...), custom_call_target="tpu_custom_call" | custom-call | flops 1000000000 | bytes 1048576 | tf_op jit(solution)/shard_map/coefficients/pallas_call | solution.py:293
  13.8 0.1 collective-permute-start.3
  13.9 1.0 %collective-permute-done.refs_0_.rest_1_ = bf16[8,48,128]{2,1,0:T(8,128)(2,1)S(1)} collective-permute-done((bf16[8,48,128]{2,1,0:T(8,128)(2,1)S(1)}, bf16[8,48,128]{2,1,0:T(8,128)(2,1)S(1)}, u32[]{:S(2)}, u32[]{:S(2)}) %collective-permute-start) | collective-permute-done | bytes 98336 | tf_op jit(solution)/shard_map/ppermute | solution.py:280
  14.9 0.0 collective-permute-done.1.refs_1_.rest_2_
  14.9 0.0 copy-done.1
  14.9 0.0 copy-done.3
  14.9 0.0 copy-done.4
  14.9 0.7 %near_part.1.g_ref = f32[8,192,128]{2,1,0:T(8,128)S(1)} custom-call(bf16[8,48,128]{2,1,0:T(8,128)(2,1)S(1)} %collective-permute-done.refs_0_.rest_1_, bf16[8,48,128]{2,1,0:T(8,128)(2,1)S(1)} %collective-permute-done.1.refs_1_.rest_2_, f32[8,192,128]{2,1,0:T(8,128)S(1)} %get-tuple-element.27.refs_2_, f32[8,192,128]{2,1,0:T(8,128)S(1)} %bitcast.14, ...), custom_call_target="tpu_custom_call" | custom-call | flops 20000000000 | bytes 4194304 | tf_op jit(solution)/shard_map/near_part/pallas_call | solution.py:293
  15.7 0.0 collective-permute-done.4.below_ref
  15.7 5.6 %collective-permute-done.3.arrived_ref = bf16[8,160,128]{2,1,0:T(8,128)(2,1)S(1)} collective-permute-done((bf16[8,160,128]{2,1,0:T(8,128)(2,1)S(1)}, bf16[8,160,128]{2,1,0:T(8,128)(2,1)S(1)}, u32[]{:S(2)}, u32[]{:S(2)}) %collective-permute-start.3) | collective-permute-done | bytes 327712 | tf_op jit(solution)/shard_map/ppermute | solution.py:275
  21.3 0.1 finish.1
  21.4 2.9 %collective-permute-start.6 = (bf16[8,48,128]{2,1,0:T(8,128)(2,1)S(1)}, bf16[8,48,128]{2,1,0:T(8,128)(2,1)S(1)}, u32[]{:S(2)}, u32[]{:S(2)}) collective-permute-start(bf16[8,48,128]{2,1,0:T(8,128)(2,1)S(1)} %get-tuple-element.41), channel_id=1, source_target_pairs={{0,3},{1,2},{2,1},{3,0},{4,7},{5,6},{6,5},{7,4},{8,11},{9,10},{10,... | collective-permute-start | bytes 294920 | tf_op jit(solution)/shard_map/ppermute | solution.py:280
  24.3 0.3 collective-permute-start.7
  24.6 1.2 %collective-permute-start.8 = (bf16[8,48,128]{2,1,0:T(8,128)(2,1)S(1)}, bf16[8,48,128]{2,1,0:T(8,128)(2,1)S(1)}, u32[]{:S(2)}, u32[]{:S(2)}) collective-permute-start(bf16[8,48,128]{2,1,0:T(8,128)(2,1)S(1)} %get-tuple-element.43), channel_id=1, source_target_pairs={{0,1},{1,0},{2,3},{3,2},{4,5},{5,4},{6,7},{7,6},{8,9},{9,8},{10,11... | collective-permute-start | bytes 294920 | tf_op jit(solution)/shard_map/ppermute | solution.py:280
  25.8 0.0 collective-permute-done.5.rest_0_
  25.9 0.8 %output.1 = (bf16[8,192,128]{2,1,0:T(8,128)(2,1)}, bf16[32,48,128]{2,1,0:T(8,128)(2,1)S(1)}) custom-call(f32[8,192,128]{2,1,0:T(8,128)S(1)} %near_part.1.g_ref, bf16[8,160,128]{2,1,0:T(8,128)(2,1)S(1)} %collective-permute-done.3.arrived_ref, bf16[8,32,128]{2,1,0:T(8,128)(2,1)S(1)} %collective-permute-done.4.below_ref, ...), custom_call_target="tpu_custom_call" | custom-call | tf_op jit(solution)/shard_map/output/pallas_call | solution.py:293
  26.7 1.3 %collective-permute-done.6 = bf16[8,48,128]{2,1,0:T(8,128)(2,1)S(1)} collective-permute-done((bf16[8,48,128]{2,1,0:T(8,128)(2,1)S(1)}, bf16[8,48,128]{2,1,0:T(8,128)(2,1)S(1)}, u32[]{:S(2)}, u32[]{:S(2)}) %collective-permute-start.6) | collective-permute-done | bytes 98336 | tf_op jit(solution)/shard_map/ppermute | solution.py:280
  28.0 2.8 %collective-permute-done.7 = bf16[8,48,128]{2,1,0:T(8,128)(2,1)S(1)} collective-permute-done((bf16[8,48,128]{2,1,0:T(8,128)(2,1)S(1)}, bf16[8,48,128]{2,1,0:T(8,128)(2,1)S(1)}, u32[]{:S(2)}, u32[]{:S(2)}) %collective-permute-start.7) | collective-permute-done | bytes 98336 | tf_op jit(solution)/shard_map/ppermute | solution.py:280
  30.8 0.0 collective-permute-done.8
  30.8 0.1 pad_maximum_fusion
  30.8 0.2 copy_bitcast_fusion
  31.0 0.3 convolution_multiply_fusion.prod_ref
  31.3 0.2 split.1
  31.5 11.8 %all_to_all.5.got_ref = f32[32,1,64]{2,1,0:T(1,128)S(1)} all-to-all(f32[32,1,64]{2,1,0:T(1,128)S(1)} %split.1), channel_id=1, replica_groups=mesh['space'=8,'band'=4] {'space','band'}, dimensions={0} | all-to-all | bytes 16384 | tf_op jit(solution)/shard_map/all_to_all | solution.py:393
  43.3 0.7 %last_sum.1 = (f32[4,8]{1,0:T(4,128)}, f32[4,8]{1,0:T(4,128)}) custom-call(f32[32,1,64]{2,1,0:T(1,128)S(1)} %all_to_all.5.got_ref), custom_call_target="tpu_custom_call" | custom-call | tf_op jit(solution)/shard_map/last_sum/pallas_call | solution.py:293
Async XLA Ops:
  0.6 1.1 %copy-start = (f32[8,6,32,128]{3,2,1,0:T(8,128)S(1)}, f32[8,6,32,128]{3,2,1,0:T(8,128)}, u32[]{:S(2)}) copy-start(f32[8,6,32,128]{3,2,1,0:T(8,128)} %param.6) | copy-start | bytes 2359300
  1.8 10.6 %collective-permute-start.2 = (bf16[8,192,128]{2,1,0:T(8,128)(2,1)S(1)}, bf16[8,192,128]{2,1,0:T(8,128)(2,1)S(1)}, u32[]{:S(2)}, u32[]{:S(2)}) collective-permute-start(bf16[8,192,128]{2,1,0:T(8,128)(2,1)S(1)} %get-tuple-element.28.own_ref), channel_id=1, source_target_pairs={{0,28},{4,0},{8,4},{12,8},{16,12},{20,16},{24,20},{28,24},{1,29},{... | collective-permute-start | bytes 1179656 | tf_op jit(solution)/shard_map/ppermute | solution.py:275
  5.2 9.7 %collective-permute-start = (bf16[8,48,128]{2,1,0:T(8,128)(2,1)S(1)}, bf16[8,48,128]{2,1,0:T(8,128)(2,1)S(1)}, u32[]{:S(2)}, u32[]{:S(2)}) collective-permute-start(bf16[8,48,128]{2,1,0:T(8,128)(2,1)S(1)} %get-tuple-element.25), channel_id=1, source_target_pairs={{0,2},{1,3},{2,0},{3,1},{4,6},{5,7},{6,4},{7,5},{8,10},{9,11},{10,... | collective-permute-start | bytes 294920 | tf_op jit(solution)/shard_map/ppermute | solution.py:280
  7.8 7.1 %collective-permute-start.1 = (bf16[8,48,128]{2,1,0:T(8,128)(2,1)S(1)}, bf16[8,48,128]{2,1,0:T(8,128)(2,1)S(1)}, u32[]{:S(2)}, u32[]{:S(2)}) collective-permute-start(bf16[8,48,128]{2,1,0:T(8,128)(2,1)S(1)} %get-tuple-element.26), channel_id=1, source_target_pairs={{0,3},{1,2},{2,1},{3,0},{4,7},{5,6},{6,5},{7,4},{8,11},{9,10},{10,... | collective-permute-start | bytes 294920 | tf_op jit(solution)/shard_map/ppermute | solution.py:280
  9.2 1.6 %copy-start.2 = (bf16[4,9,6,32,128]{4,3,2,1,0:T(8,128)(2,1)S(1)}, bf16[4,9,6,32,128]{4,3,2,1,0:T(8,128)(2,1)}, u32[]{:S(2)}) copy-start(bf16[4,9,6,32,128]{4,3,2,1,0:T(8,128)(2,1)} %proj_ref.1) | copy-start | bytes 5308420
  9.2 1.6 %copy-start.5 = (f32[32,9]{0,1:T(8,128)S(1)}, f32[32,9]{0,1:T(8,128)}, u32[]{:S(2)}) copy-start(f32[32,9]{0,1:T(8,128)} %param.10) | copy-start | bytes 3460
  9.2 1.6 %copy-start.6 = (s32[32]{0:T(128)S(1)}, s32[32]{0:T(128)}, u32[]{:S(2)}) copy-start(s32[32]{0:T(128)} %first_ref.1) | copy-start | bytes 388
  9.2 16.7 %collective-permute-start.5 = (bf16[8,48,128]{2,1,0:T(8,128)(2,1)S(1)}, bf16[8,48,128]{2,1,0:T(8,128)(2,1)S(1)}, u32[]{:S(2)}, u32[]{:S(2)}) collective-permute-start(bf16[8,48,128]{2,1,0:T(8,128)(2,1)S(1)} %get-tuple-element.37), channel_id=1, source_target_pairs={{0,1},{1,0},{2,3},{3,2},{4,5},{5,4},{6,7},{7,6},{8,9},{9,8},{10,11... | collective-permute-start | bytes 294920 | tf_op jit(solution)/shard_map/ppermute | solution.py:280
  10.7 4.9 %collective-permute-start.4 = (bf16[8,32,128]{2,1,0:T(8,128)(2,1)S(1)}, bf16[8,32,128]{2,1,0:T(8,128)(2,1)S(1)}, u32[]{:S(2)}, u32[]{:S(2)}) collective-permute-start(bf16[8,32,128]{2,1,0:T(8,128)(2,1)S(1)} %get-tuple-element.36), channel_id=1, source_target_pairs={{0,4},{4,8},{8,12},{12,16},{16,20},{20,24},{24,28},{28,0},{1,5},{5... | collective-permute-start | bytes 196616 | tf_op jit(solution)/shard_map/ppermute | solution.py:275
  12.4 2.5 %copy-start.1 = (f32[8,6,32,128]{3,2,1,0:T(8,128)S(1)}, f32[8,6,32,128]{3,2,1,0:T(8,128)}, u32[]{:S(2)}) copy-start(f32[8,6,32,128]{3,2,1,0:T(8,128)} %param.6) | copy-start | bytes 2359300
  12.4 2.5 %copy-start.3 = (f32[8,6,32,128]{3,2,1,0:T(8,128)S(1)}, f32[8,6,32,128]{3,2,1,0:T(8,128)}, u32[]{:S(2)}) copy-start(f32[8,6,32,128]{3,2,1,0:T(8,128)} %param.7) | copy-start | bytes 2359300
  12.4 2.5 %copy-start.4 = (f32[6,32,128]{2,1,0:T(8,128)S(1)}, f32[6,32,128]{2,1,0:T(8,128)}, u32[]{:S(2)}) copy-start(f32[6,32,128]{2,1,0:T(8,128)} %param.8) | copy-start | bytes 294916
  13.8 7.5 %collective-permute-start.3 = (bf16[8,160,128]{2,1,0:T(8,128)(2,1)S(1)}, bf16[8,160,128]{2,1,0:T(8,128)(2,1)S(1)}, u32[]{:S(2)}, u32[]{:S(2)}) collective-permute-start(bf16[8,160,128]{2,1,0:T(8,128)(2,1)S(1)} %get-tuple-element.35), channel_id=1, source_target_pairs={{0,4},{4,8},{8,12},{12,16},{16,20},{20,24},{24,28},{28,0},{1,5},{5... | collective-permute-start | bytes 983048 | tf_op jit(solution)/shard_map/ppermute | solution.py:275
  21.4 6.6 %collective-permute-start.6 = (bf16[8,48,128]{2,1,0:T(8,128)(2,1)S(1)}, bf16[8,48,128]{2,1,0:T(8,128)(2,1)S(1)}, u32[]{:S(2)}, u32[]{:S(2)}) collective-permute-start(bf16[8,48,128]{2,1,0:T(8,128)(2,1)S(1)} %get-tuple-element.41), channel_id=1, source_target_pairs={{0,3},{1,2},{2,1},{3,0},{4,7},{5,6},{6,5},{7,4},{8,11},{9,10},{10,... | collective-permute-start | bytes 294920 | tf_op jit(solution)/shard_map/ppermute | solution.py:280
  24.3 6.5 %collective-permute-start.7 = (bf16[8,48,128]{2,1,0:T(8,128)(2,1)S(1)}, bf16[8,48,128]{2,1,0:T(8,128)(2,1)S(1)}, u32[]{:S(2)}, u32[]{:S(2)}) collective-permute-start(bf16[8,48,128]{2,1,0:T(8,128)(2,1)S(1)} %get-tuple-element.42), channel_id=1, source_target_pairs={{0,2},{1,3},{2,0},{3,1},{4,6},{5,7},{6,4},{7,5},{8,10},{9,11},{10,... | collective-permute-start | bytes 294920 | tf_op jit(solution)/shard_map/ppermute | solution.py:280
  24.6 6.1 %collective-permute-start.8 = (bf16[8,48,128]{2,1,0:T(8,128)(2,1)S(1)}, bf16[8,48,128]{2,1,0:T(8,128)(2,1)S(1)}, u32[]{:S(2)}, u32[]{:S(2)}) collective-permute-start(bf16[8,48,128]{2,1,0:T(8,128)(2,1)S(1)} %get-tuple-element.43), channel_id=1, source_target_pairs={{0,1},{1,0},{2,3},{3,2},{4,5},{5,4},{6,7},{7,6},{8,9},{9,8},{10,11... | collective-permute-start | bytes 294920 | tf_op jit(solution)/shard_map/ppermute | solution.py:280

commit v12 on v11

--- a/solution.py
+++ b/solution.py
@@ -67,8 +67,11 @@
         out[...] = ref[:, pl.ds(begin, rows), :].astype(out.dtype)
 
 
-def cast_kernel(count, psi_ref, half_ref, *outs):
+def cast_kernel(psi_ref, half_ref):
     half_ref[...] = psi_ref[...].astype(BF16)
+
+
+def pieces_kernel(count, psi_ref, *outs):
     rows = psi_ref.shape[1] // count
     pieces_of(psi_ref, lax.axis_index("band"), count, rows, outs)
 
@@ -156,9 +159,9 @@
     e_ref[...] = overlap(own_ref, planes, ny, near_ref)
 
 
-def local_kernel(planes, psi_ref, g_ref, ahead_ref, edge_ref):
-    bands, cells, nz = psi_ref.shape
-    ny = cells // planes
+def ahead_kernel(planes, psi_ref, *refs):
+    ahead_ref, edge_ref = refs[-2:]
+    ny = psi_ref.shape[1] // planes
     edge_ref[...] = psi_ref[:, plane_rows(planes - 1, ny)].astype(BF16)
     for x in range(planes - 1):
         total = None
@@ -166,18 +169,6 @@
             term = kinetic_weights[m] * psi_ref[:, plane_rows(planes + x - m, ny)]
             total = term if total is None else total + term
         ahead_ref[:, plane_rows(x, ny)] = total
-    cz_hi, cz_lo = circulant(nz, 1)
-    cz = (jnp.concatenate([cz_hi, cz_hi], axis=0), cz_lo)
-    cy = circulant(ny, bands // 2)
-    for x in range(planes):
-        here = plane_rows(x, ny)
-        psi = psi_ref[:, here]
-        total = yz_part(psi, cz, cy) + (kinetic_weights[0] - outer * center) * psi
-        for m in range(1, HALO + 1):
-            for target in (x + m, x - m):
-                if 0 <= target < planes:
-                    total = total + kinetic_weights[m] * psi_ref[:, plane_rows(target, ny)]
-        g_ref[:, here] = total
 
 
 def coefficient_kernel(planes, upper_ref, table_ref, e_ref, s_ref, ahead_ref, w_ref, next_ref):
@@ -207,18 +198,26 @@
         next_ref[:, here] = block.astype(BF16)
 
 
-def near_kernel(planes, unused, *refs):
-    g_ref, psi_ref, prev_ref, pot_ref, w_ref, upper_ref, table_ref, out_ref = refs[unused:]
+def near_kernel(planes, psi_ref, prev_ref, pot_ref, w_ref, upper_ref, table_ref, out_ref):
     bands, cells, nz = psi_ref.shape
     ny = cells // planes
     weights = w_ref[...]
+    cz_hi, cz_lo = circulant(nz, 1)
+    cz = (jnp.concatenate([cz_hi, cz_hi], axis=0), cz_lo)
+    cy = circulant(ny, bands // 2)
     for x in range(planes):
         here = plane_rows(x, ny)
-        total = g_ref[:, here] + spread(weights, table_ref[x], nz)
-        total = total + (outer * pot_ref[here])[None] * psi_ref[:, here] - prev_ref[:, here]
-        for m in range(planes - x, HALO + 1):
-            value = upper_ref[:, plane_rows(x + m - planes, ny)].astype(F32)
-            total = total + kinetic_weights[m] * value
+        psi = psi_ref[:, here]
+        total = yz_part(psi, cz, cy) + spread(weights, table_ref[x], nz)
+        site = outer * pot_ref[here] + (kinetic_weights[0] - outer * center)
+        total = total + site[None] * psi - prev_ref[:, here]
+        for m in range(1, HALO + 1):
+            for target in (x + m, x - m):
+                if 0 <= target < planes:
+                    total = total + kinetic_weights[m] * psi_ref[:, plane_rows(target, ny)]
+                elif target >= planes:
+                    value = upper_ref[:, plane_rows(target - planes, ny)].astype(F32)
+                    total = total + kinetic_weights[m] * value
         out_ref[:, here] = total
 
 
@@ -312,22 +311,16 @@
 
     most = (bands, (planes - 1) * ny, nz)
     plane = (bands, ny, nz)
-    half, *panel = call(
-        partial(cast_kernel, n_band),
-        "cast",
-        (struct(whole, BF16),) + (struct(quarter, BF16),) * n_band,
+    half = call(cast_kernel, "cast", struct(whole, BF16), (psi,))
+    panel = call(
+        partial(pieces_kernel, n_band),
+        "pieces",
+        (struct(quarter, BF16),) * n_band,
         (psi,),
+        cost_estimate=pl.CostEstimate(flops=10**9, bytes_accessed=2**20, transcendentals=0),
     )
     upper = cyclic(half, "space", -1)
     panel = exchanged(panel)
-    g, ahead, edge = call(
-        partial(local_kernel, planes),
-        "local_part",
-        (struct(whole), struct(most), struct(plane, BF16)),
-        (psi,),
-        cost_estimate=pl.CostEstimate(flops=10**9, bytes_accessed=2**20, transcendentals=0),
-    )
-    below = cyclic(edge, "space", 1)
     atoms, npj = projectors.shape[:2]
     cols = atoms * npj * HALF
     tables, far_tables, e, s = call(
@@ -341,9 +334,19 @@
         ),
         (atom_planes, strengths.T, half, projectors),
         in_specs=[sm, sm, vm, vm],
-        out_specs=(vm, vm, vm, vm),
+        out_specs=(vm,) * 4,
         cost_estimate=pl.CostEstimate(flops=10**9, bytes_accessed=2**20, transcendentals=0),
     )
+    ahead, edge = call(
+        partial(ahead_kernel, planes),
+        "ahead",
+        (struct(most), struct(plane, BF16)),
+        (psi, panel[3], s),
+        in_specs=[vm, anywhere, anywhere],
+        out_specs=(vm, vm),
+        cost_estimate=pl.CostEstimate(flops=10**9, bytes_accessed=2**20, transcendentals=0),
+    )
+    below = cyclic(edge, "space", 1)
     w, beyond = call(
         partial(coefficient_kernel, planes),
         "coefficients",
@@ -353,12 +356,10 @@
     )
     arrived = cyclic(beyond, "space", 1)
     g = call(
-        partial(near_kernel, planes, 2),
+        partial(near_kernel, planes),
         "near_part",
         struct(whole),
-        (panel[2], panel[1], g, psi, prev, pot, w, upper, tables),
-        in_specs=[anywhere] * 2 + [vm] * 7,
-        out_specs=vm,
+        (psi, prev, pot, w, upper, tables),
         cost_estimate=pl.CostEstimate(flops=2*10**10, bytes_accessed=4 * 2**20, transcendentals=0),
     )
     mine = call(

time: 44.2 us -> 42.8 us (0.968)
  waiting for transfers between devices: 10.7 us -> 9.81 us
  blocking collectives: 11.8 us -> 11.2 us
    ppermute x6, waiting for transfers between devices: 5.13 us -> 4.06 us  [mirrored(): return lax.ppermute(value, axis, [(i, i ^ bits) for i in range(count)])]
    all_to_all x1, blocking collectives: 11.8 us -> 11.2 us  [shards(): got = lax.all_to_all(pieces, ('space', 'band'), 0, 0)]
    pallas_call x9 -> x10, Pallas kernels: 6.82 us -> 6.65 us  [call(): pl.pallas_call(kernel, out_shape=out_shape, compiler_params=params(vmem *...]
where the time goes in v12:
time: 42.8 us; the launch traced here: 42.6 us
  starting transfers between devices  12.4 us (29%)
  blocking collectives  11.2 us (26%)
  waiting for transfers between devices  9.81 us (23%)
  Pallas kernels  6.65 us (16%)
  local copies, waits for them, and re-layouts  1.32 us (3%)
  between operations  0.8 us (2%)
    all_to_all x1, blocking collectives, shards(): got = lax.all_to_all(pieces, ('space', 'band'), 0, 0)  11.2 us
    ppermute x6, starting transfers between devices, mirrored(): return lax.ppermute(value, axis, [(i, i ^ bits) for i in range(count)])  8.9 us
    pallas_call x10, Pallas kernels, call(): pl.pallas_call(kernel, out_shape=out_shape, compiler_params=params(vmem *...  6.65 us
    ppermute x3, waiting for transfers between devices, cyclic(): lax.ppermute(value, axis, [(i, (i + steps) % count) for i in range(count)])  5.75 us
    ppermute x6, waiting for transfers between devices, mirrored(): return lax.ppermute(value, axis, [(i, i ^ bits) for i in range(count)])  4.06 us
    ppermute x3, starting transfers between devices, cyclic(): lax.ppermute(value, axis, [(i, (i + steps) % count) for i in range(count)])  3.5 us
    unnamed x14, local copies, waits for them, and re-layouts  1.16 us
  transfers between devices with their start and end apart: 9, of which 4 were waited for; matrix products, arithmetic and copies ran while one was open for 0% of the time, Pallas kernels for 13%

profile of v12, /device:TPU:0, one launch (start us, length us, event | category | flops | bytes accessed | tf_op | source)
XLA Modules:
  0.0 42.6 jit_solution(15707443442048953238)
XLA Ops:
  0.6 0.0 copy-start
  0.6 1.1 %copy-done = f32[8,6,32,128]{3,2,1,0:T(8,128)S(1)} copy-done((f32[8,6,32,128]{3,2,1,0:T(8,128)S(1)}, f32[8,6,32,128]{3,2,1,0:T(8,128)}, u32[]{:S(2)}) %copy-start) | copy-done | bytes 786456
  1.8 0.0 copy-start.2
  1.8 0.0 copy-start.5
  1.8 0.0 copy-start.6
  1.8 3.4 %collective-permute-start = (bf16[8,192,128]{2,1,0:T(8,128)(2,1)S(1)}, bf16[8,192,128]{2,1,0:T(8,128)(2,1)S(1)}, u32[]{:S(2)}, u32[]{:S(2)}) collective-permute-start(bf16[8,192,128]{2,1,0:T(8,128)(2,1)S(1)} %cast.1.own_ref), channel_id=1, source_target_pairs={{0,28},{4,0},{8,4},{12,8},{16,12},{20,16},{24,20},{28,24},{1,29},{... | collective-permute-start | bytes 1179656 | tf_op jit(solution)/shard_map/ppermute | solution.py:274
  5.3 1.6 %collective-permute-start.1 = (bf16[8,48,128]{2,1,0:T(8,128)(2,1)S(1)}, bf16[8,48,128]{2,1,0:T(8,128)(2,1)S(1)}, u32[]{:S(2)}, u32[]{:S(2)}) collective-permute-start(bf16[8,48,128]{2,1,0:T(8,128)(2,1)S(1)} %get-tuple-element.26), channel_id=1, source_target_pairs={{0,1},{1,0},{2,3},{3,2},{4,5},{5,4},{6,7},{7,6},{8,9},{9,8},{10,11... | collective-permute-start | bytes 294920 | tf_op jit(solution)/shard_map/ppermute | solution.py:279
  6.9 2.6 %collective-permute-start.4 = (bf16[8,48,128]{2,1,0:T(8,128)(2,1)S(1)}, bf16[8,48,128]{2,1,0:T(8,128)(2,1)S(1)}, u32[]{:S(2)}, u32[]{:S(2)}) collective-permute-start(bf16[8,48,128]{2,1,0:T(8,128)(2,1)S(1)} %get-tuple-element.32), channel_id=1, source_target_pairs={{0,2},{1,3},{2,0},{3,1},{4,6},{5,7},{6,4},{7,5},{8,10},{9,11},{10,... | collective-permute-start | bytes 294920 | tf_op jit(solution)/shard_map/ppermute | solution.py:279
  9.5 0.2 collective-permute-start.5
  9.7 0.0 copy-done.2
  9.7 0.0 copy-done.5
  9.7 0.0 copy-done.6
  9.7 0.0 copy-start.1
  9.7 1.6 %prepare.1 = (bf16[6,576,256]{2,1,0:T(8,128)(2,1)S(1)}, bf16[5,576,256]{2,1,0:T(8,128)(2,1)S(1)}, f32[8,576]{1,0:T(8,128)S(1)}, f32[1,576]{1,0:T(1,128)S(1)}) custom-call(s32[32]{0:T(128)S(1)} %copy-done.6, f32[9,32]{1,0:T(8,128)S(1)} %bitcast.19, bf16[8,192,128]{2,1,0:T(8,128)(2,1)S(1)} %cast.1.own_ref, bf16[4,9,6,32,128]{4,3,2,1,0:T(8,128)(2,1)S(1)} %copy-done.2), custom_call_target="tpu_custom_call" | custom-call | flops 1000000000 | bytes 1048576 | tf_op jit(solution)/shard_map/prepare/pallas_call | solution.py:292
  11.3 0.0 collective-permute-done.1.refs_0_.rest_0_
  11.3 0.0 copy-done.1
  11.3 0.2 ahead.1
  11.5 0.1 collective-permute-start.3
  11.6 0.0 collective-permute-done.upper_ref
  11.6 0.0 copy-start.3
  11.6 0.0 copy-start.4
  11.6 1.3 %coefficients.1 = (bf16[128,576]{1,0:T(8,128)(2,1)S(1)}, bf16[8,160,128]{2,1,0:T(8,128)(2,1)S(1)}) custom-call(bf16[8,192,128]{2,1,0:T(8,128)(2,1)S(1)} %collective-permute-done.upper_ref, bf16[5,576,256]{2,1,0:T(8,128)(2,1)S(1)} %get-tuple-element.23.table_ref, f32[8,576]{1,0:T(8,128)S(1)} %get-tuple-element.24.e_ref, ...), custom_call_target="tpu_custom_call" | custom-call | flops 1000000000 | bytes 1048576 | tf_op jit(solution)/shard_map/coefficients/pallas_call | solution.py:292
  13.0 0.1 collective-permute-start.2
  13.0 0.0 copy-done.3
  13.1 0.0 copy-done.4
  13.1 1.6 %near_part.1.g_ref = f32[8,192,128]{2,1,0:T(8,128)S(1)} custom-call(f32[8,192,128]{2,1,0:T(8,128)S(1)} %bitcast.15, f32[8,192,128]{2,1,0:T(8,128)S(1)} %bitcast.17, f32[192,128]{1,0:T(8,128)S(1)} %bitcast.18, bf16[128,576]{1,0:T(8,128)(2,1)S(1)} %get-tuple-element.28.w_ref, bf16[8,192,128]{2,1,0:T(8,128)(2,1)S(1)} %collective-permute-done.upper_ref, ...), custom_call_target="tpu_custom_call" | custom-call | flops 20000000000 | bytes 4194304 | tf_op jit(solution)/shard_map/near_part/pallas_call | solution.py:292
  14.7 1.5 %collective-permute-done.3.below_ref = bf16[8,32,128]{2,1,0:T(8,128)(2,1)S(1)} collective-permute-done((bf16[8,32,128]{2,1,0:T(8,128)(2,1)S(1)}, bf16[8,32,128]{2,1,0:T(8,128)(2,1)S(1)}, u32[]{:S(2)}, u32[]{:S(2)}) %collective-permute-start.3) | collective-permute-done | bytes 65568 | tf_op jit(solution)/shard_map/ppermute | solution.py:274
  16.2 4.3 %collective-permute-done.2.arrived_ref = bf16[8,160,128]{2,1,0:T(8,128)(2,1)S(1)} collective-permute-done((bf16[8,160,128]{2,1,0:T(8,128)(2,1)S(1)}, bf16[8,160,128]{2,1,0:T(8,128)(2,1)S(1)}, u32[]{:S(2)}, u32[]{:S(2)}) %collective-permute-start.2) | collective-permute-done | bytes 327712 | tf_op jit(solution)/shard_map/ppermute | solution.py:274
  20.4 0.1 finish.1
  20.6 3.7 %collective-permute-start.6 = (bf16[8,48,128]{2,1,0:T(8,128)(2,1)S(1)}, bf16[8,48,128]{2,1,0:T(8,128)(2,1)S(1)}, u32[]{:S(2)}, u32[]{:S(2)}) collective-permute-start(bf16[8,48,128]{2,1,0:T(8,128)(2,1)S(1)} %get-tuple-element.37), channel_id=1, source_target_pairs={{0,3},{1,2},{2,1},{3,0},{4,7},{5,6},{6,5},{7,4},{8,11},{9,10},{10,... | collective-permute-start | bytes 294920 | tf_op jit(solution)/shard_map/ppermute | solution.py:279
  24.2 0.0 collective-permute-start.7
  24.2 0.8 %collective-permute-start.8 = (bf16[8,48,128]{2,1,0:T(8,128)(2,1)S(1)}, bf16[8,48,128]{2,1,0:T(8,128)(2,1)S(1)}, u32[]{:S(2)}, u32[]{:S(2)}) collective-permute-start(bf16[8,48,128]{2,1,0:T(8,128)(2,1)S(1)} %get-tuple-element.39), channel_id=1, source_target_pairs={{0,1},{1,0},{2,3},{3,2},{4,5},{5,4},{6,7},{7,6},{8,9},{9,8},{10,11... | collective-permute-start | bytes 294920 | tf_op jit(solution)/shard_map/ppermute | solution.py:279
  25.0 0.0 collective-permute-done.4.rest_1_
  25.0 0.0 collective-permute-done.5.rest_2_
  25.0 0.8 %output.1 = (bf16[8,192,128]{2,1,0:T(8,128)(2,1)}, bf16[32,48,128]{2,1,0:T(8,128)(2,1)S(1)}) custom-call(f32[8,192,128]{2,1,0:T(8,128)S(1)} %near_part.1.g_ref, bf16[8,160,128]{2,1,0:T(8,128)(2,1)S(1)} %collective-permute-done.2.arrived_ref, bf16[8,32,128]{2,1,0:T(8,128)(2,1)S(1)} %collective-permute-done.3.below_ref, ...), custom_call_target="tpu_custom_call" | custom-call | tf_op jit(solution)/shard_map/output/pallas_call | solution.py:292
  25.9 1.5 %collective-permute-done.6 = bf16[8,48,128]{2,1,0:T(8,128)(2,1)S(1)} collective-permute-done((bf16[8,48,128]{2,1,0:T(8,128)(2,1)S(1)}, bf16[8,48,128]{2,1,0:T(8,128)(2,1)S(1)}, u32[]{:S(2)}, u32[]{:S(2)}) %collective-permute-start.6) | collective-permute-done | bytes 98336 | tf_op jit(solution)/shard_map/ppermute | solution.py:279
  27.4 2.5 %collective-permute-done.7 = bf16[8,48,128]{2,1,0:T(8,128)(2,1)S(1)} collective-permute-done((bf16[8,48,128]{2,1,0:T(8,128)(2,1)S(1)}, bf16[8,48,128]{2,1,0:T(8,128)(2,1)S(1)}, u32[]{:S(2)}, u32[]{:S(2)}) %collective-permute-start.7) | collective-permute-done | bytes 98336 | tf_op jit(solution)/shard_map/ppermute | solution.py:279
  29.9 0.0 collective-permute-done.8
  29.9 0.1 pad_maximum_fusion
  30.0 0.2 copy_bitcast_fusion
  30.1 0.3 convolution_multiply_fusion.prod_ref
  30.5 0.2 split.1
  30.7 11.2 %all_to_all.5.got_ref = f32[32,1,64]{2,1,0:T(1,128)S(1)} all-to-all(f32[32,1,64]{2,1,0:T(1,128)S(1)} %split.1), channel_id=1, replica_groups=mesh['space'=8,'band'=4] {'space','band'}, dimensions={0} | all-to-all | bytes 16384 | tf_op jit(solution)/shard_map/all_to_all | solution.py:394
  41.9 0.7 %last_sum.1 = (f32[4,8]{1,0:T(4,128)}, f32[4,8]{1,0:T(4,128)}) custom-call(f32[32,1,64]{2,1,0:T(1,128)S(1)} %all_to_all.5.got_ref), custom_call_target="tpu_custom_call" | custom-call | tf_op jit(solution)/shard_map/last_sum/pallas_call | solution.py:292
  (2 shorter events, 0.1 us)
Async XLA Ops:
  0.6 1.1 %copy-start = (f32[8,6,32,128]{3,2,1,0:T(8,128)S(1)}, f32[8,6,32,128]{3,2,1,0:T(8,128)}, u32[]{:S(2)}) copy-start(f32[8,6,32,128]{3,2,1,0:T(8,128)} %param.6) | copy-start | bytes 2359300
  1.8 7.9 %copy-start.2 = (bf16[4,9,6,32,128]{4,3,2,1,0:T(8,128)(2,1)S(1)}, bf16[4,9,6,32,128]{4,3,2,1,0:T(8,128)(2,1)}, u32[]{:S(2)}) copy-start(bf16[4,9,6,32,128]{4,3,2,1,0:T(8,128)(2,1)} %proj_ref.1) | copy-start | bytes 5308420
  1.8 7.9 %copy-start.5 = (f32[32,9]{0,1:T(8,128)S(1)}, f32[32,9]{0,1:T(8,128)}, u32[]{:S(2)}) copy-start(f32[32,9]{0,1:T(8,128)} %param.10) | copy-start | bytes 3460
  1.8 7.9 %copy-start.6 = (s32[32]{0:T(128)S(1)}, s32[32]{0:T(128)}, u32[]{:S(2)}) copy-start(s32[32]{0:T(128)} %first_ref.1) | copy-start | bytes 388
  1.8 9.8 %collective-permute-start = (bf16[8,192,128]{2,1,0:T(8,128)(2,1)S(1)}, bf16[8,192,128]{2,1,0:T(8,128)(2,1)S(1)}, u32[]{:S(2)}, u32[]{:S(2)}) collective-permute-start(bf16[8,192,128]{2,1,0:T(8,128)(2,1)S(1)} %cast.1.own_ref), channel_id=1, source_target_pairs={{0,28},{4,0},{8,4},{12,8},{16,12},{20,16},{24,20},{28,24},{1,29},{... | collective-permute-start | bytes 1179656 | tf_op jit(solution)/shard_map/ppermute | solution.py:274
  5.3 6.0 %collective-permute-start.1 = (bf16[8,48,128]{2,1,0:T(8,128)(2,1)S(1)}, bf16[8,48,128]{2,1,0:T(8,128)(2,1)S(1)}, u32[]{:S(2)}, u32[]{:S(2)}) collective-permute-start(bf16[8,48,128]{2,1,0:T(8,128)(2,1)S(1)} %get-tuple-element.26), channel_id=1, source_target_pairs={{0,1},{1,0},{2,3},{3,2},{4,5},{5,4},{6,7},{7,6},{8,9},{9,8},{10,11... | collective-permute-start | bytes 294920 | tf_op jit(solution)/shard_map/ppermute | solution.py:279
  6.9 18.1 %collective-permute-start.4 = (bf16[8,48,128]{2,1,0:T(8,128)(2,1)S(1)}, bf16[8,48,128]{2,1,0:T(8,128)(2,1)S(1)}, u32[]{:S(2)}, u32[]{:S(2)}) collective-permute-start(bf16[8,48,128]{2,1,0:T(8,128)(2,1)S(1)} %get-tuple-element.32), channel_id=1, source_target_pairs={{0,2},{1,3},{2,0},{3,1},{4,6},{5,7},{6,4},{7,5},{8,10},{9,11},{10,... | collective-permute-start | bytes 294920 | tf_op jit(solution)/shard_map/ppermute | solution.py:279
  9.5 15.5 %collective-permute-start.5 = (bf16[8,48,128]{2,1,0:T(8,128)(2,1)S(1)}, bf16[8,48,128]{2,1,0:T(8,128)(2,1)S(1)}, u32[]{:S(2)}, u32[]{:S(2)}) collective-permute-start(bf16[8,48,128]{2,1,0:T(8,128)(2,1)S(1)} %get-tuple-element.33), channel_id=1, source_target_pairs={{0,3},{1,2},{2,1},{3,0},{4,7},{5,6},{6,5},{7,4},{8,11},{9,10},{10,... | collective-permute-start | bytes 294920 | tf_op jit(solution)/shard_map/ppermute | solution.py:279
  9.7 1.6 %copy-start.1 = (f32[8,6,32,128]{3,2,1,0:T(8,128)S(1)}, f32[8,6,32,128]{3,2,1,0:T(8,128)}, u32[]{:S(2)}) copy-start(f32[8,6,32,128]{3,2,1,0:T(8,128)} %param.6) | copy-start | bytes 2359300
  11.5 4.6 %collective-permute-start.3 = (bf16[8,32,128]{2,1,0:T(8,128)(2,1)S(1)}, bf16[8,32,128]{2,1,0:T(8,128)(2,1)S(1)}, u32[]{:S(2)}, u32[]{:S(2)}) collective-permute-start(bf16[8,32,128]{2,1,0:T(8,128)(2,1)S(1)} %get-tuple-element.31), channel_id=1, source_target_pairs={{0,4},{4,8},{8,12},{12,16},{16,20},{20,24},{24,28},{28,0},{1,5},{5... | collective-permute-start | bytes 196616 | tf_op jit(solution)/shard_map/ppermute | solution.py:274
  11.6 1.4 %copy-start.3 = (f32[8,6,32,128]{3,2,1,0:T(8,128)S(1)}, f32[8,6,32,128]{3,2,1,0:T(8,128)}, u32[]{:S(2)}) copy-start(f32[8,6,32,128]{3,2,1,0:T(8,128)} %param.7) | copy-start | bytes 2359300
  11.6 1.4 %copy-start.4 = (f32[6,32,128]{2,1,0:T(8,128)S(1)}, f32[6,32,128]{2,1,0:T(8,128)}, u32[]{:S(2)}) copy-start(f32[6,32,128]{2,1,0:T(8,128)} %param.8) | copy-start | bytes 294916
  13.0 7.5 %collective-permute-start.2 = (bf16[8,160,128]{2,1,0:T(8,128)(2,1)S(1)}, bf16[8,160,128]{2,1,0:T(8,128)(2,1)S(1)}, u32[]{:S(2)}, u32[]{:S(2)}) collective-permute-start(bf16[8,160,128]{2,1,0:T(8,128)(2,1)S(1)} %get-tuple-element.30), channel_id=1, source_target_pairs={{0,4},{4,8},{8,12},{12,16},{16,20},{20,24},{24,28},{28,0},{1,5},{5... | collective-permute-start | bytes 983048 | tf_op jit(solution)/shard_map/ppermute | solution.py:274
  20.6 6.8 %collective-permute-start.6 = (bf16[8,48,128]{2,1,0:T(8,128)(2,1)S(1)}, bf16[8,48,128]{2,1,0:T(8,128)(2,1)S(1)}, u32[]{:S(2)}, u32[]{:S(2)}) collective-permute-start(bf16[8,48,128]{2,1,0:T(8,128)(2,1)S(1)} %get-tuple-element.37), channel_id=1, source_target_pairs={{0,3},{1,2},{2,1},{3,0},{4,7},{5,6},{6,5},{7,4},{8,11},{9,10},{10,... | collective-permute-start | bytes 294920 | tf_op jit(solution)/shard_map/ppermute | solution.py:279
  24.2 5.6 %collective-permute-start.7 = (bf16[8,48,128]{2,1,0:T(8,128)(2,1)S(1)}, bf16[8,48,128]{2,1,0:T(8,128)(2,1)S(1)}, u32[]{:S(2)}, u32[]{:S(2)}) collective-permute-start(bf16[8,48,128]{2,1,0:T(8,128)(2,1)S(1)} %get-tuple-element.38), channel_id=1, source_target_pairs={{0,2},{1,3},{2,0},{3,1},{4,6},{5,7},{6,4},{7,5},{8,10},{9,11},{10,... | collective-permute-start | bytes 294920 | tf_op jit(solution)/shard_map/ppermute | solution.py:279
  24.2 5.7 %collective-permute-start.8 = (bf16[8,48,128]{2,1,0:T(8,128)(2,1)S(1)}, bf16[8,48,128]{2,1,0:T(8,128)(2,1)S(1)}, u32[]{:S(2)}, u32[]{:S(2)}) collective-permute-start(bf16[8,48,128]{2,1,0:T(8,128)(2,1)S(1)} %get-tuple-element.39), channel_id=1, source_target_pairs={{0,1},{1,0},{2,3},{3,2},{4,5},{5,4},{6,7},{7,6},{8,9},{9,8},{10,11... | collective-permute-start | bytes 294920 | tf_op jit(solution)/shard_map/ppermute | solution.py:279

commit v13 on v12

--- a/solution.py
+++ b/solution.py
@@ -239,7 +239,7 @@
     pieces, (out_ref, panel_ref) = rest[:-2], rest[-2:]
     complete(g_ref, arrived_ref, below_ref, out_ref)
     bands = g_ref.shape[0]
-    for p, piece in enumerate(reversed(pieces)):
+    for p, piece in enumerate(pieces):
         panel_ref[p * bands : (p + 1) * bands] = piece[...]
 
 
@@ -375,7 +375,7 @@
         output_kernel,
         "output",
         (struct(whole, BF16), struct((total_bands, *quarter[1:]), BF16)),
-        (g, arrived, below, *reversed(panel)),
+        (g, arrived, below, *panel),
     )
     left = jnp.concatenate(mine, axis=0).reshape(total_bands, -1)
     right = jnp.concatenate([left, panels.reshape(total_bands, -1)], axis=0)

time: 42.8 us -> 43.2 us (level)
  no operation moved by 1% of the time
where the time goes in v13:
time: 43.2 us; the launch traced here: 43.1 us
  starting transfers between devices  12.5 us (29%)
  blocking collectives  11.4 us (26%)
  waiting for transfers between devices  9.98 us (23%)
  Pallas kernels  6.65 us (15%)
  local copies, waits for them, and re-layouts  1.32 us (3%)
  between operations  0.78 us (2%)
    all_to_all x1, blocking collectives, shards(): got = lax.all_to_all(pieces, ('space', 'band'), 0, 0)  11.4 us
    ppermute x6, starting transfers between devices, mirrored(): return lax.ppermute(value, axis, [(i, i ^ bits) for i in range(count)])  9.03 us
    pallas_call x10, Pallas kernels, call(): pl.pallas_call(kernel, out_shape=out_shape, compiler_params=params(vmem *...  6.65 us
    ppermute x3, waiting for transfers between devices, cyclic(): lax.ppermute(value, axis, [(i, (i + steps) % count) for i in range(count)])  5.75 us
    ppermute x6, waiting for transfers between devices, mirrored(): return lax.ppermute(value, axis, [(i, i ^ bits) for i in range(count)])  4.23 us
    ppermute x3, starting transfers between devices, cyclic(): lax.ppermute(value, axis, [(i, (i + steps) % count) for i in range(count)])  3.5 us
    unnamed x14, local copies, waits for them, and re-layouts  1.16 us
  transfers between devices with their start and end apart: 9, of which 4 were waited for; matrix products, arithmetic and copies ran while one was open for 0% of the time, Pallas kernels for 13%

profile of v13, /device:TPU:0, one launch (start us, length us, event | category | flops | bytes accessed | tf_op | source)
XLA Modules:
  0.0 43.1 jit_solution(5714456331314804873)
XLA Ops:
  0.6 0.0 copy-start
  0.6 1.1 %copy-done = f32[8,6,32,128]{3,2,1,0:T(8,128)S(1)} copy-done((f32[8,6,32,128]{3,2,1,0:T(8,128)S(1)}, f32[8,6,32,128]{3,2,1,0:T(8,128)}, u32[]{:S(2)}) %copy-start) | copy-done | bytes 786456
  1.8 0.0 copy-start.2
  1.8 0.0 copy-start.5
  1.8 0.0 copy-start.6
  1.8 3.4 %collective-permute-start = (bf16[8,192,128]{2,1,0:T(8,128)(2,1)S(1)}, bf16[8,192,128]{2,1,0:T(8,128)(2,1)S(1)}, u32[]{:S(2)}, u32[]{:S(2)}) collective-permute-start(bf16[8,192,128]{2,1,0:T(8,128)(2,1)S(1)} %cast.1.own_ref), channel_id=1, source_target_pairs={{0,28},{4,0},{8,4},{12,8},{16,12},{20,16},{24,20},{28,24},{1,29},{... | collective-permute-start | bytes 1179656 | tf_op jit(solution)/shard_map/ppermute | solution.py:274
  5.3 1.6 %collective-permute-start.1 = (bf16[8,48,128]{2,1,0:T(8,128)(2,1)S(1)}, bf16[8,48,128]{2,1,0:T(8,128)(2,1)S(1)}, u32[]{:S(2)}, u32[]{:S(2)}) collective-permute-start(bf16[8,48,128]{2,1,0:T(8,128)(2,1)S(1)} %get-tuple-element.26), channel_id=1, source_target_pairs={{0,1},{1,0},{2,3},{3,2},{4,5},{5,4},{6,7},{7,6},{8,9},{9,8},{10,11... | collective-permute-start | bytes 294920 | tf_op jit(solution)/shard_map/ppermute | solution.py:279
  6.9 2.5 %collective-permute-start.4 = (bf16[8,48,128]{2,1,0:T(8,128)(2,1)S(1)}, bf16[8,48,128]{2,1,0:T(8,128)(2,1)S(1)}, u32[]{:S(2)}, u32[]{:S(2)}) collective-permute-start(bf16[8,48,128]{2,1,0:T(8,128)(2,1)S(1)} %get-tuple-element.33), channel_id=1, source_target_pairs={{0,3},{1,2},{2,1},{3,0},{4,7},{5,6},{6,5},{7,4},{8,11},{9,10},{10,... | collective-permute-start | bytes 294920 | tf_op jit(solution)/shard_map/ppermute | solution.py:279
  9.4 0.1 collective-permute-start.5
  9.5 0.0 copy-done.2
  9.5 0.0 copy-done.5
  9.5 0.0 copy-done.6
  9.5 0.0 copy-start.1
  9.5 1.6 %prepare.1 = (bf16[6,576,256]{2,1,0:T(8,128)(2,1)S(1)}, bf16[5,576,256]{2,1,0:T(8,128)(2,1)S(1)}, f32[8,576]{1,0:T(8,128)S(1)}, f32[1,576]{1,0:T(1,128)S(1)}) custom-call(s32[32]{0:T(128)S(1)} %copy-done.6, f32[9,32]{1,0:T(8,128)S(1)} %bitcast.19, bf16[8,192,128]{2,1,0:T(8,128)(2,1)S(1)} %cast.1.own_ref, bf16[4,9,6,32,128]{4,3,2,1,0:T(8,128)(2,1)S(1)} %copy-done.2), custom_call_target="tpu_custom_call" | custom-call | flops 1000000000 | bytes 1048576 | tf_op jit(solution)/shard_map/prepare/pallas_call | solution.py:292
  11.1 0.0 collective-permute-done.1.refs_0_.rest_3_
  11.1 0.0 copy-done.1
  11.1 0.2 ahead.1
  11.3 0.1 collective-permute-start.3
  11.4 0.0 collective-permute-done.upper_ref
  11.4 0.0 copy-start.3
  11.4 0.0 copy-start.4
  11.4 1.3 %coefficients.1 = (bf16[128,576]{1,0:T(8,128)(2,1)S(1)}, bf16[8,160,128]{2,1,0:T(8,128)(2,1)S(1)}) custom-call(bf16[8,192,128]{2,1,0:T(8,128)(2,1)S(1)} %collective-permute-done.upper_ref, bf16[5,576,256]{2,1,0:T(8,128)(2,1)S(1)} %get-tuple-element.23.table_ref, f32[8,576]{1,0:T(8,128)S(1)} %get-tuple-element.24.e_ref, ...), custom_call_target="tpu_custom_call" | custom-call | flops 1000000000 | bytes 1048576 | tf_op jit(solution)/shard_map/coefficients/pallas_call | solution.py:292
  12.8 0.1 collective-permute-start.2
  12.9 0.0 copy-done.3
  12.9 0.0 copy-done.4
  12.9 1.6 %near_part.1.g_ref = f32[8,192,128]{2,1,0:T(8,128)S(1)} custom-call(f32[8,192,128]{2,1,0:T(8,128)S(1)} %bitcast.15, f32[8,192,128]{2,1,0:T(8,128)S(1)} %bitcast.17, f32[192,128]{1,0:T(8,128)S(1)} %bitcast.18, bf16[128,576]{1,0:T(8,128)(2,1)S(1)} %get-tuple-element.28.w_ref, bf16[8,192,128]{2,1,0:T(8,128)(2,1)S(1)} %collective-permute-done.upper_ref, ...), custom_call_target="tpu_custom_call" | custom-call | flops 20000000000 | bytes 4194304 | tf_op jit(solution)/shard_map/near_part/pallas_call | solution.py:292
  14.5 1.5 %collective-permute-done.3.below_ref = bf16[8,32,128]{2,1,0:T(8,128)(2,1)S(1)} collective-permute-done((bf16[8,32,128]{2,1,0:T(8,128)(2,1)S(1)}, bf16[8,32,128]{2,1,0:T(8,128)(2,1)S(1)}, u32[]{:S(2)}, u32[]{:S(2)}) %collective-permute-start.3) | collective-permute-done | bytes 65568 | tf_op jit(solution)/shard_map/ppermute | solution.py:274
  16.0 4.3 %collective-permute-done.2.arrived_ref = bf16[8,160,128]{2,1,0:T(8,128)(2,1)S(1)} collective-permute-done((bf16[8,160,128]{2,1,0:T(8,128)(2,1)S(1)}, bf16[8,160,128]{2,1,0:T(8,128)(2,1)S(1)}, u32[]{:S(2)}, u32[]{:S(2)}) %collective-permute-start.2) | collective-permute-done | bytes 327712 | tf_op jit(solution)/shard_map/ppermute | solution.py:274
  20.2 0.1 finish.1
  20.4 4.2 %collective-permute-start.6 = (bf16[8,48,128]{2,1,0:T(8,128)(2,1)S(1)}, bf16[8,48,128]{2,1,0:T(8,128)(2,1)S(1)}, u32[]{:S(2)}, u32[]{:S(2)}) collective-permute-start(bf16[8,48,128]{2,1,0:T(8,128)(2,1)S(1)} %get-tuple-element.37), channel_id=1, source_target_pairs={{0,3},{1,2},{2,1},{3,0},{4,7},{5,6},{6,5},{7,4},{8,11},{9,10},{10,... | collective-permute-start | bytes 294920 | tf_op jit(solution)/shard_map/ppermute | solution.py:279
  24.5 0.0 collective-permute-start.7
  24.5 0.6 %collective-permute-start.8 = (bf16[8,48,128]{2,1,0:T(8,128)(2,1)S(1)}, bf16[8,48,128]{2,1,0:T(8,128)(2,1)S(1)}, u32[]{:S(2)}, u32[]{:S(2)}) collective-permute-start(bf16[8,48,128]{2,1,0:T(8,128)(2,1)S(1)} %get-tuple-element.39), channel_id=1, source_target_pairs={{0,1},{1,0},{2,3},{3,2},{4,5},{5,4},{6,7},{7,6},{8,9},{9,8},{10,11... | collective-permute-start | bytes 294920 | tf_op jit(solution)/shard_map/ppermute | solution.py:279
  25.2 0.0 collective-permute-done.4.rest_1_
  25.2 0.0 collective-permute-done.5.rest_2_
  25.2 0.8 %output.1 = (bf16[8,192,128]{2,1,0:T(8,128)(2,1)}, bf16[32,48,128]{2,1,0:T(8,128)(2,1)S(1)}) custom-call(f32[8,192,128]{2,1,0:T(8,128)S(1)} %near_part.1.g_ref, bf16[8,160,128]{2,1,0:T(8,128)(2,1)S(1)} %collective-permute-done.2.arrived_ref, bf16[8,32,128]{2,1,0:T(8,128)(2,1)S(1)} %collective-permute-done.3.below_ref, ...), custom_call_target="tpu_custom_call" | custom-call | tf_op jit(solution)/shard_map/output/pallas_call | solution.py:292
  26.0 1.2 %collective-permute-done.6 = bf16[8,48,128]{2,1,0:T(8,128)(2,1)S(1)} collective-permute-done((bf16[8,48,128]{2,1,0:T(8,128)(2,1)S(1)}, bf16[8,48,128]{2,1,0:T(8,128)(2,1)S(1)}, u32[]{:S(2)}, u32[]{:S(2)}) %collective-permute-start.6) | collective-permute-done | bytes 98336 | tf_op jit(solution)/shard_map/ppermute | solution.py:279
  27.2 2.9 %collective-permute-done.7 = bf16[8,48,128]{2,1,0:T(8,128)(2,1)S(1)} collective-permute-done((bf16[8,48,128]{2,1,0:T(8,128)(2,1)S(1)}, bf16[8,48,128]{2,1,0:T(8,128)(2,1)S(1)}, u32[]{:S(2)}, u32[]{:S(2)}) %collective-permute-start.7) | collective-permute-done | bytes 98336 | tf_op jit(solution)/shard_map/ppermute | solution.py:279
  30.2 0.0 collective-permute-done.8
  30.2 0.1 pad_maximum_fusion
  30.3 0.2 copy_bitcast_fusion
  30.4 0.3 convolution_multiply_fusion.prod_ref
  30.7 0.2 split.1
  31.0 11.4 %all_to_all.5.got_ref = f32[32,1,64]{2,1,0:T(1,128)S(1)} all-to-all(f32[32,1,64]{2,1,0:T(1,128)S(1)} %split.1), channel_id=1, replica_groups=mesh['space'=8,'band'=4] {'space','band'}, dimensions={0} | all-to-all | bytes 16384 | tf_op jit(solution)/shard_map/all_to_all | solution.py:394
  42.4 0.7 %last_sum.1 = (f32[4,8]{1,0:T(4,128)}, f32[4,8]{1,0:T(4,128)}) custom-call(f32[32,1,64]{2,1,0:T(1,128)S(1)} %all_to_all.5.got_ref), custom_call_target="tpu_custom_call" | custom-call | tf_op jit(solution)/shard_map/last_sum/pallas_call | solution.py:292
  (2 shorter events, 0.1 us)
Async XLA Ops:
  0.6 1.1 %copy-start = (f32[8,6,32,128]{3,2,1,0:T(8,128)S(1)}, f32[8,6,32,128]{3,2,1,0:T(8,128)}, u32[]{:S(2)}) copy-start(f32[8,6,32,128]{3,2,1,0:T(8,128)} %param.6) | copy-start | bytes 2359300
  1.8 7.7 %copy-start.2 = (bf16[4,9,6,32,128]{4,3,2,1,0:T(8,128)(2,1)S(1)}, bf16[4,9,6,32,128]{4,3,2,1,0:T(8,128)(2,1)}, u32[]{:S(2)}) copy-start(bf16[4,9,6,32,128]{4,3,2,1,0:T(8,128)(2,1)} %proj_ref.1) | copy-start | bytes 5308420
  1.8 7.7 %copy-start.5 = (f32[32,9]{0,1:T(8,128)S(1)}, f32[32,9]{0,1:T(8,128)}, u32[]{:S(2)}) copy-start(f32[32,9]{0,1:T(8,128)} %param.10) | copy-start | bytes 3460
  1.8 7.7 %copy-start.6 = (s32[32]{0:T(128)S(1)}, s32[32]{0:T(128)}, u32[]{:S(2)}) copy-start(s32[32]{0:T(128)} %first_ref.1) | copy-start | bytes 388
  1.8 9.6 %collective-permute-start = (bf16[8,192,128]{2,1,0:T(8,128)(2,1)S(1)}, bf16[8,192,128]{2,1,0:T(8,128)(2,1)S(1)}, u32[]{:S(2)}, u32[]{:S(2)}) collective-permute-start(bf16[8,192,128]{2,1,0:T(8,128)(2,1)S(1)} %cast.1.own_ref), channel_id=1, source_target_pairs={{0,28},{4,0},{8,4},{12,8},{16,12},{20,16},{24,20},{28,24},{1,29},{... | collective-permute-start | bytes 1179656 | tf_op jit(solution)/shard_map/ppermute | solution.py:274
  5.3 5.9 %collective-permute-start.1 = (bf16[8,48,128]{2,1,0:T(8,128)(2,1)S(1)}, bf16[8,48,128]{2,1,0:T(8,128)(2,1)S(1)}, u32[]{:S(2)}, u32[]{:S(2)}) collective-permute-start(bf16[8,48,128]{2,1,0:T(8,128)(2,1)S(1)} %get-tuple-element.26), channel_id=1, source_target_pairs={{0,1},{1,0},{2,3},{3,2},{4,5},{5,4},{6,7},{7,6},{8,9},{9,8},{10,11... | collective-permute-start | bytes 294920 | tf_op jit(solution)/shard_map/ppermute | solution.py:279
  6.9 18.3 %collective-permute-start.4 = (bf16[8,48,128]{2,1,0:T(8,128)(2,1)S(1)}, bf16[8,48,128]{2,1,0:T(8,128)(2,1)S(1)}, u32[]{:S(2)}, u32[]{:S(2)}) collective-permute-start(bf16[8,48,128]{2,1,0:T(8,128)(2,1)S(1)} %get-tuple-element.33), channel_id=1, source_target_pairs={{0,3},{1,2},{2,1},{3,0},{4,7},{5,6},{6,5},{7,4},{8,11},{9,10},{10,... | collective-permute-start | bytes 294920 | tf_op jit(solution)/shard_map/ppermute | solution.py:279
  9.4 15.8 %collective-permute-start.5 = (bf16[8,48,128]{2,1,0:T(8,128)(2,1)S(1)}, bf16[8,48,128]{2,1,0:T(8,128)(2,1)S(1)}, u32[]{:S(2)}, u32[]{:S(2)}) collective-permute-start(bf16[8,48,128]{2,1,0:T(8,128)(2,1)S(1)} %get-tuple-element.34), channel_id=1, source_target_pairs={{0,2},{1,3},{2,0},{3,1},{4,6},{5,7},{6,4},{7,5},{8,10},{9,11},{10,... | collective-permute-start | bytes 294920 | tf_op jit(solution)/shard_map/ppermute | solution.py:279
  9.5 1.6 %copy-start.1 = (f32[8,6,32,128]{3,2,1,0:T(8,128)S(1)}, f32[8,6,32,128]{3,2,1,0:T(8,128)}, u32[]{:S(2)}) copy-start(f32[8,6,32,128]{3,2,1,0:T(8,128)} %param.6) | copy-start | bytes 2359300
  11.3 4.6 %collective-permute-start.3 = (bf16[8,32,128]{2,1,0:T(8,128)(2,1)S(1)}, bf16[8,32,128]{2,1,0:T(8,128)(2,1)S(1)}, u32[]{:S(2)}, u32[]{:S(2)}) collective-permute-start(bf16[8,32,128]{2,1,0:T(8,128)(2,1)S(1)} %get-tuple-element.31), channel_id=1, source_target_pairs={{0,4},{4,8},{8,12},{12,16},{16,20},{20,24},{24,28},{28,0},{1,5},{5... | collective-permute-start | bytes 196616 | tf_op jit(solution)/shard_map/ppermute | solution.py:274
  11.4 1.4 %copy-start.3 = (f32[8,6,32,128]{3,2,1,0:T(8,128)S(1)}, f32[8,6,32,128]{3,2,1,0:T(8,128)}, u32[]{:S(2)}) copy-start(f32[8,6,32,128]{3,2,1,0:T(8,128)} %param.7) | copy-start | bytes 2359300
  11.4 1.4 %copy-start.4 = (f32[6,32,128]{2,1,0:T(8,128)S(1)}, f32[6,32,128]{2,1,0:T(8,128)}, u32[]{:S(2)}) copy-start(f32[6,32,128]{2,1,0:T(8,128)} %param.8) | copy-start | bytes 294916
  12.8 7.5 %collective-permute-start.2 = (bf16[8,160,128]{2,1,0:T(8,128)(2,1)S(1)}, bf16[8,160,128]{2,1,0:T(8,128)(2,1)S(1)}, u32[]{:S(2)}, u32[]{:S(2)}) collective-permute-start(bf16[8,160,128]{2,1,0:T(8,128)(2,1)S(1)} %get-tuple-element.30), channel_id=1, source_target_pairs={{0,4},{4,8},{8,12},{12,16},{16,20},{20,24},{24,28},{28,0},{1,5},{5... | collective-permute-start | bytes 983048 | tf_op jit(solution)/shard_map/ppermute | solution.py:274
  20.4 6.9 %collective-permute-start.6 = (bf16[8,48,128]{2,1,0:T(8,128)(2,1)S(1)}, bf16[8,48,128]{2,1,0:T(8,128)(2,1)S(1)}, u32[]{:S(2)}, u32[]{:S(2)}) collective-permute-start(bf16[8,48,128]{2,1,0:T(8,128)(2,1)S(1)} %get-tuple-element.37), channel_id=1, source_target_pairs={{0,3},{1,2},{2,1},{3,0},{4,7},{5,6},{6,5},{7,4},{8,11},{9,10},{10,... | collective-permute-start | bytes 294920 | tf_op jit(solution)/shard_map/ppermute | solution.py:279
  24.5 5.6 %collective-permute-start.7 = (bf16[8,48,128]{2,1,0:T(8,128)(2,1)S(1)}, bf16[8,48,128]{2,1,0:T(8,128)(2,1)S(1)}, u32[]{:S(2)}, u32[]{:S(2)}) collective-permute-start(bf16[8,48,128]{2,1,0:T(8,128)(2,1)S(1)} %get-tuple-element.38), channel_id=1, source_target_pairs={{0,2},{1,3},{2,0},{3,1},{4,6},{5,7},{6,4},{7,5},{8,10},{9,11},{10,... | collective-permute-start | bytes 294920 | tf_op jit(solution)/shard_map/ppermute | solution.py:279
  24.5 5.7 %collective-permute-start.8 = (bf16[8,48,128]{2,1,0:T(8,128)(2,1)S(1)}, bf16[8,48,128]{2,1,0:T(8,128)(2,1)S(1)}, u32[]{:S(2)}, u32[]{:S(2)}) collective-permute-start(bf16[8,48,128]{2,1,0:T(8,128)(2,1)S(1)} %get-tuple-element.39), channel_id=1, source_target_pairs={{0,1},{1,0},{2,3},{3,2},{4,5},{5,4},{6,7},{7,6},{8,9},{9,8},{10,11... | collective-permute-start | bytes 294920 | tf_op jit(solution)/shard_map/ppermute | solution.py:279

commit v14 on v13

--- a/solution.py
+++ b/solution.py
@@ -67,8 +67,8 @@
         out[...] = ref[:, pl.ds(begin, rows), :].astype(out.dtype)
 
 
-def cast_kernel(psi_ref, half_ref):
-    half_ref[...] = psi_ref[...].astype(BF16)
+def cast_kernel(psi_ref, up_ref):
+    up_ref[...] = psi_ref[:, : up_ref.shape[1]].astype(BF16)
 
 
 def pieces_kernel(count, psi_ref, *outs):
@@ -159,8 +159,8 @@
     e_ref[...] = overlap(own_ref, planes, ny, near_ref)
 
 
-def ahead_kernel(planes, psi_ref, *refs):
-    ahead_ref, edge_ref = refs[-2:]
+def ahead_kernel(planes, psi_ref, half_ref, ahead_ref, edge_ref):
+    half_ref[...] = psi_ref[...].astype(BF16)
     ny = psi_ref.shape[1] // planes
     edge_ref[...] = psi_ref[:, plane_rows(planes - 1, ny)].astype(BF16)
     for x in range(planes - 1):
@@ -171,10 +171,10 @@
         ahead_ref[:, plane_rows(x, ny)] = total
 
 
-def coefficient_kernel(planes, upper_ref, table_ref, e_ref, s_ref, ahead_ref, w_ref, next_ref):
+def coefficient_kernel(upper_ref, table_ref, e_ref, s_ref, ahead_ref, w_ref, next_ref):
     bands, cells, nz = upper_ref.shape
-    ny = cells // planes
     reach = BOX - 1
+    ny = cells // reach
     e = e_ref[...] + overlap(upper_ref, reach, ny, table_ref)
     cols = e.shape[1]
     tiles = -(-cols // nz)
@@ -215,29 +215,29 @@
             for target in (x + m, x - m):
                 if 0 <= target < planes:
                     total = total + kinetic_weights[m] * psi_ref[:, plane_rows(target, ny)]
-                elif target >= planes:
+                elif planes <= target < planes + BOX - 1:
                     value = upper_ref[:, plane_rows(target - planes, ny)].astype(F32)
                     total = total + kinetic_weights[m] * value
         out_ref[:, here] = total
 
 
-def complete(g_ref, arrived_ref, below_ref, out_ref):
+def complete(g_ref, arrived_ref, below_ref, above_ref, out_ref):
     cut = arrived_ref.shape[1]
     out_ref[:, :cut] = (g_ref[:, :cut] + arrived_ref[...].astype(F32)).astype(out_ref.dtype)
-    edge = kinetic_weights[HALO] * below_ref[...].astype(F32)
+    edge = kinetic_weights[HALO] * (below_ref[...].astype(F32) + above_ref[...].astype(F32))
     out_ref[:, cut:] = (g_ref[:, cut:] + edge).astype(out_ref.dtype)
 
 
-def finish_kernel(count, g_ref, arrived_ref, below_ref, *rest):
+def finish_kernel(count, g_ref, arrived_ref, below_ref, above_ref, *rest):
     outs, total = rest[:-1], rest[-1]
-    complete(g_ref, arrived_ref, below_ref, total)
+    complete(g_ref, arrived_ref, below_ref, above_ref, total)
     rows = g_ref.shape[1] // count
     pieces_of(total, lax.axis_index("band"), count, rows, outs)
 
 
-def output_kernel(g_ref, arrived_ref, below_ref, *rest):
+def output_kernel(g_ref, arrived_ref, below_ref, above_ref, *rest):
     pieces, (out_ref, panel_ref) = rest[:-2], rest[-2:]
-    complete(g_ref, arrived_ref, below_ref, out_ref)
+    complete(g_ref, arrived_ref, below_ref, above_ref, out_ref)
     bands = g_ref.shape[0]
     for p, piece in enumerate(pieces):
         panel_ref[p * bands : (p + 1) * bands] = piece[...]
@@ -311,7 +311,7 @@
 
     most = (bands, (planes - 1) * ny, nz)
     plane = (bands, ny, nz)
-    half = call(cast_kernel, "cast", struct(whole, BF16), (psi,))
+    up = call(cast_kernel, "cast", struct(most, BF16), (psi,))
     panel = call(
         partial(pieces_kernel, n_band),
         "pieces",
@@ -319,8 +319,17 @@
         (psi,),
         cost_estimate=pl.CostEstimate(flops=10**9, bytes_accessed=2**20, transcendentals=0),
     )
-    upper = cyclic(half, "space", -1)
+    upper = cyclic(up, "space", -1)
     panel = exchanged(panel)
+    half, ahead, edge = call(
+        partial(ahead_kernel, planes),
+        "ahead",
+        (struct(whole, BF16), struct(most), struct(plane, BF16)),
+        (psi,),
+        cost_estimate=pl.CostEstimate(flops=10**9, bytes_accessed=2**20, transcendentals=0),
+    )
+    below = cyclic(edge, "space", 1)
+    above = cyclic(edge, "space", -1)
     atoms, npj = projectors.shape[:2]
     cols = atoms * npj * HALF
     tables, far_tables, e, s = call(
@@ -337,18 +346,8 @@
         out_specs=(vm,) * 4,
         cost_estimate=pl.CostEstimate(flops=10**9, bytes_accessed=2**20, transcendentals=0),
     )
-    ahead, edge = call(
-        partial(ahead_kernel, planes),
-        "ahead",
-        (struct(most), struct(plane, BF16)),
-        (psi, panel[3], s),
-        in_specs=[vm, anywhere, anywhere],
-        out_specs=(vm, vm),
-        cost_estimate=pl.CostEstimate(flops=10**9, bytes_accessed=2**20, transcendentals=0),
-    )
-    below = cyclic(edge, "space", 1)
     w, beyond = call(
-        partial(coefficient_kernel, planes),
+        coefficient_kernel,
         "coefficients",
         (struct((bands * HALF, cols), BF16), struct(most, BF16)),
         (upper, far_tables, e, s, ahead),
@@ -366,7 +365,7 @@
         partial(finish_kernel, n_band),
         "finish",
         (struct(quarter, BF16),) * n_band,
-        (g, arrived, below),
+        (g, arrived, below, above),
         scratch_shapes=[pltpu.VMEM(whole, F32)],
     )
     mine = exchanged(mine)
@@ -375,7 +374,7 @@
         output_kernel,
         "output",
         (struct(whole, BF16), struct((total_bands, *quarter[1:]), BF16)),
-        (g, arrived, below, *panel),
+        (g, arrived, below, above, *panel),
     )
     left = jnp.concatenate(mine, axis=0).reshape(total_bands, -1)
     right = jnp.concatenate([left, panels.reshape(total_bands, -1)], axis=0)

time: 43.2 us -> 45.3 us (1.049)
  starting transfers between devices: 12.5 us -> 15.1 us
  waiting for transfers between devices: 9.98 us -> 8.49 us
  blocking collectives: 11.4 us -> 12.5 us
    ppermute x3 -> x4, starting transfers between devices: 3.5 us -> 6.13 us  [cyclic(): lax.ppermute(value, axis, [(i, (i + steps) % count) for i in range(count)])]
    all_to_all x1, blocking collectives: 11.4 us -> 12.5 us  [shards(): got = lax.all_to_all(pieces, ('space', 'band'), 0, 0)]
    ppermute x6, waiting for transfers between devices: 4.23 us -> 3.44 us  [mirrored(): return lax.ppermute(value, axis, [(i, i ^ bits) for i in range(count)])]
    ppermute x3 -> x4, waiting for transfers between devices: 5.75 us -> 5.05 us  [cyclic(): lax.ppermute(value, axis, [(i, (i + steps) % count) for i in range(count)])]
  transfers between devices with their start and end apart: 9 -> 10, of which waited for: 4 -> 3; matrix products, arithmetic and copies ran while one was open for 0% -> 0% of each run, Pallas kernels for 13% -> 12%
where the time goes in v14:
time: 45.3 us; the launch traced here: 45.1 us
  starting transfers between devices  15.1 us (33%)
  blocking collectives  12.5 us (28%)
  waiting for transfers between devices  8.49 us (19%)
  Pallas kernels  6.52 us (14%)
  local copies, waits for them, and re-layouts  1.32 us (3%)
  between operations  0.81 us (2%)
    all_to_all x1, blocking collectives, shards(): got = lax.all_to_all(pieces, ('space', 'band'), 0, 0)  12.5 us
    ppermute x6, starting transfers between devices, mirrored(): return lax.ppermute(value, axis, [(i, i ^ bits) for i in range(count)])  8.96 us
    pallas_call x10, Pallas kernels, call(): pl.pallas_call(kernel, out_shape=out_shape, compiler_params=params(vmem *...  6.52 us
    ppermute x4, starting transfers between devices, cyclic(): lax.ppermute(value, axis, [(i, (i + steps) % count) for i in range(count)])  6.13 us
    ppermute x4, waiting for transfers between devices, cyclic(): lax.ppermute(value, axis, [(i, (i + steps) % count) for i in range(count)])  5.05 us
    ppermute x6, waiting for transfers between devices, mirrored(): return lax.ppermute(value, axis, [(i, i ^ bits) for i in range(count)])  3.44 us
    unnamed x14, local copies, waits for them, and re-layouts  1.17 us
  transfers between devices with their start and end apart: 10, of which 3 were waited for; matrix products, arithmetic and copies ran while one was open for 0% of the time, Pallas kernels for 12%

profile of v14, /device:TPU:0, one launch (start us, length us, event | category | flops | bytes accessed | tf_op | source)
XLA Modules:
  0.0 45.1 jit_solution(866771997080637602)
XLA Ops:
  0.6 0.0 copy-start
  0.6 1.1 %copy-done = f32[8,6,32,128]{3,2,1,0:T(8,128)S(1)} copy-done((f32[8,6,32,128]{3,2,1,0:T(8,128)S(1)}, f32[8,6,32,128]{3,2,1,0:T(8,128)}, u32[]{:S(2)}) %copy-start) | copy-done | bytes 786456
  1.8 3.4 %collective-permute-start = (bf16[8,160,128]{2,1,0:T(8,128)(2,1)S(1)}, bf16[8,160,128]{2,1,0:T(8,128)(2,1)S(1)}, u32[]{:S(2)}, u32[]{:S(2)}) collective-permute-start(bf16[8,160,128]{2,1,0:T(8,128)(2,1)S(1)} %cast.1), channel_id=1, source_target_pairs={{0,28},{4,0},{8,4},{12,8},{16,12},{20,16},{24,20},{28,24},{1,29},{... | collective-permute-start | bytes 983048 | tf_op jit(solution)/shard_map/ppermute | solution.py:274
  5.2 0.2 ahead.1
  5.4 0.0 copy-start.2
  5.4 0.0 copy-start.5
  5.4 0.0 copy-start.6
  5.4 0.1 collective-permute-start.2
  5.5 2.6 %collective-permute-start.3 = (bf16[8,32,128]{2,1,0:T(8,128)(2,1)S(1)}, bf16[8,32,128]{2,1,0:T(8,128)(2,1)S(1)}, u32[]{:S(2)}, u32[]{:S(2)}) collective-permute-start(bf16[8,32,128]{2,1,0:T(8,128)(2,1)S(1)} %get-tuple-element.32), channel_id=1, source_target_pairs={{0,28},{4,0},{8,4},{12,8},{16,12},{20,16},{24,20},{28,24},{1,29},{... | collective-permute-start | bytes 196616 | tf_op jit(solution)/shard_map/ppermute | solution.py:274
  8.2 3.7 %collective-permute-start.4 = (bf16[8,48,128]{2,1,0:T(8,128)(2,1)S(1)}, bf16[8,48,128]{2,1,0:T(8,128)(2,1)S(1)}, u32[]{:S(2)}, u32[]{:S(2)}) collective-permute-start(bf16[8,48,128]{2,1,0:T(8,128)(2,1)S(1)} %get-tuple-element.34), channel_id=1, source_target_pairs={{0,3},{1,2},{2,1},{3,0},{4,7},{5,6},{6,5},{7,4},{8,11},{9,10},{10,... | collective-permute-start | bytes 294920 | tf_op jit(solution)/shard_map/ppermute | solution.py:279
  11.8 0.0 collective-permute-start.5
  11.9 0.0 copy-done.2
  11.9 0.0 copy-done.5
  11.9 0.0 copy-done.6
  11.9 1.6 %prepare.1 = (bf16[6,576,256]{2,1,0:T(8,128)(2,1)S(1)}, bf16[5,576,256]{2,1,0:T(8,128)(2,1)S(1)}, f32[8,576]{1,0:T(8,128)S(1)}, f32[1,576]{1,0:T(1,128)S(1)}) custom-call(s32[32]{0:T(128)S(1)} %copy-done.6, f32[9,32]{1,0:T(8,128)S(1)} %bitcast.19, bf16[8,192,128]{2,1,0:T(8,128)(2,1)S(1)} %get-tuple-element.24.own_ref, bf16[4,9,6,32,128]{4,3,2,1,0:T(8,128)(2,1)S(1)} %copy-done.2), custom_call_target="tpu_custom_call" | custom-call | flops 1000000000 | bytes 1048576 | tf_op jit(solution)/shard_map/prepare/pallas_call | solution.py:292
  13.4 0.0 collective-permute-done.upper_ref
  13.4 0.0 copy-start.1
  13.5 0.0 copy-start.3
  13.5 0.0 copy-start.4
  13.5 1.3 %coefficients.1 = (bf16[128,576]{1,0:T(8,128)(2,1)S(1)}, bf16[8,160,128]{2,1,0:T(8,128)(2,1)S(1)}) custom-call(bf16[8,160,128]{2,1,0:T(8,128)(2,1)S(1)} %collective-permute-done.upper_ref, bf16[5,576,256]{2,1,0:T(8,128)(2,1)S(1)} %get-tuple-element.25.table_ref, f32[8,576]{1,0:T(8,128)S(1)} %get-tuple-element.26.e_ref, ...), custom_call_target="tpu_custom_call" | custom-call | flops 1000000000 | bytes 1048576 | tf_op jit(solution)/shard_map/coefficients/pallas_call | solution.py:292
  14.8 0.1 collective-permute-start.1
  14.9 0.0 copy-done.1
  14.9 0.0 copy-done.3
  14.9 0.0 copy-done.4
  14.9 1.5 %near_part.1.g_ref = f32[8,192,128]{2,1,0:T(8,128)S(1)} custom-call(f32[8,192,128]{2,1,0:T(8,128)S(1)} %bitcast.15, f32[8,192,128]{2,1,0:T(8,128)S(1)} %bitcast.17, f32[192,128]{1,0:T(8,128)S(1)} %bitcast.18, bf16[128,576]{1,0:T(8,128)(2,1)S(1)} %get-tuple-element.29.w_ref, bf16[8,160,128]{2,1,0:T(8,128)(2,1)S(1)} %collective-permute-done.upper_ref, ...), custom_call_target="tpu_custom_call" | custom-call | flops 20000000000 | bytes 4194304 | tf_op jit(solution)/shard_map/near_part/pallas_call | solution.py:292
  16.4 0.0 collective-permute-done.2.below_ref
  16.4 0.8 %collective-permute-start.6 = (bf16[8,48,128]{2,1,0:T(8,128)(2,1)S(1)}, bf16[8,48,128]{2,1,0:T(8,128)(2,1)S(1)}, u32[]{:S(2)}, u32[]{:S(2)}) collective-permute-start(bf16[8,48,128]{2,1,0:T(8,128)(2,1)S(1)} %get-tuple-element.36), channel_id=1, source_target_pairs={{0,1},{1,0},{2,3},{3,2},{4,5},{5,4},{6,7},{7,6},{8,9},{9,8},{10,11... | collective-permute-start | bytes 294920 | tf_op jit(solution)/shard_map/ppermute | solution.py:279
  17.2 0.0 collective-permute-done.3.above_ref
  17.2 5.0 %collective-permute-done.1.arrived_ref = bf16[8,160,128]{2,1,0:T(8,128)(2,1)S(1)} collective-permute-done((bf16[8,160,128]{2,1,0:T(8,128)(2,1)S(1)}, bf16[8,160,128]{2,1,0:T(8,128)(2,1)S(1)}, u32[]{:S(2)}, u32[]{:S(2)}) %collective-permute-start.1) | collective-permute-done | bytes 327712 | tf_op jit(solution)/shard_map/ppermute | solution.py:274
  22.3 0.1 finish.1
  22.4 2.0 %collective-permute-start.7 = (bf16[8,48,128]{2,1,0:T(8,128)(2,1)S(1)}, bf16[8,48,128]{2,1,0:T(8,128)(2,1)S(1)}, u32[]{:S(2)}, u32[]{:S(2)}) collective-permute-start(bf16[8,48,128]{2,1,0:T(8,128)(2,1)S(1)} %get-tuple-element.39), channel_id=1, source_target_pairs={{0,3},{1,2},{2,1},{3,0},{4,7},{5,6},{6,5},{7,4},{8,11},{9,10},{10,... | collective-permute-start | bytes 294920 | tf_op jit(solution)/shard_map/ppermute | solution.py:279
  24.4 1.1 %collective-permute-start.8 = (bf16[8,48,128]{2,1,0:T(8,128)(2,1)S(1)}, bf16[8,48,128]{2,1,0:T(8,128)(2,1)S(1)}, u32[]{:S(2)}, u32[]{:S(2)}) collective-permute-start(bf16[8,48,128]{2,1,0:T(8,128)(2,1)S(1)} %get-tuple-element.40), channel_id=1, source_target_pairs={{0,2},{1,3},{2,0},{3,1},{4,6},{5,7},{6,4},{7,5},{8,10},{9,11},{10,... | collective-permute-start | bytes 294920 | tf_op jit(solution)/shard_map/ppermute | solution.py:279
  25.5 0.0 collective-permute-done.4.rest_1_
  25.5 1.4 %collective-permute-start.9 = (bf16[8,48,128]{2,1,0:T(8,128)(2,1)S(1)}, bf16[8,48,128]{2,1,0:T(8,128)(2,1)S(1)}, u32[]{:S(2)}, u32[]{:S(2)}) collective-permute-start(bf16[8,48,128]{2,1,0:T(8,128)(2,1)S(1)} %get-tuple-element.41), channel_id=1, source_target_pairs={{0,1},{1,0},{2,3},{3,2},{4,5},{5,4},{6,7},{7,6},{8,9},{9,8},{10,11... | collective-permute-start | bytes 294920 | tf_op jit(solution)/shard_map/ppermute | solution.py:279
  26.9 0.0 collective-permute-done.5.rest_2_
  26.9 0.0 collective-permute-done.6.rest_3_
  26.9 0.8 %output.1 = (bf16[8,192,128]{2,1,0:T(8,128)(2,1)}, bf16[32,48,128]{2,1,0:T(8,128)(2,1)S(1)}) custom-call(f32[8,192,128]{2,1,0:T(8,128)S(1)} %near_part.1.g_ref, bf16[8,160,128]{2,1,0:T(8,128)(2,1)S(1)} %collective-permute-done.1.arrived_ref, bf16[8,32,128]{2,1,0:T(8,128)(2,1)S(1)} %collective-permute-done.2.below_ref, ...), custom_call_target="tpu_custom_call" | custom-call | tf_op jit(solution)/shard_map/output/pallas_call | solution.py:292
  27.7 1.3 %collective-permute-done.7 = bf16[8,48,128]{2,1,0:T(8,128)(2,1)S(1)} collective-permute-done((bf16[8,48,128]{2,1,0:T(8,128)(2,1)S(1)}, bf16[8,48,128]{2,1,0:T(8,128)(2,1)S(1)}, u32[]{:S(2)}, u32[]{:S(2)}) %collective-permute-start.7) | collective-permute-done | bytes 98336 | tf_op jit(solution)/shard_map/ppermute | solution.py:279
  29.0 2.1 %collective-permute-done.8 = bf16[8,48,128]{2,1,0:T(8,128)(2,1)S(1)} collective-permute-done((bf16[8,48,128]{2,1,0:T(8,128)(2,1)S(1)}, bf16[8,48,128]{2,1,0:T(8,128)(2,1)S(1)}, u32[]{:S(2)}, u32[]{:S(2)}) %collective-permute-start.8) | collective-permute-done | bytes 98336 | tf_op jit(solution)/shard_map/ppermute | solution.py:279
  31.2 0.0 collective-permute-done.9
  31.2 0.1 pad_maximum_fusion
  31.2 0.2 copy_bitcast_fusion
  31.4 0.3 convolution_multiply_fusion.prod_ref
  31.7 0.2 split.1
  31.9 12.5 %all_to_all.5.got_ref = f32[32,1,64]{2,1,0:T(1,128)S(1)} all-to-all(f32[32,1,64]{2,1,0:T(1,128)S(1)} %split.1), channel_id=1, replica_groups=mesh['space'=8,'band'=4] {'space','band'}, dimensions={0} | all-to-all | bytes 16384 | tf_op jit(solution)/shard_map/all_to_all | solution.py:393
  44.4 0.7 %last_sum.1 = (f32[4,8]{1,0:T(4,128)}, f32[4,8]{1,0:T(4,128)}) custom-call(f32[32,1,64]{2,1,0:T(1,128)S(1)} %all_to_all.5.got_ref), custom_call_target="tpu_custom_call" | custom-call | tf_op jit(solution)/shard_map/last_sum/pallas_call | solution.py:292
  (2 shorter events, 0.1 us)
Async XLA Ops:
  0.6 1.1 %copy-start = (f32[8,6,32,128]{3,2,1,0:T(8,128)S(1)}, f32[8,6,32,128]{3,2,1,0:T(8,128)}, u32[]{:S(2)}) copy-start(f32[8,6,32,128]{3,2,1,0:T(8,128)} %param.6) | copy-start | bytes 2359300
  1.8 11.6 %collective-permute-start = (bf16[8,160,128]{2,1,0:T(8,128)(2,1)S(1)}, bf16[8,160,128]{2,1,0:T(8,128)(2,1)S(1)}, u32[]{:S(2)}, u32[]{:S(2)}) collective-permute-start(bf16[8,160,128]{2,1,0:T(8,128)(2,1)S(1)} %cast.1), channel_id=1, source_target_pairs={{0,28},{4,0},{8,4},{12,8},{16,12},{20,16},{24,20},{28,24},{1,29},{... | collective-permute-start | bytes 983048 | tf_op jit(solution)/shard_map/ppermute | solution.py:274
  5.4 6.5 %copy-start.2 = (bf16[4,9,6,32,128]{4,3,2,1,0:T(8,128)(2,1)S(1)}, bf16[4,9,6,32,128]{4,3,2,1,0:T(8,128)(2,1)}, u32[]{:S(2)}) copy-start(bf16[4,9,6,32,128]{4,3,2,1,0:T(8,128)(2,1)} %proj_ref.1) | copy-start | bytes 5308420
  5.4 6.4 %copy-start.5 = (f32[32,9]{0,1:T(8,128)S(1)}, f32[32,9]{0,1:T(8,128)}, u32[]{:S(2)}) copy-start(f32[32,9]{0,1:T(8,128)} %param.10) | copy-start | bytes 3460
  5.4 6.4 %copy-start.6 = (s32[32]{0:T(128)S(1)}, s32[32]{0:T(128)}, u32[]{:S(2)}) copy-start(s32[32]{0:T(128)} %first_ref.1) | copy-start | bytes 388
  5.4 11.0 %collective-permute-start.2 = (bf16[8,32,128]{2,1,0:T(8,128)(2,1)S(1)}, bf16[8,32,128]{2,1,0:T(8,128)(2,1)S(1)}, u32[]{:S(2)}, u32[]{:S(2)}) collective-permute-start(bf16[8,32,128]{2,1,0:T(8,128)(2,1)S(1)} %get-tuple-element.32), channel_id=1, source_target_pairs={{0,4},{4,8},{8,12},{12,16},{16,20},{20,24},{24,28},{28,0},{1,5},{5... | collective-permute-start | bytes 196616 | tf_op jit(solution)/shard_map/ppermute | solution.py:274
  5.5 11.7 %collective-permute-start.3 = (bf16[8,32,128]{2,1,0:T(8,128)(2,1)S(1)}, bf16[8,32,128]{2,1,0:T(8,128)(2,1)S(1)}, u32[]{:S(2)}, u32[]{:S(2)}) collective-permute-start(bf16[8,32,128]{2,1,0:T(8,128)(2,1)S(1)} %get-tuple-element.32), channel_id=1, source_target_pairs={{0,28},{4,0},{8,4},{12,8},{16,12},{20,16},{24,20},{28,24},{1,29},{... | collective-permute-start | bytes 196616 | tf_op jit(solution)/shard_map/ppermute | solution.py:274
  8.2 17.3 %collective-permute-start.4 = (bf16[8,48,128]{2,1,0:T(8,128)(2,1)S(1)}, bf16[8,48,128]{2,1,0:T(8,128)(2,1)S(1)}, u32[]{:S(2)}, u32[]{:S(2)}) collective-permute-start(bf16[8,48,128]{2,1,0:T(8,128)(2,1)S(1)} %get-tuple-element.34), channel_id=1, source_target_pairs={{0,3},{1,2},{2,1},{3,0},{4,7},{5,6},{6,5},{7,4},{8,11},{9,10},{10,... | collective-permute-start | bytes 294920 | tf_op jit(solution)/shard_map/ppermute | solution.py:279
  11.8 15.0 %collective-permute-start.5 = (bf16[8,48,128]{2,1,0:T(8,128)(2,1)S(1)}, bf16[8,48,128]{2,1,0:T(8,128)(2,1)S(1)}, u32[]{:S(2)}, u32[]{:S(2)}) collective-permute-start(bf16[8,48,128]{2,1,0:T(8,128)(2,1)S(1)} %get-tuple-element.35), channel_id=1, source_target_pairs={{0,2},{1,3},{2,0},{3,1},{4,6},{5,7},{6,4},{7,5},{8,10},{9,11},{10,... | collective-permute-start | bytes 294920 | tf_op jit(solution)/shard_map/ppermute | solution.py:279
  13.4 1.5 %copy-start.1 = (f32[8,6,32,128]{3,2,1,0:T(8,128)S(1)}, f32[8,6,32,128]{3,2,1,0:T(8,128)}, u32[]{:S(2)}) copy-start(f32[8,6,32,128]{3,2,1,0:T(8,128)} %param.6) | copy-start | bytes 2359300
  13.5 1.5 %copy-start.3 = (f32[8,6,32,128]{3,2,1,0:T(8,128)S(1)}, f32[8,6,32,128]{3,2,1,0:T(8,128)}, u32[]{:S(2)}) copy-start(f32[8,6,32,128]{3,2,1,0:T(8,128)} %param.7) | copy-start | bytes 2359300
  13.5 1.5 %copy-start.4 = (f32[6,32,128]{2,1,0:T(8,128)S(1)}, f32[6,32,128]{2,1,0:T(8,128)}, u32[]{:S(2)}) copy-start(f32[6,32,128]{2,1,0:T(8,128)} %param.8) | copy-start | bytes 294916
  14.8 7.5 %collective-permute-start.1 = (bf16[8,160,128]{2,1,0:T(8,128)(2,1)S(1)}, bf16[8,160,128]{2,1,0:T(8,128)(2,1)S(1)}, u32[]{:S(2)}, u32[]{:S(2)}) collective-permute-start(bf16[8,160,128]{2,1,0:T(8,128)(2,1)S(1)} %get-tuple-element.31), channel_id=1, source_target_pairs={{0,4},{4,8},{8,12},{12,16},{16,20},{20,24},{24,28},{28,0},{1,5},{5... | collective-permute-start | bytes 983048 | tf_op jit(solution)/shard_map/ppermute | solution.py:274
  16.4 10.5 %collective-permute-start.6 = (bf16[8,48,128]{2,1,0:T(8,128)(2,1)S(1)}, bf16[8,48,128]{2,1,0:T(8,128)(2,1)S(1)}, u32[]{:S(2)}, u32[]{:S(2)}) collective-permute-start(bf16[8,48,128]{2,1,0:T(8,128)(2,1)S(1)} %get-tuple-element.36), channel_id=1, source_target_pairs={{0,1},{1,0},{2,3},{3,2},{4,5},{5,4},{6,7},{7,6},{8,9},{9,8},{10,11... | collective-permute-start | bytes 294920 | tf_op jit(solution)/shard_map/ppermute | solution.py:279
  22.4 6.6 %collective-permute-start.7 = (bf16[8,48,128]{2,1,0:T(8,128)(2,1)S(1)}, bf16[8,48,128]{2,1,0:T(8,128)(2,1)S(1)}, u32[]{:S(2)}, u32[]{:S(2)}) collective-permute-start(bf16[8,48,128]{2,1,0:T(8,128)(2,1)S(1)} %get-tuple-element.39), channel_id=1, source_target_pairs={{0,3},{1,2},{2,1},{3,0},{4,7},{5,6},{6,5},{7,4},{8,11},{9,10},{10,... | collective-permute-start | bytes 294920 | tf_op jit(solution)/shard_map/ppermute | solution.py:279
  24.4 6.8 %collective-permute-start.8 = (bf16[8,48,128]{2,1,0:T(8,128)(2,1)S(1)}, bf16[8,48,128]{2,1,0:T(8,128)(2,1)S(1)}, u32[]{:S(2)}, u32[]{:S(2)}) collective-permute-start(bf16[8,48,128]{2,1,0:T(8,128)(2,1)S(1)} %get-tuple-element.40), channel_id=1, source_target_pairs={{0,2},{1,3},{2,0},{3,1},{4,6},{5,7},{6,4},{7,5},{8,10},{9,11},{10,... | collective-permute-start | bytes 294920 | tf_op jit(solution)/shard_map/ppermute | solution.py:279
  25.5 5.7 %collective-permute-start.9 = (bf16[8,48,128]{2,1,0:T(8,128)(2,1)S(1)}, bf16[8,48,128]{2,1,0:T(8,128)(2,1)S(1)}, u32[]{:S(2)}, u32[]{:S(2)}) collective-permute-start(bf16[8,48,128]{2,1,0:T(8,128)(2,1)S(1)} %get-tuple-element.41), channel_id=1, source_target_pairs={{0,1},{1,0},{2,3},{3,2},{4,5},{5,4},{6,7},{7,6},{8,9},{9,8},{10,11... | collective-permute-start | bytes 294920 | tf_op jit(solution)/shard_map/ppermute | solution.py:279

commit v15 on v13

--- a/solution.py
+++ b/solution.py
@@ -159,8 +159,7 @@
     e_ref[...] = overlap(own_ref, planes, ny, near_ref)
 
 
-def ahead_kernel(planes, psi_ref, *refs):
-    ahead_ref, edge_ref = refs[-2:]
+def ahead_kernel(planes, psi_ref, ahead_ref, edge_ref):
     ny = psi_ref.shape[1] // planes
     edge_ref[...] = psi_ref[:, plane_rows(planes - 1, ny)].astype(BF16)
     for x in range(planes - 1):
@@ -235,11 +234,15 @@
     pieces_of(total, lax.axis_index("band"), count, rows, outs)
 
 
+def panel_order(count):
+    return [count - 1, *range(1, count - 1), 0]
+
+
 def output_kernel(g_ref, arrived_ref, below_ref, *rest):
     pieces, (out_ref, panel_ref) = rest[:-2], rest[-2:]
     complete(g_ref, arrived_ref, below_ref, out_ref)
     bands = g_ref.shape[0]
-    for p, piece in enumerate(pieces):
+    for p, piece in zip(panel_order(len(pieces)), pieces):
         panel_ref[p * bands : (p + 1) * bands] = piece[...]
 
 
@@ -321,6 +324,14 @@
     )
     upper = cyclic(half, "space", -1)
     panel = exchanged(panel)
+    ahead, edge = call(
+        partial(ahead_kernel, planes),
+        "ahead",
+        (struct(most), struct(plane, BF16)),
+        (psi,),
+        cost_estimate=pl.CostEstimate(flops=10**9, bytes_accessed=2**20, transcendentals=0),
+    )
+    below = cyclic(edge, "space", 1)
     atoms, npj = projectors.shape[:2]
     cols = atoms * npj * HALF
     tables, far_tables, e, s = call(
@@ -337,16 +348,6 @@
         out_specs=(vm,) * 4,
         cost_estimate=pl.CostEstimate(flops=10**9, bytes_accessed=2**20, transcendentals=0),
     )
-    ahead, edge = call(
-        partial(ahead_kernel, planes),
-        "ahead",
-        (struct(most), struct(plane, BF16)),
-        (psi, panel[3], s),
-        in_specs=[vm, anywhere, anywhere],
-        out_specs=(vm, vm),
-        cost_estimate=pl.CostEstimate(flops=10**9, bytes_accessed=2**20, transcendentals=0),
-    )
-    below = cyclic(edge, "space", 1)
     w, beyond = call(
         partial(coefficient_kernel, planes),
         "coefficients",
@@ -375,7 +376,7 @@
         output_kernel,
         "output",
         (struct(whole, BF16), struct((total_bands, *quarter[1:]), BF16)),
-        (g, arrived, below, *panel),
+        (g, arrived, below, *[panel[p] for p in panel_order(n_band)]),
     )
     left = jnp.concatenate(mine, axis=0).reshape(total_bands, -1)
     right = jnp.concatenate([left, panels.reshape(total_bands, -1)], axis=0)

time: 43.2 us -> 43.2 us (level)
  transfers between devices with their start and end apart: 9 -> 9, of which waited for: 4 -> 3; matrix products, arithmetic and copies ran while one was open for 0% -> 0% of each run, Pallas kernels for 13% -> 13%
where the time goes in v15:
time: 43.2 us; the launch traced here: 43 us
  starting transfers between devices  12.2 us (28%)
  blocking collectives  11.8 us (27%)
  waiting for transfers between devices  9.99 us (23%)
  Pallas kernels  6.57 us (15%)
  local copies, waits for them, and re-layouts  1.32 us (3%)
  between operations  0.8 us (2%)
    all_to_all x1, blocking collectives, shards(): got = lax.all_to_all(pieces, ('space', 'band'), 0, 0)  11.8 us
    ppermute x6, starting transfers between devices, mirrored(): return lax.ppermute(value, axis, [(i, i ^ bits) for i in range(count)])  8.69 us
    pallas_call x10, Pallas kernels, call(): pl.pallas_call(kernel, out_shape=out_shape, compiler_params=params(vmem *...  6.57 us
    ppermute x3, waiting for transfers between devices, cyclic(): lax.ppermute(value, axis, [(i, (i + steps) % count) for i in range(count)])  5.83 us
    ppermute x6, waiting for transfers between devices, mirrored(): return lax.ppermute(value, axis, [(i, i ^ bits) for i in range(count)])  4.16 us
    ppermute x3, starting transfers between devices, cyclic(): lax.ppermute(value, axis, [(i, (i + steps) % count) for i in range(count)])  3.5 us
    unnamed x14, local copies, waits for them, and re-layouts  1.17 us
  transfers between devices with their start and end apart: 9, of which 3 were waited for; matrix products, arithmetic and copies ran while one was open for 0% of the time, Pallas kernels for 13%

profile of v15, /device:TPU:0, one launch (start us, length us, event | category | flops | bytes accessed | tf_op | source)
XLA Modules:
  0.0 43.0 jit_solution(15986624229868276349)
XLA Ops:
  0.6 0.0 copy-start
  0.6 1.1 %copy-done = f32[8,6,32,128]{3,2,1,0:T(8,128)S(1)} copy-done((f32[8,6,32,128]{3,2,1,0:T(8,128)S(1)}, f32[8,6,32,128]{3,2,1,0:T(8,128)}, u32[]{:S(2)}) %copy-start) | copy-done | bytes 786456
  1.8 3.4 %collective-permute-start = (bf16[8,192,128]{2,1,0:T(8,128)(2,1)S(1)}, bf16[8,192,128]{2,1,0:T(8,128)(2,1)S(1)}, u32[]{:S(2)}, u32[]{:S(2)}) collective-permute-start(bf16[8,192,128]{2,1,0:T(8,128)(2,1)S(1)} %cast.1.own_ref), channel_id=1, source_target_pairs={{0,28},{4,0},{8,4},{12,8},{16,12},{20,16},{24,20},{28,24},{1,29},{... | collective-permute-start | bytes 1179656 | tf_op jit(solution)/shard_map/ppermute | solution.py:277
  5.2 0.2 ahead.1
  5.4 0.0 copy-start.2
  5.4 0.0 copy-start.5
  5.4 0.0 copy-start.6
  5.4 0.1 collective-permute-start.2
  5.5 0.1 pieces.1
  5.5 1.6 %collective-permute-start.3 = (bf16[8,48,128]{2,1,0:T(8,128)(2,1)S(1)}, bf16[8,48,128]{2,1,0:T(8,128)(2,1)S(1)}, u32[]{:S(2)}, u32[]{:S(2)}) collective-permute-start(bf16[8,48,128]{2,1,0:T(8,128)(2,1)S(1)} %get-tuple-element.31), channel_id=1, source_target_pairs={{0,1},{1,0},{2,3},{3,2},{4,5},{5,4},{6,7},{7,6},{8,9},{9,8},{10,11... | collective-permute-start | bytes 294920 | tf_op jit(solution)/shard_map/ppermute | solution.py:282
  7.2 2.5 %collective-permute-start.4 = (bf16[8,48,128]{2,1,0:T(8,128)(2,1)S(1)}, bf16[8,48,128]{2,1,0:T(8,128)(2,1)S(1)}, u32[]{:S(2)}, u32[]{:S(2)}) collective-permute-start(bf16[8,48,128]{2,1,0:T(8,128)(2,1)S(1)} %get-tuple-element.32), channel_id=1, source_target_pairs={{0,3},{1,2},{2,1},{3,0},{4,7},{5,6},{6,5},{7,4},{8,11},{9,10},{10,... | collective-permute-start | bytes 294920 | tf_op jit(solution)/shard_map/ppermute | solution.py:282
  9.7 0.1 collective-permute-start.5
  9.8 0.0 copy-done.2
  9.8 0.0 copy-done.5
  9.8 0.0 copy-done.6
  9.8 1.6 %prepare.1 = (bf16[6,576,256]{2,1,0:T(8,128)(2,1)S(1)}, bf16[5,576,256]{2,1,0:T(8,128)(2,1)S(1)}, f32[8,576]{1,0:T(8,128)S(1)}, f32[1,576]{1,0:T(1,128)S(1)}) custom-call(s32[32]{0:T(128)S(1)} %copy-done.6, f32[9,32]{1,0:T(8,128)S(1)} %bitcast.19, bf16[8,192,128]{2,1,0:T(8,128)(2,1)S(1)} %cast.1.own_ref, bf16[4,9,6,32,128]{4,3,2,1,0:T(8,128)(2,1)S(1)} %copy-done.2), custom_call_target="tpu_custom_call" | custom-call | flops 1000000000 | bytes 1048576 | tf_op jit(solution)/shard_map/prepare/pallas_call | solution.py:295
  11.4 0.0 collective-permute-done.upper_ref
  11.4 0.0 copy-start.1
  11.4 0.0 copy-start.3
  11.4 0.0 copy-start.4
  11.4 1.4 %coefficients.1 = (bf16[128,576]{1,0:T(8,128)(2,1)S(1)}, bf16[8,160,128]{2,1,0:T(8,128)(2,1)S(1)}) custom-call(bf16[8,192,128]{2,1,0:T(8,128)(2,1)S(1)} %collective-permute-done.upper_ref, bf16[5,576,256]{2,1,0:T(8,128)(2,1)S(1)} %get-tuple-element.23.table_ref, f32[8,576]{1,0:T(8,128)S(1)} %get-tuple-element.24.e_ref, ...), custom_call_target="tpu_custom_call" | custom-call | flops 1000000000 | bytes 1048576 | tf_op jit(solution)/shard_map/coefficients/pallas_call | solution.py:295
  12.8 0.1 collective-permute-start.1
  12.8 0.0 copy-done.1
  12.8 0.0 copy-done.3
  12.9 0.0 copy-done.4
  12.9 1.5 %near_part.1.g_ref = f32[8,192,128]{2,1,0:T(8,128)S(1)} custom-call(f32[8,192,128]{2,1,0:T(8,128)S(1)} %bitcast.15, f32[8,192,128]{2,1,0:T(8,128)S(1)} %bitcast.17, f32[192,128]{1,0:T(8,128)S(1)} %bitcast.18, bf16[128,576]{1,0:T(8,128)(2,1)S(1)} %get-tuple-element.27.w_ref, bf16[8,192,128]{2,1,0:T(8,128)(2,1)S(1)} %collective-permute-done.upper_ref, ...), custom_call_target="tpu_custom_call" | custom-call | flops 20000000000 | bytes 4194304 | tf_op jit(solution)/shard_map/near_part/pallas_call | solution.py:295
  14.4 0.0 collective-permute-done.2.below_ref
  14.4 5.8 %collective-permute-done.1.arrived_ref = bf16[8,160,128]{2,1,0:T(8,128)(2,1)S(1)} collective-permute-done((bf16[8,160,128]{2,1,0:T(8,128)(2,1)S(1)}, bf16[8,160,128]{2,1,0:T(8,128)(2,1)S(1)}, u32[]{:S(2)}, u32[]{:S(2)}) %collective-permute-start.1) | collective-permute-done | bytes 327712 | tf_op jit(solution)/shard_map/ppermute | solution.py:277
  20.2 0.1 finish.1
  20.4 3.2 %collective-permute-start.6 = (bf16[8,48,128]{2,1,0:T(8,128)(2,1)S(1)}, bf16[8,48,128]{2,1,0:T(8,128)(2,1)S(1)}, u32[]{:S(2)}, u32[]{:S(2)}) collective-permute-start(bf16[8,48,128]{2,1,0:T(8,128)(2,1)S(1)} %get-tuple-element.37), channel_id=1, source_target_pairs={{0,3},{1,2},{2,1},{3,0},{4,7},{5,6},{6,5},{7,4},{8,11},{9,10},{10,... | collective-permute-start | bytes 294920 | tf_op jit(solution)/shard_map/ppermute | solution.py:282
  23.6 0.1 collective-permute-start.7
  23.7 0.0 collective-permute-done.3.rest_0_
  23.7 1.1 %collective-permute-start.8 = (bf16[8,48,128]{2,1,0:T(8,128)(2,1)S(1)}, bf16[8,48,128]{2,1,0:T(8,128)(2,1)S(1)}, u32[]{:S(2)}, u32[]{:S(2)}) collective-permute-start(bf16[8,48,128]{2,1,0:T(8,128)(2,1)S(1)} %get-tuple-element.39), channel_id=1, source_target_pairs={{0,1},{1,0},{2,3},{3,2},{4,5},{5,4},{6,7},{7,6},{8,9},{9,8},{10,11... | collective-permute-start | bytes 294920 | tf_op jit(solution)/shard_map/ppermute | solution.py:282
  24.8 0.0 collective-permute-done.4.rest_1_
  24.8 0.0 collective-permute-done.5.rest_2_
  24.8 0.8 %output.1 = (bf16[8,192,128]{2,1,0:T(8,128)(2,1)}, bf16[32,48,128]{2,1,0:T(8,128)(2,1)S(1)}) custom-call(f32[8,192,128]{2,1,0:T(8,128)S(1)} %near_part.1.g_ref, bf16[8,160,128]{2,1,0:T(8,128)(2,1)S(1)} %collective-permute-done.1.arrived_ref, bf16[8,32,128]{2,1,0:T(8,128)(2,1)S(1)} %collective-permute-done.2.below_ref, ...), custom_call_target="tpu_custom_call" | custom-call | tf_op jit(solution)/shard_map/output/pallas_call | solution.py:295
  25.7 1.5 %collective-permute-done.6 = bf16[8,48,128]{2,1,0:T(8,128)(2,1)S(1)} collective-permute-done((bf16[8,48,128]{2,1,0:T(8,128)(2,1)S(1)}, bf16[8,48,128]{2,1,0:T(8,128)(2,1)S(1)}, u32[]{:S(2)}, u32[]{:S(2)}) %collective-permute-start.6) | collective-permute-done | bytes 98336 | tf_op jit(solution)/shard_map/ppermute | solution.py:282
  27.2 2.6 %collective-permute-done.7 = bf16[8,48,128]{2,1,0:T(8,128)(2,1)S(1)} collective-permute-done((bf16[8,48,128]{2,1,0:T(8,128)(2,1)S(1)}, bf16[8,48,128]{2,1,0:T(8,128)(2,1)S(1)}, u32[]{:S(2)}, u32[]{:S(2)}) %collective-permute-start.7) | collective-permute-done | bytes 98336 | tf_op jit(solution)/shard_map/ppermute | solution.py:282
  29.8 0.0 collective-permute-done.8
  29.8 0.1 pad_maximum_fusion
  29.9 0.2 copy_bitcast_fusion
  30.0 0.3 convolution_multiply_fusion.prod_ref
  30.4 0.2 split.1
  30.6 11.8 %all_to_all.5.got_ref = f32[32,1,64]{2,1,0:T(1,128)S(1)} all-to-all(f32[32,1,64]{2,1,0:T(1,128)S(1)} %split.1), channel_id=1, replica_groups=mesh['space'=8,'band'=4] {'space','band'}, dimensions={0} | all-to-all | bytes 16384 | tf_op jit(solution)/shard_map/all_to_all | solution.py:395
  42.4 0.7 %last_sum.1 = (f32[4,8]{1,0:T(4,128)}, f32[4,8]{1,0:T(4,128)}) custom-call(f32[32,1,64]{2,1,0:T(1,128)S(1)} %all_to_all.5.got_ref), custom_call_target="tpu_custom_call" | custom-call | tf_op jit(solution)/shard_map/last_sum/pallas_call | solution.py:295
  (1 shorter events, 0.0 us)
Async XLA Ops:
  0.6 1.1 %copy-start = (f32[8,6,32,128]{3,2,1,0:T(8,128)S(1)}, f32[8,6,32,128]{3,2,1,0:T(8,128)}, u32[]{:S(2)}) copy-start(f32[8,6,32,128]{3,2,1,0:T(8,128)} %param.6) | copy-start | bytes 2359300
  1.8 9.6 %collective-permute-start = (bf16[8,192,128]{2,1,0:T(8,128)(2,1)S(1)}, bf16[8,192,128]{2,1,0:T(8,128)(2,1)S(1)}, u32[]{:S(2)}, u32[]{:S(2)}) collective-permute-start(bf16[8,192,128]{2,1,0:T(8,128)(2,1)S(1)} %cast.1.own_ref), channel_id=1, source_target_pairs={{0,28},{4,0},{8,4},{12,8},{16,12},{20,16},{24,20},{28,24},{1,29},{... | collective-permute-start | bytes 1179656 | tf_op jit(solution)/shard_map/ppermute | solution.py:277
  5.4 4.4 %copy-start.2 = (bf16[4,9,6,32,128]{4,3,2,1,0:T(8,128)(2,1)S(1)}, bf16[4,9,6,32,128]{4,3,2,1,0:T(8,128)(2,1)}, u32[]{:S(2)}) copy-start(bf16[4,9,6,32,128]{4,3,2,1,0:T(8,128)(2,1)} %proj_ref.1) | copy-start | bytes 5308420
  5.4 4.4 %copy-start.5 = (f32[32,9]{0,1:T(8,128)S(1)}, f32[32,9]{0,1:T(8,128)}, u32[]{:S(2)}) copy-start(f32[32,9]{0,1:T(8,128)} %param.10) | copy-start | bytes 3460
  5.4 4.4 %copy-start.6 = (s32[32]{0:T(128)S(1)}, s32[32]{0:T(128)}, u32[]{:S(2)}) copy-start(s32[32]{0:T(128)} %first_ref.1) | copy-start | bytes 388
  5.4 9.0 %collective-permute-start.2 = (bf16[8,32,128]{2,1,0:T(8,128)(2,1)S(1)}, bf16[8,32,128]{2,1,0:T(8,128)(2,1)S(1)}, u32[]{:S(2)}, u32[]{:S(2)}) collective-permute-start(bf16[8,32,128]{2,1,0:T(8,128)(2,1)S(1)} %get-tuple-element.30), channel_id=1, source_target_pairs={{0,4},{4,8},{8,12},{12,16},{16,20},{20,24},{24,28},{28,0},{1,5},{5... | collective-permute-start | bytes 196616 | tf_op jit(solution)/shard_map/ppermute | solution.py:277
  5.5 18.1 %collective-permute-start.3 = (bf16[8,48,128]{2,1,0:T(8,128)(2,1)S(1)}, bf16[8,48,128]{2,1,0:T(8,128)(2,1)S(1)}, u32[]{:S(2)}, u32[]{:S(2)}) collective-permute-start(bf16[8,48,128]{2,1,0:T(8,128)(2,1)S(1)} %get-tuple-element.31), channel_id=1, source_target_pairs={{0,1},{1,0},{2,3},{3,2},{4,5},{5,4},{6,7},{7,6},{8,9},{9,8},{10,11... | collective-permute-start | bytes 294920 | tf_op jit(solution)/shard_map/ppermute | solution.py:282
  7.2 17.6 %collective-permute-start.4 = (bf16[8,48,128]{2,1,0:T(8,128)(2,1)S(1)}, bf16[8,48,128]{2,1,0:T(8,128)(2,1)S(1)}, u32[]{:S(2)}, u32[]{:S(2)}) collective-permute-start(bf16[8,48,128]{2,1,0:T(8,128)(2,1)S(1)} %get-tuple-element.32), channel_id=1, source_target_pairs={{0,3},{1,2},{2,1},{3,0},{4,7},{5,6},{6,5},{7,4},{8,11},{9,10},{10,... | collective-permute-start | bytes 294920 | tf_op jit(solution)/shard_map/ppermute | solution.py:282
  9.7 15.2 %collective-permute-start.5 = (bf16[8,48,128]{2,1,0:T(8,128)(2,1)S(1)}, bf16[8,48,128]{2,1,0:T(8,128)(2,1)S(1)}, u32[]{:S(2)}, u32[]{:S(2)}) collective-permute-start(bf16[8,48,128]{2,1,0:T(8,128)(2,1)S(1)} %get-tuple-element.33), channel_id=1, source_target_pairs={{0,2},{1,3},{2,0},{3,1},{4,6},{5,7},{6,4},{7,5},{8,10},{9,11},{10,... | collective-permute-start | bytes 294920 | tf_op jit(solution)/shard_map/ppermute | solution.py:282
  11.4 1.5 %copy-start.1 = (f32[8,6,32,128]{3,2,1,0:T(8,128)S(1)}, f32[8,6,32,128]{3,2,1,0:T(8,128)}, u32[]{:S(2)}) copy-start(f32[8,6,32,128]{3,2,1,0:T(8,128)} %param.6) | copy-start | bytes 2359300
  11.4 1.5 %copy-start.3 = (f32[8,6,32,128]{3,2,1,0:T(8,128)S(1)}, f32[8,6,32,128]{3,2,1,0:T(8,128)}, u32[]{:S(2)}) copy-start(f32[8,6,32,128]{3,2,1,0:T(8,128)} %param.7) | copy-start | bytes 2359300
  11.4 1.5 %copy-start.4 = (f32[6,32,128]{2,1,0:T(8,128)S(1)}, f32[6,32,128]{2,1,0:T(8,128)}, u32[]{:S(2)}) copy-start(f32[6,32,128]{2,1,0:T(8,128)} %param.8) | copy-start | bytes 294916
  12.8 7.5 %collective-permute-start.1 = (bf16[8,160,128]{2,1,0:T(8,128)(2,1)S(1)}, bf16[8,160,128]{2,1,0:T(8,128)(2,1)S(1)}, u32[]{:S(2)}, u32[]{:S(2)}) collective-permute-start(bf16[8,160,128]{2,1,0:T(8,128)(2,1)S(1)} %get-tuple-element.29), channel_id=1, source_target_pairs={{0,4},{4,8},{8,12},{12,16},{16,20},{20,24},{24,28},{28,0},{1,5},{5... | collective-permute-start | bytes 983048 | tf_op jit(solution)/shard_map/ppermute | solution.py:277
  20.4 6.8 %collective-permute-start.6 = (bf16[8,48,128]{2,1,0:T(8,128)(2,1)S(1)}, bf16[8,48,128]{2,1,0:T(8,128)(2,1)S(1)}, u32[]{:S(2)}, u32[]{:S(2)}) collective-permute-start(bf16[8,48,128]{2,1,0:T(8,128)(2,1)S(1)} %get-tuple-element.37), channel_id=1, source_target_pairs={{0,3},{1,2},{2,1},{3,0},{4,7},{5,6},{6,5},{7,4},{8,11},{9,10},{10,... | collective-permute-start | bytes 294920 | tf_op jit(solution)/shard_map/ppermute | solution.py:282
  23.6 6.2 %collective-permute-start.7 = (bf16[8,48,128]{2,1,0:T(8,128)(2,1)S(1)}, bf16[8,48,128]{2,1,0:T(8,128)(2,1)S(1)}, u32[]{:S(2)}, u32[]{:S(2)}) collective-permute-start(bf16[8,48,128]{2,1,0:T(8,128)(2,1)S(1)} %get-tuple-element.38), channel_id=1, source_target_pairs={{0,2},{1,3},{2,0},{3,1},{4,6},{5,7},{6,4},{7,5},{8,10},{9,11},{10,... | collective-permute-start | bytes 294920 | tf_op jit(solution)/shard_map/ppermute | solution.py:282
  23.7 6.1 %collective-permute-start.8 = (bf16[8,48,128]{2,1,0:T(8,128)(2,1)S(1)}, bf16[8,48,128]{2,1,0:T(8,128)(2,1)S(1)}, u32[]{:S(2)}, u32[]{:S(2)}) collective-permute-start(bf16[8,48,128]{2,1,0:T(8,128)(2,1)S(1)} %get-tuple-element.39), channel_id=1, source_target_pairs={{0,1},{1,0},{2,3},{3,2},{4,5},{5,4},{6,7},{7,6},{8,9},{9,8},{10,11... | collective-permute-start | bytes 294920 | tf_op jit(solution)/shard_map/ppermute | solution.py:282

commit v16 on v15

--- a/solution.py
+++ b/solution.py
@@ -63,12 +63,20 @@
 def pieces_of(ref, index, count, rows, outs):
     for bits, out in zip(partners(count), outs):
         quarter = jnp.bitwise_xor(index, bits)
-        begin = pl.multiple_of(quarter * rows, 8)
+        begin = pl.multiple_of(quarter * rows, 16 if rows % 16 == 0 else 8)
         out[...] = ref[:, pl.ds(begin, rows), :].astype(out.dtype)
 
 
-def cast_kernel(psi_ref, half_ref):
-    half_ref[...] = psi_ref[...].astype(BF16)
+def cast_kernel(psi_hbm, half_ref, psi_ref, sems):
+    copies = [
+        pltpu.make_async_copy(psi_hbm.at[b], psi_ref.at[b], sems.at[b])
+        for b in range(psi_ref.shape[0])
+    ]
+    for copy in copies:
+        copy.start()
+    for b, copy in enumerate(copies):
+        copy.wait()
+        half_ref[b] = psi_ref[b].astype(BF16)
 
 
 def pieces_kernel(count, psi_ref, *outs):
@@ -159,10 +167,9 @@
     e_ref[...] = overlap(own_ref, planes, ny, near_ref)
 
 
-def ahead_kernel(planes, psi_ref, ahead_ref, edge_ref):
+def ahead_kernel(planes, psi_ref, ahead_ref):
     ny = psi_ref.shape[1] // planes
-    edge_ref[...] = psi_ref[:, plane_rows(planes - 1, ny)].astype(BF16)
-    for x in range(planes - 1):
+    for x in range(planes):
         total = None
         for m in range(x + 1, HALO + 1):
             term = kinetic_weights[m] * psi_ref[:, plane_rows(planes + x - m, ny)]
@@ -195,6 +202,8 @@
         here = plane_rows(q, ny)
         block = spread(weights, table_ref[q], nz) + ahead_ref[:, here]
         next_ref[:, here] = block.astype(BF16)
+    rest = slice(reach * ny, planes * ny)
+    next_ref[:, rest] = ahead_ref[:, rest].astype(BF16)
 
 
 def near_kernel(planes, psi_ref, prev_ref, pot_ref, w_ref, upper_ref, table_ref, out_ref):
@@ -220,29 +229,18 @@
         out_ref[:, here] = total
 
 
-def complete(g_ref, arrived_ref, below_ref, out_ref):
-    cut = arrived_ref.shape[1]
-    out_ref[:, :cut] = (g_ref[:, :cut] + arrived_ref[...].astype(F32)).astype(out_ref.dtype)
-    edge = kinetic_weights[HALO] * below_ref[...].astype(F32)
-    out_ref[:, cut:] = (g_ref[:, cut:] + edge).astype(out_ref.dtype)
-
-
-def finish_kernel(count, g_ref, arrived_ref, below_ref, *rest):
+def finish_kernel(count, g_ref, arrived_ref, *rest):
     outs, total = rest[:-1], rest[-1]
-    complete(g_ref, arrived_ref, below_ref, total)
+    total[...] = g_ref[...] + arrived_ref[...].astype(F32)
     rows = g_ref.shape[1] // count
     pieces_of(total, lax.axis_index("band"), count, rows, outs)
 
 
-def panel_order(count):
-    return [count - 1, *range(1, count - 1), 0]
-
-
-def output_kernel(g_ref, arrived_ref, below_ref, *rest):
+def output_kernel(g_ref, arrived_ref, *rest):
     pieces, (out_ref, panel_ref) = rest[:-2], rest[-2:]
-    complete(g_ref, arrived_ref, below_ref, out_ref)
+    out_ref[...] = (g_ref[...] + arrived_ref[...].astype(F32)).astype(BF16)
     bands = g_ref.shape[0]
-    for p, piece in zip(panel_order(len(pieces)), pieces):
+    for p, piece in enumerate(pieces):
         panel_ref[p * bands : (p + 1) * bands] = piece[...]
 
 
@@ -293,7 +291,7 @@
 
 def call(kernel, name, out_shape, args, vmem=48, **extra):
     return pl.pallas_call(
-        kernel, out_shape=out_shape, compiler_params=params(vmem * 2**20), name=name, **extra
+        kernel, out_shape=out_shape, compiler_params=params(int(vmem * 2**20)), name=name, **extra
     )(*args)
 
 
@@ -310,28 +308,33 @@
 
     vm = pl.BlockSpec(memory_space=pltpu.VMEM)
     sm = pl.BlockSpec(memory_space=pltpu.SMEM)
-    anywhere = pl.BlockSpec(memory_space=pl.ANY)
-
-    most = (bands, (planes - 1) * ny, nz)
-    plane = (bands, ny, nz)
-    half = call(cast_kernel, "cast", struct(whole, BF16), (psi,))
+
+    half = call(
+        cast_kernel,
+        "cast",
+        struct(whole, BF16),
+        (psi,),
+        vmem=53.2,
+        in_specs=[pl.BlockSpec(memory_space=pl.ANY)],
+        out_specs=vm,
+        scratch_shapes=[pltpu.VMEM(whole, F32), pltpu.SemaphoreType.DMA((bands,))],
+    )
     panel = call(
         partial(pieces_kernel, n_band),
         "pieces",
         (struct(quarter, BF16),) * n_band,
+        (half if quarter[1] % 16 == 0 else psi,),
+        cost_estimate=pl.CostEstimate(flops=10**9, bytes_accessed=2**20, transcendentals=0),
+    )
+    upper = cyclic(half, "space", -1)
+    panel = exchanged(panel)
+    ahead = call(
+        partial(ahead_kernel, planes),
+        "ahead",
+        struct(whole),
         (psi,),
         cost_estimate=pl.CostEstimate(flops=10**9, bytes_accessed=2**20, transcendentals=0),
     )
-    upper = cyclic(half, "space", -1)
-    panel = exchanged(panel)
-    ahead, edge = call(
-        partial(ahead_kernel, planes),
-        "ahead",
-        (struct(most), struct(plane, BF16)),
-        (psi,),
-        cost_estimate=pl.CostEstimate(flops=10**9, bytes_accessed=2**20, transcendentals=0),
-    )
-    below = cyclic(edge, "space", 1)
     atoms, npj = projectors.shape[:2]
     cols = atoms * npj * HALF
     tables, far_tables, e, s = call(
@@ -351,7 +354,7 @@
     w, beyond = call(
         partial(coefficient_kernel, planes),
         "coefficients",
-        (struct((bands * HALF, cols), BF16), struct(most, BF16)),
+        (struct((bands * HALF, cols), BF16), struct(whole, BF16)),
         (upper, far_tables, e, s, ahead),
         cost_estimate=pl.CostEstimate(flops=10**9, bytes_accessed=2**20, transcendentals=0),
     )
@@ -367,7 +370,7 @@
         partial(finish_kernel, n_band),
         "finish",
         (struct(quarter, BF16),) * n_band,
-        (g, arrived, below),
+        (g, arrived),
         scratch_shapes=[pltpu.VMEM(whole, F32)],
     )
     mine = exchanged(mine)
@@ -376,7 +379,7 @@
         output_kernel,
         "output",
         (struct(whole, BF16), struct((total_bands, *quarter[1:]), BF16)),
-        (g, arrived, below, *[panel[p] for p in panel_order(n_band)]),
+        (g, arrived, *panel),
     )
     left = jnp.concatenate(mine, axis=0).reshape(total_bands, -1)
     right = jnp.concatenate([left, panels.reshape(total_bands, -1)], axis=0)

time: 43.2 us -> 44.8 us (1.037)
  Pallas kernels: 6.57 us -> 7.95 us
  waiting for transfers between devices: 9.99 us -> 10.7 us
  local copies, waits for them, and re-layouts: 1.32 us -> 0.67 us
    pallas_call x10, Pallas kernels: 6.57 us -> 7.95 us  [call(): pl.pallas_call(kernel, out_shape=out_shape, compiler_params=params(int(vm...]
    unnamed x14 -> x12, local copies, waits for them, and re-layouts: 1.17 us -> 0.52 us
    ppermute x3 -> x2, waiting for transfers between devices: 5.83 us -> 6.41 us  [cyclic(): lax.ppermute(value, axis, [(i, (i + steps) % count) for i in range(count)])]
    ppermute x3 -> x2, starting transfers between devices: 3.5 us -> 3.44 us  [cyclic(): lax.ppermute(value, axis, [(i, (i + steps) % count) for i in range(count)])]
  transfers between devices with their start and end apart: 9 -> 8, of which waited for: 3 -> 3; matrix products, arithmetic and copies ran while one was open for 0% -> 0% of each run, Pallas kernels for 13% -> 13%
where the time goes in v16:
time: 44.8 us; the launch traced here: 44.6 us
  starting transfers between devices  12.3 us (27%)
  blocking collectives  11.8 us (26%)
  waiting for transfers between devices  10.7 us (24%)
  Pallas kernels  7.95 us (18%)
  between operations  0.76 us (2%)
  local copies, waits for them, and re-layouts  0.67 us (1%)
    all_to_all x1, blocking collectives, shards(): got = lax.all_to_all(pieces, ('space', 'band'), 0, 0)  11.8 us
    ppermute x6, starting transfers between devices, mirrored(): return lax.ppermute(value, axis, [(i, i ^ bits) for i in range(count)])  8.9 us
    pallas_call x10, Pallas kernels, call(): pl.pallas_call(kernel, out_shape=out_shape, compiler_params=params(int(vm...  7.95 us
    ppermute x2, waiting for transfers between devices, cyclic(): lax.ppermute(value, axis, [(i, (i + steps) % count) for i in range(count)])  6.41 us
    ppermute x6, waiting for transfers between devices, mirrored(): return lax.ppermute(value, axis, [(i, i ^ bits) for i in range(count)])  4.26 us
    ppermute x2, starting transfers between devices, cyclic(): lax.ppermute(value, axis, [(i, (i + steps) % count) for i in range(count)])  3.44 us
  transfers between devices with their start and end apart: 8, of which 3 were waited for; matrix products, arithmetic and copies ran while one was open for 0% of the time, Pallas kernels for 13%

profile of v16, /device:TPU:0, one launch (start us, length us, event | category | flops | bytes accessed | tf_op | source)
XLA Modules:
  0.0 44.6 jit_solution(13486403520151773476)
XLA Ops:
  0.6 1.3 %cast.1.own_ref.psi_ref = bf16[8,192,128]{2,1,0:T(8,128)(2,1)S(1)} custom-call(f32[8,192,128]{2,1,0:T(8,128)} %bitcast.12), custom_call_target="tpu_custom_call" | custom-call | tf_op jit(solution)/shard_map/cast/pallas_call | solution.py:293
  1.9 0.0 copy-start
  1.9 3.4 %collective-permute-start = (bf16[8,192,128]{2,1,0:T(8,128)(2,1)S(1)}, bf16[8,192,128]{2,1,0:T(8,128)(2,1)S(1)}, u32[]{:S(2)}, u32[]{:S(2)}) collective-permute-start(bf16[8,192,128]{2,1,0:T(8,128)(2,1)S(1)} %cast.1.own_ref.psi_ref), channel_id=1, source_target_pairs={{0,28},{4,0},{8,4},{12,8},{16,12},{20,16},{24,20},{28,24},{1,29},{... | collective-permute-start | bytes 1179656 | tf_op jit(solution)/shard_map/ppermute | solution.py:275
  5.4 3.7 %collective-permute-start.2 = (bf16[8,48,128]{2,1,0:T(8,128)(2,1)S(1)}, bf16[8,48,128]{2,1,0:T(8,128)(2,1)S(1)}, u32[]{:S(2)}, u32[]{:S(2)}) collective-permute-start(bf16[8,48,128]{2,1,0:T(8,128)(2,1)S(1)} %get-tuple-element.28), channel_id=1, source_target_pairs={{0,3},{1,2},{2,1},{3,0},{4,7},{5,6},{6,5},{7,4},{8,11},{9,10},{10,... | collective-permute-start | bytes 294920 | tf_op jit(solution)/shard_map/ppermute | solution.py:280
  9.0 0.0 collective-permute-start.3
  9.0 0.0 copy-start.1
  9.0 0.0 copy-start.4
  9.0 0.0 copy-start.5
  9.0 0.8 %collective-permute-start.4 = (bf16[8,48,128]{2,1,0:T(8,128)(2,1)S(1)}, bf16[8,48,128]{2,1,0:T(8,128)(2,1)S(1)}, u32[]{:S(2)}, u32[]{:S(2)}) collective-permute-start(bf16[8,48,128]{2,1,0:T(8,128)(2,1)S(1)} %get-tuple-element.30), channel_id=1, source_target_pairs={{0,1},{1,0},{2,3},{3,2},{4,5},{5,4},{6,7},{7,6},{8,9},{9,8},{10,11... | collective-permute-start | bytes 294920 | tf_op jit(solution)/shard_map/ppermute | solution.py:280
  9.8 0.0 copy-done
  9.8 0.2 ahead.1.ahead_ref
  10.0 0.5 %copy-done.1 = bf16[4,9,6,32,128]{4,3,2,1,0:T(8,128)(2,1)S(1)} copy-done((bf16[4,9,6,32,128]{4,3,2,1,0:T(8,128)(2,1)S(1)}, bf16[4,9,6,32,128]{4,3,2,1,0:T(8,128)(2,1)}, u32[]{:S(2)}) %copy-start.1) | copy-done | bytes 1769496
  10.5 0.0 copy-done.4
  10.5 0.0 copy-done.5
  10.5 1.6 %prepare.1 = (bf16[6,576,256]{2,1,0:T(8,128)(2,1)S(1)}, bf16[5,576,256]{2,1,0:T(8,128)(2,1)S(1)}, f32[8,576]{1,0:T(8,128)S(1)}, f32[1,576]{1,0:T(1,128)S(1)}) custom-call(s32[32]{0:T(128)S(1)} %copy-done.5, f32[9,32]{1,0:T(8,128)S(1)} %bitcast.18, bf16[8,192,128]{2,1,0:T(8,128)(2,1)S(1)} %cast.1.own_ref.psi_ref, bf16[4,9,6,32,128]{4,3,2,1,0:T(8,128)(2,1)S(1)} %copy-done.1), custom_call_target="tpu_custom_call" | custom-call | flops 1000000000 | bytes 1048576 | tf_op jit(solution)/shard_map/prepare/pallas_call | solution.py:293
  12.1 0.0 collective-permute-done.upper_ref
  12.1 0.0 copy-start.2
  12.1 0.0 copy-start.3
  12.1 1.4 %coefficients.1 = (bf16[128,576]{1,0:T(8,128)(2,1)S(1)}, bf16[8,192,128]{2,1,0:T(8,128)(2,1)S(1)}) custom-call(bf16[8,192,128]{2,1,0:T(8,128)(2,1)S(1)} %collective-permute-done.upper_ref, bf16[5,576,256]{2,1,0:T(8,128)(2,1)S(1)} %get-tuple-element.21.table_ref, f32[8,576]{1,0:T(8,128)S(1)} %get-tuple-element.22.e_ref, ...), custom_call_target="tpu_custom_call" | custom-call | flops 1000000000 | bytes 1048576 | tf_op jit(solution)/shard_map/coefficients/pallas_call | solution.py:293
  13.5 0.1 collective-permute-start.1
  13.5 0.0 copy-done.2
  13.6 0.0 copy-done.3
  13.6 1.7 %near_part.1.g_ref = f32[8,192,128]{2,1,0:T(8,128)S(1)} custom-call(f32[8,192,128]{2,1,0:T(8,128)S(1)} %bitcast.14, f32[8,192,128]{2,1,0:T(8,128)S(1)} %bitcast.16, f32[192,128]{1,0:T(8,128)S(1)} %bitcast.17, bf16[128,576]{1,0:T(8,128)(2,1)S(1)} %get-tuple-element.24.w_ref, bf16[8,192,128]{2,1,0:T(8,128)(2,1)S(1)} %collective-permute-done.upper_ref, ...), custom_call_target="tpu_custom_call" | custom-call | flops 20000000000 | bytes 4194304 | tf_op jit(solution)/shard_map/near_part/pallas_call | solution.py:293
  15.2 6.4 %collective-permute-done.1.arrived_ref = bf16[8,192,128]{2,1,0:T(8,128)(2,1)S(1)} collective-permute-done((bf16[8,192,128]{2,1,0:T(8,128)(2,1)S(1)}, bf16[8,192,128]{2,1,0:T(8,128)(2,1)S(1)}, u32[]{:S(2)}, u32[]{:S(2)}) %collective-permute-start.1) | collective-permute-done | bytes 393248 | tf_op jit(solution)/shard_map/ppermute | solution.py:275
  21.6 0.1 finish.1
  21.8 3.2 %collective-permute-start.5 = (bf16[8,48,128]{2,1,0:T(8,128)(2,1)S(1)}, bf16[8,48,128]{2,1,0:T(8,128)(2,1)S(1)}, u32[]{:S(2)}, u32[]{:S(2)}) collective-permute-start(bf16[8,48,128]{2,1,0:T(8,128)(2,1)S(1)} %get-tuple-element.33), channel_id=1, source_target_pairs={{0,3},{1,2},{2,1},{3,0},{4,7},{5,6},{6,5},{7,4},{8,11},{9,10},{10,... | collective-permute-start | bytes 294920 | tf_op jit(solution)/shard_map/ppermute | solution.py:280
  25.0 0.0 collective-permute-start.6
  25.0 0.0 collective-permute-done.2.rest_1_
  25.0 1.2 %collective-permute-start.7 = (bf16[8,48,128]{2,1,0:T(8,128)(2,1)S(1)}, bf16[8,48,128]{2,1,0:T(8,128)(2,1)S(1)}, u32[]{:S(2)}, u32[]{:S(2)}) collective-permute-start(bf16[8,48,128]{2,1,0:T(8,128)(2,1)S(1)} %get-tuple-element.35), channel_id=1, source_target_pairs={{0,1},{1,0},{2,3},{3,2},{4,5},{5,4},{6,7},{7,6},{8,9},{9,8},{10,11... | collective-permute-start | bytes 294920 | tf_op jit(solution)/shard_map/ppermute | solution.py:280
  26.2 0.0 collective-permute-done.3.rest_2_
  26.2 0.0 collective-permute-done.4.rest_3_
  26.2 0.8 %output.1 = (bf16[8,192,128]{2,1,0:T(8,128)(2,1)}, bf16[32,48,128]{2,1,0:T(8,128)(2,1)S(1)}) custom-call(f32[8,192,128]{2,1,0:T(8,128)S(1)} %near_part.1.g_ref, bf16[8,192,128]{2,1,0:T(8,128)(2,1)S(1)} %collective-permute-done.1.arrived_ref, bf16[8,48,128]{2,1,0:T(8,128)(2,1)S(1)} %get-tuple-element.27.rest_0_, ...), custom_call_target="tpu_custom_call" | custom-call | tf_op jit(solution)/shard_map/output/pallas_call | solution.py:293
  27.1 1.3 %collective-permute-done.5 = bf16[8,48,128]{2,1,0:T(8,128)(2,1)S(1)} collective-permute-done((bf16[8,48,128]{2,1,0:T(8,128)(2,1)S(1)}, bf16[8,48,128]{2,1,0:T(8,128)(2,1)S(1)}, u32[]{:S(2)}, u32[]{:S(2)}) %collective-permute-start.5) | collective-permute-done | bytes 98336 | tf_op jit(solution)/shard_map/ppermute | solution.py:280
  28.4 3.0 %collective-permute-done.6 = bf16[8,48,128]{2,1,0:T(8,128)(2,1)S(1)} collective-permute-done((bf16[8,48,128]{2,1,0:T(8,128)(2,1)S(1)}, bf16[8,48,128]{2,1,0:T(8,128)(2,1)S(1)}, u32[]{:S(2)}, u32[]{:S(2)}) %collective-permute-start.6) | collective-permute-done | bytes 98336 | tf_op jit(solution)/shard_map/ppermute | solution.py:280
  31.3 0.0 collective-permute-done.7
  31.3 0.1 pad_maximum_fusion
  31.4 0.2 copy_bitcast_fusion
  31.5 0.3 convolution_multiply_fusion.prod_ref
  31.9 0.2 split.1
  32.1 11.8 %all_to_all.5.got_ref = f32[32,1,64]{2,1,0:T(1,128)S(1)} all-to-all(f32[32,1,64]{2,1,0:T(1,128)S(1)} %split.1), channel_id=1, replica_groups=mesh['space'=8,'band'=4] {'space','band'}, dimensions={0} | all-to-all | bytes 16384 | tf_op jit(solution)/shard_map/all_to_all | solution.py:398
  43.9 0.7 %last_sum.1 = (f32[4,8]{1,0:T(4,128)}, f32[4,8]{1,0:T(4,128)}) custom-call(f32[32,1,64]{2,1,0:T(1,128)S(1)} %all_to_all.5.got_ref), custom_call_target="tpu_custom_call" | custom-call | tf_op jit(solution)/shard_map/last_sum/pallas_call | solution.py:293
  (1 shorter events, 0.0 us)
Async XLA Ops:
  1.9 7.9 %copy-start = (f32[8,6,32,128]{3,2,1,0:T(8,128)S(1)}, f32[8,6,32,128]{3,2,1,0:T(8,128)}, u32[]{:S(2)}) copy-start(f32[8,6,32,128]{3,2,1,0:T(8,128)} %param.6) | copy-start | bytes 2359300
  1.9 10.1 %collective-permute-start = (bf16[8,192,128]{2,1,0:T(8,128)(2,1)S(1)}, bf16[8,192,128]{2,1,0:T(8,128)(2,1)S(1)}, u32[]{:S(2)}, u32[]{:S(2)}) collective-permute-start(bf16[8,192,128]{2,1,0:T(8,128)(2,1)S(1)} %cast.1.own_ref.psi_ref), channel_id=1, source_target_pairs={{0,28},{4,0},{8,4},{12,8},{16,12},{20,16},{24,20},{28,24},{1,29},{... | collective-permute-start | bytes 1179656 | tf_op jit(solution)/shard_map/ppermute | solution.py:275
  5.4 19.6 %collective-permute-start.2 = (bf16[8,48,128]{2,1,0:T(8,128)(2,1)S(1)}, bf16[8,48,128]{2,1,0:T(8,128)(2,1)S(1)}, u32[]{:S(2)}, u32[]{:S(2)}) collective-permute-start(bf16[8,48,128]{2,1,0:T(8,128)(2,1)S(1)} %get-tuple-element.28), channel_id=1, source_target_pairs={{0,3},{1,2},{2,1},{3,0},{4,7},{5,6},{6,5},{7,4},{8,11},{9,10},{10,... | collective-permute-start | bytes 294920 | tf_op jit(solution)/shard_map/ppermute | solution.py:280
  9.0 17.2 %collective-permute-start.3 = (bf16[8,48,128]{2,1,0:T(8,128)(2,1)S(1)}, bf16[8,48,128]{2,1,0:T(8,128)(2,1)S(1)}, u32[]{:S(2)}, u32[]{:S(2)}) collective-permute-start(bf16[8,48,128]{2,1,0:T(8,128)(2,1)S(1)} %get-tuple-element.29), channel_id=1, source_target_pairs={{0,2},{1,3},{2,0},{3,1},{4,6},{5,7},{6,4},{7,5},{8,10},{9,11},{10,... | collective-permute-start | bytes 294920 | tf_op jit(solution)/shard_map/ppermute | solution.py:280
  9.0 1.5 %copy-start.1 = (bf16[4,9,6,32,128]{4,3,2,1,0:T(8,128)(2,1)S(1)}, bf16[4,9,6,32,128]{4,3,2,1,0:T(8,128)(2,1)}, u32[]{:S(2)}) copy-start(bf16[4,9,6,32,128]{4,3,2,1,0:T(8,128)(2,1)} %proj_ref.1) | copy-start | bytes 5308420
  9.0 1.5 %copy-start.4 = (f32[32,9]{0,1:T(8,128)S(1)}, f32[32,9]{0,1:T(8,128)}, u32[]{:S(2)}) copy-start(f32[32,9]{0,1:T(8,128)} %param.10) | copy-start | bytes 3460
  9.0 1.5 %copy-start.5 = (s32[32]{0:T(128)S(1)}, s32[32]{0:T(128)}, u32[]{:S(2)}) copy-start(s32[32]{0:T(128)} %first_ref.1) | copy-start | bytes 388
  9.0 17.2 %collective-permute-start.4 = (bf16[8,48,128]{2,1,0:T(8,128)(2,1)S(1)}, bf16[8,48,128]{2,1,0:T(8,128)(2,1)S(1)}, u32[]{:S(2)}, u32[]{:S(2)}) collective-permute-start(bf16[8,48,128]{2,1,0:T(8,128)(2,1)S(1)} %get-tuple-element.30), channel_id=1, source_target_pairs={{0,1},{1,0},{2,3},{3,2},{4,5},{5,4},{6,7},{7,6},{8,9},{9,8},{10,11... | collective-permute-start | bytes 294920 | tf_op jit(solution)/shard_map/ppermute | solution.py:280
  12.1 1.5 %copy-start.2 = (f32[8,6,32,128]{3,2,1,0:T(8,128)S(1)}, f32[8,6,32,128]{3,2,1,0:T(8,128)}, u32[]{:S(2)}) copy-start(f32[8,6,32,128]{3,2,1,0:T(8,128)} %param.7) | copy-start | bytes 2359300
  12.1 1.5 %copy-start.3 = (f32[6,32,128]{2,1,0:T(8,128)S(1)}, f32[6,32,128]{2,1,0:T(8,128)}, u32[]{:S(2)}) copy-start(f32[6,32,128]{2,1,0:T(8,128)} %param.8) | copy-start | bytes 294916
  13.5 8.2 %collective-permute-start.1 = (bf16[8,192,128]{2,1,0:T(8,128)(2,1)S(1)}, bf16[8,192,128]{2,1,0:T(8,128)(2,1)S(1)}, u32[]{:S(2)}, u32[]{:S(2)}) collective-permute-start(bf16[8,192,128]{2,1,0:T(8,128)(2,1)S(1)} %get-tuple-element.26), channel_id=1, source_target_pairs={{0,4},{4,8},{8,12},{12,16},{16,20},{20,24},{24,28},{28,0},{1,5},{5... | collective-permute-start | bytes 1179656 | tf_op jit(solution)/shard_map/ppermute | solution.py:275
  21.8 6.6 %collective-permute-start.5 = (bf16[8,48,128]{2,1,0:T(8,128)(2,1)S(1)}, bf16[8,48,128]{2,1,0:T(8,128)(2,1)S(1)}, u32[]{:S(2)}, u32[]{:S(2)}) collective-permute-start(bf16[8,48,128]{2,1,0:T(8,128)(2,1)S(1)} %get-tuple-element.33), channel_id=1, source_target_pairs={{0,3},{1,2},{2,1},{3,0},{4,7},{5,6},{6,5},{7,4},{8,11},{9,10},{10,... | collective-permute-start | bytes 294920 | tf_op jit(solution)/shard_map/ppermute | solution.py:280
  25.0 6.3 %collective-permute-start.6 = (bf16[8,48,128]{2,1,0:T(8,128)(2,1)S(1)}, bf16[8,48,128]{2,1,0:T(8,128)(2,1)S(1)}, u32[]{:S(2)}, u32[]{:S(2)}) collective-permute-start(bf16[8,48,128]{2,1,0:T(8,128)(2,1)S(1)} %get-tuple-element.34), channel_id=1, source_target_pairs={{0,2},{1,3},{2,0},{3,1},{4,6},{5,7},{6,4},{7,5},{8,10},{9,11},{10,... | collective-permute-start | bytes 294920 | tf_op jit(solution)/shard_map/ppermute | solution.py:280
  25.0 6.3 %collective-permute-start.7 = (bf16[8,48,128]{2,1,0:T(8,128)(2,1)S(1)}, bf16[8,48,128]{2,1,0:T(8,128)(2,1)S(1)}, u32[]{:S(2)}, u32[]{:S(2)}) collective-permute-start(bf16[8,48,128]{2,1,0:T(8,128)(2,1)S(1)} %get-tuple-element.35), channel_id=1, source_target_pairs={{0,1},{1,0},{2,3},{3,2},{4,5},{5,4},{6,7},{7,6},{8,9},{9,8},{10,11... | collective-permute-start | bytes 294920 | tf_op jit(solution)/shard_map/ppermute | solution.py:280

commit v17 on v12

--- a/solution.py
+++ b/solution.py
@@ -243,9 +243,10 @@
         panel_ref[p * bands : (p + 1) * bands] = piece[...]
 
 
-def split_kernel(n_space, n_band, prod_ref, out_ref, held, pair):
+def split_kernel(n_space, n_band, prod_ref, keep_ref, give_ref, held, pair):
     bands = prod_ref.shape[0] // n_band
     me = lax.axis_index("band")
+    parity = jnp.bitwise_and(lax.axis_index("space"), 1)
     for p, bits in enumerate(partners(n_band)):
         begin = pl.multiple_of(jnp.bitwise_xor(me, bits) * bands, 8)
         held[pl.ds(begin, bands), :] = prod_ref[p * bands : (p + 1) * bands]
@@ -254,10 +255,18 @@
         cols = [slice((h * n_band + p) * bands, (h * n_band + p + 1) * bands) for h in (0, 1)]
         pair[p] = jnp.concatenate([held[:, c] for c in cols], axis=1)
         owner = jnp.bitwise_xor(me, bits)
-        lines = [pair[p, pl.ds(r, n_space, stride=rows), :] for r in range(rows)]
-        packed = jnp.concatenate(lines, axis=1)
-        for i in range(n_space):
-            out_ref[i * n_band + owner] = packed[i : i + 1]
+        step = 2 * rows
+        for ref, odd in ((keep_ref, parity), (give_ref, 1 - parity)):
+            lines = [
+                pair[p, pl.ds(odd * rows + r, n_space // 2, stride=step), :] for r in range(rows)
+            ]
+            packed = jnp.concatenate(lines, axis=1)
+            for i in range(n_space // 2):
+                ref[i * n_band + owner] = packed[i : i + 1]
+
+
+def join_kernel(keep_ref, got_ref, out_ref):
+    out_ref[...] = keep_ref[...] + got_ref[...]
 
 
 def last_kernel(got_ref, margin_ref, projection_ref):
@@ -381,17 +390,27 @@
     right = jnp.concatenate([left, panels.reshape(total_bands, -1)], axis=0)
     products = dot(left, right, ((1,), (1,))) * (1.0 / (cells * n_space * nz))
     out_rows = total_bands // n_space
-    pieces = call(
+    half_pieces = struct((n_space // 2 * n_band, 1, out_rows * 2 * bands))
+    keep, give = call(
         partial(split_kernel, n_space, n_band),
         "split",
-        struct((n_space * n_band, 1, out_rows * 2 * bands)),
+        (half_pieces, half_pieces),
         (products,),
         scratch_shapes=[
             pltpu.VMEM(products.shape, F32),
             pltpu.VMEM((n_band, total_bands, 2 * bands), F32),
         ],
     )
-    got = lax.all_to_all(pieces, ("space", "band"), 0, 0)
+    pieces = call(join_kernel, "join", half_pieces, (keep, mirrored(give, "space", 1)))
+    got = lax.all_to_all(
+        pieces,
+        ("space", "band"),
+        0,
+        0,
+        axis_index_groups=[
+            [s * n_band + k for s in range(odd, n_space, 2) for k in range(n_band)] for odd in (0, 1)
+        ],
+    )
     margin, projection = call(
         last_kernel, "last_sum", (struct((out_rows, bands)), struct((out_rows, bands))), (got,)
     )

time: 42.8 us -> 45.1 us (1.054)
  waiting for transfers between devices: 9.81 us -> 11 us
  blocking collectives: 11.2 us -> 12.3 us
    ppermute x6 -> x7, waiting for transfers between devices: 4.06 us -> 5.21 us  [mirrored(): return lax.ppermute(value, axis, [(i, i ^ bits) for i in range(count)])]
    all_to_all x1, blocking collectives: 11.2 us -> 12.3 us  [shards(): lax.all_to_all(pieces, ('space', 'band'), 0, 0, axis_index_groups=[[s * n...]
    ppermute x6 -> x7, starting transfers between devices: 8.9 us -> 8.98 us  [mirrored(): return lax.ppermute(value, axis, [(i, i ^ bits) for i in range(count)])]
    pallas_call x10 -> x11, Pallas kernels: 6.65 us -> 6.65 us  [call(): pl.pallas_call(kernel, out_shape=out_shape, compiler_params=params(vmem *...]
  transfers between devices with their start and end apart: 9 -> 10, of which waited for: 4 -> 5; matrix products, arithmetic and copies ran while one was open for 0% -> 0% of each run, Pallas kernels for 13% -> 13%
where the time goes in v17:
time: 45.1 us; the launch traced here: 44.9 us
  starting transfers between devices  12.5 us (28%)
  blocking collectives  12.3 us (27%)
  waiting for transfers between devices  11 us (24%)
  Pallas kernels  6.65 us (15%)
  local copies, waits for them, and re-layouts  1.32 us (3%)
  between operations  0.81 us (2%)
    all_to_all x1, blocking collectives, shards(): lax.all_to_all(pieces, ('space', 'band'), 0, 0, axis_index_groups=[[s * n...  12.3 us
    ppermute x7, starting transfers between devices, mirrored(): return lax.ppermute(value, axis, [(i, i ^ bits) for i in range(count)])  8.98 us
    pallas_call x11, Pallas kernels, call(): pl.pallas_call(kernel, out_shape=out_shape, compiler_params=params(vmem *...  6.65 us
    ppermute x3, waiting for transfers between devices, cyclic(): lax.ppermute(value, axis, [(i, (i + steps) % count) for i in range(count)])  5.75 us
    ppermute x7, waiting for transfers between devices, mirrored(): return lax.ppermute(value, axis, [(i, i ^ bits) for i in range(count)])  5.21 us
    ppermute x3, starting transfers between devices, cyclic(): lax.ppermute(value, axis, [(i, (i + steps) % count) for i in range(count)])  3.5 us
    unnamed x14, local copies, waits for them, and re-layouts  1.16 us
  transfers between devices with their start and end apart: 10, of which 5 were waited for; matrix products, arithmetic and copies ran while one was open for 0% of the time, Pallas kernels for 13%

profile of v17, /device:TPU:0, one launch (start us, length us, event | category | flops | bytes accessed | tf_op | source)
XLA Modules:
  0.0 44.9 jit_solution(11363736840312772904)
XLA Ops:
  0.6 0.0 copy-start
  0.6 1.1 %copy-done = f32[8,6,32,128]{3,2,1,0:T(8,128)S(1)} copy-done((f32[8,6,32,128]{3,2,1,0:T(8,128)S(1)}, f32[8,6,32,128]{3,2,1,0:T(8,128)}, u32[]{:S(2)}) %copy-start) | copy-done | bytes 786456
  1.8 0.0 copy-start.2
  1.8 0.0 copy-start.5
  1.8 0.0 copy-start.6
  1.8 3.4 %collective-permute-start = (bf16[8,192,128]{2,1,0:T(8,128)(2,1)S(1)}, bf16[8,192,128]{2,1,0:T(8,128)(2,1)S(1)}, u32[]{:S(2)}, u32[]{:S(2)}) collective-permute-start(bf16[8,192,128]{2,1,0:T(8,128)(2,1)S(1)} %cast.1.own_ref), channel_id=1, source_target_pairs={{0,28},{4,0},{8,4},{12,8},{16,12},{20,16},{24,20},{28,24},{1,29},{... | collective-permute-start | bytes 1179656 | tf_op jit(solution)/shard_map/ppermute | solution.py:283
  5.3 1.6 %collective-permute-start.1 = (bf16[8,48,128]{2,1,0:T(8,128)(2,1)S(1)}, bf16[8,48,128]{2,1,0:T(8,128)(2,1)S(1)}, u32[]{:S(2)}, u32[]{:S(2)}) collective-permute-start(bf16[8,48,128]{2,1,0:T(8,128)(2,1)S(1)} %get-tuple-element.28), channel_id=1, source_target_pairs={{0,1},{1,0},{2,3},{3,2},{4,5},{5,4},{6,7},{7,6},{8,9},{9,8},{10,11... | collective-permute-start | bytes 294920 | tf_op jit(solution)/shard_map/ppermute | solution.py:288
  6.9 2.6 %collective-permute-start.4 = (bf16[8,48,128]{2,1,0:T(8,128)(2,1)S(1)}, bf16[8,48,128]{2,1,0:T(8,128)(2,1)S(1)}, u32[]{:S(2)}, u32[]{:S(2)}) collective-permute-start(bf16[8,48,128]{2,1,0:T(8,128)(2,1)S(1)} %get-tuple-element.34), channel_id=1, source_target_pairs={{0,2},{1,3},{2,0},{3,1},{4,6},{5,7},{6,4},{7,5},{8,10},{9,11},{10,... | collective-permute-start | bytes 294920 | tf_op jit(solution)/shard_map/ppermute | solution.py:288
  9.5 0.2 collective-permute-start.5
  9.7 0.0 copy-done.2
  9.7 0.0 copy-done.5
  9.7 0.0 copy-done.6
  9.7 0.0 copy-start.1
  9.7 1.6 %prepare.1 = (bf16[6,576,256]{2,1,0:T(8,128)(2,1)S(1)}, bf16[5,576,256]{2,1,0:T(8,128)(2,1)S(1)}, f32[8,576]{1,0:T(8,128)S(1)}, f32[1,576]{1,0:T(1,128)S(1)}) custom-call(s32[32]{0:T(128)S(1)} %copy-done.6, f32[9,32]{1,0:T(8,128)S(1)} %bitcast.19, bf16[8,192,128]{2,1,0:T(8,128)(2,1)S(1)} %cast.1.own_ref, bf16[4,9,6,32,128]{4,3,2,1,0:T(8,128)(2,1)S(1)} %copy-done.2), custom_call_target="tpu_custom_call" | custom-call | flops 1000000000 | bytes 1048576 | tf_op jit(solution)/shard_map/prepare/pallas_call | solution.py:301
  11.3 0.0 collective-permute-done.1.refs_0_.rest_0_
  11.3 0.0 copy-done.1
  11.3 0.2 ahead.1
  11.5 0.1 collective-permute-start.3
  11.6 0.0 collective-permute-done.upper_ref
  11.6 0.0 copy-start.3
  11.6 0.0 copy-start.4
  11.6 1.3 %coefficients.1 = (bf16[128,576]{1,0:T(8,128)(2,1)S(1)}, bf16[8,160,128]{2,1,0:T(8,128)(2,1)S(1)}) custom-call(bf16[8,192,128]{2,1,0:T(8,128)(2,1)S(1)} %collective-permute-done.upper_ref, bf16[5,576,256]{2,1,0:T(8,128)(2,1)S(1)} %get-tuple-element.25.table_ref, f32[8,576]{1,0:T(8,128)S(1)} %get-tuple-element.26.e_ref, ...), custom_call_target="tpu_custom_call" | custom-call | flops 1000000000 | bytes 1048576 | tf_op jit(solution)/shard_map/coefficients/pallas_call | solution.py:301
  13.0 0.1 collective-permute-start.2
  13.1 0.0 copy-done.3
  13.1 0.0 copy-done.4
  13.1 1.6 %near_part.1.g_ref = f32[8,192,128]{2,1,0:T(8,128)S(1)} custom-call(f32[8,192,128]{2,1,0:T(8,128)S(1)} %bitcast.15, f32[8,192,128]{2,1,0:T(8,128)S(1)} %bitcast.17, f32[192,128]{1,0:T(8,128)S(1)} %bitcast.18, bf16[128,576]{1,0:T(8,128)(2,1)S(1)} %get-tuple-element.30.w_ref, bf16[8,192,128]{2,1,0:T(8,128)(2,1)S(1)} %collective-permute-done.upper_ref, ...), custom_call_target="tpu_custom_call" | custom-call | flops 20000000000 | bytes 4194304 | tf_op jit(solution)/shard_map/near_part/pallas_call | solution.py:301
  14.7 1.5 %collective-permute-done.3.below_ref = bf16[8,32,128]{2,1,0:T(8,128)(2,1)S(1)} collective-permute-done((bf16[8,32,128]{2,1,0:T(8,128)(2,1)S(1)}, bf16[8,32,128]{2,1,0:T(8,128)(2,1)S(1)}, u32[]{:S(2)}, u32[]{:S(2)}) %collective-permute-start.3) | collective-permute-done | bytes 65568 | tf_op jit(solution)/shard_map/ppermute | solution.py:283
  16.2 4.3 %collective-permute-done.2.arrived_ref = bf16[8,160,128]{2,1,0:T(8,128)(2,1)S(1)} collective-permute-done((bf16[8,160,128]{2,1,0:T(8,128)(2,1)S(1)}, bf16[8,160,128]{2,1,0:T(8,128)(2,1)S(1)}, u32[]{:S(2)}, u32[]{:S(2)}) %collective-permute-start.2) | collective-permute-done | bytes 327712 | tf_op jit(solution)/shard_map/ppermute | solution.py:283
  20.4 0.1 finish.1
  20.6 3.7 %collective-permute-start.6 = (bf16[8,48,128]{2,1,0:T(8,128)(2,1)S(1)}, bf16[8,48,128]{2,1,0:T(8,128)(2,1)S(1)}, u32[]{:S(2)}, u32[]{:S(2)}) collective-permute-start(bf16[8,48,128]{2,1,0:T(8,128)(2,1)S(1)} %get-tuple-element.39), channel_id=1, source_target_pairs={{0,3},{1,2},{2,1},{3,0},{4,7},{5,6},{6,5},{7,4},{8,11},{9,10},{10,... | collective-permute-start | bytes 294920 | tf_op jit(solution)/shard_map/ppermute | solution.py:288
  24.3 0.0 collective-permute-start.7
  24.3 0.8 %collective-permute-start.8 = (bf16[8,48,128]{2,1,0:T(8,128)(2,1)S(1)}, bf16[8,48,128]{2,1,0:T(8,128)(2,1)S(1)}, u32[]{:S(2)}, u32[]{:S(2)}) collective-permute-start(bf16[8,48,128]{2,1,0:T(8,128)(2,1)S(1)} %get-tuple-element.41), channel_id=1, source_target_pairs={{0,1},{1,0},{2,3},{3,2},{4,5},{5,4},{6,7},{7,6},{8,9},{9,8},{10,11... | collective-permute-start | bytes 294920 | tf_op jit(solution)/shard_map/ppermute | solution.py:288
  25.0 0.0 collective-permute-done.4.rest_1_
  25.0 0.0 collective-permute-done.5.rest_2_
  25.0 0.8 %output.1 = (bf16[8,192,128]{2,1,0:T(8,128)(2,1)}, bf16[32,48,128]{2,1,0:T(8,128)(2,1)S(1)}) custom-call(f32[8,192,128]{2,1,0:T(8,128)S(1)} %near_part.1.g_ref, bf16[8,160,128]{2,1,0:T(8,128)(2,1)S(1)} %collective-permute-done.2.arrived_ref, bf16[8,32,128]{2,1,0:T(8,128)(2,1)S(1)} %collective-permute-done.3.below_ref, ...), custom_call_target="tpu_custom_call" | custom-call | tf_op jit(solution)/shard_map/output/pallas_call | solution.py:301
  25.9 1.5 %collective-permute-done.6 = bf16[8,48,128]{2,1,0:T(8,128)(2,1)S(1)} collective-permute-done((bf16[8,48,128]{2,1,0:T(8,128)(2,1)S(1)}, bf16[8,48,128]{2,1,0:T(8,128)(2,1)S(1)}, u32[]{:S(2)}, u32[]{:S(2)}) %collective-permute-start.6) | collective-permute-done | bytes 98336 | tf_op jit(solution)/shard_map/ppermute | solution.py:288
  27.4 2.5 %collective-permute-done.7 = bf16[8,48,128]{2,1,0:T(8,128)(2,1)S(1)} collective-permute-done((bf16[8,48,128]{2,1,0:T(8,128)(2,1)S(1)}, bf16[8,48,128]{2,1,0:T(8,128)(2,1)S(1)}, u32[]{:S(2)}, u32[]{:S(2)}) %collective-permute-start.7) | collective-permute-done | bytes 98336 | tf_op jit(solution)/shard_map/ppermute | solution.py:288
  29.9 0.0 collective-permute-done.8
  29.9 0.1 pad_maximum_fusion
  30.0 0.2 copy_bitcast_fusion
  30.1 0.3 convolution_multiply_fusion.prod_ref
  30.5 0.2 split.1
  30.7 0.1 collective-permute-start.9
  30.8 1.2 %collective-permute-done.9.got_ref = f32[16,1,64]{2,1,0:T(1,128)S(1)} collective-permute-done((f32[16,1,64]{2,1,0:T(1,128)S(1)}, f32[16,1,64]{2,1,0:T(1,128)S(1)}, u32[]{:S(2)}, u32[]{:S(2)}) %collective-permute-start.9) | collective-permute-done | bytes 4128 | tf_op jit(solution)/shard_map/ppermute | solution.py:288
  31.9 12.3 %all_to_all.5.got_ref = f32[16,1,64]{2,1,0:T(1,128)S(1)} all-to-all(f32[16,1,64]{2,1,0:T(1,128)S(1)} %join.1), channel_id=1, replica_groups={{0,1,2,3,8,9,10,11,16,17,18,19,24,25,26,27},{4,5,6,7,12,13,14,15,20,21,..., dimensions={0} | all-to-all | bytes 8192 | tf_op jit(solution)/shard_map/all_to_all | solution.py:405
  44.2 0.7 %last_sum.1 = (f32[4,8]{1,0:T(4,128)}, f32[4,8]{1,0:T(4,128)}) custom-call(f32[16,1,64]{2,1,0:T(1,128)S(1)} %all_to_all.5.got_ref), custom_call_target="tpu_custom_call" | custom-call | tf_op jit(solution)/shard_map/last_sum/pallas_call | solution.py:301
  (3 shorter events, 0.1 us)
Async XLA Ops:
  0.6 1.1 %copy-start = (f32[8,6,32,128]{3,2,1,0:T(8,128)S(1)}, f32[8,6,32,128]{3,2,1,0:T(8,128)}, u32[]{:S(2)}) copy-start(f32[8,6,32,128]{3,2,1,0:T(8,128)} %param.6) | copy-start | bytes 2359300
  1.8 7.9 %copy-start.2 = (bf16[4,9,6,32,128]{4,3,2,1,0:T(8,128)(2,1)S(1)}, bf16[4,9,6,32,128]{4,3,2,1,0:T(8,128)(2,1)}, u32[]{:S(2)}) copy-start(bf16[4,9,6,32,128]{4,3,2,1,0:T(8,128)(2,1)} %proj_ref.1) | copy-start | bytes 5308420
  1.8 7.9 %copy-start.5 = (f32[32,9]{0,1:T(8,128)S(1)}, f32[32,9]{0,1:T(8,128)}, u32[]{:S(2)}) copy-start(f32[32,9]{0,1:T(8,128)} %param.10) | copy-start | bytes 3460
  1.8 7.9 %copy-start.6 = (s32[32]{0:T(128)S(1)}, s32[32]{0:T(128)}, u32[]{:S(2)}) copy-start(s32[32]{0:T(128)} %first_ref.1) | copy-start | bytes 388
  1.8 9.8 %collective-permute-start = (bf16[8,192,128]{2,1,0:T(8,128)(2,1)S(1)}, bf16[8,192,128]{2,1,0:T(8,128)(2,1)S(1)}, u32[]{:S(2)}, u32[]{:S(2)}) collective-permute-start(bf16[8,192,128]{2,1,0:T(8,128)(2,1)S(1)} %cast.1.own_ref), channel_id=1, source_target_pairs={{0,28},{4,0},{8,4},{12,8},{16,12},{20,16},{24,20},{28,24},{1,29},{... | collective-permute-start | bytes 1179656 | tf_op jit(solution)/shard_map/ppermute | solution.py:283
  5.3 6.0 %collective-permute-start.1 = (bf16[8,48,128]{2,1,0:T(8,128)(2,1)S(1)}, bf16[8,48,128]{2,1,0:T(8,128)(2,1)S(1)}, u32[]{:S(2)}, u32[]{:S(2)}) collective-permute-start(bf16[8,48,128]{2,1,0:T(8,128)(2,1)S(1)} %get-tuple-element.28), channel_id=1, source_target_pairs={{0,1},{1,0},{2,3},{3,2},{4,5},{5,4},{6,7},{7,6},{8,9},{9,8},{10,11... | collective-permute-start | bytes 294920 | tf_op jit(solution)/shard_map/ppermute | solution.py:288
  6.9 18.1 %collective-permute-start.4 = (bf16[8,48,128]{2,1,0:T(8,128)(2,1)S(1)}, bf16[8,48,128]{2,1,0:T(8,128)(2,1)S(1)}, u32[]{:S(2)}, u32[]{:S(2)}) collective-permute-start(bf16[8,48,128]{2,1,0:T(8,128)(2,1)S(1)} %get-tuple-element.34), channel_id=1, source_target_pairs={{0,2},{1,3},{2,0},{3,1},{4,6},{5,7},{6,4},{7,5},{8,10},{9,11},{10,... | collective-permute-start | bytes 294920 | tf_op jit(solution)/shard_map/ppermute | solution.py:288
  9.5 15.5 %collective-permute-start.5 = (bf16[8,48,128]{2,1,0:T(8,128)(2,1)S(1)}, bf16[8,48,128]{2,1,0:T(8,128)(2,1)S(1)}, u32[]{:S(2)}, u32[]{:S(2)}) collective-permute-start(bf16[8,48,128]{2,1,0:T(8,128)(2,1)S(1)} %get-tuple-element.35), channel_id=1, source_target_pairs={{0,3},{1,2},{2,1},{3,0},{4,7},{5,6},{6,5},{7,4},{8,11},{9,10},{10,... | collective-permute-start | bytes 294920 | tf_op jit(solution)/shard_map/ppermute | solution.py:288
  9.7 1.6 %copy-start.1 = (f32[8,6,32,128]{3,2,1,0:T(8,128)S(1)}, f32[8,6,32,128]{3,2,1,0:T(8,128)}, u32[]{:S(2)}) copy-start(f32[8,6,32,128]{3,2,1,0:T(8,128)} %param.6) | copy-start | bytes 2359300
  11.5 4.6 %collective-permute-start.3 = (bf16[8,32,128]{2,1,0:T(8,128)(2,1)S(1)}, bf16[8,32,128]{2,1,0:T(8,128)(2,1)S(1)}, u32[]{:S(2)}, u32[]{:S(2)}) collective-permute-start(bf16[8,32,128]{2,1,0:T(8,128)(2,1)S(1)} %get-tuple-element.33), channel_id=1, source_target_pairs={{0,4},{4,8},{8,12},{12,16},{16,20},{20,24},{24,28},{28,0},{1,5},{5... | collective-permute-start | bytes 196616 | tf_op jit(solution)/shard_map/ppermute | solution.py:283
  11.6 1.4 %copy-start.3 = (f32[8,6,32,128]{3,2,1,0:T(8,128)S(1)}, f32[8,6,32,128]{3,2,1,0:T(8,128)}, u32[]{:S(2)}) copy-start(f32[8,6,32,128]{3,2,1,0:T(8,128)} %param.7) | copy-start | bytes 2359300
  11.6 1.4 %copy-start.4 = (f32[6,32,128]{2,1,0:T(8,128)S(1)}, f32[6,32,128]{2,1,0:T(8,128)}, u32[]{:S(2)}) copy-start(f32[6,32,128]{2,1,0:T(8,128)} %param.8) | copy-start | bytes 294916
  13.0 7.5 %collective-permute-start.2 = (bf16[8,160,128]{2,1,0:T(8,128)(2,1)S(1)}, bf16[8,160,128]{2,1,0:T(8,128)(2,1)S(1)}, u32[]{:S(2)}, u32[]{:S(2)}) collective-permute-start(bf16[8,160,128]{2,1,0:T(8,128)(2,1)S(1)} %get-tuple-element.32), channel_id=1, source_target_pairs={{0,4},{4,8},{8,12},{12,16},{16,20},{20,24},{24,28},{28,0},{1,5},{5... | collective-permute-start | bytes 983048 | tf_op jit(solution)/shard_map/ppermute | solution.py:283
  20.6 6.8 %collective-permute-start.6 = (bf16[8,48,128]{2,1,0:T(8,128)(2,1)S(1)}, bf16[8,48,128]{2,1,0:T(8,128)(2,1)S(1)}, u32[]{:S(2)}, u32[]{:S(2)}) collective-permute-start(bf16[8,48,128]{2,1,0:T(8,128)(2,1)S(1)} %get-tuple-element.39), channel_id=1, source_target_pairs={{0,3},{1,2},{2,1},{3,0},{4,7},{5,6},{6,5},{7,4},{8,11},{9,10},{10,... | collective-permute-start | bytes 294920 | tf_op jit(solution)/shard_map/ppermute | solution.py:288
  24.3 5.6 %collective-permute-start.7 = (bf16[8,48,128]{2,1,0:T(8,128)(2,1)S(1)}, bf16[8,48,128]{2,1,0:T(8,128)(2,1)S(1)}, u32[]{:S(2)}, u32[]{:S(2)}) collective-permute-start(bf16[8,48,128]{2,1,0:T(8,128)(2,1)S(1)} %get-tuple-element.40), channel_id=1, source_target_pairs={{0,2},{1,3},{2,0},{3,1},{4,6},{5,7},{6,4},{7,5},{8,10},{9,11},{10,... | collective-permute-start | bytes 294920 | tf_op jit(solution)/shard_map/ppermute | solution.py:288
  24.3 5.7 %collective-permute-start.8 = (bf16[8,48,128]{2,1,0:T(8,128)(2,1)S(1)}, bf16[8,48,128]{2,1,0:T(8,128)(2,1)S(1)}, u32[]{:S(2)}, u32[]{:S(2)}) collective-permute-start(bf16[8,48,128]{2,1,0:T(8,128)(2,1)S(1)} %get-tuple-element.41), channel_id=1, source_target_pairs={{0,1},{1,0},{2,3},{3,2},{4,5},{5,4},{6,7},{7,6},{8,9},{9,8},{10,11... | collective-permute-start | bytes 294920 | tf_op jit(solution)/shard_map/ppermute | solution.py:288
  30.7 1.2 %collective-permute-start.9 = (f32[16,1,64]{2,1,0:T(1,128)S(1)}, f32[16,1,64]{2,1,0:T(1,128)S(1)}, u32[]{:S(2)}, u32[]{:S(2)}) collective-permute-start(f32[16,1,64]{2,1,0:T(1,128)S(1)} %get-tuple-element.44), channel_id=1, source_target_pairs={{0,4},{4,0},{8,12},{12,8},{16,20},{20,16},{24,28},{28,24},{1,5},{5... | collective-permute-start | bytes 12296 | tf_op jit(solution)/shard_map/ppermute | solution.py:288

commit v18 on v12

--- a/solution.py
+++ b/solution.py
@@ -122,33 +122,36 @@
     return jnp.concatenate(halves, axis=1)
 
 
-def overlap(field_ref, planes, ny, table_ref):
+def plane_table(proj_ref, starts, q):
+    parts = []
+    for a, start in enumerate(starts):
+        p = q - start
+        inside = jnp.logical_and(p >= 0, p < BOX)
+        part = table(proj_ref, a, jnp.clip(p, 0, BOX - 1))
+        parts.append(part * jnp.where(inside, 1.0, 0.0).astype(BF16))
+    return jnp.concatenate(parts, axis=0)
+
+
+def box_starts(first_ref, atoms, planes):
+    me = lax.axis_index("space")
+    return [first_ref[me * atoms + a] - me * planes for a in range(atoms)]
+
+
+def overlap(field_ref, tables, ny):
     bands = field_ref.shape[0]
-    left = [halves_along(field_ref[:, plane_rows(x, ny)], 1) for x in range(planes)]
-    right = [table_ref[x] for x in range(planes)]
-    d = dot(jnp.concatenate(left, axis=1), jnp.concatenate(right, axis=1), ((1,), (1,)))
+    left = [halves_along(field_ref[:, plane_rows(x, ny)], 1) for x in range(len(tables))]
+    d = dot(jnp.concatenate(left, axis=1), jnp.concatenate(tables, axis=1), ((1,), (1,)))
     rows, cols = d.shape
     return (d * same_cell(rows, cols)).reshape(bands, HALF, cols).sum(axis=1)
 
 
-def prepare_kernel(
-    planes, first_ref, strength_ref, own_ref, proj_ref, near_ref, far_ref, e_ref, s_ref
-):
+def prepare_kernel(planes, first_ref, strength_ref, own_ref, proj_ref, far_ref, e_ref, s_ref):
     ny = own_ref.shape[1] // planes
     atoms, npj = proj_ref.shape[:2]
     me = lax.axis_index("space")
-    for q in range(planes + BOX - 1):
-        parts = []
-        for a in range(atoms):
-            p = q - (first_ref[me * atoms + a] - me * planes)
-            inside = jnp.logical_and(p >= 0, p < BOX)
-            part = table(proj_ref, a, jnp.clip(p, 0, BOX - 1))
-            parts.append(part * jnp.where(inside, 1.0, 0.0).astype(BF16))
-        whole = jnp.concatenate(parts, axis=0)
-        if q < planes:
-            near_ref[q] = whole
-        else:
-            far_ref[q - planes] = whole
+    starts = box_starts(first_ref, atoms, planes)
+    for q in range(BOX - 1):
+        far_ref[q] = plane_table(proj_ref, starts, planes + q)
     owner = lax.broadcasted_iota(jnp.int32, s_ref.shape, 1)
     scale = jnp.zeros(s_ref.shape, F32)
     for a in range(atoms):
@@ -156,7 +159,7 @@
             value = outer * strength_ref[j, me * atoms + a]
             scale = jnp.where(owner >= (a * npj + j) * HALF, value, scale)
     s_ref[...] = scale
-    e_ref[...] = overlap(own_ref, planes, ny, near_ref)
+    e_ref[...] = overlap(own_ref, [plane_table(proj_ref, starts, q) for q in range(planes)], ny)
 
 
 def ahead_kernel(planes, psi_ref, *refs):
@@ -175,7 +178,7 @@
     bands, cells, nz = upper_ref.shape
     ny = cells // planes
     reach = BOX - 1
-    e = e_ref[...] + overlap(upper_ref, reach, ny, table_ref)
+    e = e_ref[...] + overlap(upper_ref, [table_ref[q] for q in range(reach)], ny)
     cols = e.shape[1]
     tiles = -(-cols // nz)
     e = jnp.concatenate([e, jnp.zeros((bands, tiles * nz - cols), F32)], axis=1)
@@ -185,7 +188,7 @@
     group = jnp.where(jnp.bitwise_xor(gi, gj) < HALF, 1.0, 0.0).astype(BF16)
     e_hi = e.astype(BF16)
     e_lo = (e - e_hi.astype(F32)).astype(BF16)
-    coef = dot(e_hi, group) + dot(e_lo, group)
+    coef = dot(jnp.concatenate([e_hi, e_lo], axis=1), jnp.concatenate([group, group], axis=0))
     coef = jnp.concatenate([coef[t * bands : (t + 1) * bands] for t in range(tiles)], axis=1)
     w = coef[:, :cols] * s_ref[...]
     rows = bands * HALF
@@ -198,17 +201,20 @@
         next_ref[:, here] = block.astype(BF16)
 
 
-def near_kernel(planes, psi_ref, prev_ref, pot_ref, w_ref, upper_ref, table_ref, out_ref):
+def near_kernel(
+    planes, first_ref, psi_ref, prev_ref, pot_ref, w_ref, upper_ref, proj_ref, out_ref
+):
     bands, cells, nz = psi_ref.shape
     ny = cells // planes
     weights = w_ref[...]
+    starts = box_starts(first_ref, proj_ref.shape[0], planes)
     cz_hi, cz_lo = circulant(nz, 1)
     cz = (jnp.concatenate([cz_hi, cz_hi], axis=0), cz_lo)
     cy = circulant(ny, bands // 2)
     for x in range(planes):
         here = plane_rows(x, ny)
         psi = psi_ref[:, here]
-        total = yz_part(psi, cz, cy) + spread(weights, table_ref[x], nz)
+        total = yz_part(psi, cz, cy) + spread(weights, plane_table(proj_ref, starts, x), nz)
         site = outer * pot_ref[here] + (kinetic_weights[0] - outer * center)
         total = total + site[None] * psi - prev_ref[:, here]
         for m in range(1, HALO + 1):
@@ -323,18 +329,17 @@
     panel = exchanged(panel)
     atoms, npj = projectors.shape[:2]
     cols = atoms * npj * HALF
-    tables, far_tables, e, s = call(
+    far_tables, e, s = call(
         partial(prepare_kernel, planes),
         "prepare",
         (
-            struct((planes, cols, ny // HALF * nz), BF16),
             struct((BOX - 1, cols, ny // HALF * nz), BF16),
             struct((bands, cols)),
             struct((1, cols)),
         ),
         (atom_planes, strengths.T, half, projectors),
         in_specs=[sm, sm, vm, vm],
-        out_specs=(vm,) * 4,
+        out_specs=(vm,) * 3,
         cost_estimate=pl.CostEstimate(flops=10**9, bytes_accessed=2**20, transcendentals=0),
     )
     ahead, edge = call(
@@ -359,7 +364,9 @@
         partial(near_kernel, planes),
         "near_part",
         struct(whole),
-        (psi, prev, pot, w, upper, tables),
+        (atom_planes, psi, prev, pot, w, upper, projectors),
+        in_specs=[sm] + [vm] * 6,
+        out_specs=vm,
         cost_estimate=pl.CostEstimate(flops=2*10**10, bytes_accessed=4 * 2**20, transcendentals=0),
     )
     mine = call(

time: 42.8 us -> 42.7 us (level)
  waiting for transfers between devices: 9.81 us -> 9.18 us
  Pallas kernels: 6.65 us -> 7.23 us
    ppermute x3, waiting for transfers between devices: 5.75 us -> 5.11 us  [cyclic(): lax.ppermute(value, axis, [(i, (i + steps) % count) for i in range(count)])]
    pallas_call x10, Pallas kernels: 6.65 us -> 7.23 us  [call(): pl.pallas_call(kernel, out_shape=out_shape, compiler_params=params(vmem *...]
  transfers between devices with their start and end apart: 9 -> 9, of which waited for: 4 -> 4; matrix products, arithmetic and copies ran while one was open for 0% -> 0% of each run, Pallas kernels for 13% -> 15%
where the time goes in v18:
time: 42.7 us; the launch traced here: 42.6 us
  starting transfers between devices  12.4 us (29%)
  blocking collectives  11.2 us (26%)
  waiting for transfers between devices  9.18 us (21%)
  Pallas kernels  7.23 us (17%)
  local copies, waits for them, and re-layouts  1.32 us (3%)
  between operations  0.8 us (2%)
    all_to_all x1, blocking collectives, shards(): got = lax.all_to_all(pieces, ('space', 'band'), 0, 0)  11.2 us
    ppermute x6, starting transfers between devices, mirrored(): return lax.ppermute(value, axis, [(i, i ^ bits) for i in range(count)])  8.9 us
    pallas_call x10, Pallas kernels, call(): pl.pallas_call(kernel, out_shape=out_shape, compiler_params=params(vmem *...  7.23 us
    ppermute x3, waiting for transfers between devices, cyclic(): lax.ppermute(value, axis, [(i, (i + steps) % count) for i in range(count)])  5.11 us
    ppermute x6, waiting for transfers between devices, mirrored(): return lax.ppermute(value, axis, [(i, i ^ bits) for i in range(count)])  4.07 us
    ppermute x3, starting transfers between devices, cyclic(): lax.ppermute(value, axis, [(i, (i + steps) % count) for i in range(count)])  3.5 us
    unnamed x14, local copies, waits for them, and re-layouts  1.16 us
  transfers between devices with their start and end apart: 9, of which 4 were waited for; matrix products, arithmetic and copies ran while one was open for 0% of the time, Pallas kernels for 15%

profile of v18, /device:TPU:0, one launch (start us, length us, event | category | flops | bytes accessed | tf_op | source)
XLA Modules:
  0.0 42.6 jit_solution(2306012403471616663)
XLA Ops:
  0.6 0.0 copy-start
  0.6 1.1 %copy-done = f32[8,6,32,128]{3,2,1,0:T(8,128)S(1)} copy-done((f32[8,6,32,128]{3,2,1,0:T(8,128)S(1)}, f32[8,6,32,128]{3,2,1,0:T(8,128)}, u32[]{:S(2)}) %copy-start) | copy-done | bytes 786456
  1.8 0.0 copy-start.2
  1.8 0.0 copy-start.5
  1.8 0.0 copy-start.6
  1.8 3.4 %collective-permute-start = (bf16[8,192,128]{2,1,0:T(8,128)(2,1)S(1)}, bf16[8,192,128]{2,1,0:T(8,128)(2,1)S(1)}, u32[]{:S(2)}, u32[]{:S(2)}) collective-permute-start(bf16[8,192,128]{2,1,0:T(8,128)(2,1)S(1)} %cast.1.own_ref), channel_id=1, source_target_pairs={{0,28},{4,0},{8,4},{12,8},{16,12},{20,16},{24,20},{28,24},{1,29},{... | collective-permute-start | bytes 1179656 | tf_op jit(solution)/shard_map/ppermute | solution.py:280
  5.3 1.6 %collective-permute-start.1 = (bf16[8,48,128]{2,1,0:T(8,128)(2,1)S(1)}, bf16[8,48,128]{2,1,0:T(8,128)(2,1)S(1)}, u32[]{:S(2)}, u32[]{:S(2)}) collective-permute-start(bf16[8,48,128]{2,1,0:T(8,128)(2,1)S(1)} %get-tuple-element.25), channel_id=1, source_target_pairs={{0,1},{1,0},{2,3},{3,2},{4,5},{5,4},{6,7},{7,6},{8,9},{9,8},{10,11... | collective-permute-start | bytes 294920 | tf_op jit(solution)/shard_map/ppermute | solution.py:285
  6.9 2.6 %collective-permute-start.4 = (bf16[8,48,128]{2,1,0:T(8,128)(2,1)S(1)}, bf16[8,48,128]{2,1,0:T(8,128)(2,1)S(1)}, u32[]{:S(2)}, u32[]{:S(2)}) collective-permute-start(bf16[8,48,128]{2,1,0:T(8,128)(2,1)S(1)} %get-tuple-element.30), channel_id=1, source_target_pairs={{0,2},{1,3},{2,0},{3,1},{4,6},{5,7},{6,4},{7,5},{8,10},{9,11},{10,... | collective-permute-start | bytes 294920 | tf_op jit(solution)/shard_map/ppermute | solution.py:285
  9.5 0.2 collective-permute-start.5
  9.7 0.0 copy-done.2
  9.7 0.0 copy-done.5
  9.7 0.0 copy-done.6
  9.7 0.0 copy-start.1
  9.7 1.5 %prepare.1 = (bf16[5,576,256]{2,1,0:T(8,128)(2,1)S(1)}, f32[8,576]{1,0:T(8,128)S(1)}, f32[1,576]{1,0:T(1,128)S(1)}) custom-call(s32[32]{0:T(128)S(1)} %copy-done.6, f32[9,32]{1,0:T(8,128)S(1)} %bitcast.19, bf16[8,192,128]{2,1,0:T(8,128)(2,1)S(1)} %cast.1.own_ref, bf16[4,9,6,32,128]{4,3,2,1,0:T(8,128)(2,1)S(1)} %copy-done.2), custom_call_target="tpu_custom_call" | custom-call | flops 1000000000 | bytes 1048576 | tf_op jit(solution)/shard_map/prepare/pallas_call | solution.py:298
  11.3 0.0 collective-permute-done.1.refs_0_.rest_0_
  11.3 0.0 copy-done.1
  11.3 0.2 ahead.1
  11.5 0.1 collective-permute-start.3
  11.6 0.0 collective-permute-done.upper_ref
  11.6 0.0 copy-start.3
  11.6 0.0 copy-start.4
  11.6 1.3 %coefficients.1 = (bf16[128,576]{1,0:T(8,128)(2,1)S(1)}, bf16[8,160,128]{2,1,0:T(8,128)(2,1)S(1)}) custom-call(bf16[8,192,128]{2,1,0:T(8,128)(2,1)S(1)} %collective-permute-done.upper_ref, bf16[5,576,256]{2,1,0:T(8,128)(2,1)S(1)} %get-tuple-element.22.table_ref, f32[8,576]{1,0:T(8,128)S(1)} %get-tuple-element.23.e_ref, ...), custom_call_target="tpu_custom_call" | custom-call | flops 1000000000 | bytes 1048576 | tf_op jit(solution)/shard_map/coefficients/pallas_call | solution.py:298
  12.9 0.1 collective-permute-start.2
  13.0 0.0 copy-done.3
  13.0 0.0 copy-done.4
  13.0 2.3 %near_part.1.g_ref = f32[8,192,128]{2,1,0:T(8,128)S(1)} custom-call(s32[32]{0:T(128)S(1)} %copy-done.6, f32[8,192,128]{2,1,0:T(8,128)S(1)} %bitcast.15, f32[8,192,128]{2,1,0:T(8,128)S(1)} %bitcast.17, f32[192,128]{1,0:T(8,128)S(1)} %bitcast.18, bf16[128,576]{1,0:T(8,128)(2,1)S(1)} %get-tuple-element.27.w_ref, ...), custom_call_target="tpu_custom_call" | custom-call | flops 20000000000 | bytes 4194304 | tf_op jit(solution)/shard_map/near_part/pallas_call | solution.py:298
  15.3 0.9 %collective-permute-done.3.below_ref = bf16[8,32,128]{2,1,0:T(8,128)(2,1)S(1)} collective-permute-done((bf16[8,32,128]{2,1,0:T(8,128)(2,1)S(1)}, bf16[8,32,128]{2,1,0:T(8,128)(2,1)S(1)}, u32[]{:S(2)}, u32[]{:S(2)}) %collective-permute-start.3) | collective-permute-done | bytes 65568 | tf_op jit(solution)/shard_map/ppermute | solution.py:280
  16.1 4.2 %collective-permute-done.2.arrived_ref = bf16[8,160,128]{2,1,0:T(8,128)(2,1)S(1)} collective-permute-done((bf16[8,160,128]{2,1,0:T(8,128)(2,1)S(1)}, bf16[8,160,128]{2,1,0:T(8,128)(2,1)S(1)}, u32[]{:S(2)}, u32[]{:S(2)}) %collective-permute-start.2) | collective-permute-done | bytes 327712 | tf_op jit(solution)/shard_map/ppermute | solution.py:280
  20.4 0.1 finish.1
  20.5 3.7 %collective-permute-start.6 = (bf16[8,48,128]{2,1,0:T(8,128)(2,1)S(1)}, bf16[8,48,128]{2,1,0:T(8,128)(2,1)S(1)}, u32[]{:S(2)}, u32[]{:S(2)}) collective-permute-start(bf16[8,48,128]{2,1,0:T(8,128)(2,1)S(1)} %get-tuple-element.35), channel_id=1, source_target_pairs={{0,3},{1,2},{2,1},{3,0},{4,7},{5,6},{6,5},{7,4},{8,11},{9,10},{10,... | collective-permute-start | bytes 294920 | tf_op jit(solution)/shard_map/ppermute | solution.py:285
  24.2 0.0 collective-permute-start.7
  24.2 0.8 %collective-permute-start.8 = (bf16[8,48,128]{2,1,0:T(8,128)(2,1)S(1)}, bf16[8,48,128]{2,1,0:T(8,128)(2,1)S(1)}, u32[]{:S(2)}, u32[]{:S(2)}) collective-permute-start(bf16[8,48,128]{2,1,0:T(8,128)(2,1)S(1)} %get-tuple-element.37), channel_id=1, source_target_pairs={{0,1},{1,0},{2,3},{3,2},{4,5},{5,4},{6,7},{7,6},{8,9},{9,8},{10,11... | collective-permute-start | bytes 294920 | tf_op jit(solution)/shard_map/ppermute | solution.py:285
  25.0 0.0 collective-permute-done.4.rest_1_
  25.0 0.0 collective-permute-done.5.rest_2_
  25.0 0.8 %output.1 = (bf16[8,192,128]{2,1,0:T(8,128)(2,1)}, bf16[32,48,128]{2,1,0:T(8,128)(2,1)S(1)}) custom-call(f32[8,192,128]{2,1,0:T(8,128)S(1)} %near_part.1.g_ref, bf16[8,160,128]{2,1,0:T(8,128)(2,1)S(1)} %collective-permute-done.2.arrived_ref, bf16[8,32,128]{2,1,0:T(8,128)(2,1)S(1)} %collective-permute-done.3.below_ref, ...), custom_call_target="tpu_custom_call" | custom-call | tf_op jit(solution)/shard_map/output/pallas_call | solution.py:298
  25.8 1.5 %collective-permute-done.6 = bf16[8,48,128]{2,1,0:T(8,128)(2,1)S(1)} collective-permute-done((bf16[8,48,128]{2,1,0:T(8,128)(2,1)S(1)}, bf16[8,48,128]{2,1,0:T(8,128)(2,1)S(1)}, u32[]{:S(2)}, u32[]{:S(2)}) %collective-permute-start.6) | collective-permute-done | bytes 98336 | tf_op jit(solution)/shard_map/ppermute | solution.py:285
  27.3 2.5 %collective-permute-done.7 = bf16[8,48,128]{2,1,0:T(8,128)(2,1)S(1)} collective-permute-done((bf16[8,48,128]{2,1,0:T(8,128)(2,1)S(1)}, bf16[8,48,128]{2,1,0:T(8,128)(2,1)S(1)}, u32[]{:S(2)}, u32[]{:S(2)}) %collective-permute-start.7) | collective-permute-done | bytes 98336 | tf_op jit(solution)/shard_map/ppermute | solution.py:285
  29.8 0.0 collective-permute-done.8
  29.9 0.1 pad_maximum_fusion
  29.9 0.2 copy_bitcast_fusion
  30.1 0.3 convolution_multiply_fusion.prod_ref
  30.4 0.2 split.1
  30.6 11.2 %all_to_all.5.got_ref = f32[32,1,64]{2,1,0:T(1,128)S(1)} all-to-all(f32[32,1,64]{2,1,0:T(1,128)S(1)} %split.1), channel_id=1, replica_groups=mesh['space'=8,'band'=4] {'space','band'}, dimensions={0} | all-to-all | bytes 16384 | tf_op jit(solution)/shard_map/all_to_all | solution.py:401
  41.9 0.7 %last_sum.1 = (f32[4,8]{1,0:T(4,128)}, f32[4,8]{1,0:T(4,128)}) custom-call(f32[32,1,64]{2,1,0:T(1,128)S(1)} %all_to_all.5.got_ref), custom_call_target="tpu_custom_call" | custom-call | tf_op jit(solution)/shard_map/last_sum/pallas_call | solution.py:298
  (2 shorter events, 0.1 us)
Async XLA Ops:
  0.6 1.1 %copy-start = (f32[8,6,32,128]{3,2,1,0:T(8,128)S(1)}, f32[8,6,32,128]{3,2,1,0:T(8,128)}, u32[]{:S(2)}) copy-start(f32[8,6,32,128]{3,2,1,0:T(8,128)} %param.6) | copy-start | bytes 2359300
  1.8 7.9 %copy-start.2 = (bf16[4,9,6,32,128]{4,3,2,1,0:T(8,128)(2,1)S(1)}, bf16[4,9,6,32,128]{4,3,2,1,0:T(8,128)(2,1)}, u32[]{:S(2)}) copy-start(bf16[4,9,6,32,128]{4,3,2,1,0:T(8,128)(2,1)} %proj_ref.3) | copy-start | bytes 5308420
  1.8 7.9 %copy-start.5 = (f32[32,9]{0,1:T(8,128)S(1)}, f32[32,9]{0,1:T(8,128)}, u32[]{:S(2)}) copy-start(f32[32,9]{0,1:T(8,128)} %param.10) | copy-start | bytes 3460
  1.8 7.9 %copy-start.6 = (s32[32]{0:T(128)S(1)}, s32[32]{0:T(128)}, u32[]{:S(2)}) copy-start(s32[32]{0:T(128)} %first_ref.3) | copy-start | bytes 388
  1.8 9.7 %collective-permute-start = (bf16[8,192,128]{2,1,0:T(8,128)(2,1)S(1)}, bf16[8,192,128]{2,1,0:T(8,128)(2,1)S(1)}, u32[]{:S(2)}, u32[]{:S(2)}) collective-permute-start(bf16[8,192,128]{2,1,0:T(8,128)(2,1)S(1)} %cast.1.own_ref), channel_id=1, source_target_pairs={{0,28},{4,0},{8,4},{12,8},{16,12},{20,16},{24,20},{28,24},{1,29},{... | collective-permute-start | bytes 1179656 | tf_op jit(solution)/shard_map/ppermute | solution.py:280
  5.3 6.0 %collective-permute-start.1 = (bf16[8,48,128]{2,1,0:T(8,128)(2,1)S(1)}, bf16[8,48,128]{2,1,0:T(8,128)(2,1)S(1)}, u32[]{:S(2)}, u32[]{:S(2)}) collective-permute-start(bf16[8,48,128]{2,1,0:T(8,128)(2,1)S(1)} %get-tuple-element.25), channel_id=1, source_target_pairs={{0,1},{1,0},{2,3},{3,2},{4,5},{5,4},{6,7},{7,6},{8,9},{9,8},{10,11... | collective-permute-start | bytes 294920 | tf_op jit(solution)/shard_map/ppermute | solution.py:285
  6.9 18.1 %collective-permute-start.4 = (bf16[8,48,128]{2,1,0:T(8,128)(2,1)S(1)}, bf16[8,48,128]{2,1,0:T(8,128)(2,1)S(1)}, u32[]{:S(2)}, u32[]{:S(2)}) collective-permute-start(bf16[8,48,128]{2,1,0:T(8,128)(2,1)S(1)} %get-tuple-element.30), channel_id=1, source_target_pairs={{0,2},{1,3},{2,0},{3,1},{4,6},{5,7},{6,4},{7,5},{8,10},{9,11},{10,... | collective-permute-start | bytes 294920 | tf_op jit(solution)/shard_map/ppermute | solution.py:285
  9.5 15.5 %collective-permute-start.5 = (bf16[8,48,128]{2,1,0:T(8,128)(2,1)S(1)}, bf16[8,48,128]{2,1,0:T(8,128)(2,1)S(1)}, u32[]{:S(2)}, u32[]{:S(2)}) collective-permute-start(bf16[8,48,128]{2,1,0:T(8,128)(2,1)S(1)} %get-tuple-element.31), channel_id=1, source_target_pairs={{0,3},{1,2},{2,1},{3,0},{4,7},{5,6},{6,5},{7,4},{8,11},{9,10},{10,... | collective-permute-start | bytes 294920 | tf_op jit(solution)/shard_map/ppermute | solution.py:285
  9.7 1.6 %copy-start.1 = (f32[8,6,32,128]{3,2,1,0:T(8,128)S(1)}, f32[8,6,32,128]{3,2,1,0:T(8,128)}, u32[]{:S(2)}) copy-start(f32[8,6,32,128]{3,2,1,0:T(8,128)} %param.6) | copy-start | bytes 2359300
  11.5 4.6 %collective-permute-start.3 = (bf16[8,32,128]{2,1,0:T(8,128)(2,1)S(1)}, bf16[8,32,128]{2,1,0:T(8,128)(2,1)S(1)}, u32[]{:S(2)}, u32[]{:S(2)}) collective-permute-start(bf16[8,32,128]{2,1,0:T(8,128)(2,1)S(1)} %get-tuple-element.29), channel_id=1, source_target_pairs={{0,4},{4,8},{8,12},{12,16},{16,20},{20,24},{24,28},{28,0},{1,5},{5... | collective-permute-start | bytes 196616 | tf_op jit(solution)/shard_map/ppermute | solution.py:280
  11.6 1.4 %copy-start.3 = (f32[8,6,32,128]{3,2,1,0:T(8,128)S(1)}, f32[8,6,32,128]{3,2,1,0:T(8,128)}, u32[]{:S(2)}) copy-start(f32[8,6,32,128]{3,2,1,0:T(8,128)} %param.7) | copy-start | bytes 2359300
  11.6 1.4 %copy-start.4 = (f32[6,32,128]{2,1,0:T(8,128)S(1)}, f32[6,32,128]{2,1,0:T(8,128)}, u32[]{:S(2)}) copy-start(f32[6,32,128]{2,1,0:T(8,128)} %param.8) | copy-start | bytes 294916
  12.9 7.5 %collective-permute-start.2 = (bf16[8,160,128]{2,1,0:T(8,128)(2,1)S(1)}, bf16[8,160,128]{2,1,0:T(8,128)(2,1)S(1)}, u32[]{:S(2)}, u32[]{:S(2)}) collective-permute-start(bf16[8,160,128]{2,1,0:T(8,128)(2,1)S(1)} %get-tuple-element.28), channel_id=1, source_target_pairs={{0,4},{4,8},{8,12},{12,16},{16,20},{20,24},{24,28},{28,0},{1,5},{5... | collective-permute-start | bytes 983048 | tf_op jit(solution)/shard_map/ppermute | solution.py:280
  20.5 6.8 %collective-permute-start.6 = (bf16[8,48,128]{2,1,0:T(8,128)(2,1)S(1)}, bf16[8,48,128]{2,1,0:T(8,128)(2,1)S(1)}, u32[]{:S(2)}, u32[]{:S(2)}) collective-permute-start(bf16[8,48,128]{2,1,0:T(8,128)(2,1)S(1)} %get-tuple-element.35), channel_id=1, source_target_pairs={{0,3},{1,2},{2,1},{3,0},{4,7},{5,6},{6,5},{7,4},{8,11},{9,10},{10,... | collective-permute-start | bytes 294920 | tf_op jit(solution)/shard_map/ppermute | solution.py:285
  24.2 5.6 %collective-permute-start.7 = (bf16[8,48,128]{2,1,0:T(8,128)(2,1)S(1)}, bf16[8,48,128]{2,1,0:T(8,128)(2,1)S(1)}, u32[]{:S(2)}, u32[]{:S(2)}) collective-permute-start(bf16[8,48,128]{2,1,0:T(8,128)(2,1)S(1)} %get-tuple-element.36), channel_id=1, source_target_pairs={{0,2},{1,3},{2,0},{3,1},{4,6},{5,7},{6,4},{7,5},{8,10},{9,11},{10,... | collective-permute-start | bytes 294920 | tf_op jit(solution)/shard_map/ppermute | solution.py:285
  24.2 5.7 %collective-permute-start.8 = (bf16[8,48,128]{2,1,0:T(8,128)(2,1)S(1)}, bf16[8,48,128]{2,1,0:T(8,128)(2,1)S(1)}, u32[]{:S(2)}, u32[]{:S(2)}) collective-permute-start(bf16[8,48,128]{2,1,0:T(8,128)(2,1)S(1)} %get-tuple-element.37), channel_id=1, source_target_pairs={{0,1},{1,0},{2,3},{3,2},{4,5},{5,4},{6,7},{7,6},{8,9},{9,8},{10,11... | collective-permute-start | bytes 294920 | tf_op jit(solution)/shard_map/ppermute | solution.py:285

commit v19 on v18

--- a/solution.py
+++ b/solution.py
@@ -138,11 +138,10 @@
 
 
 def overlap(field_ref, tables, ny):
-    bands = field_ref.shape[0]
     left = [halves_along(field_ref[:, plane_rows(x, ny)], 1) for x in range(len(tables))]
-    d = dot(jnp.concatenate(left, axis=1), jnp.concatenate(tables, axis=1), ((1,), (1,)))
+    d = dot(jnp.concatenate(tables, axis=1), jnp.concatenate(left, axis=1), ((1,), (1,)))
     rows, cols = d.shape
-    return (d * same_cell(rows, cols)).reshape(bands, HALF, cols).sum(axis=1)
+    return (d * same_cell(rows, cols)).reshape(rows // HALF, HALF, cols).sum(axis=1)
 
 
 def prepare_kernel(planes, first_ref, strength_ref, own_ref, proj_ref, far_ref, e_ref, s_ref):
@@ -157,7 +156,7 @@
     for a in range(atoms):
         for j in range(npj):
             value = outer * strength_ref[j, me * atoms + a]
-            scale = jnp.where(owner >= (a * npj + j) * HALF, value, scale)
+            scale = jnp.where(owner == a * npj + j, value, scale)
     s_ref[...] = scale
     e_ref[...] = overlap(own_ref, [plane_table(proj_ref, starts, q) for q in range(planes)], ny)
 
@@ -179,21 +178,22 @@
     ny = cells // planes
     reach = BOX - 1
     e = e_ref[...] + overlap(upper_ref, [table_ref[q] for q in range(reach)], ny)
-    cols = e.shape[1]
-    tiles = -(-cols // nz)
-    e = jnp.concatenate([e, jnp.zeros((bands, tiles * nz - cols), F32)], axis=1)
-    e = jnp.concatenate([e[:, t * nz : (t + 1) * nz] for t in range(tiles)], axis=0)
-    gi = lax.broadcasted_iota(jnp.int32, (nz, nz), 0)
-    gj = lax.broadcasted_iota(jnp.int32, (nz, nz), 1)
-    group = jnp.where(jnp.bitwise_xor(gi, gj) < HALF, 1.0, 0.0).astype(BF16)
+    count, rows = e.shape
+    wide = s_ref.shape[1]
+    cols = count * HALF
+    e = jnp.transpose(jnp.concatenate([e, jnp.zeros((wide - count, rows), F32)], axis=0))
     e_hi = e.astype(BF16)
     e_lo = (e - e_hi.astype(F32)).astype(BF16)
-    coef = dot(jnp.concatenate([e_hi, e_lo], axis=1), jnp.concatenate([group, group], axis=0))
-    coef = jnp.concatenate([coef[t * bands : (t + 1) * bands] for t in range(tiles)], axis=1)
-    w = coef[:, :cols] * s_ref[...]
-    rows = bands * HALF
-    full = jnp.broadcast_to(w[:, None, :], (bands, HALF, cols)).reshape(rows, cols)
-    weights = (full * same_cell(rows, cols)).astype(BF16)
+    gi = lax.broadcasted_iota(jnp.int32, (rows, rows), 0)
+    gj = lax.broadcasted_iota(jnp.int32, (rows, rows), 1)
+    group = jnp.where(jnp.bitwise_xor(gi, gj) < HALF, 1.0, 0.0).astype(BF16)
+    coef = dot(jnp.concatenate([group, group], axis=1), jnp.concatenate([e_hi, e_lo], axis=0))
+    w = (coef * s_ref[...]).astype(BF16)
+    pi = lax.broadcasted_iota(jnp.int32, (wide, cols), 0)
+    pj = lax.broadcasted_iota(jnp.int32, (wide, cols), 1)
+    ahead = pj - pi * HALF
+    repeat = jnp.where(jnp.logical_and(ahead >= 0, ahead < HALF), 1.0, 0.0).astype(BF16)
+    weights = (dot(w, repeat) * same_cell(rows, cols)).astype(BF16)
     w_ref[...] = weights
     for q in range(reach):
         here = plane_rows(q, ny)
@@ -334,8 +334,8 @@
         "prepare",
         (
             struct((BOX - 1, cols, ny // HALF * nz), BF16),
-            struct((bands, cols)),
-            struct((1, cols)),
+            struct((atoms * npj, bands * HALF)),
+            struct((1, nz)),
         ),
         (atom_planes, strengths.T, half, projectors),
         in_specs=[sm, sm, vm, vm],

time: 42.7 us -> 43.2 us (1.012)
  transfers between devices with their start and end apart: 9 -> 9, of which waited for: 4 -> 4; matrix products, arithmetic and copies ran while one was open for 0% -> 0% of each run, Pallas kernels for 15% -> 16%
where the time goes in v19:
time: 43.2 us; the launch traced here: 43.1 us
  starting transfers between devices  12.4 us (29%)
  blocking collectives  11.3 us (26%)
  waiting for transfers between devices  9.17 us (21%)
  Pallas kernels  7.66 us (18%)
  local copies, waits for them, and re-layouts  1.32 us (3%)
  between operations  0.8 us (2%)
    all_to_all x1, blocking collectives, shards(): got = lax.all_to_all(pieces, ('space', 'band'), 0, 0)  11.3 us
    ppermute x6, starting transfers between devices, mirrored(): return lax.ppermute(value, axis, [(i, i ^ bits) for i in range(count)])  8.9 us
    pallas_call x10, Pallas kernels, call(): pl.pallas_call(kernel, out_shape=out_shape, compiler_params=params(vmem *...  7.66 us
    ppermute x3, waiting for transfers between devices, cyclic(): lax.ppermute(value, axis, [(i, (i + steps) % count) for i in range(count)])  5.11 us
    ppermute x6, waiting for transfers between devices, mirrored(): return lax.ppermute(value, axis, [(i, i ^ bits) for i in range(count)])  4.06 us
    ppermute x3, starting transfers between devices, cyclic(): lax.ppermute(value, axis, [(i, (i + steps) % count) for i in range(count)])  3.5 us
    unnamed x14, local copies, waits for them, and re-layouts  1.16 us
  transfers between devices with their start and end apart: 9, of which 4 were waited for; matrix products, arithmetic and copies ran while one was open for 0% of the time, Pallas kernels for 16%

profile of v19, /device:TPU:0, one launch (start us, length us, event | category | flops | bytes accessed | tf_op | source)
XLA Modules:
  0.0 43.1 jit_solution(5118326305803787924)
XLA Ops:
  0.6 0.0 copy-start
  0.6 1.1 %copy-done = f32[8,6,32,128]{3,2,1,0:T(8,128)S(1)} copy-done((f32[8,6,32,128]{3,2,1,0:T(8,128)S(1)}, f32[8,6,32,128]{3,2,1,0:T(8,128)}, u32[]{:S(2)}) %copy-start) | copy-done | bytes 786456
  1.8 0.0 copy-start.2
  1.8 0.0 copy-start.5
  1.8 0.0 copy-start.6
  1.8 3.4 %collective-permute-start = (bf16[8,192,128]{2,1,0:T(8,128)(2,1)S(1)}, bf16[8,192,128]{2,1,0:T(8,128)(2,1)S(1)}, u32[]{:S(2)}, u32[]{:S(2)}) collective-permute-start(bf16[8,192,128]{2,1,0:T(8,128)(2,1)S(1)} %cast.1.own_ref), channel_id=1, source_target_pairs={{0,28},{4,0},{8,4},{12,8},{16,12},{20,16},{24,20},{28,24},{1,29},{... | collective-permute-start | bytes 1179656 | tf_op jit(solution)/shard_map/ppermute | solution.py:280
  5.3 1.6 %collective-permute-start.1 = (bf16[8,48,128]{2,1,0:T(8,128)(2,1)S(1)}, bf16[8,48,128]{2,1,0:T(8,128)(2,1)S(1)}, u32[]{:S(2)}, u32[]{:S(2)}) collective-permute-start(bf16[8,48,128]{2,1,0:T(8,128)(2,1)S(1)} %get-tuple-element.25), channel_id=1, source_target_pairs={{0,1},{1,0},{2,3},{3,2},{4,5},{5,4},{6,7},{7,6},{8,9},{9,8},{10,11... | collective-permute-start | bytes 294920 | tf_op jit(solution)/shard_map/ppermute | solution.py:285
  6.9 2.6 %collective-permute-start.4 = (bf16[8,48,128]{2,1,0:T(8,128)(2,1)S(1)}, bf16[8,48,128]{2,1,0:T(8,128)(2,1)S(1)}, u32[]{:S(2)}, u32[]{:S(2)}) collective-permute-start(bf16[8,48,128]{2,1,0:T(8,128)(2,1)S(1)} %get-tuple-element.30), channel_id=1, source_target_pairs={{0,2},{1,3},{2,0},{3,1},{4,6},{5,7},{6,4},{7,5},{8,10},{9,11},{10,... | collective-permute-start | bytes 294920 | tf_op jit(solution)/shard_map/ppermute | solution.py:285
  9.5 0.2 collective-permute-start.5
  9.7 0.0 copy-done.2
  9.7 0.0 copy-done.5
  9.7 0.0 copy-done.6
  9.7 0.0 copy-start.1
  9.7 1.5 %prepare.1 = (bf16[5,576,256]{2,1,0:T(8,128)(2,1)S(1)}, f32[36,128]{1,0:T(8,128)S(1)}, f32[1,128]{1,0:T(1,128)S(1)}) custom-call(s32[32]{0:T(128)S(1)} %copy-done.6, f32[9,32]{1,0:T(8,128)S(1)} %bitcast.19, bf16[8,192,128]{2,1,0:T(8,128)(2,1)S(1)} %cast.1.own_ref, bf16[4,9,6,32,128]{4,3,2,1,0:T(8,128)(2,1)S(1)} %copy-done.2), custom_call_target="tpu_custom_call" | custom-call | flops 1000000000 | bytes 1048576 | tf_op jit(solution)/shard_map/prepare/pallas_call | solution.py:298
  11.2 0.0 collective-permute-done.1.refs_0_.rest_0_
  11.2 0.0 copy-done.1
  11.2 0.2 ahead.1
  11.4 0.1 collective-permute-start.3
  11.5 0.0 collective-permute-done.upper_ref
  11.5 0.0 copy-start.3
  11.5 0.0 copy-start.4
  11.5 1.8 %coefficients.1 = (bf16[128,576]{1,0:T(8,128)(2,1)S(1)}, bf16[8,160,128]{2,1,0:T(8,128)(2,1)S(1)}) custom-call(bf16[8,192,128]{2,1,0:T(8,128)(2,1)S(1)} %collective-permute-done.upper_ref, bf16[5,576,256]{2,1,0:T(8,128)(2,1)S(1)} %get-tuple-element.22.table_ref, f32[36,128]{1,0:T(8,128)S(1)} %get-tuple-element.23.e_ref, ...), custom_call_target="tpu_custom_call" | custom-call | flops 1000000000 | bytes 1048576 | tf_op jit(solution)/shard_map/coefficients/pallas_call | solution.py:298
  13.4 0.1 collective-permute-start.2
  13.4 0.0 copy-done.3
  13.4 0.0 copy-done.4
  13.4 2.2 %near_part.1.g_ref = f32[8,192,128]{2,1,0:T(8,128)S(1)} custom-call(s32[32]{0:T(128)S(1)} %copy-done.6, f32[8,192,128]{2,1,0:T(8,128)S(1)} %bitcast.15, f32[8,192,128]{2,1,0:T(8,128)S(1)} %bitcast.17, f32[192,128]{1,0:T(8,128)S(1)} %bitcast.18, bf16[128,576]{1,0:T(8,128)(2,1)S(1)} %get-tuple-element.27.w_ref, ...), custom_call_target="tpu_custom_call" | custom-call | flops 20000000000 | bytes 4194304 | tf_op jit(solution)/shard_map/near_part/pallas_call | solution.py:298
  15.7 0.4 collective-permute-done.3.below_ref
  16.1 4.7 %collective-permute-done.2.arrived_ref = bf16[8,160,128]{2,1,0:T(8,128)(2,1)S(1)} collective-permute-done((bf16[8,160,128]{2,1,0:T(8,128)(2,1)S(1)}, bf16[8,160,128]{2,1,0:T(8,128)(2,1)S(1)}, u32[]{:S(2)}, u32[]{:S(2)}) %collective-permute-start.2) | collective-permute-done | bytes 327712 | tf_op jit(solution)/shard_map/ppermute | solution.py:280
  20.8 0.1 finish.1
  20.9 3.7 %collective-permute-start.6 = (bf16[8,48,128]{2,1,0:T(8,128)(2,1)S(1)}, bf16[8,48,128]{2,1,0:T(8,128)(2,1)S(1)}, u32[]{:S(2)}, u32[]{:S(2)}) collective-permute-start(bf16[8,48,128]{2,1,0:T(8,128)(2,1)S(1)} %get-tuple-element.35), channel_id=1, source_target_pairs={{0,3},{1,2},{2,1},{3,0},{4,7},{5,6},{6,5},{7,4},{8,11},{9,10},{10,... | collective-permute-start | bytes 294920 | tf_op jit(solution)/shard_map/ppermute | solution.py:285
  24.6 0.0 collective-permute-start.7
  24.6 0.8 %collective-permute-start.8 = (bf16[8,48,128]{2,1,0:T(8,128)(2,1)S(1)}, bf16[8,48,128]{2,1,0:T(8,128)(2,1)S(1)}, u32[]{:S(2)}, u32[]{:S(2)}) collective-permute-start(bf16[8,48,128]{2,1,0:T(8,128)(2,1)S(1)} %get-tuple-element.37), channel_id=1, source_target_pairs={{0,1},{1,0},{2,3},{3,2},{4,5},{5,4},{6,7},{7,6},{8,9},{9,8},{10,11... | collective-permute-start | bytes 294920 | tf_op jit(solution)/shard_map/ppermute | solution.py:285
  25.4 0.0 collective-permute-done.4.rest_1_
  25.4 0.0 collective-permute-done.5.rest_2_
  25.4 0.8 %output.1 = (bf16[8,192,128]{2,1,0:T(8,128)(2,1)}, bf16[32,48,128]{2,1,0:T(8,128)(2,1)S(1)}) custom-call(f32[8,192,128]{2,1,0:T(8,128)S(1)} %near_part.1.g_ref, bf16[8,160,128]{2,1,0:T(8,128)(2,1)S(1)} %collective-permute-done.2.arrived_ref, bf16[8,32,128]{2,1,0:T(8,128)(2,1)S(1)} %collective-permute-done.3.below_ref, ...), custom_call_target="tpu_custom_call" | custom-call | tf_op jit(solution)/shard_map/output/pallas_call | solution.py:298
  26.2 1.6 %collective-permute-done.6 = bf16[8,48,128]{2,1,0:T(8,128)(2,1)S(1)} collective-permute-done((bf16[8,48,128]{2,1,0:T(8,128)(2,1)S(1)}, bf16[8,48,128]{2,1,0:T(8,128)(2,1)S(1)}, u32[]{:S(2)}, u32[]{:S(2)}) %collective-permute-start.6) | collective-permute-done | bytes 98336 | tf_op jit(solution)/shard_map/ppermute | solution.py:285
  27.9 2.4 %collective-permute-done.7 = bf16[8,48,128]{2,1,0:T(8,128)(2,1)S(1)} collective-permute-done((bf16[8,48,128]{2,1,0:T(8,128)(2,1)S(1)}, bf16[8,48,128]{2,1,0:T(8,128)(2,1)S(1)}, u32[]{:S(2)}, u32[]{:S(2)}) %collective-permute-start.7) | collective-permute-done | bytes 98336 | tf_op jit(solution)/shard_map/ppermute | solution.py:285
  30.2 0.0 collective-permute-done.8
  30.3 0.1 pad_maximum_fusion
  30.4 0.2 copy_bitcast_fusion
  30.5 0.3 convolution_multiply_fusion.prod_ref
  30.8 0.2 split.1
  31.0 11.3 %all_to_all.5.got_ref = f32[32,1,64]{2,1,0:T(1,128)S(1)} all-to-all(f32[32,1,64]{2,1,0:T(1,128)S(1)} %split.1), channel_id=1, replica_groups=mesh['space'=8,'band'=4] {'space','band'}, dimensions={0} | all-to-all | bytes 16384 | tf_op jit(solution)/shard_map/all_to_all | solution.py:401
  42.4 0.7 %last_sum.1 = (f32[4,8]{1,0:T(4,128)}, f32[4,8]{1,0:T(4,128)}) custom-call(f32[32,1,64]{2,1,0:T(1,128)S(1)} %all_to_all.5.got_ref), custom_call_target="tpu_custom_call" | custom-call | tf_op jit(solution)/shard_map/last_sum/pallas_call | solution.py:298
  (2 shorter events, 0.1 us)
Async XLA Ops:
  0.6 1.1 %copy-start = (f32[8,6,32,128]{3,2,1,0:T(8,128)S(1)}, f32[8,6,32,128]{3,2,1,0:T(8,128)}, u32[]{:S(2)}) copy-start(f32[8,6,32,128]{3,2,1,0:T(8,128)} %param.6) | copy-start | bytes 2359300
  1.8 7.9 %copy-start.2 = (bf16[4,9,6,32,128]{4,3,2,1,0:T(8,128)(2,1)S(1)}, bf16[4,9,6,32,128]{4,3,2,1,0:T(8,128)(2,1)}, u32[]{:S(2)}) copy-start(bf16[4,9,6,32,128]{4,3,2,1,0:T(8,128)(2,1)} %proj_ref.3) | copy-start | bytes 5308420
  1.8 7.9 %copy-start.5 = (f32[32,9]{0,1:T(8,128)S(1)}, f32[32,9]{0,1:T(8,128)}, u32[]{:S(2)}) copy-start(f32[32,9]{0,1:T(8,128)} %param.10) | copy-start | bytes 3460
  1.8 7.9 %copy-start.6 = (s32[32]{0:T(128)S(1)}, s32[32]{0:T(128)}, u32[]{:S(2)}) copy-start(s32[32]{0:T(128)} %first_ref.3) | copy-start | bytes 388
  1.8 9.6 %collective-permute-start = (bf16[8,192,128]{2,1,0:T(8,128)(2,1)S(1)}, bf16[8,192,128]{2,1,0:T(8,128)(2,1)S(1)}, u32[]{:S(2)}, u32[]{:S(2)}) collective-permute-start(bf16[8,192,128]{2,1,0:T(8,128)(2,1)S(1)} %cast.1.own_ref), channel_id=1, source_target_pairs={{0,28},{4,0},{8,4},{12,8},{16,12},{20,16},{24,20},{28,24},{1,29},{... | collective-permute-start | bytes 1179656 | tf_op jit(solution)/shard_map/ppermute | solution.py:280
  5.3 5.9 %collective-permute-start.1 = (bf16[8,48,128]{2,1,0:T(8,128)(2,1)S(1)}, bf16[8,48,128]{2,1,0:T(8,128)(2,1)S(1)}, u32[]{:S(2)}, u32[]{:S(2)}) collective-permute-start(bf16[8,48,128]{2,1,0:T(8,128)(2,1)S(1)} %get-tuple-element.25), channel_id=1, source_target_pairs={{0,1},{1,0},{2,3},{3,2},{4,5},{5,4},{6,7},{7,6},{8,9},{9,8},{10,11... | collective-permute-start | bytes 294920 | tf_op jit(solution)/shard_map/ppermute | solution.py:285
  6.9 18.5 %collective-permute-start.4 = (bf16[8,48,128]{2,1,0:T(8,128)(2,1)S(1)}, bf16[8,48,128]{2,1,0:T(8,128)(2,1)S(1)}, u32[]{:S(2)}, u32[]{:S(2)}) collective-permute-start(bf16[8,48,128]{2,1,0:T(8,128)(2,1)S(1)} %get-tuple-element.30), channel_id=1, source_target_pairs={{0,2},{1,3},{2,0},{3,1},{4,6},{5,7},{6,4},{7,5},{8,10},{9,11},{10,... | collective-permute-start | bytes 294920 | tf_op jit(solution)/shard_map/ppermute | solution.py:285
  9.5 15.9 %collective-permute-start.5 = (bf16[8,48,128]{2,1,0:T(8,128)(2,1)S(1)}, bf16[8,48,128]{2,1,0:T(8,128)(2,1)S(1)}, u32[]{:S(2)}, u32[]{:S(2)}) collective-permute-start(bf16[8,48,128]{2,1,0:T(8,128)(2,1)S(1)} %get-tuple-element.31), channel_id=1, source_target_pairs={{0,3},{1,2},{2,1},{3,0},{4,7},{5,6},{6,5},{7,4},{8,11},{9,10},{10,... | collective-permute-start | bytes 294920 | tf_op jit(solution)/shard_map/ppermute | solution.py:285
  9.7 1.5 %copy-start.1 = (f32[8,6,32,128]{3,2,1,0:T(8,128)S(1)}, f32[8,6,32,128]{3,2,1,0:T(8,128)}, u32[]{:S(2)}) copy-start(f32[8,6,32,128]{3,2,1,0:T(8,128)} %param.6) | copy-start | bytes 2359300
  11.4 4.6 %collective-permute-start.3 = (bf16[8,32,128]{2,1,0:T(8,128)(2,1)S(1)}, bf16[8,32,128]{2,1,0:T(8,128)(2,1)S(1)}, u32[]{:S(2)}, u32[]{:S(2)}) collective-permute-start(bf16[8,32,128]{2,1,0:T(8,128)(2,1)S(1)} %get-tuple-element.29), channel_id=1, source_target_pairs={{0,4},{4,8},{8,12},{12,16},{16,20},{20,24},{24,28},{28,0},{1,5},{5... | collective-permute-start | bytes 196616 | tf_op jit(solution)/shard_map/ppermute | solution.py:280
  11.5 1.9 %copy-start.3 = (f32[8,6,32,128]{3,2,1,0:T(8,128)S(1)}, f32[8,6,32,128]{3,2,1,0:T(8,128)}, u32[]{:S(2)}) copy-start(f32[8,6,32,128]{3,2,1,0:T(8,128)} %param.7) | copy-start | bytes 2359300
  11.5 1.9 %copy-start.4 = (f32[6,32,128]{2,1,0:T(8,128)S(1)}, f32[6,32,128]{2,1,0:T(8,128)}, u32[]{:S(2)}) copy-start(f32[6,32,128]{2,1,0:T(8,128)} %param.8) | copy-start | bytes 294916
  13.4 7.5 %collective-permute-start.2 = (bf16[8,160,128]{2,1,0:T(8,128)(2,1)S(1)}, bf16[8,160,128]{2,1,0:T(8,128)(2,1)S(1)}, u32[]{:S(2)}, u32[]{:S(2)}) collective-permute-start(bf16[8,160,128]{2,1,0:T(8,128)(2,1)S(1)} %get-tuple-element.28), channel_id=1, source_target_pairs={{0,4},{4,8},{8,12},{12,16},{16,20},{20,24},{24,28},{28,0},{1,5},{5... | collective-permute-start | bytes 983048 | tf_op jit(solution)/shard_map/ppermute | solution.py:280
  20.9 6.9 %collective-permute-start.6 = (bf16[8,48,128]{2,1,0:T(8,128)(2,1)S(1)}, bf16[8,48,128]{2,1,0:T(8,128)(2,1)S(1)}, u32[]{:S(2)}, u32[]{:S(2)}) collective-permute-start(bf16[8,48,128]{2,1,0:T(8,128)(2,1)S(1)} %get-tuple-element.35), channel_id=1, source_target_pairs={{0,3},{1,2},{2,1},{3,0},{4,7},{5,6},{6,5},{7,4},{8,11},{9,10},{10,... | collective-permute-start | bytes 294920 | tf_op jit(solution)/shard_map/ppermute | solution.py:285
  24.6 5.6 %collective-permute-start.7 = (bf16[8,48,128]{2,1,0:T(8,128)(2,1)S(1)}, bf16[8,48,128]{2,1,0:T(8,128)(2,1)S(1)}, u32[]{:S(2)}, u32[]{:S(2)}) collective-permute-start(bf16[8,48,128]{2,1,0:T(8,128)(2,1)S(1)} %get-tuple-element.36), channel_id=1, source_target_pairs={{0,2},{1,3},{2,0},{3,1},{4,6},{5,7},{6,4},{7,5},{8,10},{9,11},{10,... | collective-permute-start | bytes 294920 | tf_op jit(solution)/shard_map/ppermute | solution.py:285
  24.6 5.7 %collective-permute-start.8 = (bf16[8,48,128]{2,1,0:T(8,128)(2,1)S(1)}, bf16[8,48,128]{2,1,0:T(8,128)(2,1)S(1)}, u32[]{:S(2)}, u32[]{:S(2)}) collective-permute-start(bf16[8,48,128]{2,1,0:T(8,128)(2,1)S(1)} %get-tuple-element.37), channel_id=1, source_target_pairs={{0,1},{1,0},{2,3},{3,2},{4,5},{5,4},{6,7},{7,6},{8,9},{9,8},{10,11... | collective-permute-start | bytes 294920 | tf_op jit(solution)/shard_map/ppermute | solution.py:285

commit v20 on v18

--- a/solution.py
+++ b/solution.py
@@ -162,8 +162,7 @@
     e_ref[...] = overlap(own_ref, [plane_table(proj_ref, starts, q) for q in range(planes)], ny)
 
 
-def ahead_kernel(planes, psi_ref, *refs):
-    ahead_ref, edge_ref = refs[-2:]
+def ahead_kernel(planes, psi_ref, ahead_ref, edge_ref):
     ny = psi_ref.shape[1] // planes
     edge_ref[...] = psi_ref[:, plane_rows(planes - 1, ny)].astype(BF16)
     for x in range(planes - 1):
@@ -201,9 +200,8 @@
         next_ref[:, here] = block.astype(BF16)
 
 
-def near_kernel(
-    planes, first_ref, psi_ref, prev_ref, pot_ref, w_ref, upper_ref, proj_ref, out_ref
-):
+def near_kernel(planes, unused, first_ref, *refs):
+    psi_ref, prev_ref, pot_ref, w_ref, upper_ref, proj_ref, out_ref = refs[unused:]
     bands, cells, nz = psi_ref.shape
     ny = cells // planes
     weights = w_ref[...]
@@ -241,11 +239,15 @@
     pieces_of(total, lax.axis_index("band"), count, rows, outs)
 
 
+def panel_order(count):
+    return [*range(1, count), 0]
+
+
 def output_kernel(g_ref, arrived_ref, below_ref, *rest):
     pieces, (out_ref, panel_ref) = rest[:-2], rest[-2:]
     complete(g_ref, arrived_ref, below_ref, out_ref)
     bands = g_ref.shape[0]
-    for p, piece in enumerate(reversed(pieces)):
+    for p, piece in zip(panel_order(len(pieces)), pieces):
         panel_ref[p * bands : (p + 1) * bands] = piece[...]
 
 
@@ -327,6 +329,14 @@
     )
     upper = cyclic(half, "space", -1)
     panel = exchanged(panel)
+    ahead, edge = call(
+        partial(ahead_kernel, planes),
+        "ahead",
+        (struct(most), struct(plane, BF16)),
+        (psi,),
+        cost_estimate=pl.CostEstimate(flops=10**9, bytes_accessed=2**20, transcendentals=0),
+    )
+    below = cyclic(edge, "space", 1)
     atoms, npj = projectors.shape[:2]
     cols = atoms * npj * HALF
     far_tables, e, s = call(
@@ -342,16 +352,6 @@
         out_specs=(vm,) * 3,
         cost_estimate=pl.CostEstimate(flops=10**9, bytes_accessed=2**20, transcendentals=0),
     )
-    ahead, edge = call(
-        partial(ahead_kernel, planes),
-        "ahead",
-        (struct(most), struct(plane, BF16)),
-        (psi, panel[3], s),
-        in_specs=[vm, anywhere, anywhere],
-        out_specs=(vm, vm),
-        cost_estimate=pl.CostEstimate(flops=10**9, bytes_accessed=2**20, transcendentals=0),
-    )
-    below = cyclic(edge, "space", 1)
     w, beyond = call(
         partial(coefficient_kernel, planes),
         "coefficients",
@@ -361,11 +361,11 @@
     )
     arrived = cyclic(beyond, "space", 1)
     g = call(
-        partial(near_kernel, planes),
+        partial(near_kernel, planes, 1),
         "near_part",
         struct(whole),
-        (atom_planes, psi, prev, pot, w, upper, projectors),
-        in_specs=[sm] + [vm] * 6,
+        (atom_planes, panel[1], psi, prev, pot, w, upper, projectors),
+        in_specs=[sm] + [anywhere] * 1 + [vm] * 6,
         out_specs=vm,
         cost_estimate=pl.CostEstimate(flops=2*10**10, bytes_accessed=4 * 2**20, transcendentals=0),
     )
@@ -382,7 +382,7 @@
         output_kernel,
         "output",
         (struct(whole, BF16), struct((total_bands, *quarter[1:]), BF16)),
-        (g, arrived, below, *reversed(panel)),
+        (g, arrived, below, *[panel[p] for p in panel_order(n_band)]),
     )
     left = jnp.concatenate(mine, axis=0).reshape(total_bands, -1)
     right = jnp.concatenate([left, panels.reshape(total_bands, -1)], axis=0)

time: 42.7 us -> 43.1 us (level)
  transfers between devices with their start and end apart: 9 -> 9, of which waited for: 4 -> 3; matrix products, arithmetic and copies ran while one was open for 0% -> 0% of each run, Pallas kernels for 15% -> 15%
where the time goes in v20:
time: 43.1 us; the launch traced here: 43 us
  starting transfers between devices  12.5 us (29%)
  blocking collectives  11.6 us (27%)
  waiting for transfers between devices  9.15 us (21%)
  Pallas kernels  7.23 us (17%)
  local copies, waits for them, and re-layouts  1.32 us (3%)
  between operations  0.81 us (2%)
    all_to_all x1, blocking collectives, shards(): got = lax.all_to_all(pieces, ('space', 'band'), 0, 0)  11.6 us
    ppermute x6, starting transfers between devices, mirrored(): return lax.ppermute(value, axis, [(i, i ^ bits) for i in range(count)])  8.96 us
    pallas_call x10, Pallas kernels, call(): pl.pallas_call(kernel, out_shape=out_shape, compiler_params=params(vmem *...  7.23 us
    ppermute x3, waiting for transfers between devices, cyclic(): lax.ppermute(value, axis, [(i, (i + steps) % count) for i in range(count)])  5.09 us
    ppermute x6, waiting for transfers between devices, mirrored(): return lax.ppermute(value, axis, [(i, i ^ bits) for i in range(count)])  4.06 us
    ppermute x3, starting transfers between devices, cyclic(): lax.ppermute(value, axis, [(i, (i + steps) % count) for i in range(count)])  3.5 us
    unnamed x14, local copies, waits for them, and re-layouts  1.17 us
  transfers between devices with their start and end apart: 9, of which 3 were waited for; matrix products, arithmetic and copies ran while one was open for 0% of the time, Pallas kernels for 15%

profile of v20, /device:TPU:0, one launch (start us, length us, event | category | flops | bytes accessed | tf_op | source)
XLA Modules:
  0.0 43.0 jit_solution(16003784506183651968)
XLA Ops:
  0.6 0.0 copy-start
  0.6 1.1 %copy-done = f32[8,6,32,128]{3,2,1,0:T(8,128)S(1)} copy-done((f32[8,6,32,128]{3,2,1,0:T(8,128)S(1)}, f32[8,6,32,128]{3,2,1,0:T(8,128)}, u32[]{:S(2)}) %copy-start) | copy-done | bytes 786456
  1.8 3.4 %collective-permute-start.1 = (bf16[8,192,128]{2,1,0:T(8,128)(2,1)S(1)}, bf16[8,192,128]{2,1,0:T(8,128)(2,1)S(1)}, u32[]{:S(2)}, u32[]{:S(2)}) collective-permute-start(bf16[8,192,128]{2,1,0:T(8,128)(2,1)S(1)} %cast.1.own_ref), channel_id=1, source_target_pairs={{0,28},{4,0},{8,4},{12,8},{16,12},{20,16},{24,20},{28,24},{1,29},{... | collective-permute-start | bytes 1179656 | tf_op jit(solution)/shard_map/ppermute | solution.py:282
  5.2 0.0 copy-start.2
  5.3 0.0 copy-start.5
  5.3 0.0 copy-start.6
  5.3 3.7 %collective-permute-start = (bf16[8,48,128]{2,1,0:T(8,128)(2,1)S(1)}, bf16[8,48,128]{2,1,0:T(8,128)(2,1)S(1)}, u32[]{:S(2)}, u32[]{:S(2)}) collective-permute-start(bf16[8,48,128]{2,1,0:T(8,128)(2,1)S(1)} %get-tuple-element.22), channel_id=1, source_target_pairs={{0,3},{1,2},{2,1},{3,0},{4,7},{5,6},{6,5},{7,4},{8,11},{9,10},{10,... | collective-permute-start | bytes 294920 | tf_op jit(solution)/shard_map/ppermute | solution.py:287
  8.9 0.2 ahead.1
  9.1 0.1 collective-permute-start.3
  9.2 0.1 collective-permute-start.4
  9.3 0.8 %collective-permute-start.5 = (bf16[8,48,128]{2,1,0:T(8,128)(2,1)S(1)}, bf16[8,48,128]{2,1,0:T(8,128)(2,1)S(1)}, u32[]{:S(2)}, u32[]{:S(2)}) collective-permute-start(bf16[8,48,128]{2,1,0:T(8,128)(2,1)S(1)} %get-tuple-element.31), channel_id=1, source_target_pairs={{0,1},{1,0},{2,3},{3,2},{4,5},{5,4},{6,7},{7,6},{8,9},{9,8},{10,11... | collective-permute-start | bytes 294920 | tf_op jit(solution)/shard_map/ppermute | solution.py:287
  10.1 0.0 copy-done.2
  10.1 0.0 copy-done.5
  10.1 0.0 copy-done.6
  10.1 1.5 %prepare.1 = (bf16[5,576,256]{2,1,0:T(8,128)(2,1)S(1)}, f32[8,576]{1,0:T(8,128)S(1)}, f32[1,576]{1,0:T(1,128)S(1)}) custom-call(s32[32]{0:T(128)S(1)} %copy-done.6, f32[9,32]{1,0:T(8,128)S(1)} %bitcast.19, bf16[8,192,128]{2,1,0:T(8,128)(2,1)S(1)} %cast.1.own_ref, bf16[4,9,6,32,128]{4,3,2,1,0:T(8,128)(2,1)S(1)} %copy-done.2), custom_call_target="tpu_custom_call" | custom-call | flops 1000000000 | bytes 1048576 | tf_op jit(solution)/shard_map/prepare/pallas_call | solution.py:300
  11.6 0.0 collective-permute-done.1.upper_ref.refs_5_
  11.6 0.0 copy-start.1
  11.6 0.0 copy-start.3
  11.6 0.0 copy-start.4
  11.6 1.3 %coefficients.1 = (bf16[128,576]{1,0:T(8,128)(2,1)S(1)}, bf16[8,160,128]{2,1,0:T(8,128)(2,1)S(1)}) custom-call(bf16[8,192,128]{2,1,0:T(8,128)(2,1)S(1)} %collective-permute-done.1.upper_ref.refs_5_, bf16[5,576,256]{2,1,0:T(8,128)(2,1)S(1)} %get-tuple-element.23.table_ref, f32[8,576]{1,0:T(8,128)S(1)} %get-tuple-element.24.e_ref, ...), custom_call_target="tpu_custom_call" | custom-call | flops 1000000000 | bytes 1048576 | tf_op jit(solution)/shard_map/coefficients/pallas_call | solution.py:300
  13.0 0.1 collective-permute-start.2
  13.0 0.0 collective-permute-done.refs_0_.rest_0_
  13.0 0.0 copy-done.1
  13.1 0.0 copy-done.3
  13.1 0.0 copy-done.4
  13.1 2.2 %near_part.1.g_ref = f32[8,192,128]{2,1,0:T(8,128)S(1)} custom-call(s32[32]{0:T(128)S(1)} %copy-done.6, bf16[8,48,128]{2,1,0:T(8,128)(2,1)S(1)} %collective-permute-done.refs_0_.rest_0_, f32[8,192,128]{2,1,0:T(8,128)S(1)} %bitcast.15, f32[8,192,128]{2,1,0:T(8,128)S(1)} %bitcast.17, f32[192,128]{1,0:T(8,128)S(1)} %bitcast.18, ...), custom_call_target="tpu_custom_call" | custom-call | flops 20000000000 | bytes 4194304 | tf_op jit(solution)/shard_map/near_part/pallas_call | solution.py:300
  15.3 0.0 collective-permute-done.3.below_ref
  15.3 5.1 %collective-permute-done.2.arrived_ref = bf16[8,160,128]{2,1,0:T(8,128)(2,1)S(1)} collective-permute-done((bf16[8,160,128]{2,1,0:T(8,128)(2,1)S(1)}, bf16[8,160,128]{2,1,0:T(8,128)(2,1)S(1)}, u32[]{:S(2)}, u32[]{:S(2)}) %collective-permute-start.2) | collective-permute-done | bytes 327712 | tf_op jit(solution)/shard_map/ppermute | solution.py:282
  20.4 0.1 finish.1
  20.6 3.7 %collective-permute-start.6 = (bf16[8,48,128]{2,1,0:T(8,128)(2,1)S(1)}, bf16[8,48,128]{2,1,0:T(8,128)(2,1)S(1)}, u32[]{:S(2)}, u32[]{:S(2)}) collective-permute-start(bf16[8,48,128]{2,1,0:T(8,128)(2,1)S(1)} %get-tuple-element.35), channel_id=1, source_target_pairs={{0,3},{1,2},{2,1},{3,0},{4,7},{5,6},{6,5},{7,4},{8,11},{9,10},{10,... | collective-permute-start | bytes 294920 | tf_op jit(solution)/shard_map/ppermute | solution.py:287
  24.2 0.0 collective-permute-start.7
  24.2 0.8 %collective-permute-start.8 = (bf16[8,48,128]{2,1,0:T(8,128)(2,1)S(1)}, bf16[8,48,128]{2,1,0:T(8,128)(2,1)S(1)}, u32[]{:S(2)}, u32[]{:S(2)}) collective-permute-start(bf16[8,48,128]{2,1,0:T(8,128)(2,1)S(1)} %get-tuple-element.37), channel_id=1, source_target_pairs={{0,1},{1,0},{2,3},{3,2},{4,5},{5,4},{6,7},{7,6},{8,9},{9,8},{10,11... | collective-permute-start | bytes 294920 | tf_op jit(solution)/shard_map/ppermute | solution.py:287
  25.0 0.0 collective-permute-done.4.rest_1_
  25.0 0.0 collective-permute-done.5.rest_2_
  25.0 0.8 %output.1 = (bf16[8,192,128]{2,1,0:T(8,128)(2,1)}, bf16[32,48,128]{2,1,0:T(8,128)(2,1)S(1)}) custom-call(f32[8,192,128]{2,1,0:T(8,128)S(1)} %near_part.1.g_ref, bf16[8,160,128]{2,1,0:T(8,128)(2,1)S(1)} %collective-permute-done.2.arrived_ref, bf16[8,32,128]{2,1,0:T(8,128)(2,1)S(1)} %collective-permute-done.3.below_ref, ...), custom_call_target="tpu_custom_call" | custom-call | tf_op jit(solution)/shard_map/output/pallas_call | solution.py:300
  25.9 1.4 %collective-permute-done.6 = bf16[8,48,128]{2,1,0:T(8,128)(2,1)S(1)} collective-permute-done((bf16[8,48,128]{2,1,0:T(8,128)(2,1)S(1)}, bf16[8,48,128]{2,1,0:T(8,128)(2,1)S(1)}, u32[]{:S(2)}, u32[]{:S(2)}) %collective-permute-start.6) | collective-permute-done | bytes 98336 | tf_op jit(solution)/shard_map/ppermute | solution.py:287
  27.2 2.6 %collective-permute-done.7 = bf16[8,48,128]{2,1,0:T(8,128)(2,1)S(1)} collective-permute-done((bf16[8,48,128]{2,1,0:T(8,128)(2,1)S(1)}, bf16[8,48,128]{2,1,0:T(8,128)(2,1)S(1)}, u32[]{:S(2)}, u32[]{:S(2)}) %collective-permute-start.7) | collective-permute-done | bytes 98336 | tf_op jit(solution)/shard_map/ppermute | solution.py:287
  29.9 0.0 collective-permute-done.8
  29.9 0.1 pad_maximum_fusion
  30.0 0.2 copy_bitcast_fusion
  30.1 0.3 convolution_multiply_fusion.prod_ref
  30.5 0.2 split.1
  30.7 11.6 %all_to_all.5.got_ref = f32[32,1,64]{2,1,0:T(1,128)S(1)} all-to-all(f32[32,1,64]{2,1,0:T(1,128)S(1)} %split.1), channel_id=1, replica_groups=mesh['space'=8,'band'=4] {'space','band'}, dimensions={0} | all-to-all | bytes 16384 | tf_op jit(solution)/shard_map/all_to_all | solution.py:401
  42.3 0.7 %last_sum.1 = (f32[4,8]{1,0:T(4,128)}, f32[4,8]{1,0:T(4,128)}) custom-call(f32[32,1,64]{2,1,0:T(1,128)S(1)} %all_to_all.5.got_ref), custom_call_target="tpu_custom_call" | custom-call | tf_op jit(solution)/shard_map/last_sum/pallas_call | solution.py:300
  (2 shorter events, 0.1 us)
Async XLA Ops:
  0.6 1.1 %copy-start = (f32[8,6,32,128]{3,2,1,0:T(8,128)S(1)}, f32[8,6,32,128]{3,2,1,0:T(8,128)}, u32[]{:S(2)}) copy-start(f32[8,6,32,128]{3,2,1,0:T(8,128)} %param.6) | copy-start | bytes 2359300
  1.8 9.8 %collective-permute-start.1 = (bf16[8,192,128]{2,1,0:T(8,128)(2,1)S(1)}, bf16[8,192,128]{2,1,0:T(8,128)(2,1)S(1)}, u32[]{:S(2)}, u32[]{:S(2)}) collective-permute-start(bf16[8,192,128]{2,1,0:T(8,128)(2,1)S(1)} %cast.1.own_ref), channel_id=1, source_target_pairs={{0,28},{4,0},{8,4},{12,8},{16,12},{20,16},{24,20},{28,24},{1,29},{... | collective-permute-start | bytes 1179656 | tf_op jit(solution)/shard_map/ppermute | solution.py:282
  5.2 4.8 %copy-start.2 = (bf16[4,9,6,32,128]{4,3,2,1,0:T(8,128)(2,1)S(1)}, bf16[4,9,6,32,128]{4,3,2,1,0:T(8,128)(2,1)}, u32[]{:S(2)}) copy-start(bf16[4,9,6,32,128]{4,3,2,1,0:T(8,128)(2,1)} %refs_6_.1) | copy-start | bytes 5308420
  5.3 4.8 %copy-start.5 = (f32[32,9]{0,1:T(8,128)S(1)}, f32[32,9]{0,1:T(8,128)}, u32[]{:S(2)}) copy-start(f32[32,9]{0,1:T(8,128)} %param.10) | copy-start | bytes 3460
  5.3 4.8 %copy-start.6 = (s32[32]{0:T(128)S(1)}, s32[32]{0:T(128)}, u32[]{:S(2)}) copy-start(s32[32]{0:T(128)} %first_ref.3) | copy-start | bytes 388
  5.3 7.8 %collective-permute-start = (bf16[8,48,128]{2,1,0:T(8,128)(2,1)S(1)}, bf16[8,48,128]{2,1,0:T(8,128)(2,1)S(1)}, u32[]{:S(2)}, u32[]{:S(2)}) collective-permute-start(bf16[8,48,128]{2,1,0:T(8,128)(2,1)S(1)} %get-tuple-element.22), channel_id=1, source_target_pairs={{0,3},{1,2},{2,1},{3,0},{4,7},{5,6},{6,5},{7,4},{8,11},{9,10},{10,... | collective-permute-start | bytes 294920 | tf_op jit(solution)/shard_map/ppermute | solution.py:287
  9.1 6.2 %collective-permute-start.3 = (bf16[8,32,128]{2,1,0:T(8,128)(2,1)S(1)}, bf16[8,32,128]{2,1,0:T(8,128)(2,1)S(1)}, u32[]{:S(2)}, u32[]{:S(2)}) collective-permute-start(bf16[8,32,128]{2,1,0:T(8,128)(2,1)S(1)} %get-tuple-element.29), channel_id=1, source_target_pairs={{0,4},{4,8},{8,12},{12,16},{16,20},{20,24},{24,28},{28,0},{1,5},{5... | collective-permute-start | bytes 196616 | tf_op jit(solution)/shard_map/ppermute | solution.py:282
  9.2 15.8 %collective-permute-start.4 = (bf16[8,48,128]{2,1,0:T(8,128)(2,1)S(1)}, bf16[8,48,128]{2,1,0:T(8,128)(2,1)S(1)}, u32[]{:S(2)}, u32[]{:S(2)}) collective-permute-start(bf16[8,48,128]{2,1,0:T(8,128)(2,1)S(1)} %get-tuple-element.30), channel_id=1, source_target_pairs={{0,2},{1,3},{2,0},{3,1},{4,6},{5,7},{6,4},{7,5},{8,10},{9,11},{10,... | collective-permute-start | bytes 294920 | tf_op jit(solution)/shard_map/ppermute | solution.py:287
  9.3 15.7 %collective-permute-start.5 = (bf16[8,48,128]{2,1,0:T(8,128)(2,1)S(1)}, bf16[8,48,128]{2,1,0:T(8,128)(2,1)S(1)}, u32[]{:S(2)}, u32[]{:S(2)}) collective-permute-start(bf16[8,48,128]{2,1,0:T(8,128)(2,1)S(1)} %get-tuple-element.31), channel_id=1, source_target_pairs={{0,1},{1,0},{2,3},{3,2},{4,5},{5,4},{6,7},{7,6},{8,9},{9,8},{10,11... | collective-permute-start | bytes 294920 | tf_op jit(solution)/shard_map/ppermute | solution.py:287
  11.6 1.4 %copy-start.1 = (f32[8,6,32,128]{3,2,1,0:T(8,128)S(1)}, f32[8,6,32,128]{3,2,1,0:T(8,128)}, u32[]{:S(2)}) copy-start(f32[8,6,32,128]{3,2,1,0:T(8,128)} %param.6) | copy-start | bytes 2359300
  11.6 1.4 %copy-start.3 = (f32[8,6,32,128]{3,2,1,0:T(8,128)S(1)}, f32[8,6,32,128]{3,2,1,0:T(8,128)}, u32[]{:S(2)}) copy-start(f32[8,6,32,128]{3,2,1,0:T(8,128)} %param.7) | copy-start | bytes 2359300
  11.6 1.4 %copy-start.4 = (f32[6,32,128]{2,1,0:T(8,128)S(1)}, f32[6,32,128]{2,1,0:T(8,128)}, u32[]{:S(2)}) copy-start(f32[6,32,128]{2,1,0:T(8,128)} %param.8) | copy-start | bytes 294916
  13.0 7.5 %collective-permute-start.2 = (bf16[8,160,128]{2,1,0:T(8,128)(2,1)S(1)}, bf16[8,160,128]{2,1,0:T(8,128)(2,1)S(1)}, u32[]{:S(2)}, u32[]{:S(2)}) collective-permute-start(bf16[8,160,128]{2,1,0:T(8,128)(2,1)S(1)} %get-tuple-element.28), channel_id=1, source_target_pairs={{0,4},{4,8},{8,12},{12,16},{16,20},{20,24},{24,28},{28,0},{1,5},{5... | collective-permute-start | bytes 983048 | tf_op jit(solution)/shard_map/ppermute | solution.py:282
  20.6 6.7 %collective-permute-start.6 = (bf16[8,48,128]{2,1,0:T(8,128)(2,1)S(1)}, bf16[8,48,128]{2,1,0:T(8,128)(2,1)S(1)}, u32[]{:S(2)}, u32[]{:S(2)}) collective-permute-start(bf16[8,48,128]{2,1,0:T(8,128)(2,1)S(1)} %get-tuple-element.35), channel_id=1, source_target_pairs={{0,3},{1,2},{2,1},{3,0},{4,7},{5,6},{6,5},{7,4},{8,11},{9,10},{10,... | collective-permute-start | bytes 294920 | tf_op jit(solution)/shard_map/ppermute | solution.py:287
  24.2 5.6 %collective-permute-start.7 = (bf16[8,48,128]{2,1,0:T(8,128)(2,1)S(1)}, bf16[8,48,128]{2,1,0:T(8,128)(2,1)S(1)}, u32[]{:S(2)}, u32[]{:S(2)}) collective-permute-start(bf16[8,48,128]{2,1,0:T(8,128)(2,1)S(1)} %get-tuple-element.36), channel_id=1, source_target_pairs={{0,2},{1,3},{2,0},{3,1},{4,6},{5,7},{6,4},{7,5},{8,10},{9,11},{10,... | collective-permute-start | bytes 294920 | tf_op jit(solution)/shard_map/ppermute | solution.py:287
  24.2 5.7 %collective-permute-start.8 = (bf16[8,48,128]{2,1,0:T(8,128)(2,1)S(1)}, bf16[8,48,128]{2,1,0:T(8,128)(2,1)S(1)}, u32[]{:S(2)}, u32[]{:S(2)}) collective-permute-start(bf16[8,48,128]{2,1,0:T(8,128)(2,1)S(1)} %get-tuple-element.37), channel_id=1, source_target_pairs={{0,1},{1,0},{2,3},{3,2},{4,5},{5,4},{6,7},{7,6},{8,9},{9,8},{10,11... | collective-permute-start | bytes 294920 | tf_op jit(solution)/shard_map/ppermute | solution.py:287

commit v21 on v18

--- a/solution.py
+++ b/solution.py
@@ -57,7 +57,7 @@
 
 
 def partners(count):
-    return [0, *reversed(range(1, count))]
+    return [0, *range(count // 2, count), *range(1, count // 2)]
 
 
 def pieces_of(ref, index, count, rows, outs):

time: 42.7 us -> 43.3 us (1.014)
  transfers between devices with their start and end apart: 9 -> 9, of which waited for: 4 -> 6; matrix products, arithmetic and copies ran while one was open for 0% -> 0% of each run, Pallas kernels for 15% -> 15%
where the time goes in v21:
time: 43.3 us; the launch traced here: 43.1 us
  starting transfers between devices  12.5 us (29%)
  blocking collectives  11.4 us (26%)
  waiting for transfers between devices  9.53 us (22%)
  Pallas kernels  7.23 us (17%)
  local copies, waits for them, and re-layouts  1.32 us (3%)
  between operations  0.78 us (2%)
    all_to_all x1, blocking collectives, shards(): got = lax.all_to_all(pieces, ('space', 'band'), 0, 0)  11.4 us
    ppermute x6, starting transfers between devices, mirrored(): return lax.ppermute(value, axis, [(i, i ^ bits) for i in range(count)])  8.95 us
    pallas_call x10, Pallas kernels, call(): pl.pallas_call(kernel, out_shape=out_shape, compiler_params=params(vmem *...  7.23 us
    ppermute x3, waiting for transfers between devices, cyclic(): lax.ppermute(value, axis, [(i, (i + steps) % count) for i in range(count)])  5.12 us
    ppermute x6, waiting for transfers between devices, mirrored(): return lax.ppermute(value, axis, [(i, i ^ bits) for i in range(count)])  4.41 us
    ppermute x3, starting transfers between devices, cyclic(): lax.ppermute(value, axis, [(i, (i + steps) % count) for i in range(count)])  3.5 us
    unnamed x14, local copies, waits for them, and re-layouts  1.16 us
  transfers between devices with their start and end apart: 9, of which 6 were waited for; matrix products, arithmetic and copies ran while one was open for 0% of the time, Pallas kernels for 15%

profile of v21, /device:TPU:0, one launch (start us, length us, event | category | flops | bytes accessed | tf_op | source)
XLA Modules:
  0.0 43.1 jit_solution(13216083466257663952)
XLA Ops:
  0.6 0.0 copy-start
  0.6 1.1 %copy-done = f32[8,6,32,128]{3,2,1,0:T(8,128)S(1)} copy-done((f32[8,6,32,128]{3,2,1,0:T(8,128)S(1)}, f32[8,6,32,128]{3,2,1,0:T(8,128)}, u32[]{:S(2)}) %copy-start) | copy-done | bytes 786456
  1.8 0.0 copy-start.2
  1.8 0.0 copy-start.5
  1.8 0.0 copy-start.6
  1.8 3.4 %collective-permute-start = (bf16[8,192,128]{2,1,0:T(8,128)(2,1)S(1)}, bf16[8,192,128]{2,1,0:T(8,128)(2,1)S(1)}, u32[]{:S(2)}, u32[]{:S(2)}) collective-permute-start(bf16[8,192,128]{2,1,0:T(8,128)(2,1)S(1)} %cast.1.own_ref), channel_id=1, source_target_pairs={{0,28},{4,0},{8,4},{12,8},{16,12},{20,16},{24,20},{28,24},{1,29},{... | collective-permute-start | bytes 1179656 | tf_op jit(solution)/shard_map/ppermute | solution.py:280
  5.3 1.6 %collective-permute-start.1 = (bf16[8,48,128]{2,1,0:T(8,128)(2,1)S(1)}, bf16[8,48,128]{2,1,0:T(8,128)(2,1)S(1)}, u32[]{:S(2)}, u32[]{:S(2)}) collective-permute-start(bf16[8,48,128]{2,1,0:T(8,128)(2,1)S(1)} %get-tuple-element.25), channel_id=1, source_target_pairs={{0,1},{1,0},{2,3},{3,2},{4,5},{5,4},{6,7},{7,6},{8,9},{9,8},{10,11... | collective-permute-start | bytes 294920 | tf_op jit(solution)/shard_map/ppermute | solution.py:285
  6.9 2.5 %collective-permute-start.4 = (bf16[8,48,128]{2,1,0:T(8,128)(2,1)S(1)}, bf16[8,48,128]{2,1,0:T(8,128)(2,1)S(1)}, u32[]{:S(2)}, u32[]{:S(2)}) collective-permute-start(bf16[8,48,128]{2,1,0:T(8,128)(2,1)S(1)} %get-tuple-element.30), channel_id=1, source_target_pairs={{0,3},{1,2},{2,1},{3,0},{4,7},{5,6},{6,5},{7,4},{8,11},{9,10},{10,... | collective-permute-start | bytes 294920 | tf_op jit(solution)/shard_map/ppermute | solution.py:285
  9.4 0.1 collective-permute-start.5
  9.5 0.0 copy-done.2
  9.5 0.0 copy-done.5
  9.5 0.0 copy-done.6
  9.5 0.0 copy-start.1
  9.5 1.5 %prepare.1 = (bf16[5,576,256]{2,1,0:T(8,128)(2,1)S(1)}, f32[8,576]{1,0:T(8,128)S(1)}, f32[1,576]{1,0:T(1,128)S(1)}) custom-call(s32[32]{0:T(128)S(1)} %copy-done.6, f32[9,32]{1,0:T(8,128)S(1)} %bitcast.19, bf16[8,192,128]{2,1,0:T(8,128)(2,1)S(1)} %cast.1.own_ref, bf16[4,9,6,32,128]{4,3,2,1,0:T(8,128)(2,1)S(1)} %copy-done.2), custom_call_target="tpu_custom_call" | custom-call | flops 1000000000 | bytes 1048576 | tf_op jit(solution)/shard_map/prepare/pallas_call | solution.py:298
  11.1 0.1 collective-permute-done.1.refs_0_.rest_0_
  11.1 0.0 copy-done.1
  11.1 0.2 ahead.1
  11.3 0.1 collective-permute-start.3
  11.4 0.0 collective-permute-done.upper_ref
  11.4 0.0 copy-start.3
  11.4 0.0 copy-start.4
  11.4 1.3 %coefficients.1 = (bf16[128,576]{1,0:T(8,128)(2,1)S(1)}, bf16[8,160,128]{2,1,0:T(8,128)(2,1)S(1)}) custom-call(bf16[8,192,128]{2,1,0:T(8,128)(2,1)S(1)} %collective-permute-done.upper_ref, bf16[5,576,256]{2,1,0:T(8,128)(2,1)S(1)} %get-tuple-element.22.table_ref, f32[8,576]{1,0:T(8,128)S(1)} %get-tuple-element.23.e_ref, ...), custom_call_target="tpu_custom_call" | custom-call | flops 1000000000 | bytes 1048576 | tf_op jit(solution)/shard_map/coefficients/pallas_call | solution.py:298
  12.8 0.1 collective-permute-start.2
  12.8 0.0 copy-done.3
  12.8 0.0 copy-done.4
  12.8 2.2 %near_part.1.g_ref = f32[8,192,128]{2,1,0:T(8,128)S(1)} custom-call(s32[32]{0:T(128)S(1)} %copy-done.6, f32[8,192,128]{2,1,0:T(8,128)S(1)} %bitcast.15, f32[8,192,128]{2,1,0:T(8,128)S(1)} %bitcast.17, f32[192,128]{1,0:T(8,128)S(1)} %bitcast.18, bf16[128,576]{1,0:T(8,128)(2,1)S(1)} %get-tuple-element.27.w_ref, ...), custom_call_target="tpu_custom_call" | custom-call | flops 20000000000 | bytes 4194304 | tf_op jit(solution)/shard_map/near_part/pallas_call | solution.py:298
  15.1 0.9 %collective-permute-done.3.below_ref = bf16[8,32,128]{2,1,0:T(8,128)(2,1)S(1)} collective-permute-done((bf16[8,32,128]{2,1,0:T(8,128)(2,1)S(1)}, bf16[8,32,128]{2,1,0:T(8,128)(2,1)S(1)}, u32[]{:S(2)}, u32[]{:S(2)}) %collective-permute-start.3) | collective-permute-done | bytes 65568 | tf_op jit(solution)/shard_map/ppermute | solution.py:280
  16.0 4.2 %collective-permute-done.2.arrived_ref = bf16[8,160,128]{2,1,0:T(8,128)(2,1)S(1)} collective-permute-done((bf16[8,160,128]{2,1,0:T(8,128)(2,1)S(1)}, bf16[8,160,128]{2,1,0:T(8,128)(2,1)S(1)}, u32[]{:S(2)}, u32[]{:S(2)}) %collective-permute-start.2) | collective-permute-done | bytes 327712 | tf_op jit(solution)/shard_map/ppermute | solution.py:280
  20.2 0.1 finish.1
  20.3 2.8 %collective-permute-start.6 = (bf16[8,48,128]{2,1,0:T(8,128)(2,1)S(1)}, bf16[8,48,128]{2,1,0:T(8,128)(2,1)S(1)}, u32[]{:S(2)}, u32[]{:S(2)}) collective-permute-start(bf16[8,48,128]{2,1,0:T(8,128)(2,1)S(1)} %get-tuple-element.35), channel_id=1, source_target_pairs={{0,2},{1,3},{2,0},{3,1},{4,6},{5,7},{6,4},{7,5},{8,10},{9,11},{10,... | collective-permute-start | bytes 294920 | tf_op jit(solution)/shard_map/ppermute | solution.py:285
  23.2 1.4 %collective-permute-start.7 = (bf16[8,48,128]{2,1,0:T(8,128)(2,1)S(1)}, bf16[8,48,128]{2,1,0:T(8,128)(2,1)S(1)}, u32[]{:S(2)}, u32[]{:S(2)}) collective-permute-start(bf16[8,48,128]{2,1,0:T(8,128)(2,1)S(1)} %get-tuple-element.36), channel_id=1, source_target_pairs={{0,3},{1,2},{2,1},{3,0},{4,7},{5,6},{6,5},{7,4},{8,11},{9,10},{10,... | collective-permute-start | bytes 294920 | tf_op jit(solution)/shard_map/ppermute | solution.py:285
  24.6 0.5 %collective-permute-start.8 = (bf16[8,48,128]{2,1,0:T(8,128)(2,1)S(1)}, bf16[8,48,128]{2,1,0:T(8,128)(2,1)S(1)}, u32[]{:S(2)}, u32[]{:S(2)}) collective-permute-start(bf16[8,48,128]{2,1,0:T(8,128)(2,1)S(1)} %get-tuple-element.37), channel_id=1, source_target_pairs={{0,1},{1,0},{2,3},{3,2},{4,5},{5,4},{6,7},{7,6},{8,9},{9,8},{10,11... | collective-permute-start | bytes 294920 | tf_op jit(solution)/shard_map/ppermute | solution.py:285
  25.1 0.0 collective-permute-done.4.rest_1_
  25.1 0.0 collective-permute-done.5.rest_2_
  25.1 0.8 %output.1 = (bf16[8,192,128]{2,1,0:T(8,128)(2,1)}, bf16[32,48,128]{2,1,0:T(8,128)(2,1)S(1)}) custom-call(f32[8,192,128]{2,1,0:T(8,128)S(1)} %near_part.1.g_ref, bf16[8,160,128]{2,1,0:T(8,128)(2,1)S(1)} %collective-permute-done.2.arrived_ref, bf16[8,32,128]{2,1,0:T(8,128)(2,1)S(1)} %collective-permute-done.3.below_ref, ...), custom_call_target="tpu_custom_call" | custom-call | tf_op jit(solution)/shard_map/output/pallas_call | solution.py:298
  25.9 0.1 collective-permute-done.6
  26.0 3.8 %collective-permute-done.7 = bf16[8,48,128]{2,1,0:T(8,128)(2,1)S(1)} collective-permute-done((bf16[8,48,128]{2,1,0:T(8,128)(2,1)S(1)}, bf16[8,48,128]{2,1,0:T(8,128)(2,1)S(1)}, u32[]{:S(2)}, u32[]{:S(2)}) %collective-permute-start.7) | collective-permute-done | bytes 98336 | tf_op jit(solution)/shard_map/ppermute | solution.py:285
  29.7 0.5 %collective-permute-done.8 = bf16[8,48,128]{2,1,0:T(8,128)(2,1)S(1)} collective-permute-done((bf16[8,48,128]{2,1,0:T(8,128)(2,1)S(1)}, bf16[8,48,128]{2,1,0:T(8,128)(2,1)S(1)}, u32[]{:S(2)}, u32[]{:S(2)}) %collective-permute-start.8) | collective-permute-done | bytes 98336 | tf_op jit(solution)/shard_map/ppermute | solution.py:285
  30.2 0.1 pad_maximum_fusion
  30.3 0.2 copy_bitcast_fusion
  30.5 0.3 convolution_multiply_fusion.prod_ref
  30.8 0.2 split.1
  31.0 11.4 %all_to_all.5.got_ref = f32[32,1,64]{2,1,0:T(1,128)S(1)} all-to-all(f32[32,1,64]{2,1,0:T(1,128)S(1)} %split.1), channel_id=1, replica_groups=mesh['space'=8,'band'=4] {'space','band'}, dimensions={0} | all-to-all | bytes 16384 | tf_op jit(solution)/shard_map/all_to_all | solution.py:401
  42.5 0.7 %last_sum.1 = (f32[4,8]{1,0:T(4,128)}, f32[4,8]{1,0:T(4,128)}) custom-call(f32[32,1,64]{2,1,0:T(1,128)S(1)} %all_to_all.5.got_ref), custom_call_target="tpu_custom_call" | custom-call | tf_op jit(solution)/shard_map/last_sum/pallas_call | solution.py:298
  (2 shorter events, 0.1 us)
Async XLA Ops:
  0.6 1.1 %copy-start = (f32[8,6,32,128]{3,2,1,0:T(8,128)S(1)}, f32[8,6,32,128]{3,2,1,0:T(8,128)}, u32[]{:S(2)}) copy-start(f32[8,6,32,128]{3,2,1,0:T(8,128)} %param.6) | copy-start | bytes 2359300
  1.8 7.7 %copy-start.2 = (bf16[4,9,6,32,128]{4,3,2,1,0:T(8,128)(2,1)S(1)}, bf16[4,9,6,32,128]{4,3,2,1,0:T(8,128)(2,1)}, u32[]{:S(2)}) copy-start(bf16[4,9,6,32,128]{4,3,2,1,0:T(8,128)(2,1)} %proj_ref.3) | copy-start | bytes 5308420
  1.8 7.7 %copy-start.5 = (f32[32,9]{0,1:T(8,128)S(1)}, f32[32,9]{0,1:T(8,128)}, u32[]{:S(2)}) copy-start(f32[32,9]{0,1:T(8,128)} %param.10) | copy-start | bytes 3460
  1.8 7.7 %copy-start.6 = (s32[32]{0:T(128)S(1)}, s32[32]{0:T(128)}, u32[]{:S(2)}) copy-start(s32[32]{0:T(128)} %first_ref.3) | copy-start | bytes 388
  1.8 9.6 %collective-permute-start = (bf16[8,192,128]{2,1,0:T(8,128)(2,1)S(1)}, bf16[8,192,128]{2,1,0:T(8,128)(2,1)S(1)}, u32[]{:S(2)}, u32[]{:S(2)}) collective-permute-start(bf16[8,192,128]{2,1,0:T(8,128)(2,1)S(1)} %cast.1.own_ref), channel_id=1, source_target_pairs={{0,28},{4,0},{8,4},{12,8},{16,12},{20,16},{24,20},{28,24},{1,29},{... | collective-permute-start | bytes 1179656 | tf_op jit(solution)/shard_map/ppermute | solution.py:280
  5.3 5.9 %collective-permute-start.1 = (bf16[8,48,128]{2,1,0:T(8,128)(2,1)S(1)}, bf16[8,48,128]{2,1,0:T(8,128)(2,1)S(1)}, u32[]{:S(2)}, u32[]{:S(2)}) collective-permute-start(bf16[8,48,128]{2,1,0:T(8,128)(2,1)S(1)} %get-tuple-element.25), channel_id=1, source_target_pairs={{0,1},{1,0},{2,3},{3,2},{4,5},{5,4},{6,7},{7,6},{8,9},{9,8},{10,11... | collective-permute-start | bytes 294920 | tf_op jit(solution)/shard_map/ppermute | solution.py:285
  6.9 18.2 %collective-permute-start.4 = (bf16[8,48,128]{2,1,0:T(8,128)(2,1)S(1)}, bf16[8,48,128]{2,1,0:T(8,128)(2,1)S(1)}, u32[]{:S(2)}, u32[]{:S(2)}) collective-permute-start(bf16[8,48,128]{2,1,0:T(8,128)(2,1)S(1)} %get-tuple-element.30), channel_id=1, source_target_pairs={{0,3},{1,2},{2,1},{3,0},{4,7},{5,6},{6,5},{7,4},{8,11},{9,10},{10,... | collective-permute-start | bytes 294920 | tf_op jit(solution)/shard_map/ppermute | solution.py:285
  9.4 15.7 %collective-permute-start.5 = (bf16[8,48,128]{2,1,0:T(8,128)(2,1)S(1)}, bf16[8,48,128]{2,1,0:T(8,128)(2,1)S(1)}, u32[]{:S(2)}, u32[]{:S(2)}) collective-permute-start(bf16[8,48,128]{2,1,0:T(8,128)(2,1)S(1)} %get-tuple-element.31), channel_id=1, source_target_pairs={{0,2},{1,3},{2,0},{3,1},{4,6},{5,7},{6,4},{7,5},{8,10},{9,11},{10,... | collective-permute-start | bytes 294920 | tf_op jit(solution)/shard_map/ppermute | solution.py:285
  9.5 1.6 %copy-start.1 = (f32[8,6,32,128]{3,2,1,0:T(8,128)S(1)}, f32[8,6,32,128]{3,2,1,0:T(8,128)}, u32[]{:S(2)}) copy-start(f32[8,6,32,128]{3,2,1,0:T(8,128)} %param.6) | copy-start | bytes 2359300
  11.3 4.6 %collective-permute-start.3 = (bf16[8,32,128]{2,1,0:T(8,128)(2,1)S(1)}, bf16[8,32,128]{2,1,0:T(8,128)(2,1)S(1)}, u32[]{:S(2)}, u32[]{:S(2)}) collective-permute-start(bf16[8,32,128]{2,1,0:T(8,128)(2,1)S(1)} %get-tuple-element.29), channel_id=1, source_target_pairs={{0,4},{4,8},{8,12},{12,16},{16,20},{20,24},{24,28},{28,0},{1,5},{5... | collective-permute-start | bytes 196616 | tf_op jit(solution)/shard_map/ppermute | solution.py:280
  11.4 1.4 %copy-start.3 = (f32[8,6,32,128]{3,2,1,0:T(8,128)S(1)}, f32[8,6,32,128]{3,2,1,0:T(8,128)}, u32[]{:S(2)}) copy-start(f32[8,6,32,128]{3,2,1,0:T(8,128)} %param.7) | copy-start | bytes 2359300
  11.4 1.4 %copy-start.4 = (f32[6,32,128]{2,1,0:T(8,128)S(1)}, f32[6,32,128]{2,1,0:T(8,128)}, u32[]{:S(2)}) copy-start(f32[6,32,128]{2,1,0:T(8,128)} %param.8) | copy-start | bytes 294916
  12.8 7.5 %collective-permute-start.2 = (bf16[8,160,128]{2,1,0:T(8,128)(2,1)S(1)}, bf16[8,160,128]{2,1,0:T(8,128)(2,1)S(1)}, u32[]{:S(2)}, u32[]{:S(2)}) collective-permute-start(bf16[8,160,128]{2,1,0:T(8,128)(2,1)S(1)} %get-tuple-element.28), channel_id=1, source_target_pairs={{0,4},{4,8},{8,12},{12,16},{16,20},{20,24},{24,28},{28,0},{1,5},{5... | collective-permute-start | bytes 983048 | tf_op jit(solution)/shard_map/ppermute | solution.py:280
  20.3 5.6 %collective-permute-start.6 = (bf16[8,48,128]{2,1,0:T(8,128)(2,1)S(1)}, bf16[8,48,128]{2,1,0:T(8,128)(2,1)S(1)}, u32[]{:S(2)}, u32[]{:S(2)}) collective-permute-start(bf16[8,48,128]{2,1,0:T(8,128)(2,1)S(1)} %get-tuple-element.35), channel_id=1, source_target_pairs={{0,2},{1,3},{2,0},{3,1},{4,6},{5,7},{6,4},{7,5},{8,10},{9,11},{10,... | collective-permute-start | bytes 294920 | tf_op jit(solution)/shard_map/ppermute | solution.py:285
  23.2 6.6 %collective-permute-start.7 = (bf16[8,48,128]{2,1,0:T(8,128)(2,1)S(1)}, bf16[8,48,128]{2,1,0:T(8,128)(2,1)S(1)}, u32[]{:S(2)}, u32[]{:S(2)}) collective-permute-start(bf16[8,48,128]{2,1,0:T(8,128)(2,1)S(1)} %get-tuple-element.36), channel_id=1, source_target_pairs={{0,3},{1,2},{2,1},{3,0},{4,7},{5,6},{6,5},{7,4},{8,11},{9,10},{10,... | collective-permute-start | bytes 294920 | tf_op jit(solution)/shard_map/ppermute | solution.py:285
  24.6 5.7 %collective-permute-start.8 = (bf16[8,48,128]{2,1,0:T(8,128)(2,1)S(1)}, bf16[8,48,128]{2,1,0:T(8,128)(2,1)S(1)}, u32[]{:S(2)}, u32[]{:S(2)}) collective-permute-start(bf16[8,48,128]{2,1,0:T(8,128)(2,1)S(1)} %get-tuple-element.37), channel_id=1, source_target_pairs={{0,1},{1,0},{2,3},{3,2},{4,5},{5,4},{6,7},{7,6},{8,9},{9,8},{10,11... | collective-permute-start | bytes 294920 | tf_op jit(solution)/shard_map/ppermute | solution.py:285

commit v22 on v18

--- a/solution.py
+++ b/solution.py
@@ -263,7 +263,7 @@
         lines = [pair[p, pl.ds(r, n_space, stride=rows), :] for r in range(rows)]
         packed = jnp.concatenate(lines, axis=1)
         for i in range(n_space):
-            out_ref[i * n_band + owner] = packed[i : i + 1]
+            out_ref[owner * n_space + i] = packed[i : i + 1]
 
 
 def last_kernel(got_ref, margin_ref, projection_ref):
@@ -398,7 +398,7 @@
             pltpu.VMEM((n_band, total_bands, 2 * bands), F32),
         ],
     )
-    got = lax.all_to_all(pieces, ("space", "band"), 0, 0)
+    got = lax.all_to_all(pieces, ("band", "space"), 0, 0)
     margin, projection = call(
         last_kernel, "last_sum", (struct((out_rows, bands)), struct((out_rows, bands))), (got,)
     )

time: 42.7 us -> 42.7 us (level)
  no operation moved by 1% of the time
where the time goes in v22:
time: 42.7 us; the launch traced here: 42.5 us
  starting transfers between devices  12.4 us (29%)
  blocking collectives  11.2 us (26%)
  waiting for transfers between devices  9.17 us (21%)
  Pallas kernels  7.23 us (17%)
  local copies, waits for them, and re-layouts  1.32 us (3%)
  between operations  0.8 us (2%)
    all_to_all x1, blocking collectives, shards(): got = lax.all_to_all(pieces, ('band', 'space'), 0, 0)  11.2 us
    ppermute x6, starting transfers between devices, mirrored(): return lax.ppermute(value, axis, [(i, i ^ bits) for i in range(count)])  8.9 us
    pallas_call x10, Pallas kernels, call(): pl.pallas_call(kernel, out_shape=out_shape, compiler_params=params(vmem *...  7.23 us
    ppermute x3, waiting for transfers between devices, cyclic(): lax.ppermute(value, axis, [(i, (i + steps) % count) for i in range(count)])  5.12 us
    ppermute x6, waiting for transfers between devices, mirrored(): return lax.ppermute(value, axis, [(i, i ^ bits) for i in range(count)])  4.05 us
    ppermute x3, starting transfers between devices, cyclic(): lax.ppermute(value, axis, [(i, (i + steps) % count) for i in range(count)])  3.5 us
    unnamed x14, local copies, waits for them, and re-layouts  1.16 us
  transfers between devices with their start and end apart: 9, of which 4 were waited for; matrix products, arithmetic and copies ran while one was open for 0% of the time, Pallas kernels for 15%

profile of v22, /device:TPU:0, one launch (start us, length us, event | category | flops | bytes accessed | tf_op | source)
XLA Modules:
  0.0 42.5 jit_solution(13568753194405587280)
XLA Ops:
  0.6 0.0 copy-start
  0.6 1.1 %copy-done = f32[8,6,32,128]{3,2,1,0:T(8,128)S(1)} copy-done((f32[8,6,32,128]{3,2,1,0:T(8,128)S(1)}, f32[8,6,32,128]{3,2,1,0:T(8,128)}, u32[]{:S(2)}) %copy-start) | copy-done | bytes 786456
  1.8 0.0 copy-start.2
  1.8 0.0 copy-start.5
  1.8 0.0 copy-start.6
  1.8 3.4 %collective-permute-start = (bf16[8,192,128]{2,1,0:T(8,128)(2,1)S(1)}, bf16[8,192,128]{2,1,0:T(8,128)(2,1)S(1)}, u32[]{:S(2)}, u32[]{:S(2)}) collective-permute-start(bf16[8,192,128]{2,1,0:T(8,128)(2,1)S(1)} %cast.1.own_ref), channel_id=1, source_target_pairs={{0,28},{4,0},{8,4},{12,8},{16,12},{20,16},{24,20},{28,24},{1,29},{... | collective-permute-start | bytes 1179656 | tf_op jit(solution)/shard_map/ppermute | solution.py:280
  5.3 1.6 %collective-permute-start.1 = (bf16[8,48,128]{2,1,0:T(8,128)(2,1)S(1)}, bf16[8,48,128]{2,1,0:T(8,128)(2,1)S(1)}, u32[]{:S(2)}, u32[]{:S(2)}) collective-permute-start(bf16[8,48,128]{2,1,0:T(8,128)(2,1)S(1)} %get-tuple-element.25), channel_id=1, source_target_pairs={{0,1},{1,0},{2,3},{3,2},{4,5},{5,4},{6,7},{7,6},{8,9},{9,8},{10,11... | collective-permute-start | bytes 294920 | tf_op jit(solution)/shard_map/ppermute | solution.py:285
  6.9 2.6 %collective-permute-start.4 = (bf16[8,48,128]{2,1,0:T(8,128)(2,1)S(1)}, bf16[8,48,128]{2,1,0:T(8,128)(2,1)S(1)}, u32[]{:S(2)}, u32[]{:S(2)}) collective-permute-start(bf16[8,48,128]{2,1,0:T(8,128)(2,1)S(1)} %get-tuple-element.30), channel_id=1, source_target_pairs={{0,2},{1,3},{2,0},{3,1},{4,6},{5,7},{6,4},{7,5},{8,10},{9,11},{10,... | collective-permute-start | bytes 294920 | tf_op jit(solution)/shard_map/ppermute | solution.py:285
  9.5 0.2 collective-permute-start.5
  9.7 0.0 copy-done.2
  9.7 0.0 copy-done.5
  9.7 0.0 copy-done.6
  9.7 0.0 copy-start.1
  9.7 1.5 %prepare.1 = (bf16[5,576,256]{2,1,0:T(8,128)(2,1)S(1)}, f32[8,576]{1,0:T(8,128)S(1)}, f32[1,576]{1,0:T(1,128)S(1)}) custom-call(s32[32]{0:T(128)S(1)} %copy-done.6, f32[9,32]{1,0:T(8,128)S(1)} %bitcast.19, bf16[8,192,128]{2,1,0:T(8,128)(2,1)S(1)} %cast.1.own_ref, bf16[4,9,6,32,128]{4,3,2,1,0:T(8,128)(2,1)S(1)} %copy-done.2), custom_call_target="tpu_custom_call" | custom-call | flops 1000000000 | bytes 1048576 | tf_op jit(solution)/shard_map/prepare/pallas_call | solution.py:298
  11.3 0.0 collective-permute-done.1.refs_0_.rest_0_
  11.3 0.0 copy-done.1
  11.3 0.2 ahead.1
  11.5 0.1 collective-permute-start.3
  11.6 0.0 collective-permute-done.upper_ref
  11.6 0.0 copy-start.3
  11.6 0.0 copy-start.4
  11.6 1.3 %coefficients.1 = (bf16[128,576]{1,0:T(8,128)(2,1)S(1)}, bf16[8,160,128]{2,1,0:T(8,128)(2,1)S(1)}) custom-call(bf16[8,192,128]{2,1,0:T(8,128)(2,1)S(1)} %collective-permute-done.upper_ref, bf16[5,576,256]{2,1,0:T(8,128)(2,1)S(1)} %get-tuple-element.22.table_ref, f32[8,576]{1,0:T(8,128)S(1)} %get-tuple-element.23.e_ref, ...), custom_call_target="tpu_custom_call" | custom-call | flops 1000000000 | bytes 1048576 | tf_op jit(solution)/shard_map/coefficients/pallas_call | solution.py:298
  12.9 0.1 collective-permute-start.2
  13.0 0.0 copy-done.3
  13.0 0.0 copy-done.4
  13.0 2.2 %near_part.1.g_ref = f32[8,192,128]{2,1,0:T(8,128)S(1)} custom-call(s32[32]{0:T(128)S(1)} %copy-done.6, f32[8,192,128]{2,1,0:T(8,128)S(1)} %bitcast.15, f32[8,192,128]{2,1,0:T(8,128)S(1)} %bitcast.17, f32[192,128]{1,0:T(8,128)S(1)} %bitcast.18, bf16[128,576]{1,0:T(8,128)(2,1)S(1)} %get-tuple-element.27.w_ref, ...), custom_call_target="tpu_custom_call" | custom-call | flops 20000000000 | bytes 4194304 | tf_op jit(solution)/shard_map/near_part/pallas_call | solution.py:298
  15.3 0.9 %collective-permute-done.3.below_ref = bf16[8,32,128]{2,1,0:T(8,128)(2,1)S(1)} collective-permute-done((bf16[8,32,128]{2,1,0:T(8,128)(2,1)S(1)}, bf16[8,32,128]{2,1,0:T(8,128)(2,1)S(1)}, u32[]{:S(2)}, u32[]{:S(2)}) %collective-permute-start.3) | collective-permute-done | bytes 65568 | tf_op jit(solution)/shard_map/ppermute | solution.py:280
  16.2 4.2 %collective-permute-done.2.arrived_ref = bf16[8,160,128]{2,1,0:T(8,128)(2,1)S(1)} collective-permute-done((bf16[8,160,128]{2,1,0:T(8,128)(2,1)S(1)}, bf16[8,160,128]{2,1,0:T(8,128)(2,1)S(1)}, u32[]{:S(2)}, u32[]{:S(2)}) %collective-permute-start.2) | collective-permute-done | bytes 327712 | tf_op jit(solution)/shard_map/ppermute | solution.py:280
  20.4 0.1 finish.1
  20.5 3.7 %collective-permute-start.6 = (bf16[8,48,128]{2,1,0:T(8,128)(2,1)S(1)}, bf16[8,48,128]{2,1,0:T(8,128)(2,1)S(1)}, u32[]{:S(2)}, u32[]{:S(2)}) collective-permute-start(bf16[8,48,128]{2,1,0:T(8,128)(2,1)S(1)} %get-tuple-element.35), channel_id=1, source_target_pairs={{0,3},{1,2},{2,1},{3,0},{4,7},{5,6},{6,5},{7,4},{8,11},{9,10},{10,... | collective-permute-start | bytes 294920 | tf_op jit(solution)/shard_map/ppermute | solution.py:285
  24.2 0.0 collective-permute-start.7
  24.2 0.8 %collective-permute-start.8 = (bf16[8,48,128]{2,1,0:T(8,128)(2,1)S(1)}, bf16[8,48,128]{2,1,0:T(8,128)(2,1)S(1)}, u32[]{:S(2)}, u32[]{:S(2)}) collective-permute-start(bf16[8,48,128]{2,1,0:T(8,128)(2,1)S(1)} %get-tuple-element.37), channel_id=1, source_target_pairs={{0,1},{1,0},{2,3},{3,2},{4,5},{5,4},{6,7},{7,6},{8,9},{9,8},{10,11... | collective-permute-start | bytes 294920 | tf_op jit(solution)/shard_map/ppermute | solution.py:285
  25.0 0.0 collective-permute-done.4.rest_1_
  25.0 0.0 collective-permute-done.5.rest_2_
  25.0 0.8 %output.1 = (bf16[8,192,128]{2,1,0:T(8,128)(2,1)}, bf16[32,48,128]{2,1,0:T(8,128)(2,1)S(1)}) custom-call(f32[8,192,128]{2,1,0:T(8,128)S(1)} %near_part.1.g_ref, bf16[8,160,128]{2,1,0:T(8,128)(2,1)S(1)} %collective-permute-done.2.arrived_ref, bf16[8,32,128]{2,1,0:T(8,128)(2,1)S(1)} %collective-permute-done.3.below_ref, ...), custom_call_target="tpu_custom_call" | custom-call | tf_op jit(solution)/shard_map/output/pallas_call | solution.py:298
  25.8 1.5 %collective-permute-done.6 = bf16[8,48,128]{2,1,0:T(8,128)(2,1)S(1)} collective-permute-done((bf16[8,48,128]{2,1,0:T(8,128)(2,1)S(1)}, bf16[8,48,128]{2,1,0:T(8,128)(2,1)S(1)}, u32[]{:S(2)}, u32[]{:S(2)}) %collective-permute-start.6) | collective-permute-done | bytes 98336 | tf_op jit(solution)/shard_map/ppermute | solution.py:285
  27.3 2.5 %collective-permute-done.7 = bf16[8,48,128]{2,1,0:T(8,128)(2,1)S(1)} collective-permute-done((bf16[8,48,128]{2,1,0:T(8,128)(2,1)S(1)}, bf16[8,48,128]{2,1,0:T(8,128)(2,1)S(1)}, u32[]{:S(2)}, u32[]{:S(2)}) %collective-permute-start.7) | collective-permute-done | bytes 98336 | tf_op jit(solution)/shard_map/ppermute | solution.py:285
  29.8 0.0 collective-permute-done.8
  29.9 0.1 pad_maximum_fusion
  29.9 0.2 copy_bitcast_fusion
  30.1 0.3 convolution_multiply_fusion.prod_ref
  30.4 0.2 split.1
  30.6 11.2 %all_to_all.5.got_ref = f32[32,1,64]{2,1,0:T(1,128)S(1)} all-to-all(f32[32,1,64]{2,1,0:T(1,128)S(1)} %split.1), channel_id=1, replica_groups=mesh['space'=8,'band'=4] {'band','space'}, dimensions={0} | all-to-all | bytes 16384 | tf_op jit(solution)/shard_map/all_to_all | solution.py:401
  41.8 0.7 %last_sum.1 = (f32[4,8]{1,0:T(4,128)}, f32[4,8]{1,0:T(4,128)}) custom-call(f32[32,1,64]{2,1,0:T(1,128)S(1)} %all_to_all.5.got_ref), custom_call_target="tpu_custom_call" | custom-call | tf_op jit(solution)/shard_map/last_sum/pallas_call | solution.py:298
  (2 shorter events, 0.1 us)
Async XLA Ops:
  0.6 1.1 %copy-start = (f32[8,6,32,128]{3,2,1,0:T(8,128)S(1)}, f32[8,6,32,128]{3,2,1,0:T(8,128)}, u32[]{:S(2)}) copy-start(f32[8,6,32,128]{3,2,1,0:T(8,128)} %param.6) | copy-start | bytes 2359300
  1.8 7.9 %copy-start.2 = (bf16[4,9,6,32,128]{4,3,2,1,0:T(8,128)(2,1)S(1)}, bf16[4,9,6,32,128]{4,3,2,1,0:T(8,128)(2,1)}, u32[]{:S(2)}) copy-start(bf16[4,9,6,32,128]{4,3,2,1,0:T(8,128)(2,1)} %proj_ref.3) | copy-start | bytes 5308420
  1.8 7.9 %copy-start.5 = (f32[32,9]{0,1:T(8,128)S(1)}, f32[32,9]{0,1:T(8,128)}, u32[]{:S(2)}) copy-start(f32[32,9]{0,1:T(8,128)} %param.10) | copy-start | bytes 3460
  1.8 7.9 %copy-start.6 = (s32[32]{0:T(128)S(1)}, s32[32]{0:T(128)}, u32[]{:S(2)}) copy-start(s32[32]{0:T(128)} %first_ref.3) | copy-start | bytes 388
  1.8 9.7 %collective-permute-start = (bf16[8,192,128]{2,1,0:T(8,128)(2,1)S(1)}, bf16[8,192,128]{2,1,0:T(8,128)(2,1)S(1)}, u32[]{:S(2)}, u32[]{:S(2)}) collective-permute-start(bf16[8,192,128]{2,1,0:T(8,128)(2,1)S(1)} %cast.1.own_ref), channel_id=1, source_target_pairs={{0,28},{4,0},{8,4},{12,8},{16,12},{20,16},{24,20},{28,24},{1,29},{... | collective-permute-start | bytes 1179656 | tf_op jit(solution)/shard_map/ppermute | solution.py:280
  5.3 6.0 %collective-permute-start.1 = (bf16[8,48,128]{2,1,0:T(8,128)(2,1)S(1)}, bf16[8,48,128]{2,1,0:T(8,128)(2,1)S(1)}, u32[]{:S(2)}, u32[]{:S(2)}) collective-permute-start(bf16[8,48,128]{2,1,0:T(8,128)(2,1)S(1)} %get-tuple-element.25), channel_id=1, source_target_pairs={{0,1},{1,0},{2,3},{3,2},{4,5},{5,4},{6,7},{7,6},{8,9},{9,8},{10,11... | collective-permute-start | bytes 294920 | tf_op jit(solution)/shard_map/ppermute | solution.py:285
  6.9 18.1 %collective-permute-start.4 = (bf16[8,48,128]{2,1,0:T(8,128)(2,1)S(1)}, bf16[8,48,128]{2,1,0:T(8,128)(2,1)S(1)}, u32[]{:S(2)}, u32[]{:S(2)}) collective-permute-start(bf16[8,48,128]{2,1,0:T(8,128)(2,1)S(1)} %get-tuple-element.30), channel_id=1, source_target_pairs={{0,2},{1,3},{2,0},{3,1},{4,6},{5,7},{6,4},{7,5},{8,10},{9,11},{10,... | collective-permute-start | bytes 294920 | tf_op jit(solution)/shard_map/ppermute | solution.py:285
  9.5 15.5 %collective-permute-start.5 = (bf16[8,48,128]{2,1,0:T(8,128)(2,1)S(1)}, bf16[8,48,128]{2,1,0:T(8,128)(2,1)S(1)}, u32[]{:S(2)}, u32[]{:S(2)}) collective-permute-start(bf16[8,48,128]{2,1,0:T(8,128)(2,1)S(1)} %get-tuple-element.31), channel_id=1, source_target_pairs={{0,3},{1,2},{2,1},{3,0},{4,7},{5,6},{6,5},{7,4},{8,11},{9,10},{10,... | collective-permute-start | bytes 294920 | tf_op jit(solution)/shard_map/ppermute | solution.py:285
  9.7 1.6 %copy-start.1 = (f32[8,6,32,128]{3,2,1,0:T(8,128)S(1)}, f32[8,6,32,128]{3,2,1,0:T(8,128)}, u32[]{:S(2)}) copy-start(f32[8,6,32,128]{3,2,1,0:T(8,128)} %param.6) | copy-start | bytes 2359300
  11.5 4.6 %collective-permute-start.3 = (bf16[8,32,128]{2,1,0:T(8,128)(2,1)S(1)}, bf16[8,32,128]{2,1,0:T(8,128)(2,1)S(1)}, u32[]{:S(2)}, u32[]{:S(2)}) collective-permute-start(bf16[8,32,128]{2,1,0:T(8,128)(2,1)S(1)} %get-tuple-element.29), channel_id=1, source_target_pairs={{0,4},{4,8},{8,12},{12,16},{16,20},{20,24},{24,28},{28,0},{1,5},{5... | collective-permute-start | bytes 196616 | tf_op jit(solution)/shard_map/ppermute | solution.py:280
  11.6 1.4 %copy-start.3 = (f32[8,6,32,128]{3,2,1,0:T(8,128)S(1)}, f32[8,6,32,128]{3,2,1,0:T(8,128)}, u32[]{:S(2)}) copy-start(f32[8,6,32,128]{3,2,1,0:T(8,128)} %param.7) | copy-start | bytes 2359300
  11.6 1.4 %copy-start.4 = (f32[6,32,128]{2,1,0:T(8,128)S(1)}, f32[6,32,128]{2,1,0:T(8,128)}, u32[]{:S(2)}) copy-start(f32[6,32,128]{2,1,0:T(8,128)} %param.8) | copy-start | bytes 294916
  12.9 7.5 %collective-permute-start.2 = (bf16[8,160,128]{2,1,0:T(8,128)(2,1)S(1)}, bf16[8,160,128]{2,1,0:T(8,128)(2,1)S(1)}, u32[]{:S(2)}, u32[]{:S(2)}) collective-permute-start(bf16[8,160,128]{2,1,0:T(8,128)(2,1)S(1)} %get-tuple-element.28), channel_id=1, source_target_pairs={{0,4},{4,8},{8,12},{12,16},{16,20},{20,24},{24,28},{28,0},{1,5},{5... | collective-permute-start | bytes 983048 | tf_op jit(solution)/shard_map/ppermute | solution.py:280
  20.5 6.8 %collective-permute-start.6 = (bf16[8,48,128]{2,1,0:T(8,128)(2,1)S(1)}, bf16[8,48,128]{2,1,0:T(8,128)(2,1)S(1)}, u32[]{:S(2)}, u32[]{:S(2)}) collective-permute-start(bf16[8,48,128]{2,1,0:T(8,128)(2,1)S(1)} %get-tuple-element.35), channel_id=1, source_target_pairs={{0,3},{1,2},{2,1},{3,0},{4,7},{5,6},{6,5},{7,4},{8,11},{9,10},{10,... | collective-permute-start | bytes 294920 | tf_op jit(solution)/shard_map/ppermute | solution.py:285
  24.2 5.6 %collective-permute-start.7 = (bf16[8,48,128]{2,1,0:T(8,128)(2,1)S(1)}, bf16[8,48,128]{2,1,0:T(8,128)(2,1)S(1)}, u32[]{:S(2)}, u32[]{:S(2)}) collective-permute-start(bf16[8,48,128]{2,1,0:T(8,128)(2,1)S(1)} %get-tuple-element.36), channel_id=1, source_target_pairs={{0,2},{1,3},{2,0},{3,1},{4,6},{5,7},{6,4},{7,5},{8,10},{9,11},{10,... | collective-permute-start | bytes 294920 | tf_op jit(solution)/shard_map/ppermute | solution.py:285
  24.2 5.7 %collective-permute-start.8 = (bf16[8,48,128]{2,1,0:T(8,128)(2,1)S(1)}, bf16[8,48,128]{2,1,0:T(8,128)(2,1)S(1)}, u32[]{:S(2)}, u32[]{:S(2)}) collective-permute-start(bf16[8,48,128]{2,1,0:T(8,128)(2,1)S(1)} %get-tuple-element.37), channel_id=1, source_target_pairs={{0,1},{1,0},{2,3},{3,2},{4,5},{5,4},{6,7},{7,6},{8,9},{9,8},{10,11... | collective-permute-start | bytes 294920 | tf_op jit(solution)/shard_map/ppermute | solution.py:285

commit v23 on v12

--- a/solution.py
+++ b/solution.py
@@ -378,7 +378,8 @@
         (g, arrived, below, *reversed(panel)),
     )
     left = jnp.concatenate(mine, axis=0).reshape(total_bands, -1)
-    right = jnp.concatenate([left, panels.reshape(total_bands, -1)], axis=0)
+    filtered, rows = lax.optimization_barrier((filtered, panels.reshape(total_bands, -1)))
+    right = jnp.concatenate([left, rows], axis=0)
     products = dot(left, right, ((1,), (1,))) * (1.0 / (cells * n_space * nz))
     out_rows = total_bands // n_space
     pieces = call(

time: 42.8 us -> 42.7 us (level)
    unnamed x14 -> x16, local copies, waits for them, and re-layouts: 1.16 us -> 1.37 us
where the time goes in v23:
time: 42.7 us; the launch traced here: 42.5 us
  starting transfers between devices  12.4 us (29%)
  blocking collectives  11.2 us (26%)
  waiting for transfers between devices  9.7 us (23%)
  Pallas kernels  6.66 us (16%)
  local copies, waits for them, and re-layouts  1.37 us (3%)
  between operations  0.8 us (2%)
    all_to_all x1, blocking collectives, shards(): got = lax.all_to_all(pieces, ('space', 'band'), 0, 0)  11.2 us
    ppermute x6, starting transfers between devices, mirrored(): return lax.ppermute(value, axis, [(i, i ^ bits) for i in range(count)])  8.9 us
    pallas_call x10, Pallas kernels, call(): pl.pallas_call(kernel, out_shape=out_shape, compiler_params=params(vmem *...  6.66 us
    ppermute x3, waiting for transfers between devices, cyclic(): lax.ppermute(value, axis, [(i, (i + steps) % count) for i in range(count)])  5.75 us
    ppermute x6, waiting for transfers between devices, mirrored(): return lax.ppermute(value, axis, [(i, i ^ bits) for i in range(count)])  3.95 us
    ppermute x3, starting transfers between devices, cyclic(): lax.ppermute(value, axis, [(i, (i + steps) % count) for i in range(count)])  3.5 us
    unnamed x16, local copies, waits for them, and re-layouts  1.37 us
  transfers between devices with their start and end apart: 9, of which 4 were waited for; matrix products, arithmetic and copies ran while one was open for 0% of the time, Pallas kernels for 13%

profile of v23, /device:TPU:0, one launch (start us, length us, event | category | flops | bytes accessed | tf_op | source)
XLA Modules:
  0.0 42.5 jit_solution(1644725549923077507)
XLA Ops:
  0.6 0.0 copy-start
  0.6 1.1 %copy-done = f32[8,6,32,128]{3,2,1,0:T(8,128)S(1)} copy-done((f32[8,6,32,128]{3,2,1,0:T(8,128)S(1)}, f32[8,6,32,128]{3,2,1,0:T(8,128)}, u32[]{:S(2)}) %copy-start) | copy-done | bytes 786456
  1.8 0.0 copy-start.2
  1.8 0.0 copy-start.5
  1.8 0.0 copy-start.6
  1.8 3.4 %collective-permute-start = (bf16[8,192,128]{2,1,0:T(8,128)(2,1)S(1)}, bf16[8,192,128]{2,1,0:T(8,128)(2,1)S(1)}, u32[]{:S(2)}, u32[]{:S(2)}) collective-permute-start(bf16[8,192,128]{2,1,0:T(8,128)(2,1)S(1)} %cast.1.own_ref), channel_id=1, source_target_pairs={{0,28},{4,0},{8,4},{12,8},{16,12},{20,16},{24,20},{28,24},{1,29},{... | collective-permute-start | bytes 1179656 | tf_op jit(solution)/shard_map/ppermute | solution.py:274
  5.3 1.6 %collective-permute-start.1 = (bf16[8,48,128]{2,1,0:T(8,128)(2,1)S(1)}, bf16[8,48,128]{2,1,0:T(8,128)(2,1)S(1)}, u32[]{:S(2)}, u32[]{:S(2)}) collective-permute-start(bf16[8,48,128]{2,1,0:T(8,128)(2,1)S(1)} %get-tuple-element.28), channel_id=1, source_target_pairs={{0,1},{1,0},{2,3},{3,2},{4,5},{5,4},{6,7},{7,6},{8,9},{9,8},{10,11... | collective-permute-start | bytes 294920 | tf_op jit(solution)/shard_map/ppermute | solution.py:279
  6.9 2.6 %collective-permute-start.4 = (bf16[8,48,128]{2,1,0:T(8,128)(2,1)S(1)}, bf16[8,48,128]{2,1,0:T(8,128)(2,1)S(1)}, u32[]{:S(2)}, u32[]{:S(2)}) collective-permute-start(bf16[8,48,128]{2,1,0:T(8,128)(2,1)S(1)} %get-tuple-element.34), channel_id=1, source_target_pairs={{0,2},{1,3},{2,0},{3,1},{4,6},{5,7},{6,4},{7,5},{8,10},{9,11},{10,... | collective-permute-start | bytes 294920 | tf_op jit(solution)/shard_map/ppermute | solution.py:279
  9.5 0.2 collective-permute-start.5
  9.7 0.0 copy-done.2
  9.7 0.0 copy-done.5
  9.7 0.0 copy-done.6
  9.7 0.0 copy-start.1
  9.7 1.6 %prepare.1 = (bf16[6,576,256]{2,1,0:T(8,128)(2,1)S(1)}, bf16[5,576,256]{2,1,0:T(8,128)(2,1)S(1)}, f32[8,576]{1,0:T(8,128)S(1)}, f32[1,576]{1,0:T(1,128)S(1)}) custom-call(s32[32]{0:T(128)S(1)} %copy-done.6, f32[9,32]{1,0:T(8,128)S(1)} %bitcast.21, bf16[8,192,128]{2,1,0:T(8,128)(2,1)S(1)} %cast.1.own_ref, bf16[4,9,6,32,128]{4,3,2,1,0:T(8,128)(2,1)S(1)} %copy-done.2), custom_call_target="tpu_custom_call" | custom-call | flops 1000000000 | bytes 1048576 | tf_op jit(solution)/shard_map/prepare/pallas_call | solution.py:292
  11.3 0.0 collective-permute-done.1.refs_0_.rest_0_
  11.3 0.0 copy-done.1
  11.3 0.2 ahead.1
  11.5 0.1 collective-permute-start.3
  11.6 0.0 collective-permute-done.upper_ref
  11.6 0.0 copy-start.3
  11.6 0.0 copy-start.4
  11.6 1.3 %coefficients.1 = (bf16[128,576]{1,0:T(8,128)(2,1)S(1)}, bf16[8,160,128]{2,1,0:T(8,128)(2,1)S(1)}) custom-call(bf16[8,192,128]{2,1,0:T(8,128)(2,1)S(1)} %collective-permute-done.upper_ref, bf16[5,576,256]{2,1,0:T(8,128)(2,1)S(1)} %get-tuple-element.25.table_ref, f32[8,576]{1,0:T(8,128)S(1)} %get-tuple-element.26.e_ref, ...), custom_call_target="tpu_custom_call" | custom-call | flops 1000000000 | bytes 1048576 | tf_op jit(solution)/shard_map/coefficients/pallas_call | solution.py:292
  13.0 0.1 collective-permute-start.2
  13.1 0.0 copy-done.3
  13.1 0.0 copy-done.4
  13.1 1.6 %near_part.1.g_ref = f32[8,192,128]{2,1,0:T(8,128)S(1)} custom-call(f32[8,192,128]{2,1,0:T(8,128)S(1)} %bitcast.17, f32[8,192,128]{2,1,0:T(8,128)S(1)} %bitcast.19, f32[192,128]{1,0:T(8,128)S(1)} %bitcast.20, bf16[128,576]{1,0:T(8,128)(2,1)S(1)} %get-tuple-element.30.w_ref, bf16[8,192,128]{2,1,0:T(8,128)(2,1)S(1)} %collective-permute-done.upper_ref, ...), custom_call_target="tpu_custom_call" | custom-call | flops 20000000000 | bytes 4194304 | tf_op jit(solution)/shard_map/near_part/pallas_call | solution.py:292
  14.7 1.5 %collective-permute-done.3.below_ref = bf16[8,32,128]{2,1,0:T(8,128)(2,1)S(1)} collective-permute-done((bf16[8,32,128]{2,1,0:T(8,128)(2,1)S(1)}, bf16[8,32,128]{2,1,0:T(8,128)(2,1)S(1)}, u32[]{:S(2)}, u32[]{:S(2)}) %collective-permute-start.3) | collective-permute-done | bytes 65568 | tf_op jit(solution)/shard_map/ppermute | solution.py:274
  16.2 4.3 %collective-permute-done.2.arrived_ref = bf16[8,160,128]{2,1,0:T(8,128)(2,1)S(1)} collective-permute-done((bf16[8,160,128]{2,1,0:T(8,128)(2,1)S(1)}, bf16[8,160,128]{2,1,0:T(8,128)(2,1)S(1)}, u32[]{:S(2)}, u32[]{:S(2)}) %collective-permute-start.2) | collective-permute-done | bytes 327712 | tf_op jit(solution)/shard_map/ppermute | solution.py:274
  20.4 0.1 finish.1
  20.6 3.7 %collective-permute-start.6 = (bf16[8,48,128]{2,1,0:T(8,128)(2,1)S(1)}, bf16[8,48,128]{2,1,0:T(8,128)(2,1)S(1)}, u32[]{:S(2)}, u32[]{:S(2)}) collective-permute-start(bf16[8,48,128]{2,1,0:T(8,128)(2,1)S(1)} %get-tuple-element.41), channel_id=1, source_target_pairs={{0,3},{1,2},{2,1},{3,0},{4,7},{5,6},{6,5},{7,4},{8,11},{9,10},{10,... | collective-permute-start | bytes 294920 | tf_op jit(solution)/shard_map/ppermute | solution.py:279
  24.3 0.0 collective-permute-start.7
  24.3 0.8 %collective-permute-start.8 = (bf16[8,48,128]{2,1,0:T(8,128)(2,1)S(1)}, bf16[8,48,128]{2,1,0:T(8,128)(2,1)S(1)}, u32[]{:S(2)}, u32[]{:S(2)}) collective-permute-start(bf16[8,48,128]{2,1,0:T(8,128)(2,1)S(1)} %get-tuple-element.43), channel_id=1, source_target_pairs={{0,1},{1,0},{2,3},{3,2},{4,5},{5,4},{6,7},{7,6},{8,9},{9,8},{10,11... | collective-permute-start | bytes 294920 | tf_op jit(solution)/shard_map/ppermute | solution.py:279
  25.0 0.0 collective-permute-done.4.rest_1_
  25.0 0.0 collective-permute-done.5.rest_2_
  25.0 0.8 %output.1 = (bf16[8,192,128]{2,1,0:T(8,128)(2,1)}, bf16[32,48,128]{2,1,0:T(8,128)(2,1)S(1)}) custom-call(f32[8,192,128]{2,1,0:T(8,128)S(1)} %near_part.1.g_ref, bf16[8,160,128]{2,1,0:T(8,128)(2,1)S(1)} %collective-permute-done.2.arrived_ref, bf16[8,32,128]{2,1,0:T(8,128)(2,1)S(1)} %collective-permute-done.3.below_ref, ...), custom_call_target="tpu_custom_call" | custom-call | tf_op jit(solution)/shard_map/output/pallas_call | solution.py:292
  25.9 0.1 copy.14
  26.0 1.4 %collective-permute-done.6 = bf16[8,48,128]{2,1,0:T(8,128)(2,1)S(1)} collective-permute-done((bf16[8,48,128]{2,1,0:T(8,128)(2,1)S(1)}, bf16[8,48,128]{2,1,0:T(8,128)(2,1)S(1)}, u32[]{:S(2)}, u32[]{:S(2)}) %collective-permute-start.6) | collective-permute-done | bytes 98336 | tf_op jit(solution)/shard_map/ppermute | solution.py:279
  27.4 2.5 %collective-permute-done.7 = bf16[8,48,128]{2,1,0:T(8,128)(2,1)S(1)} collective-permute-done((bf16[8,48,128]{2,1,0:T(8,128)(2,1)S(1)}, bf16[8,48,128]{2,1,0:T(8,128)(2,1)S(1)}, u32[]{:S(2)}, u32[]{:S(2)}) %collective-permute-start.7) | collective-permute-done | bytes 98336 | tf_op jit(solution)/shard_map/ppermute | solution.py:279
  29.9 0.0 collective-permute-done.8
  29.9 0.1 pad_maximum_fusion
  30.0 0.1 copy.13
  30.1 0.3 convolution_multiply_fusion.prod_ref
  30.4 0.2 split.1
  30.6 11.2 %all_to_all.5.got_ref = f32[32,1,64]{2,1,0:T(1,128)S(1)} all-to-all(f32[32,1,64]{2,1,0:T(1,128)S(1)} %split.1), channel_id=1, replica_groups=mesh['space'=8,'band'=4] {'space','band'}, dimensions={0} | all-to-all | bytes 16384 | tf_op jit(solution)/shard_map/all_to_all | solution.py:395
  41.8 0.7 %last_sum.1 = (f32[4,8]{1,0:T(4,128)}, f32[4,8]{1,0:T(4,128)}) custom-call(f32[32,1,64]{2,1,0:T(1,128)S(1)} %all_to_all.5.got_ref), custom_call_target="tpu_custom_call" | custom-call | tf_op jit(solution)/shard_map/last_sum/pallas_call | solution.py:292
  (2 shorter events, 0.1 us)
Async XLA Ops:
  0.6 1.1 %copy-start = (f32[8,6,32,128]{3,2,1,0:T(8,128)S(1)}, f32[8,6,32,128]{3,2,1,0:T(8,128)}, u32[]{:S(2)}) copy-start(f32[8,6,32,128]{3,2,1,0:T(8,128)} %param.6) | copy-start | bytes 2359300
  1.8 7.9 %copy-start.2 = (bf16[4,9,6,32,128]{4,3,2,1,0:T(8,128)(2,1)S(1)}, bf16[4,9,6,32,128]{4,3,2,1,0:T(8,128)(2,1)}, u32[]{:S(2)}) copy-start(bf16[4,9,6,32,128]{4,3,2,1,0:T(8,128)(2,1)} %proj_ref.1) | copy-start | bytes 5308420
  1.8 7.9 %copy-start.5 = (f32[32,9]{0,1:T(8,128)S(1)}, f32[32,9]{0,1:T(8,128)}, u32[]{:S(2)}) copy-start(f32[32,9]{0,1:T(8,128)} %param.10) | copy-start | bytes 3460
  1.8 7.9 %copy-start.6 = (s32[32]{0:T(128)S(1)}, s32[32]{0:T(128)}, u32[]{:S(2)}) copy-start(s32[32]{0:T(128)} %first_ref.1) | copy-start | bytes 388
  1.8 9.8 %collective-permute-start = (bf16[8,192,128]{2,1,0:T(8,128)(2,1)S(1)}, bf16[8,192,128]{2,1,0:T(8,128)(2,1)S(1)}, u32[]{:S(2)}, u32[]{:S(2)}) collective-permute-start(bf16[8,192,128]{2,1,0:T(8,128)(2,1)S(1)} %cast.1.own_ref), channel_id=1, source_target_pairs={{0,28},{4,0},{8,4},{12,8},{16,12},{20,16},{24,20},{28,24},{1,29},{... | collective-permute-start | bytes 1179656 | tf_op jit(solution)/shard_map/ppermute | solution.py:274
  5.3 6.0 %collective-permute-start.1 = (bf16[8,48,128]{2,1,0:T(8,128)(2,1)S(1)}, bf16[8,48,128]{2,1,0:T(8,128)(2,1)S(1)}, u32[]{:S(2)}, u32[]{:S(2)}) collective-permute-start(bf16[8,48,128]{2,1,0:T(8,128)(2,1)S(1)} %get-tuple-element.28), channel_id=1, source_target_pairs={{0,1},{1,0},{2,3},{3,2},{4,5},{5,4},{6,7},{7,6},{8,9},{9,8},{10,11... | collective-permute-start | bytes 294920 | tf_op jit(solution)/shard_map/ppermute | solution.py:279
  6.9 18.1 %collective-permute-start.4 = (bf16[8,48,128]{2,1,0:T(8,128)(2,1)S(1)}, bf16[8,48,128]{2,1,0:T(8,128)(2,1)S(1)}, u32[]{:S(2)}, u32[]{:S(2)}) collective-permute-start(bf16[8,48,128]{2,1,0:T(8,128)(2,1)S(1)} %get-tuple-element.34), channel_id=1, source_target_pairs={{0,2},{1,3},{2,0},{3,1},{4,6},{5,7},{6,4},{7,5},{8,10},{9,11},{10,... | collective-permute-start | bytes 294920 | tf_op jit(solution)/shard_map/ppermute | solution.py:279
  9.5 15.5 %collective-permute-start.5 = (bf16[8,48,128]{2,1,0:T(8,128)(2,1)S(1)}, bf16[8,48,128]{2,1,0:T(8,128)(2,1)S(1)}, u32[]{:S(2)}, u32[]{:S(2)}) collective-permute-start(bf16[8,48,128]{2,1,0:T(8,128)(2,1)S(1)} %get-tuple-element.35), channel_id=1, source_target_pairs={{0,3},{1,2},{2,1},{3,0},{4,7},{5,6},{6,5},{7,4},{8,11},{9,10},{10,... | collective-permute-start | bytes 294920 | tf_op jit(solution)/shard_map/ppermute | solution.py:279
  9.7 1.6 %copy-start.1 = (f32[8,6,32,128]{3,2,1,0:T(8,128)S(1)}, f32[8,6,32,128]{3,2,1,0:T(8,128)}, u32[]{:S(2)}) copy-start(f32[8,6,32,128]{3,2,1,0:T(8,128)} %param.6) | copy-start | bytes 2359300
  11.5 4.6 %collective-permute-start.3 = (bf16[8,32,128]{2,1,0:T(8,128)(2,1)S(1)}, bf16[8,32,128]{2,1,0:T(8,128)(2,1)S(1)}, u32[]{:S(2)}, u32[]{:S(2)}) collective-permute-start(bf16[8,32,128]{2,1,0:T(8,128)(2,1)S(1)} %get-tuple-element.33), channel_id=1, source_target_pairs={{0,4},{4,8},{8,12},{12,16},{16,20},{20,24},{24,28},{28,0},{1,5},{5... | collective-permute-start | bytes 196616 | tf_op jit(solution)/shard_map/ppermute | solution.py:274
  11.6 1.4 %copy-start.3 = (f32[8,6,32,128]{3,2,1,0:T(8,128)S(1)}, f32[8,6,32,128]{3,2,1,0:T(8,128)}, u32[]{:S(2)}) copy-start(f32[8,6,32,128]{3,2,1,0:T(8,128)} %param.7) | copy-start | bytes 2359300
  11.6 1.4 %copy-start.4 = (f32[6,32,128]{2,1,0:T(8,128)S(1)}, f32[6,32,128]{2,1,0:T(8,128)}, u32[]{:S(2)}) copy-start(f32[6,32,128]{2,1,0:T(8,128)} %param.8) | copy-start | bytes 294916
  13.0 7.5 %collective-permute-start.2 = (bf16[8,160,128]{2,1,0:T(8,128)(2,1)S(1)}, bf16[8,160,128]{2,1,0:T(8,128)(2,1)S(1)}, u32[]{:S(2)}, u32[]{:S(2)}) collective-permute-start(bf16[8,160,128]{2,1,0:T(8,128)(2,1)S(1)} %get-tuple-element.32), channel_id=1, source_target_pairs={{0,4},{4,8},{8,12},{12,16},{16,20},{20,24},{24,28},{28,0},{1,5},{5... | collective-permute-start | bytes 983048 | tf_op jit(solution)/shard_map/ppermute | solution.py:274
  20.6 6.8 %collective-permute-start.6 = (bf16[8,48,128]{2,1,0:T(8,128)(2,1)S(1)}, bf16[8,48,128]{2,1,0:T(8,128)(2,1)S(1)}, u32[]{:S(2)}, u32[]{:S(2)}) collective-permute-start(bf16[8,48,128]{2,1,0:T(8,128)(2,1)S(1)} %get-tuple-element.41), channel_id=1, source_target_pairs={{0,3},{1,2},{2,1},{3,0},{4,7},{5,6},{6,5},{7,4},{8,11},{9,10},{10,... | collective-permute-start | bytes 294920 | tf_op jit(solution)/shard_map/ppermute | solution.py:279
  24.3 5.6 %collective-permute-start.7 = (bf16[8,48,128]{2,1,0:T(8,128)(2,1)S(1)}, bf16[8,48,128]{2,1,0:T(8,128)(2,1)S(1)}, u32[]{:S(2)}, u32[]{:S(2)}) collective-permute-start(bf16[8,48,128]{2,1,0:T(8,128)(2,1)S(1)} %get-tuple-element.42), channel_id=1, source_target_pairs={{0,2},{1,3},{2,0},{3,1},{4,6},{5,7},{6,4},{7,5},{8,10},{9,11},{10,... | collective-permute-start | bytes 294920 | tf_op jit(solution)/shard_map/ppermute | solution.py:279
  24.3 5.7 %collective-permute-start.8 = (bf16[8,48,128]{2,1,0:T(8,128)(2,1)S(1)}, bf16[8,48,128]{2,1,0:T(8,128)(2,1)S(1)}, u32[]{:S(2)}, u32[]{:S(2)}) collective-permute-start(bf16[8,48,128]{2,1,0:T(8,128)(2,1)S(1)} %get-tuple-element.43), channel_id=1, source_target_pairs={{0,1},{1,0},{2,3},{3,2},{4,5},{5,4},{6,7},{7,6},{8,9},{9,8},{10,11... | collective-permute-start | bytes 294920 | tf_op jit(solution)/shard_map/ppermute | solution.py:279

commit v24 on v23

--- a/solution.py
+++ b/solution.py
@@ -63,12 +63,8 @@
 def pieces_of(ref, index, count, rows, outs):
     for bits, out in zip(partners(count), outs):
         quarter = jnp.bitwise_xor(index, bits)
-        begin = pl.multiple_of(quarter * rows, 8)
+        begin = pl.multiple_of(quarter * rows, 16 if rows % 16 == 0 else 8)
         out[...] = ref[:, pl.ds(begin, rows), :].astype(out.dtype)
-
-
-def cast_kernel(psi_ref, half_ref):
-    half_ref[...] = psi_ref[...].astype(BF16)
 
 
 def pieces_kernel(count, psi_ref, *outs):
@@ -311,12 +307,12 @@
 
     most = (bands, (planes - 1) * ny, nz)
     plane = (bands, ny, nz)
-    half = call(cast_kernel, "cast", struct(whole, BF16), (psi,))
+    half = psi.astype(BF16)
     panel = call(
         partial(pieces_kernel, n_band),
         "pieces",
         (struct(quarter, BF16),) * n_band,
-        (psi,),
+        (half if quarter[1] % 16 == 0 else psi,),
         cost_estimate=pl.CostEstimate(flops=10**9, bytes_accessed=2**20, transcendentals=0),
     )
     upper = cyclic(half, "space", -1)

time: 42.7 us -> 42.7 us (level)
  other arithmetic: 0.05 us -> 1.24 us
  local copies, waits for them, and re-layouts: 1.37 us -> 0.24 us
    convert_element_type x0 -> x1, other arithmetic: none -> 1.19 us  [shards(): half = psi.astype(BF16)]
    unnamed x16 -> x14, local copies, waits for them, and re-layouts: 1.37 us -> 0.24 us
    pallas_call x10 -> x9, Pallas kernels: 6.66 us -> 6.61 us  [call(): pl.pallas_call(kernel, out_shape=out_shape, compiler_params=params(vmem *...]
where the time goes in v24:
time: 42.7 us; the launch traced here: 42.6 us
  starting transfers between devices  12.4 us (29%)
  blocking collectives  11.2 us (26%)
  waiting for transfers between devices  9.7 us (23%)
  Pallas kernels  6.61 us (15%)
  other arithmetic  1.24 us (3%)
  between operations  0.8 us (2%)
    all_to_all x1, blocking collectives, shards(): got = lax.all_to_all(pieces, ('space', 'band'), 0, 0)  11.2 us
    ppermute x6, starting transfers between devices, mirrored(): return lax.ppermute(value, axis, [(i, i ^ bits) for i in range(count)])  8.9 us
    pallas_call x9, Pallas kernels, call(): pl.pallas_call(kernel, out_shape=out_shape, compiler_params=params(vmem *...  6.61 us
    ppermute x3, waiting for transfers between devices, cyclic(): lax.ppermute(value, axis, [(i, (i + steps) % count) for i in range(count)])  5.75 us
    ppermute x6, waiting for transfers between devices, mirrored(): return lax.ppermute(value, axis, [(i, i ^ bits) for i in range(count)])  3.95 us
    ppermute x3, starting transfers between devices, cyclic(): lax.ppermute(value, axis, [(i, (i + steps) % count) for i in range(count)])  3.5 us
    convert_element_type x1, other arithmetic, shards(): half = psi.astype(BF16)  1.19 us
  transfers between devices with their start and end apart: 9, of which 4 were waited for; matrix products, arithmetic and copies ran while one was open for 0% of the time, Pallas kernels for 13%

profile of v24, /device:TPU:0, one launch (start us, length us, event | category | flops | bytes accessed | tf_op | source)
XLA Modules:
  0.0 42.6 jit_solution(12837572384872967483)
XLA Ops:
  0.6 1.2 %bitcast_convert_fusion.own_ref.psi_ref = bf16[8,192,128]{2,1,0:T(8,128)(2,1)S(1)} fusion(f32[8,6,32,128]{3,2,1,0:T(8,128)} %param.6), kind=kLoop, calls=%fused_computation.8 | loop fusion | flops 196608 | bytes 1179648 | tf_op jit(solution)/shard_map/convert_element_type | solution.py:310
  1.8 0.0 copy-start.1
  1.8 0.0 copy-start.4
  1.9 0.0 copy-start.5
  1.9 3.4 %collective-permute-start = (bf16[8,192,128]{2,1,0:T(8,128)(2,1)S(1)}, bf16[8,192,128]{2,1,0:T(8,128)(2,1)S(1)}, u32[]{:S(2)}, u32[]{:S(2)}) collective-permute-start(bf16[8,192,128]{2,1,0:T(8,128)(2,1)S(1)} %bitcast_convert_fusion.own_ref.psi_ref), channel_id=1, source_target_pairs={{0,28},{4,0},{8,4},{12,8},{16,12},{20,16},{24,20},{28,24},{1,29},{... | collective-permute-start | bytes 1179656 | tf_op jit(solution)/shard_map/ppermute | solution.py:270
  5.3 1.6 %collective-permute-start.1 = (bf16[8,48,128]{2,1,0:T(8,128)(2,1)S(1)}, bf16[8,48,128]{2,1,0:T(8,128)(2,1)S(1)}, u32[]{:S(2)}, u32[]{:S(2)}) collective-permute-start(bf16[8,48,128]{2,1,0:T(8,128)(2,1)S(1)} %get-tuple-element.28), channel_id=1, source_target_pairs={{0,1},{1,0},{2,3},{3,2},{4,5},{5,4},{6,7},{7,6},{8,9},{9,8},{10,11... | collective-permute-start | bytes 294920 | tf_op jit(solution)/shard_map/ppermute | solution.py:275
  6.9 2.6 %collective-permute-start.4 = (bf16[8,48,128]{2,1,0:T(8,128)(2,1)S(1)}, bf16[8,48,128]{2,1,0:T(8,128)(2,1)S(1)}, u32[]{:S(2)}, u32[]{:S(2)}) collective-permute-start(bf16[8,48,128]{2,1,0:T(8,128)(2,1)S(1)} %get-tuple-element.34), channel_id=1, source_target_pairs={{0,2},{1,3},{2,0},{3,1},{4,6},{5,7},{6,4},{7,5},{8,10},{9,11},{10,... | collective-permute-start | bytes 294920 | tf_op jit(solution)/shard_map/ppermute | solution.py:275
  9.5 0.2 collective-permute-start.5
  9.7 0.0 copy-done.1
  9.7 0.0 copy-done.4
  9.7 0.0 copy-done.5
  9.7 0.0 copy-start
  9.8 1.6 %prepare.1 = (bf16[6,576,256]{2,1,0:T(8,128)(2,1)S(1)}, bf16[5,576,256]{2,1,0:T(8,128)(2,1)S(1)}, f32[8,576]{1,0:T(8,128)S(1)}, f32[1,576]{1,0:T(1,128)S(1)}) custom-call(s32[32]{0:T(128)S(1)} %copy-done.5, f32[9,32]{1,0:T(8,128)S(1)} %bitcast.20, bf16[8,192,128]{2,1,0:T(8,128)(2,1)S(1)} %bitcast_convert_fusion.own_ref.psi_ref, ...), custom_call_target="tpu_custom_call" | custom-call | flops 1000000000 | bytes 1048576 | tf_op jit(solution)/shard_map/prepare/pallas_call | solution.py:288
  11.3 0.0 collective-permute-done.1.refs_0_.rest_0_
  11.3 0.0 copy-done
  11.3 0.2 ahead.1
  11.5 0.1 collective-permute-start.3
  11.6 0.0 collective-permute-done.upper_ref
  11.6 0.0 copy-start.2
  11.6 0.0 copy-start.3
  11.6 1.4 %coefficients.1 = (bf16[128,576]{1,0:T(8,128)(2,1)S(1)}, bf16[8,160,128]{2,1,0:T(8,128)(2,1)S(1)}) custom-call(bf16[8,192,128]{2,1,0:T(8,128)(2,1)S(1)} %collective-permute-done.upper_ref, bf16[5,576,256]{2,1,0:T(8,128)(2,1)S(1)} %get-tuple-element.25.table_ref, f32[8,576]{1,0:T(8,128)S(1)} %get-tuple-element.26.e_ref, ...), custom_call_target="tpu_custom_call" | custom-call | flops 1000000000 | bytes 1048576 | tf_op jit(solution)/shard_map/coefficients/pallas_call | solution.py:288
  13.0 0.1 collective-permute-start.2
  13.1 0.0 copy-done.2
  13.1 0.0 copy-done.3
  13.1 1.6 %near_part.1.g_ref = f32[8,192,128]{2,1,0:T(8,128)S(1)} custom-call(f32[8,192,128]{2,1,0:T(8,128)S(1)} %bitcast.16, f32[8,192,128]{2,1,0:T(8,128)S(1)} %bitcast.18, f32[192,128]{1,0:T(8,128)S(1)} %bitcast.19, bf16[128,576]{1,0:T(8,128)(2,1)S(1)} %get-tuple-element.30.w_ref, bf16[8,192,128]{2,1,0:T(8,128)(2,1)S(1)} %collective-permute-done.upper_ref, ...), custom_call_target="tpu_custom_call" | custom-call | flops 20000000000 | bytes 4194304 | tf_op jit(solution)/shard_map/near_part/pallas_call | solution.py:288
  14.7 1.5 %collective-permute-done.3.below_ref = bf16[8,32,128]{2,1,0:T(8,128)(2,1)S(1)} collective-permute-done((bf16[8,32,128]{2,1,0:T(8,128)(2,1)S(1)}, bf16[8,32,128]{2,1,0:T(8,128)(2,1)S(1)}, u32[]{:S(2)}, u32[]{:S(2)}) %collective-permute-start.3) | collective-permute-done | bytes 65568 | tf_op jit(solution)/shard_map/ppermute | solution.py:270
  16.2 4.3 %collective-permute-done.2.arrived_ref = bf16[8,160,128]{2,1,0:T(8,128)(2,1)S(1)} collective-permute-done((bf16[8,160,128]{2,1,0:T(8,128)(2,1)S(1)}, bf16[8,160,128]{2,1,0:T(8,128)(2,1)S(1)}, u32[]{:S(2)}, u32[]{:S(2)}) %collective-permute-start.2) | collective-permute-done | bytes 327712 | tf_op jit(solution)/shard_map/ppermute | solution.py:270
  20.5 0.1 finish.1
  20.6 3.7 %collective-permute-start.6 = (bf16[8,48,128]{2,1,0:T(8,128)(2,1)S(1)}, bf16[8,48,128]{2,1,0:T(8,128)(2,1)S(1)}, u32[]{:S(2)}, u32[]{:S(2)}) collective-permute-start(bf16[8,48,128]{2,1,0:T(8,128)(2,1)S(1)} %get-tuple-element.41), channel_id=1, source_target_pairs={{0,3},{1,2},{2,1},{3,0},{4,7},{5,6},{6,5},{7,4},{8,11},{9,10},{10,... | collective-permute-start | bytes 294920 | tf_op jit(solution)/shard_map/ppermute | solution.py:275
  24.3 0.0 collective-permute-start.7
  24.3 0.8 %collective-permute-start.8 = (bf16[8,48,128]{2,1,0:T(8,128)(2,1)S(1)}, bf16[8,48,128]{2,1,0:T(8,128)(2,1)S(1)}, u32[]{:S(2)}, u32[]{:S(2)}) collective-permute-start(bf16[8,48,128]{2,1,0:T(8,128)(2,1)S(1)} %get-tuple-element.43), channel_id=1, source_target_pairs={{0,1},{1,0},{2,3},{3,2},{4,5},{5,4},{6,7},{7,6},{8,9},{9,8},{10,11... | collective-permute-start | bytes 294920 | tf_op jit(solution)/shard_map/ppermute | solution.py:275
  25.0 0.0 collective-permute-done.4.rest_1_
  25.1 0.0 collective-permute-done.5.rest_2_
  25.1 0.8 %output.1 = (bf16[8,192,128]{2,1,0:T(8,128)(2,1)}, bf16[32,48,128]{2,1,0:T(8,128)(2,1)S(1)}) custom-call(f32[8,192,128]{2,1,0:T(8,128)S(1)} %near_part.1.g_ref, bf16[8,160,128]{2,1,0:T(8,128)(2,1)S(1)} %collective-permute-done.2.arrived_ref, bf16[8,32,128]{2,1,0:T(8,128)(2,1)S(1)} %collective-permute-done.3.below_ref, ...), custom_call_target="tpu_custom_call" | custom-call | tf_op jit(solution)/shard_map/output/pallas_call | solution.py:288
  25.9 0.1 copy.14
  26.0 1.4 %collective-permute-done.6 = bf16[8,48,128]{2,1,0:T(8,128)(2,1)S(1)} collective-permute-done((bf16[8,48,128]{2,1,0:T(8,128)(2,1)S(1)}, bf16[8,48,128]{2,1,0:T(8,128)(2,1)S(1)}, u32[]{:S(2)}, u32[]{:S(2)}) %collective-permute-start.6) | collective-permute-done | bytes 98336 | tf_op jit(solution)/shard_map/ppermute | solution.py:275
  27.4 2.5 %collective-permute-done.7 = bf16[8,48,128]{2,1,0:T(8,128)(2,1)S(1)} collective-permute-done((bf16[8,48,128]{2,1,0:T(8,128)(2,1)S(1)}, bf16[8,48,128]{2,1,0:T(8,128)(2,1)S(1)}, u32[]{:S(2)}, u32[]{:S(2)}) %collective-permute-start.7) | collective-permute-done | bytes 98336 | tf_op jit(solution)/shard_map/ppermute | solution.py:275
  29.9 0.0 collective-permute-done.8
  29.9 0.1 pad_maximum_fusion
  30.0 0.1 copy.13
  30.1 0.3 convolution_multiply_fusion.prod_ref
  30.4 0.2 split.1
  30.6 11.2 %all_to_all.5.got_ref = f32[32,1,64]{2,1,0:T(1,128)S(1)} all-to-all(f32[32,1,64]{2,1,0:T(1,128)S(1)} %split.1), channel_id=1, replica_groups=mesh['space'=8,'band'=4] {'space','band'}, dimensions={0} | all-to-all | bytes 16384 | tf_op jit(solution)/shard_map/all_to_all | solution.py:391
  41.9 0.7 %last_sum.1 = (f32[4,8]{1,0:T(4,128)}, f32[4,8]{1,0:T(4,128)}) custom-call(f32[32,1,64]{2,1,0:T(1,128)S(1)} %all_to_all.5.got_ref), custom_call_target="tpu_custom_call" | custom-call | tf_op jit(solution)/shard_map/last_sum/pallas_call | solution.py:288
  (1 shorter events, 0.0 us)
Async XLA Ops:
  1.8 7.9 %copy-start.1 = (bf16[4,9,6,32,128]{4,3,2,1,0:T(8,128)(2,1)S(1)}, bf16[4,9,6,32,128]{4,3,2,1,0:T(8,128)(2,1)}, u32[]{:S(2)}) copy-start(bf16[4,9,6,32,128]{4,3,2,1,0:T(8,128)(2,1)} %proj_ref.1) | copy-start | bytes 5308420
  1.8 7.9 %copy-start.4 = (f32[32,9]{0,1:T(8,128)S(1)}, f32[32,9]{0,1:T(8,128)}, u32[]{:S(2)}) copy-start(f32[32,9]{0,1:T(8,128)} %param.10) | copy-start | bytes 3460
  1.9 7.9 %copy-start.5 = (s32[32]{0:T(128)S(1)}, s32[32]{0:T(128)}, u32[]{:S(2)}) copy-start(s32[32]{0:T(128)} %first_ref.1) | copy-start | bytes 388
  1.9 9.7 %collective-permute-start = (bf16[8,192,128]{2,1,0:T(8,128)(2,1)S(1)}, bf16[8,192,128]{2,1,0:T(8,128)(2,1)S(1)}, u32[]{:S(2)}, u32[]{:S(2)}) collective-permute-start(bf16[8,192,128]{2,1,0:T(8,128)(2,1)S(1)} %bitcast_convert_fusion.own_ref.psi_ref), channel_id=1, source_target_pairs={{0,28},{4,0},{8,4},{12,8},{16,12},{20,16},{24,20},{28,24},{1,29},{... | collective-permute-start | bytes 1179656 | tf_op jit(solution)/shard_map/ppermute | solution.py:270
  5.3 6.0 %collective-permute-start.1 = (bf16[8,48,128]{2,1,0:T(8,128)(2,1)S(1)}, bf16[8,48,128]{2,1,0:T(8,128)(2,1)S(1)}, u32[]{:S(2)}, u32[]{:S(2)}) collective-permute-start(bf16[8,48,128]{2,1,0:T(8,128)(2,1)S(1)} %get-tuple-element.28), channel_id=1, source_target_pairs={{0,1},{1,0},{2,3},{3,2},{4,5},{5,4},{6,7},{7,6},{8,9},{9,8},{10,11... | collective-permute-start | bytes 294920 | tf_op jit(solution)/shard_map/ppermute | solution.py:275
  6.9 18.1 %collective-permute-start.4 = (bf16[8,48,128]{2,1,0:T(8,128)(2,1)S(1)}, bf16[8,48,128]{2,1,0:T(8,128)(2,1)S(1)}, u32[]{:S(2)}, u32[]{:S(2)}) collective-permute-start(bf16[8,48,128]{2,1,0:T(8,128)(2,1)S(1)} %get-tuple-element.34), channel_id=1, source_target_pairs={{0,2},{1,3},{2,0},{3,1},{4,6},{5,7},{6,4},{7,5},{8,10},{9,11},{10,... | collective-permute-start | bytes 294920 | tf_op jit(solution)/shard_map/ppermute | solution.py:275
  9.5 15.5 %collective-permute-start.5 = (bf16[8,48,128]{2,1,0:T(8,128)(2,1)S(1)}, bf16[8,48,128]{2,1,0:T(8,128)(2,1)S(1)}, u32[]{:S(2)}, u32[]{:S(2)}) collective-permute-start(bf16[8,48,128]{2,1,0:T(8,128)(2,1)S(1)} %get-tuple-element.35), channel_id=1, source_target_pairs={{0,3},{1,2},{2,1},{3,0},{4,7},{5,6},{6,5},{7,4},{8,11},{9,10},{10,... | collective-permute-start | bytes 294920 | tf_op jit(solution)/shard_map/ppermute | solution.py:275
  9.7 1.6 %copy-start = (f32[8,6,32,128]{3,2,1,0:T(8,128)S(1)}, f32[8,6,32,128]{3,2,1,0:T(8,128)}, u32[]{:S(2)}) copy-start(f32[8,6,32,128]{3,2,1,0:T(8,128)} %param.6) | copy-start | bytes 2359300
  11.5 4.6 %collective-permute-start.3 = (bf16[8,32,128]{2,1,0:T(8,128)(2,1)S(1)}, bf16[8,32,128]{2,1,0:T(8,128)(2,1)S(1)}, u32[]{:S(2)}, u32[]{:S(2)}) collective-permute-start(bf16[8,32,128]{2,1,0:T(8,128)(2,1)S(1)} %get-tuple-element.33), channel_id=1, source_target_pairs={{0,4},{4,8},{8,12},{12,16},{16,20},{20,24},{24,28},{28,0},{1,5},{5... | collective-permute-start | bytes 196616 | tf_op jit(solution)/shard_map/ppermute | solution.py:270
  11.6 1.5 %copy-start.2 = (f32[8,6,32,128]{3,2,1,0:T(8,128)S(1)}, f32[8,6,32,128]{3,2,1,0:T(8,128)}, u32[]{:S(2)}) copy-start(f32[8,6,32,128]{3,2,1,0:T(8,128)} %param.7) | copy-start | bytes 2359300
  11.6 1.5 %copy-start.3 = (f32[6,32,128]{2,1,0:T(8,128)S(1)}, f32[6,32,128]{2,1,0:T(8,128)}, u32[]{:S(2)}) copy-start(f32[6,32,128]{2,1,0:T(8,128)} %param.8) | copy-start | bytes 294916
  13.0 7.5 %collective-permute-start.2 = (bf16[8,160,128]{2,1,0:T(8,128)(2,1)S(1)}, bf16[8,160,128]{2,1,0:T(8,128)(2,1)S(1)}, u32[]{:S(2)}, u32[]{:S(2)}) collective-permute-start(bf16[8,160,128]{2,1,0:T(8,128)(2,1)S(1)} %get-tuple-element.32), channel_id=1, source_target_pairs={{0,4},{4,8},{8,12},{12,16},{16,20},{20,24},{24,28},{28,0},{1,5},{5... | collective-permute-start | bytes 983048 | tf_op jit(solution)/shard_map/ppermute | solution.py:270
  20.6 6.8 %collective-permute-start.6 = (bf16[8,48,128]{2,1,0:T(8,128)(2,1)S(1)}, bf16[8,48,128]{2,1,0:T(8,128)(2,1)S(1)}, u32[]{:S(2)}, u32[]{:S(2)}) collective-permute-start(bf16[8,48,128]{2,1,0:T(8,128)(2,1)S(1)} %get-tuple-element.41), channel_id=1, source_target_pairs={{0,3},{1,2},{2,1},{3,0},{4,7},{5,6},{6,5},{7,4},{8,11},{9,10},{10,... | collective-permute-start | bytes 294920 | tf_op jit(solution)/shard_map/ppermute | solution.py:275
  24.3 5.6 %collective-permute-start.7 = (bf16[8,48,128]{2,1,0:T(8,128)(2,1)S(1)}, bf16[8,48,128]{2,1,0:T(8,128)(2,1)S(1)}, u32[]{:S(2)}, u32[]{:S(2)}) collective-permute-start(bf16[8,48,128]{2,1,0:T(8,128)(2,1)S(1)} %get-tuple-element.42), channel_id=1, source_target_pairs={{0,2},{1,3},{2,0},{3,1},{4,6},{5,7},{6,4},{7,5},{8,10},{9,11},{10,... | collective-permute-start | bytes 294920 | tf_op jit(solution)/shard_map/ppermute | solution.py:275
  24.3 5.7 %collective-permute-start.8 = (bf16[8,48,128]{2,1,0:T(8,128)(2,1)S(1)}, bf16[8,48,128]{2,1,0:T(8,128)(2,1)S(1)}, u32[]{:S(2)}, u32[]{:S(2)}) collective-permute-start(bf16[8,48,128]{2,1,0:T(8,128)(2,1)S(1)} %get-tuple-element.43), channel_id=1, source_target_pairs={{0,1},{1,0},{2,3},{3,2},{4,5},{5,4},{6,7},{7,6},{8,9},{9,8},{10,11... | collective-permute-start | bytes 294920 | tf_op jit(solution)/shard_map/ppermute | solution.py:275

commit v25 on v18

--- a/solution.py
+++ b/solution.py
@@ -385,7 +385,8 @@
         (g, arrived, below, *reversed(panel)),
     )
     left = jnp.concatenate(mine, axis=0).reshape(total_bands, -1)
-    right = jnp.concatenate([left, panels.reshape(total_bands, -1)], axis=0)
+    filtered, rows = lax.optimization_barrier((filtered, panels.reshape(total_bands, -1)))
+    right = jnp.concatenate([left, rows], axis=0)
     products = dot(left, right, ((1,), (1,))) * (1.0 / (cells * n_space * nz))
     out_rows = total_bands // n_space
     pieces = call(

time: 42.7 us -> 42.7 us (level)
    unnamed x14 -> x16, local copies, waits for them, and re-layouts: 1.16 us -> 1.37 us
where the time goes in v25:
time: 42.7 us; the launch traced here: 42.5 us
  starting transfers between devices  12.4 us (29%)
  blocking collectives  11.2 us (26%)
  waiting for transfers between devices  9.08 us (21%)
  Pallas kernels  7.23 us (17%)
  local copies, waits for them, and re-layouts  1.37 us (3%)
  between operations  0.8 us (2%)
    all_to_all x1, blocking collectives, shards(): got = lax.all_to_all(pieces, ('space', 'band'), 0, 0)  11.2 us
    ppermute x6, starting transfers between devices, mirrored(): return lax.ppermute(value, axis, [(i, i ^ bits) for i in range(count)])  8.9 us
    pallas_call x10, Pallas kernels, call(): pl.pallas_call(kernel, out_shape=out_shape, compiler_params=params(vmem *...  7.23 us
    ppermute x3, waiting for transfers between devices, cyclic(): lax.ppermute(value, axis, [(i, (i + steps) % count) for i in range(count)])  5.12 us
    ppermute x6, waiting for transfers between devices, mirrored(): return lax.ppermute(value, axis, [(i, i ^ bits) for i in range(count)])  3.96 us
    ppermute x3, starting transfers between devices, cyclic(): lax.ppermute(value, axis, [(i, (i + steps) % count) for i in range(count)])  3.5 us
    unnamed x16, local copies, waits for them, and re-layouts  1.37 us
  transfers between devices with their start and end apart: 9, of which 4 were waited for; matrix products, arithmetic and copies ran while one was open for 0% of the time, Pallas kernels for 15%

profile of v25, /device:TPU:0, one launch (start us, length us, event | category | flops | bytes accessed | tf_op | source)
XLA Modules:
  0.0 42.5 jit_solution(4880532278490840173)
XLA Ops:
  0.6 0.0 copy-start
  0.6 1.1 %copy-done = f32[8,6,32,128]{3,2,1,0:T(8,128)S(1)} copy-done((f32[8,6,32,128]{3,2,1,0:T(8,128)S(1)}, f32[8,6,32,128]{3,2,1,0:T(8,128)}, u32[]{:S(2)}) %copy-start) | copy-done | bytes 786456
  1.8 0.0 copy-start.2
  1.8 0.0 copy-start.5
  1.8 0.0 copy-start.6
  1.8 3.4 %collective-permute-start = (bf16[8,192,128]{2,1,0:T(8,128)(2,1)S(1)}, bf16[8,192,128]{2,1,0:T(8,128)(2,1)S(1)}, u32[]{:S(2)}, u32[]{:S(2)}) collective-permute-start(bf16[8,192,128]{2,1,0:T(8,128)(2,1)S(1)} %cast.1.own_ref), channel_id=1, source_target_pairs={{0,28},{4,0},{8,4},{12,8},{16,12},{20,16},{24,20},{28,24},{1,29},{... | collective-permute-start | bytes 1179656 | tf_op jit(solution)/shard_map/ppermute | solution.py:280
  5.3 1.6 %collective-permute-start.1 = (bf16[8,48,128]{2,1,0:T(8,128)(2,1)S(1)}, bf16[8,48,128]{2,1,0:T(8,128)(2,1)S(1)}, u32[]{:S(2)}, u32[]{:S(2)}) collective-permute-start(bf16[8,48,128]{2,1,0:T(8,128)(2,1)S(1)} %get-tuple-element.27), channel_id=1, source_target_pairs={{0,1},{1,0},{2,3},{3,2},{4,5},{5,4},{6,7},{7,6},{8,9},{9,8},{10,11... | collective-permute-start | bytes 294920 | tf_op jit(solution)/shard_map/ppermute | solution.py:285
  6.9 2.6 %collective-permute-start.4 = (bf16[8,48,128]{2,1,0:T(8,128)(2,1)S(1)}, bf16[8,48,128]{2,1,0:T(8,128)(2,1)S(1)}, u32[]{:S(2)}, u32[]{:S(2)}) collective-permute-start(bf16[8,48,128]{2,1,0:T(8,128)(2,1)S(1)} %get-tuple-element.32), channel_id=1, source_target_pairs={{0,2},{1,3},{2,0},{3,1},{4,6},{5,7},{6,4},{7,5},{8,10},{9,11},{10,... | collective-permute-start | bytes 294920 | tf_op jit(solution)/shard_map/ppermute | solution.py:285
  9.5 0.2 collective-permute-start.5
  9.7 0.0 copy-done.2
  9.7 0.0 copy-done.5
  9.7 0.0 copy-done.6
  9.7 0.0 copy-start.1
  9.7 1.5 %prepare.1 = (bf16[5,576,256]{2,1,0:T(8,128)(2,1)S(1)}, f32[8,576]{1,0:T(8,128)S(1)}, f32[1,576]{1,0:T(1,128)S(1)}) custom-call(s32[32]{0:T(128)S(1)} %copy-done.6, f32[9,32]{1,0:T(8,128)S(1)} %bitcast.21, bf16[8,192,128]{2,1,0:T(8,128)(2,1)S(1)} %cast.1.own_ref, bf16[4,9,6,32,128]{4,3,2,1,0:T(8,128)(2,1)S(1)} %copy-done.2), custom_call_target="tpu_custom_call" | custom-call | flops 1000000000 | bytes 1048576 | tf_op jit(solution)/shard_map/prepare/pallas_call | solution.py:298
  11.3 0.0 collective-permute-done.1.refs_0_.rest_0_
  11.3 0.0 copy-done.1
  11.3 0.2 ahead.1
  11.5 0.1 collective-permute-start.3
  11.6 0.0 collective-permute-done.upper_ref
  11.6 0.0 copy-start.3
  11.6 0.0 copy-start.4
  11.6 1.3 %coefficients.1 = (bf16[128,576]{1,0:T(8,128)(2,1)S(1)}, bf16[8,160,128]{2,1,0:T(8,128)(2,1)S(1)}) custom-call(bf16[8,192,128]{2,1,0:T(8,128)(2,1)S(1)} %collective-permute-done.upper_ref, bf16[5,576,256]{2,1,0:T(8,128)(2,1)S(1)} %get-tuple-element.24.table_ref, f32[8,576]{1,0:T(8,128)S(1)} %get-tuple-element.25.e_ref, ...), custom_call_target="tpu_custom_call" | custom-call | flops 1000000000 | bytes 1048576 | tf_op jit(solution)/shard_map/coefficients/pallas_call | solution.py:298
  12.9 0.1 collective-permute-start.2
  13.0 0.0 copy-done.3
  13.0 0.0 copy-done.4
  13.0 2.2 %near_part.1.g_ref = f32[8,192,128]{2,1,0:T(8,128)S(1)} custom-call(s32[32]{0:T(128)S(1)} %copy-done.6, f32[8,192,128]{2,1,0:T(8,128)S(1)} %bitcast.17, f32[8,192,128]{2,1,0:T(8,128)S(1)} %bitcast.19, f32[192,128]{1,0:T(8,128)S(1)} %bitcast.20, bf16[128,576]{1,0:T(8,128)(2,1)S(1)} %get-tuple-element.29.w_ref, ...), custom_call_target="tpu_custom_call" | custom-call | flops 20000000000 | bytes 4194304 | tf_op jit(solution)/shard_map/near_part/pallas_call | solution.py:298
  15.3 0.9 %collective-permute-done.3.below_ref = bf16[8,32,128]{2,1,0:T(8,128)(2,1)S(1)} collective-permute-done((bf16[8,32,128]{2,1,0:T(8,128)(2,1)S(1)}, bf16[8,32,128]{2,1,0:T(8,128)(2,1)S(1)}, u32[]{:S(2)}, u32[]{:S(2)}) %collective-permute-start.3) | collective-permute-done | bytes 65568 | tf_op jit(solution)/shard_map/ppermute | solution.py:280
  16.1 4.2 %collective-permute-done.2.arrived_ref = bf16[8,160,128]{2,1,0:T(8,128)(2,1)S(1)} collective-permute-done((bf16[8,160,128]{2,1,0:T(8,128)(2,1)S(1)}, bf16[8,160,128]{2,1,0:T(8,128)(2,1)S(1)}, u32[]{:S(2)}, u32[]{:S(2)}) %collective-permute-start.2) | collective-permute-done | bytes 327712 | tf_op jit(solution)/shard_map/ppermute | solution.py:280
  20.4 0.1 finish.1
  20.5 3.7 %collective-permute-start.6 = (bf16[8,48,128]{2,1,0:T(8,128)(2,1)S(1)}, bf16[8,48,128]{2,1,0:T(8,128)(2,1)S(1)}, u32[]{:S(2)}, u32[]{:S(2)}) collective-permute-start(bf16[8,48,128]{2,1,0:T(8,128)(2,1)S(1)} %get-tuple-element.39), channel_id=1, source_target_pairs={{0,3},{1,2},{2,1},{3,0},{4,7},{5,6},{6,5},{7,4},{8,11},{9,10},{10,... | collective-permute-start | bytes 294920 | tf_op jit(solution)/shard_map/ppermute | solution.py:285
  24.2 0.0 collective-permute-start.7
  24.2 0.8 %collective-permute-start.8 = (bf16[8,48,128]{2,1,0:T(8,128)(2,1)S(1)}, bf16[8,48,128]{2,1,0:T(8,128)(2,1)S(1)}, u32[]{:S(2)}, u32[]{:S(2)}) collective-permute-start(bf16[8,48,128]{2,1,0:T(8,128)(2,1)S(1)} %get-tuple-element.41), channel_id=1, source_target_pairs={{0,1},{1,0},{2,3},{3,2},{4,5},{5,4},{6,7},{7,6},{8,9},{9,8},{10,11... | collective-permute-start | bytes 294920 | tf_op jit(solution)/shard_map/ppermute | solution.py:285
  25.0 0.0 collective-permute-done.4.rest_1_
  25.0 0.0 collective-permute-done.5.rest_2_
  25.0 0.8 %output.1 = (bf16[8,192,128]{2,1,0:T(8,128)(2,1)}, bf16[32,48,128]{2,1,0:T(8,128)(2,1)S(1)}) custom-call(f32[8,192,128]{2,1,0:T(8,128)S(1)} %near_part.1.g_ref, bf16[8,160,128]{2,1,0:T(8,128)(2,1)S(1)} %collective-permute-done.2.arrived_ref, bf16[8,32,128]{2,1,0:T(8,128)(2,1)S(1)} %collective-permute-done.3.below_ref, ...), custom_call_target="tpu_custom_call" | custom-call | tf_op jit(solution)/shard_map/output/pallas_call | solution.py:298
  25.8 0.1 copy.14
  25.9 1.4 %collective-permute-done.6 = bf16[8,48,128]{2,1,0:T(8,128)(2,1)S(1)} collective-permute-done((bf16[8,48,128]{2,1,0:T(8,128)(2,1)S(1)}, bf16[8,48,128]{2,1,0:T(8,128)(2,1)S(1)}, u32[]{:S(2)}, u32[]{:S(2)}) %collective-permute-start.6) | collective-permute-done | bytes 98336 | tf_op jit(solution)/shard_map/ppermute | solution.py:285
  27.3 2.5 %collective-permute-done.7 = bf16[8,48,128]{2,1,0:T(8,128)(2,1)S(1)} collective-permute-done((bf16[8,48,128]{2,1,0:T(8,128)(2,1)S(1)}, bf16[8,48,128]{2,1,0:T(8,128)(2,1)S(1)}, u32[]{:S(2)}, u32[]{:S(2)}) %collective-permute-start.7) | collective-permute-done | bytes 98336 | tf_op jit(solution)/shard_map/ppermute | solution.py:285
  29.8 0.0 collective-permute-done.8
  29.9 0.1 pad_maximum_fusion
  29.9 0.1 copy.13
  30.0 0.3 convolution_multiply_fusion.prod_ref
  30.4 0.2 split.1
  30.6 11.2 %all_to_all.5.got_ref = f32[32,1,64]{2,1,0:T(1,128)S(1)} all-to-all(f32[32,1,64]{2,1,0:T(1,128)S(1)} %split.1), channel_id=1, replica_groups=mesh['space'=8,'band'=4] {'space','band'}, dimensions={0} | all-to-all | bytes 16384 | tf_op jit(solution)/shard_map/all_to_all | solution.py:402
  41.8 0.7 %last_sum.1 = (f32[4,8]{1,0:T(4,128)}, f32[4,8]{1,0:T(4,128)}) custom-call(f32[32,1,64]{2,1,0:T(1,128)S(1)} %all_to_all.5.got_ref), custom_call_target="tpu_custom_call" | custom-call | tf_op jit(solution)/shard_map/last_sum/pallas_call | solution.py:298
  (2 shorter events, 0.1 us)
Async XLA Ops:
  0.6 1.1 %copy-start = (f32[8,6,32,128]{3,2,1,0:T(8,128)S(1)}, f32[8,6,32,128]{3,2,1,0:T(8,128)}, u32[]{:S(2)}) copy-start(f32[8,6,32,128]{3,2,1,0:T(8,128)} %param.6) | copy-start | bytes 2359300
  1.8 7.9 %copy-start.2 = (bf16[4,9,6,32,128]{4,3,2,1,0:T(8,128)(2,1)S(1)}, bf16[4,9,6,32,128]{4,3,2,1,0:T(8,128)(2,1)}, u32[]{:S(2)}) copy-start(bf16[4,9,6,32,128]{4,3,2,1,0:T(8,128)(2,1)} %proj_ref.3) | copy-start | bytes 5308420
  1.8 7.9 %copy-start.5 = (f32[32,9]{0,1:T(8,128)S(1)}, f32[32,9]{0,1:T(8,128)}, u32[]{:S(2)}) copy-start(f32[32,9]{0,1:T(8,128)} %param.10) | copy-start | bytes 3460
  1.8 7.9 %copy-start.6 = (s32[32]{0:T(128)S(1)}, s32[32]{0:T(128)}, u32[]{:S(2)}) copy-start(s32[32]{0:T(128)} %first_ref.3) | copy-start | bytes 388
  1.8 9.7 %collective-permute-start = (bf16[8,192,128]{2,1,0:T(8,128)(2,1)S(1)}, bf16[8,192,128]{2,1,0:T(8,128)(2,1)S(1)}, u32[]{:S(2)}, u32[]{:S(2)}) collective-permute-start(bf16[8,192,128]{2,1,0:T(8,128)(2,1)S(1)} %cast.1.own_ref), channel_id=1, source_target_pairs={{0,28},{4,0},{8,4},{12,8},{16,12},{20,16},{24,20},{28,24},{1,29},{... | collective-permute-start | bytes 1179656 | tf_op jit(solution)/shard_map/ppermute | solution.py:280
  5.3 6.0 %collective-permute-start.1 = (bf16[8,48,128]{2,1,0:T(8,128)(2,1)S(1)}, bf16[8,48,128]{2,1,0:T(8,128)(2,1)S(1)}, u32[]{:S(2)}, u32[]{:S(2)}) collective-permute-start(bf16[8,48,128]{2,1,0:T(8,128)(2,1)S(1)} %get-tuple-element.27), channel_id=1, source_target_pairs={{0,1},{1,0},{2,3},{3,2},{4,5},{5,4},{6,7},{7,6},{8,9},{9,8},{10,11... | collective-permute-start | bytes 294920 | tf_op jit(solution)/shard_map/ppermute | solution.py:285
  6.9 18.1 %collective-permute-start.4 = (bf16[8,48,128]{2,1,0:T(8,128)(2,1)S(1)}, bf16[8,48,128]{2,1,0:T(8,128)(2,1)S(1)}, u32[]{:S(2)}, u32[]{:S(2)}) collective-permute-start(bf16[8,48,128]{2,1,0:T(8,128)(2,1)S(1)} %get-tuple-element.32), channel_id=1, source_target_pairs={{0,2},{1,3},{2,0},{3,1},{4,6},{5,7},{6,4},{7,5},{8,10},{9,11},{10,... | collective-permute-start | bytes 294920 | tf_op jit(solution)/shard_map/ppermute | solution.py:285
  9.5 15.5 %collective-permute-start.5 = (bf16[8,48,128]{2,1,0:T(8,128)(2,1)S(1)}, bf16[8,48,128]{2,1,0:T(8,128)(2,1)S(1)}, u32[]{:S(2)}, u32[]{:S(2)}) collective-permute-start(bf16[8,48,128]{2,1,0:T(8,128)(2,1)S(1)} %get-tuple-element.33), channel_id=1, source_target_pairs={{0,3},{1,2},{2,1},{3,0},{4,7},{5,6},{6,5},{7,4},{8,11},{9,10},{10,... | collective-permute-start | bytes 294920 | tf_op jit(solution)/shard_map/ppermute | solution.py:285
  9.7 1.6 %copy-start.1 = (f32[8,6,32,128]{3,2,1,0:T(8,128)S(1)}, f32[8,6,32,128]{3,2,1,0:T(8,128)}, u32[]{:S(2)}) copy-start(f32[8,6,32,128]{3,2,1,0:T(8,128)} %param.6) | copy-start | bytes 2359300
  11.5 4.6 %collective-permute-start.3 = (bf16[8,32,128]{2,1,0:T(8,128)(2,1)S(1)}, bf16[8,32,128]{2,1,0:T(8,128)(2,1)S(1)}, u32[]{:S(2)}, u32[]{:S(2)}) collective-permute-start(bf16[8,32,128]{2,1,0:T(8,128)(2,1)S(1)} %get-tuple-element.31), channel_id=1, source_target_pairs={{0,4},{4,8},{8,12},{12,16},{16,20},{20,24},{24,28},{28,0},{1,5},{5... | collective-permute-start | bytes 196616 | tf_op jit(solution)/shard_map/ppermute | solution.py:280
  11.6 1.4 %copy-start.3 = (f32[8,6,32,128]{3,2,1,0:T(8,128)S(1)}, f32[8,6,32,128]{3,2,1,0:T(8,128)}, u32[]{:S(2)}) copy-start(f32[8,6,32,128]{3,2,1,0:T(8,128)} %param.7) | copy-start | bytes 2359300
  11.6 1.4 %copy-start.4 = (f32[6,32,128]{2,1,0:T(8,128)S(1)}, f32[6,32,128]{2,1,0:T(8,128)}, u32[]{:S(2)}) copy-start(f32[6,32,128]{2,1,0:T(8,128)} %param.8) | copy-start | bytes 294916
  12.9 7.5 %collective-permute-start.2 = (bf16[8,160,128]{2,1,0:T(8,128)(2,1)S(1)}, bf16[8,160,128]{2,1,0:T(8,128)(2,1)S(1)}, u32[]{:S(2)}, u32[]{:S(2)}) collective-permute-start(bf16[8,160,128]{2,1,0:T(8,128)(2,1)S(1)} %get-tuple-element.30), channel_id=1, source_target_pairs={{0,4},{4,8},{8,12},{12,16},{16,20},{20,24},{24,28},{28,0},{1,5},{5... | collective-permute-start | bytes 983048 | tf_op jit(solution)/shard_map/ppermute | solution.py:280
  20.5 6.8 %collective-permute-start.6 = (bf16[8,48,128]{2,1,0:T(8,128)(2,1)S(1)}, bf16[8,48,128]{2,1,0:T(8,128)(2,1)S(1)}, u32[]{:S(2)}, u32[]{:S(2)}) collective-permute-start(bf16[8,48,128]{2,1,0:T(8,128)(2,1)S(1)} %get-tuple-element.39), channel_id=1, source_target_pairs={{0,3},{1,2},{2,1},{3,0},{4,7},{5,6},{6,5},{7,4},{8,11},{9,10},{10,... | collective-permute-start | bytes 294920 | tf_op jit(solution)/shard_map/ppermute | solution.py:285
  24.2 5.6 %collective-permute-start.7 = (bf16[8,48,128]{2,1,0:T(8,128)(2,1)S(1)}, bf16[8,48,128]{2,1,0:T(8,128)(2,1)S(1)}, u32[]{:S(2)}, u32[]{:S(2)}) collective-permute-start(bf16[8,48,128]{2,1,0:T(8,128)(2,1)S(1)} %get-tuple-element.40), channel_id=1, source_target_pairs={{0,2},{1,3},{2,0},{3,1},{4,6},{5,7},{6,4},{7,5},{8,10},{9,11},{10,... | collective-permute-start | bytes 294920 | tf_op jit(solution)/shard_map/ppermute | solution.py:285
  24.2 5.7 %collective-permute-start.8 = (bf16[8,48,128]{2,1,0:T(8,128)(2,1)S(1)}, bf16[8,48,128]{2,1,0:T(8,128)(2,1)S(1)}, u32[]{:S(2)}, u32[]{:S(2)}) collective-permute-start(bf16[8,48,128]{2,1,0:T(8,128)(2,1)S(1)} %get-tuple-element.41), channel_id=1, source_target_pairs={{0,1},{1,0},{2,3},{3,2},{4,5},{5,4},{6,7},{7,6},{8,9},{9,8},{10,11... | collective-permute-start | bytes 294920 | tf_op jit(solution)/shard_map/ppermute | solution.py:285
